TPU v7x, 32 devices: a whole 2x2x4 slice. The times are simulated.
32 devices in a mesh: dp: 16 (over z, x, core), tensor: 2 (over y).
Axes of the slice: x: 2, y: 2, z: 4, core: 2. Of those that a mesh axis runs over, the one named last changes fastest.
Arguments:
- tokens: bfloat16 [64, 256, 768], P('dp'), may hold values from -6 to 6
- segment_ids: int32 [64, 256], P('dp'), may hold values from 0 to 3, never falling along the last dimension, each value on 1 to 128 neighbouring positions
- pass_embed: float32 [768], replicated, may hold values from -5 to 5
- w_qkv: bfloat16 [3, 768, 768], P(None, None, 'tensor'), may hold values from -0.21875 to 0.21875
- w_out: bfloat16 [768, 768], P('tensor'), may hold values from -0.75 to 0.75
- w_up: bfloat16 [768, 3072], P(None, 'tensor'), may hold values from -0.21875 to 0.21875
- w_down: bfloat16 [3072, 768], P('tensor'), may hold values from -0.109375 to 0.109375
- ln_gain: float32 [2, 768], replicated, may hold values from 0.5 to 1.5
- ln_bias: float32 [2, 768], replicated, may hold values from -1.5 to 1.5
- cotangent: bfloat16 [64, 512, 768], P('dp'), may hold values from -6 to 6
Outputs:
- out: bfloat16 [64, 512, 768], P('dp')
- grad_tokens: float32 [64, 256, 768], P('dp')
- grad_qkv: float32 [3, 768, 768], P(None, None, 'tensor')
- grad_out: float32 [768, 768], P('tensor')
- grad_up: float32 [768, 3072], P(None, 'tensor')
- grad_down: float32 [3072, 768], P('tensor')
- grad_gain: float32 [2, 768], replicated
- grad_bias: float32 [2, 768], replicated
- grad_pass: float32 [768], replicated
Inputs may be any that keep to these rules, and one draw needn't show every extreme that they name: `segment_ids`: along a row the ids never fall; a document holds at most 128 tokens and one in each row holds exactly 128.
All inputs are finite; a program needn't handle non-finite values.
Results may differ from a plain program's by a relative error of at most 0.019.
Values may be sent and summed in bfloat16 or wider, within the bound.
No kernel may reach another device: no remote copies, remote signals or barrier semaphores. Data moves between devices by JAX's collectives and lax.ppermute only.
A program may use at most 256 MiB of HBM per device.

v0:
```python
import functools

import jax
import jax.numpy as jnp
from jax import lax
from jax.experimental import pallas as pl
from jax.experimental.pallas import tpu as pltpu
from jax.sharding import Mesh
from jax.sharding import PartitionSpec as P

HD = 64
EPS = 1e-05
NEG = -1000000000.0
F32 = jnp.float32
BF16 = jnp.bfloat16
ROWS_OVER = ("o", "x", "core")
FLIP = ((0, 1), (1, 0))
VMEM_LIMIT = 60 * 1024 * 1024


def ordered(flag, mine, theirs):
    first = flag == 0
    return jnp.stack([jnp.where(first, mine, theirs), jnp.where(first, theirs, mine)])


def take_half(array, index):
    half = array.shape[0] // 2
    return lax.dynamic_slice_in_dim(array, index * half, half, 0)


def flip_bit(array, axis, size, bit):
    return lax.ppermute(array, axis, [(i, i ^ bit) for i in range(size)])


def steps_of(outer):
    steps = [("x", 2, 1)]
    bit = 1
    while bit < outer:
        steps.append(("o", outer, bit))
        bit *= 2
    return steps


def my_bit(axis, bit):
    return (lax.axis_index(axis) // bit) % 2


def dot(a, b):
    return lax.dot_general(a, b, (((1,), (0,)), ((), ())), preferred_element_type=F32)


def dot_nt(a, b):
    return lax.dot_general(a, b, (((1,), (1,)), ((), ())), preferred_element_type=F32)


def dot_tn(a, b):
    return lax.dot_general(a, b, (((0,), (0,)), ((), ())), preferred_element_type=F32)


def norm_stats(h):
    centred = h - jnp.mean(h, axis=-1, keepdims=True)
    inverse = lax.rsqrt(jnp.mean(centred * centred, axis=-1, keepdims=True) + EPS)
    return centred * inverse, inverse


def norm_back(grad, normal, inverse, gain):
    scaled = grad * gain
    centre = jnp.mean(scaled, axis=-1, keepdims=True)
    proj = jnp.mean(scaled * normal, axis=-1, keepdims=True)
    return inverse * (scaled - centre - normal * proj)


def gelu_parts(u):
    c = 0.7978845608028654
    a = 0.044715 * c
    square = u * u
    half = 0.5 + 0.5 * jnp.tanh(u * (c + a * square))
    g = u * half
    return g, half + g * (1.0 - half) * (2.0 * c + 6.0 * a * square)


def whole(shape):
    return pl.BlockSpec(shape, lambda *_: (0,) * len(shape))


def call(body, grid, ins, outs, scratch=(), cost=(0, 0), name=None, vmem=VMEM_LIMIT):
    return pl.pallas_call(
        body,
        grid=grid,
        in_specs=[s for _, s in ins],
        out_specs=[s for _, s in outs],
        out_shape=[a for a, _ in outs],
        scratch_shapes=scratch,
        compiler_params=pltpu.CompilerParams(
            dimension_semantics=("arbitrary",) * len(grid), vmem_limit_bytes=vmem
        ),
        cost_estimate=pl.CostEstimate(
            flops=int(cost[0]) // 16, bytes_accessed=int(cost[1]), transcendentals=0
        ),
        name=name,
    )(*[a for a, _ in ins])


FAR = pl.BlockSpec(memory_space=pl.ANY)


def resident(body, ins, outs, scratch=(), flops=0, vmem=16, aliases={}, name=None):
    spec = pl.BlockSpec(memory_space=pltpu.VMEM)
    ins, outs = ([o if isinstance(o, tuple) else (o, spec) for o in t] for t in (ins, outs))
    ins = [(pltpu.with_memory_space_constraint(a, pltpu.HBM) if s is FAR else a, s) for a, s in ins]
    outs = [(pltpu.HBM(a.shape, a.dtype) if s is FAR else a, s) for a, s in outs]
    return pl.pallas_call(
        body,
        in_specs=[s for _, s in ins],
        out_specs=[s for _, s in outs],
        out_shape=[a for a, _ in outs],
        scratch_shapes=scratch,
        input_output_aliases=aliases,
        compiler_params=pltpu.CompilerParams(vmem_limit_bytes=vmem * 1024 * 1024),
        cost_estimate=pl.CostEstimate(flops=int(flops) // 16, bytes_accessed=0, transcendentals=0),
        name=name,
    )(*[a for a, _ in ins])


def sds(shape, dtype):
    return jax.ShapeDtypeStruct(shape, dtype)


QB = 128
GROUP = 256


def lanes_of(ref, g):
    return ref.at[(slice(None),) * (len(ref.shape) - 1) + (pl.ds(pl.multiple_of(g * GROUP, GROUP), GROUP),)]


class Moves:
    def __init__(self, sems):
        self.sems, self.used = sems, 0

    def take(self, number):
        self.used += number
        return self.used - number

    def whole(self, source, target):
        copy = pltpu.make_async_copy(source, target, self.sems.at[self.take(1)])
        copy.start()
        return copy.wait

    def later(self, source, target):
        sem = self.sems.at[self.take(1)]
        copy = lambda: pltpu.make_async_copy(source, target, sem)
        return (lambda: copy().start()), (lambda: copy().wait())

    def groups(self, source, target):
        first = self.take(source.shape[-1] // GROUP)

        def copy(g):
            return pltpu.make_async_copy(lanes_of(source, g), lanes_of(target, g), self.sems.at[first + g])

        return (lambda g: copy(g).start()), (lambda g: copy(g).wait())


def cat_heads(t, scale=1.0):
    lane = lax.broadcasted_iota(jnp.int32, (1, 2 * HD), 1)
    parts = [t * jnp.where((lane < HD) == (h == 0), scale, 0.0).astype(t.dtype) for h in range(2)]
    return jnp.concatenate(parts, axis=0)


def own_lanes(t, scale=None):
    if scale is not None:
        t = t * scale
    return jnp.concatenate([t[:HD, :QB], t[HD:, QB:]], axis=0)


def twice(t):
    return jnp.concatenate([t, t], axis=1)


def pair_row(rows, p):
    return jnp.concatenate([rows[2 * p : 2 * p + 1], rows[2 * p + 1 : 2 * p + 2]], axis=1)


def put_pair(ref, p, cols, value):
    ref[2 * p : 2 * p + 1, cols] = value[:, :QB]
    ref[2 * p + 1 : 2 * p + 2, cols] = value[:, QB:]


def columns(t, r, seq, qb):
    return t[:, pl.ds(pl.multiple_of(r * seq + qb * QB, QB), QB)]


def rows_of(r, seq, qb):
    return pl.ds(pl.multiple_of(r * seq + qb * QB, QB), QB)


def in_turn(arrive, group, groups):
    for _, wait in arrive:
        wait(group)

    @pl.when(group + 2 < groups)
    def _():
        for start, _ in arrive:
            start(group + 2)


def attend_first_body(rows, seq, pairs, a_ref, w_ref, bias_ref, qkv_ref, o_ref, lse_ref):
    a = a_ref[...]
    for j in range(3):
        qkv_ref[j] = dot(a, w_ref[j]).astype(BF16)
    for r in range(rows):
        work = []
        for p in range(pairs):
            ln = slice(p * 2 * HD, (p + 1) * 2 * HD)
            k = qkv_ref[1, r * seq : (r + 1) * seq, ln]
            for b in range(seq // QB):
                sl, n = slice(r * seq + b * QB, r * seq + (b + 1) * QB), (b + 1) * QB
                q = cat_heads(qkv_ref[0, sl, ln], HD**-0.5)
                s = dot_nt(k[:n], q) + twice(bias_ref[r, :n, b * QB : n])
                work.append((p, ln, sl, n, s))
        done = []
        for p, ln, sl, n, s in work:
            top = jnp.max(s, axis=0, keepdims=True)
            e = jnp.exp(s - top)
            mass = jnp.sum(e, axis=0, keepdims=True)
            put_pair(lse_ref, p, sl, top + jnp.log(mass))
            done.append((e.astype(BF16), 1.0 / mass))
        for (p, ln, sl, n, _), (e, inv) in zip(work, done):
            vt = qkv_ref[2, r * seq : (r + 1) * seq, ln].T
            o_ref[sl, ln] = own_lanes(dot(vt[:, :n], e), inv).T.astype(BF16)


def attend_first(a, w, bias):
    rows, seq = bias.shape[0], bias.shape[1]
    n, d = a.shape
    f = w.shape[2]
    return resident(
        functools.partial(attend_first_body, rows, seq, f // (2 * HD)),
        (a, w, bias),
        [sds((3, n, f), BF16), sds((n, f), BF16), sds((f // HD, n), F32)],
        flops=6 * n * d * f + 16 * n * seq * f,
        name="attend_first",
    )


def attend_second_body(
    rows, seq, a_far, w_far, incl_far, strict_far, qkve_far, o1_far, lse1_ref,
    qkvo_far, o2_far, lse2_ref,
    a_ref, w_ref, incl_ref, strict_ref, qkve_ref, o1_ref, qkvo_ref, o2_ref, sems,
):
    groups = lse1_ref.shape[0]
    moves = Moves(sems)
    ready = [moves.whole(a_far, a_ref), moves.whole(w_far.at[0], w_ref.at[0])]
    arrive = [moves.groups(*t) for t in ((qkve_far, qkve_ref), (o1_far, o1_ref))]
    leave = moves.groups(o2_ref, o2_far)
    for wait in ready:
        wait()
    ready = [moves.whole(w_far.at[j], w_ref.at[j]) for j in (1, 2)]
    a = a_ref[...]
    sent = []
    for j in range(3):
        if j:
            ready[j - 1]()
        if j == 1:
            masks = [moves.whole(*t) for t in ((incl_far, incl_ref), (strict_far, strict_ref))]
            for g in range(2):
                for start, _ in arrive:
                    start(g)
        qkvo_ref[j] = dot(a, w_ref[j]).astype(BF16)
        sent.append(moves.whole(qkvo_ref.at[j], qkvo_far.at[j]))
    for wait in masks:
        wait()

    def next_group(group):
        in_turn(arrive, group, groups)

    def row(i, _):
        r, group = i % rows, i // rows
        lanes = pl.multiple_of(group * GROUP, GROUP)
        all_of = pl.ds(pl.multiple_of(r * seq, seq), seq)

        @pl.when(r == 0)
        def _():
            next_group(group)

        for p in range(GROUP // (2 * HD)):
            ln = pl.ds(lanes + p * 2 * HD, 2 * HD)
            ke, ko = qkve_ref[1, all_of, ln], qkvo_ref[1, all_of, ln]
            vte, vto = qkve_ref[2, all_of, ln].T, qkvo_ref[2, all_of, ln].T
            work = []
            for b in range(seq // QB):
                sl, n = rows_of(r, seq, b), (b + 1) * QB
                cols = slice(b * QB, n)
                incl, strict = twice(incl_ref[r, :n, cols]), twice(strict_ref[r, :n, cols])
                q = cat_heads(qkve_ref[0, sl, ln], HD**-0.5)
                work.append([dot_nt(ko[:n], q) + strict])
                q = cat_heads(qkvo_ref[0, sl, ln], HD**-0.5)
                work.append([dot_nt(ko[:n], q) + incl, dot_nt(ke[:n], q) + incl])
            for b in range(seq // QB):
                sl, n = rows_of(r, seq, b), (b + 1) * QB
                (s,), (so, se) = work[2 * b : 2 * b + 2]
                old = pair_row(lse1_ref[group, :, sl], p)
                top = jnp.maximum(old, jnp.max(s, axis=0, keepdims=True))
                e = jnp.exp(s - top)
                kept = jnp.exp(old - top)
                mass = kept + jnp.sum(e, axis=0, keepdims=True)
                work[2 * b] = (e.astype(BF16), kept, 1.0 / mass)
                put_pair(lse2_ref.at[0, group], p, sl, top + jnp.log(mass))
                top = jnp.max(jnp.maximum(se, so), axis=0, keepdims=True)
                ee, eo = jnp.exp(se - top), jnp.exp(so - top)
                mass = jnp.sum(ee + eo, axis=0, keepdims=True)
                work[2 * b + 1] = (ee.astype(BF16), eo.astype(BF16), 1.0 / mass)
                put_pair(lse2_ref.at[1, group], p, sl, top + jnp.log(mass))
            for b in range(seq // QB):
                sl, n = rows_of(r, seq, b), (b + 1) * QB
                (e, kept, inv), (ee, eo, inv2) = work[2 * b : 2 * b + 2]
                o1 = o1_ref[sl, ln].astype(F32).T
                o = own_lanes(dot(vto[:, :n], e), inv) + own_lanes(twice(o1), kept * inv)
                o2_ref[0, sl, ln] = o.T.astype(BF16)
                o = dot(vte[:, :n], ee) + dot(vto[:, :n], eo)
                o2_ref[1, sl, ln] = own_lanes(o, inv2).T.astype(BF16)

        @pl.when(r == rows - 1)
        def _():
            leave[0](group)

        return 0

    lax.fori_loop(0, rows * groups, row, 0)
    for wait in sent:
        wait()
    for g in range(groups):
        leave[1](g)


def attend_second(a, w, incl, strict, qkve, o1, lse1):
    rows, seq = incl.shape[0], incl.shape[1]
    n, d = a.shape
    f = w.shape[2]
    qkv, o2 = sds((3, n, f), BF16), sds((2, n, f), BF16)
    near = (a, w, incl, strict, qkve, o1, qkv, o2)
    return resident(
        functools.partial(attend_second_body, rows, seq),
        [(t, FAR) for t in (a, w, incl, strict, qkve, o1)] + [lse1],
        [(qkv, FAR), (o2, FAR), sds((2, *lse1.shape), F32)],
        scratch=[pltpu.VMEM(t.shape, t.dtype) for t in near] + [pltpu.SemaphoreType.DMA((32,))],
        flops=6 * n * d * f + 48 * n * seq * f,
        vmem=32,
        name="attend_second",
    )


def row_products(a, b):
    prod = cat_heads((a * b).astype(BF16))
    return dot_nt(jnp.ones((8, 2 * HD), BF16), prod)[:1]


def query_parts(sl, ln, group, p, i, qkv_ref, o_ref, lse_ref, do_ref):
    do = do_ref[i, sl, ln]
    delta = row_products(do.astype(F32), o_ref[i, sl, ln].astype(F32))
    return cat_heads(qkv_ref[0, sl, ln], HD**-0.5), cat_heads(do), pair_row(lse_ref[i, group, :, sl], p), delta


def blocks_back(tasks):
    scores = [dot_nt(k, q) + bias - lse for k, _, _, bias, q, _, lse, _ in tasks]
    moved = [dot_nt(v, do) - delta for _, v, _, _, _, do, _, delta in tasks]
    probs = [jnp.exp(s) for s in scores]
    ds = [(p * m).astype(BF16) for p, m in zip(probs, moved)]
    return [
        (dot(p.astype(BF16), do), dot(d, q), dot(kt, d))
        for (_, _, kt, _, q, do, _, _), p, d in zip(tasks, probs, ds)
    ]


def add_rows(total, part):
    if total is None:
        return part
    n = part.shape[0]
    return jnp.concatenate([total[:n] + part, total[n:]], axis=0)


def attend_back_body(
    rows, seq, w_far, incl_far, strict_far, qkve_far, qkvo_far, o2_far, lse2_ref, do_far,
    dh1_far, ho_far, gb_ref,
    dqkvo_far, dqkve_far, dy_far, sums_ref,
    w_ref, incl_ref, strict_ref, qkve_ref, qkvo_ref, o2_ref, do_ref, dh1_ref, ho_ref,
    dqkvo_ref, dqkve_ref, da_ref, dy_ref, sems,
):
    groups = lse2_ref.shape[1]
    moves = Moves(sems)
    arrive = [
        moves.groups(*t)
        for t in ((qkve_far, qkve_ref), (qkvo_far, qkvo_ref), (o2_far, o2_ref), (do_far, do_ref))
    ]
    leave = [moves.groups(*t) for t in ((dqkvo_ref, dqkvo_far), (dqkve_ref, dqkve_far))]
    for start, _ in arrive:
        start(0)
    masks = [moves.whole(*t) for t in ((incl_far, incl_ref), (strict_far, strict_ref))]
    for start, _ in arrive:
        start(1)
    odd = pl.ds(rows * seq, rows * seq)
    late = [moves.later(*t) for t in ((w_far, w_ref), (dh1_far.at[odd], dh1_ref), (ho_far, ho_ref))]
    for wait in masks:
        wait()

    def next_group(group):
        in_turn(arrive, group, groups)

        @pl.when(group == groups - 2)
        def _():
            for start, _ in late:
                start()

    sc = HD**-0.5

    def row(i, _):
        r, group = i % rows, i // rows
        lanes = pl.multiple_of(group * GROUP, GROUP)
        all_of = pl.ds(pl.multiple_of(r * seq, seq), seq)

        @pl.when(r == 0)
        def _():
            next_group(group)

        for p in range(GROUP // (2 * HD)):
            ln = pl.ds(lanes + p * 2 * HD, 2 * HD)
            ke, ve = qkve_ref[1, all_of, ln], qkve_ref[2, all_of, ln]
            ko, vo = qkvo_ref[1, all_of, ln], qkvo_ref[2, all_of, ln]
            kte, kto = ke.T, ko.T
            tasks = []
            for b in reversed(range(seq // QB)):
                sl, n = rows_of(r, seq, b), (b + 1) * QB
                cols = slice(b * QB, n)
                incl, strict = twice(incl_ref[r, :n, cols]), twice(strict_ref[r, :n, cols])
                even = query_parts(sl, ln, group, p, 0, qkve_ref, o2_ref, lse2_ref, do_ref)
                odd = query_parts(sl, ln, group, p, 1, qkvo_ref, o2_ref, lse2_ref, do_ref)
                tasks.append((ko[:n], vo[:n], kto[:, :n], strict, *even))
                tasks.append((ko[:n], vo[:n], kto[:, :n], incl, *odd))
                tasks.append((ke[:n], ve[:n], kte[:, :n], incl, *odd))
            done = blocks_back(tasks)
            dke = dve = dko = dvo = None
            for b in reversed(range(seq // QB)):
                sl = rows_of(r, seq, b)
                (dv, dk, dqe), (dv2, dk2, dqo), (dv3, dk3, dqo2) = done[:3]
                done = done[3:]
                dvo, dko = add_rows(dvo, dv + dv2), add_rows(dko, dk + dk2)
                dve, dke = add_rows(dve, dv3), add_rows(dke, dk3)
                dqkve_ref[0, sl, ln] = (own_lanes(dqe).T * sc).astype(BF16)
                dqkvo_ref[0, sl, ln] = (own_lanes(dqo + dqo2).T * sc).astype(BF16)
            dqkve_ref[1, all_of, ln] = dke.astype(BF16)
            dqkve_ref[2, all_of, ln] = dve.astype(BF16)
            dqkvo_ref[1, all_of, ln] = dko.astype(BF16)
            dqkvo_ref[2, all_of, ln] = dvo.astype(BF16)

        @pl.when(r == rows - 1)
        def _():
            for start, _ in leave:
                start(group)

        return 0

    lax.fori_loop(0, rows * groups, row, 0)
    for _, wait in late:
        wait()
    da = dot_nt(dqkvo_ref[0], w_ref[0])
    da += dot_nt(dqkvo_ref[1], w_ref[1])
    da += dot_nt(dqkvo_ref[2], w_ref[2])
    da_ref[...] = da
    sums_ref[...] = jnp.zeros_like(sums_ref)

    def finish(i, _):
        sl = pl.ds(pl.multiple_of(i * ROWS_AT_ONCE, ROWS_AT_ONCE), ROWS_AT_ONCE)
        normal, inverse = norm_stats(ho_ref[sl])
        da = da_ref[sl]
        dy = dh1_ref[sl] + norm_back(da, normal, inverse, gb_ref[0:1])
        dy_ref[sl] = dy
        for k, t in enumerate((da * normal, da, dy)):
            sums_ref[k : k + 1] += jnp.sum(t, axis=0, keepdims=True)
        return 0

    lax.fori_loop(0, rows * seq // ROWS_AT_ONCE, finish, 0)
    kept = [moves.whole(dy_ref, dy_far)]
    for g in range(groups):
        for _, wait in leave:
            wait(g)
    for wait in kept:
        wait()


def attend_back(w, incl, strict, qkve, qkvo, o2, lse2, do, dh1, ho, gb):
    rows, seq = incl.shape[0], incl.shape[1]
    n, d = ho.shape
    f = w.shape[2]
    do = do.reshape(2, n, f)
    qkv = sds((3, n, f), BF16)
    near = (w, incl, strict, qkve, qkvo, o2, do, sds((n, d), F32), ho, qkv, qkv, sds((n, d), F32))
    return resident(
        functools.partial(attend_back_body, rows, seq),
        [(t, FAR) for t in (w, incl, strict, qkve, qkvo, o2)]
        + [lse2]
        + [(t, FAR) for t in (do, dh1, ho)]
        + [gb],
        [(qkv, FAR), (qkv, FAR), (sds((n, d), F32), FAR), sds((3, d), F32)],
        scratch=[pltpu.VMEM(t.shape, t.dtype) for t in near + (sds((n, d), F32),)] + [pltpu.SemaphoreType.DMA((32,))],
        flops=6 * n * d * f + 120 * n * seq * f,
        vmem=44,
        name="attend_back",
    )


def attend_back_even_body(
    rows, seq, w_far, incl_far, qkve_far, o1_far, lse1_ref, do1_far, o2_far, lse2_ref, do2_far,
    part_far, dh1_far, dh2_far, x_far, gb_ref,
    dqkv_far, gt_ref, sums_ref,
    w_ref, incl_ref, qkve_ref, o1_ref, do1_ref, o2_ref, do2_ref, part_ref, dh1_ref, dh2_ref, x_ref,
    dqkv_ref, da_ref, sems,
):
    groups = lse1_ref.shape[0]
    moves = Moves(sems)
    even = pl.ds(0, rows * seq)
    arrive = [
        moves.groups(*t)
        for t in (
            (qkve_far, qkve_ref), (o1_far, o1_ref), (do1_far, do1_ref), (o2_far.at[0], o2_ref),
            (do2_far.at[0], do2_ref), (part_far, part_ref),
        )
    ]
    leave = [moves.groups(dqkv_ref, dqkv_far)]
    for start, _ in arrive:
        start(0)
    mask = moves.whole(incl_far, incl_ref)
    for start, _ in arrive:
        start(1)
    late = [
        moves.later(*t)
        for t in ((w_far, w_ref), (dh1_far, dh1_ref), (dh2_far.at[even], dh2_ref), (x_far, x_ref))
    ]
    mask()

    def next_group(group):
        in_turn(arrive, group, groups)

        @pl.when(group == groups - 2)
        def _():
            for start, _ in late:
                start()

    sc = HD**-0.5

    def row(i, _):
        r, group = i % rows, i // rows
        lanes = pl.multiple_of(group * GROUP, GROUP)
        all_of = pl.ds(pl.multiple_of(r * seq, seq), seq)

        @pl.when(r == 0)
        def _():
            next_group(group)

        for p in range(GROUP // (2 * HD)):
            ln = pl.ds(lanes + p * 2 * HD, 2 * HD)
            k, v = qkve_ref[1, all_of, ln], qkve_ref[2, all_of, ln]
            kt = k.T
            tasks = []
            for b in reversed(range(seq // QB)):
                sl, n = rows_of(r, seq, b), (b + 1) * QB
                incl = twice(incl_ref[r, :n, b * QB : n])
                lse1 = pair_row(lse1_ref[group, :, sl], p)
                ratio = jnp.exp(lse1 - pair_row(lse2_ref[0, group, :, sl], p))
                do1, do2 = do1_ref[sl, ln].astype(F32), do2_ref[sl, ln].astype(F32)
                delta = row_products(do1, o1_ref[sl, ln].astype(F32))
                delta += ratio * row_products(do2, o2_ref[sl, ln].astype(F32))
                both = do1 + own_lanes(twice(do2.T), ratio).T
                q, do = cat_heads(qkve_ref[0, sl, ln], sc), cat_heads(both.astype(BF16))
                tasks.append((k[:n], v[:n], kt[:, :n], incl, q, do, lse1, delta))
            dka = dva = None
            for b, (dv, dk, dq) in zip(reversed(range(seq // QB)), blocks_back(tasks)):
                sl = rows_of(r, seq, b)
                dva, dka = add_rows(dva, dv), add_rows(dka, dk)
                dqkv_ref[0, sl, ln] = (own_lanes(dq).T * sc + part_ref[0, sl, ln].astype(F32)).astype(BF16)
            dqkv_ref[1, all_of, ln] = (dka + part_ref[1, all_of, ln].astype(F32)).astype(BF16)
            dqkv_ref[2, all_of, ln] = (dva + part_ref[2, all_of, ln].astype(F32)).astype(BF16)

        @pl.when(r == rows - 1)
        def _():
            for start, _ in leave:
                start(group)

        return 0

    lax.fori_loop(0, rows * groups, row, 0)
    for _, wait in late:
        wait()
    da = dot_nt(dqkv_ref[0], w_ref[0])
    da += dot_nt(dqkv_ref[1], w_ref[1])
    da += dot_nt(dqkv_ref[2], w_ref[2])
    da_ref[...] = da
    sums_ref[...] = jnp.zeros_like(sums_ref)

    def finish(i, _):
        sl = pl.ds(pl.multiple_of(i * ROWS_AT_ONCE, ROWS_AT_ONCE), ROWS_AT_ONCE)
        normal, inverse = norm_stats(x_ref[sl].astype(F32))
        da = da_ref[sl]
        sums_ref[0:1] += jnp.sum(da * normal, axis=0, keepdims=True)
        sums_ref[1:2] += jnp.sum(da, axis=0, keepdims=True)
        back = norm_back(da, normal, inverse, gb_ref[0:1])
        gt_ref[sl] = (dh1_ref[sl] + dh2_ref[sl] + back).astype(BF16)
        return 0

    lax.fori_loop(0, rows * seq // ROWS_AT_ONCE, finish, 0)
    for g in range(groups):
        for _, wait in leave:
            wait(g)


def attend_back_even(w, incl, qkve, o1, lse1, do1, o2, lse2, do2, part, dh1, dh2, x, gb):
    rows, seq = incl.shape[0], incl.shape[1]
    n, d = x.shape
    f = w.shape[2]
    qkv, one = sds((3, n, f), BF16), sds((n, f), BF16)
    near = (w, incl, qkv, one, one, one, one, qkv, dh1, dh1, x, qkv, sds((n, d), F32))
    far = lambda *ts: [(t, FAR) for t in ts]
    return resident(
        functools.partial(attend_back_even_body, rows, seq),
        far(w, incl, qkve, o1)
        + [lse1]
        + far(do1, o2)
        + [lse2]
        + far(do2.reshape(2, n, f), part, dh1, dh2, x)
        + [gb],
        [(qkv, FAR), sds((n, d), BF16), sds((2, d), F32)],
        scratch=[pltpu.VMEM(t.shape, t.dtype) for t in near] + [pltpu.SemaphoreType.DMA((32,))],
        flops=6 * n * d * f + 40 * n * seq * f,
        vmem=40,
        name="attend_back_even",
    )


CHUNK = 512
ROWS_AT_ONCE = 256


def chunk_of(ref, j, axis):
    at = pl.ds(pl.multiple_of(j * CHUNK, CHUNK), CHUNK)
    return ref.at[:, at] if axis else ref.at[at]


class Chunks:
    def __init__(self, moves, far, near, axis, ring=False, leave=False):
        self.first = moves.take(far.shape[axis] // CHUNK)
        self.sems, self.far, self.near = moves.sems, far, near
        self.axis, self.ring, self.leave = axis, ring, leave

    def copy(self, j):
        near = self.near.at[j % self.near.shape[0]] if self.ring else chunk_of(self.near, j, self.axis)
        ends = (chunk_of(self.far, j, self.axis), near)
        return pltpu.make_async_copy(*(ends[::-1] if self.leave else ends), self.sems.at[self.first + j])

    def start(self, j):
        self.copy(j).start()

    def wait(self, j):
        self.copy(j).wait()


class Weight:
    def __init__(self, moves, pieces, near, axis):
        self.axis, self.near = axis, near
        self.own = Chunks(moves, pieces[0], near, axis) if pieces[0] is not None else None
        self.number = near.shape[axis] // CHUNK // 2
        self.others, start = [], near.shape[axis] // 2
        for far in pieces[1:]:
            at = pl.ds(start, far.shape[axis])
            self.others.append(moves.later(far, near.at[:, at] if axis else near.at[at]))
            start += far.shape[axis]

    def start_others(self):
        for start, _ in self.others:
            start()

    def wait_others(self):
        for _, wait in self.others:
            wait()


def load_in_turn(j, *weights):
    number = weights[0].number

    @pl.when(j < number)
    def _():
        for w in weights:
            w.own.wait(j)

    @pl.when(j + 2 < number)
    def _():
        for w in weights:
            w.own.start(j + 2)

    @pl.when(j + 2 == number)
    def _():
        for w in weights:
            w.start_others()

    @pl.when(j == number)
    def _():
        for w in weights:
            w.wait_others()


def start_loads(*weights):
    for j in range(2):
        for w in weights:
            w.own.start(j)


def feed_chunk(n2_ref, wup_ref, wdown_ref, j, g_buf, d_buf, ho_ref, gs, ds, first):
    @pl.when(first >= 2)
    def _():
        gs.wait(j - 2)
        ds.wait(j - 2)

    half = n2_ref.shape[0] // 2
    parts = []
    for sl in (slice(0, half), slice(half, 2 * half)):
        g, d = gelu_parts(dot(n2_ref[sl], chunk_of(wup_ref, j, 1)[...]))
        parts.append(g.astype(BF16))
        g_buf[j % 2, sl] = parts[-1]
        d_buf[j % 2, sl] = d.astype(BF16)
    gs.start(j)
    ds.start(j)
    for i, g in enumerate(parts):
        ho_ref[i * half : (i + 1) * half] += dot(g, chunk_of(wdown_ref, j, 0)[...])


def start_norm(x_ref, h1_ref, n2_ref, gb_ref, ho_ref=None):
    def part(k, _):
        sl = pl.ds(pl.multiple_of(k * ROWS_AT_ONCE, ROWS_AT_ONCE), ROWS_AT_ONCE)
        h1 = x_ref[sl].astype(F32) + h1_ref[sl]
        h1_ref[sl] = h1
        normal, _ = norm_stats(h1)
        n2_ref[sl] = (normal * gb_ref[1:2] + gb_ref[3:4]).astype(BF16)
        if ho_ref is not None:
            ho_ref[sl] = h1 + gb_ref[4:5]
        return 0

    lax.fori_loop(0, h1_ref.shape[0] // ROWS_AT_ONCE, part, 0)


def mlp_own_body(
    x_far, o_far, wout_far, gb_ref, wup_far, wdown_far,
    h1_far, n2_far, g_far, d_far, ho_far,
    x_ref, o_ref, wout_ref, wup_ref, wdown_ref, h1_ref, n2_ref, ho_ref, g_buf, d_buf, sems,
):
    moves = Moves(sems)
    first = [moves.whole(*t) for t in ((o_far, o_ref), (wout_far, wout_ref), (x_far, x_ref))]
    ups, downs = Chunks(moves, wup_far, wup_ref, 1), Chunks(moves, wdown_far, wdown_ref, 0)
    gs, ds = (Chunks(moves, f, b, 1, True, True) for f, b in ((g_far, g_buf), (d_far, d_buf)))
    number = wup_far.shape[1] // CHUNK
    for wait in first:
        wait()
    for j in range(number):
        ups.start(j)
        downs.start(j)
    h1_ref[...] = dot(o_ref[...], wout_ref[...])
    start_norm(x_ref, h1_ref, n2_ref, gb_ref, ho_ref)
    kept = [moves.whole(*t) for t in ((h1_ref, h1_far), (n2_ref, n2_far))]

    def step(j, _):
        ups.wait(j)
        downs.wait(j)
        feed_chunk(n2_ref, wup_ref, wdown_ref, j, g_buf, d_buf, ho_ref, gs, ds, j)
        return 0

    lax.fori_loop(0, number, step, 0)
    kept.append(moves.whole(ho_ref, ho_far))
    for wait in kept:
        wait()
    for j in range(number - 2, number):
        gs.wait(j)
        ds.wait(j)


def mlp_other_body(number_up, number_down, n2_far, part_far, g_in, d_in, gb_ref, *refs):
    ups_far, refs = refs[:number_up], refs[number_up:]
    downs_far, refs = refs[:number_down], refs[number_down:]
    g_far, d_far, ho_far, ao_far, n2_ref, wup_ref, wdown_ref, ho_ref, ao_ref, g_buf, d_buf, sems = refs
    moves = Moves(sems)
    up = Weight(moves, (None,) + ups_far, wup_ref, 1)
    down = Weight(moves, (None,) + downs_far, wdown_ref, 0)
    gs, ds = (Chunks(moves, f, b, 1, True, True) for f, b in ((g_far, g_buf), (d_far, d_buf)))
    ready = [moves.whole(*t) for t in ((n2_far, n2_ref), (part_far, ho_ref))]
    up.start_others()
    down.start_others()
    for wait in ready:
        wait()
    up.wait_others()
    down.wait_others()

    def step(i, _):
        feed_chunk(n2_ref, wup_ref, wdown_ref, up.number + i, g_buf, d_buf, ho_ref, gs, ds, i)
        return 0

    lax.fori_loop(0, up.number, step, 0)
    sent = moves.whole(ho_ref, ho_far)

    def norm(k, _):
        sl = pl.ds(pl.multiple_of(k * ROWS_AT_ONCE, ROWS_AT_ONCE), ROWS_AT_ONCE)
        normal, _ = norm_stats(ho_ref[sl])
        ao_ref[sl] = (normal * gb_ref[0:1] + gb_ref[2:3]).astype(BF16)
        return 0

    lax.fori_loop(0, ho_ref.shape[0] // ROWS_AT_ONCE, norm, 0)
    moves.whole(ao_ref, ao_far)()
    sent()
    for j in range(2 * up.number - 2, 2 * up.number):
        gs.wait(j)
        ds.wait(j)


def near_of(*arrays):
    return [pltpu.VMEM(t.shape, t.dtype) for t in arrays]


def far_of(*arrays):
    return [(t, FAR) for t in arrays]


def mlp_own(x, o, wout, gb, wup, wdown):
    n, d = x.shape
    ff = 2 * wup.shape[1]
    h1, low, wide = sds((n, d), F32), sds((n, d), BF16), sds((n, ff), BF16)
    return resident(
        mlp_own_body,
        far_of(x, o, wout) + [gb] + far_of(wup, wdown),
        far_of(h1, low, wide, wide, h1),
        scratch=near_of(x, o, wout, wup, wdown, h1, low, h1)
        + [pltpu.VMEM((2, n, CHUNK), BF16)] * 2
        + [pltpu.SemaphoreType.DMA((40,))],
        vmem=36,
        name="mlp_own",
    )


def mlp_other(n2, part, g, dgelu, gb, ups, downs):
    n, d = n2.shape
    ff = g.shape[1]
    return resident(
        functools.partial(mlp_other_body, len(ups), len(downs)),
        far_of(n2, part, g, dgelu) + [gb] + far_of(*ups, *downs),
        far_of(sds(g.shape, BF16), sds(g.shape, BF16), sds(part.shape, F32), sds(n2.shape, BF16)),
        scratch=near_of(n2, sds((d, ff), BF16), sds((ff, d), BF16), part, n2)
        + [pltpu.VMEM((2, n, CHUNK), BF16)] * 2
        + [pltpu.SemaphoreType.DMA((40,))],
        vmem=40,
        aliases={2: 0, 3: 1},
        name="mlp_other",
    )


def weave(seq):
    i = lax.broadcasted_iota(jnp.int32, (2 * seq, 2 * seq), 0)
    k = lax.broadcasted_iota(jnp.int32, (2 * seq, 2 * seq), 1)
    place = jnp.where(k < seq, 2 * k, 2 * (k - seq) + 1)
    return jnp.where(i == place, 1.0, 0.0).astype(BF16)


def after_norm_back(
    moves, size, h1_ref, dn_ref, db_ref, wout_ref, gb_ref, sums_ref, dp_ref, do_ref, dh1_far, dp_far, do_far
):
    gain_sum = jnp.zeros_like(gb_ref[0:1])
    bias_sum = jnp.zeros_like(gb_ref[0:1])
    waits = []
    for i in range(h1_ref.shape[0] // size):
        sl = slice(i * size, (i + 1) * size)
        normal, inverse = norm_stats(h1_ref[sl])
        dn = dn_ref[sl]
        gain_sum += jnp.sum(dn * normal, axis=0, keepdims=True)
        bias_sum += jnp.sum(dn, axis=0, keepdims=True)
        dh1 = db_ref[sl].astype(F32) + norm_back(dn, normal, inverse, gb_ref[1:2])
        dn_ref[sl] = dh1
        dp_ref[sl] = dh1.astype(BF16)
    sums_ref[0:1] = gain_sum
    sums_ref[1:2] = bias_sum
    waits += [moves.whole(dn_ref, dh1_far), moves.whole(dp_ref, dp_far)]
    do_ref[...] = dot_nt(dp_ref[...], wout_ref[...]).astype(BF16)
    return waits + [moves.whole(do_ref, do_far)]


def mlp_second_body(rows, seq, number_up, number_down, x_far, ho_far, o_far, cot_far, wout_far, gb_ref, *refs):
    mlp_second_work(rows, seq, x_far, ho_far, o_far, cot_far, wout_far, gb_ref, *in_pieces(refs, number_up, number_down))


def in_pieces(refs, *numbers):
    out = []
    for k in numbers:
        out.append(refs[:k])
        refs = refs[k:]
    return out + list(refs)


def mlp_second_work(
    rows, seq, x_far, ho_far, o_far, cot_far, wout_far, gb_ref, ups_far, downs_far,
    outs_far, outs2_far, n2_far, g_far, du_far, dh1_far, dp_far, do_far, sums_ref, dm_far,
    x_ref, ho_ref, o_ref, cot_ref, wout_ref, wup_ref, wdown_ref, n2_ref, dm_ref,
    h1_ref, z_ref, dn_ref, dp_ref, do_ref, g_buf, du_buf, sems,
):
    n = rows * seq
    moves = Moves(sems)
    halves = (slice(0, n), slice(n, 2 * n))
    cot_there = moves.whole(cot_far, cot_ref)
    first = [moves.whole(*t) for t in ((o_far, o_ref), (wout_far, wout_ref), (x_far, x_ref))]
    up, down = Weight(moves, ups_far, wup_ref, 1), Weight(moves, downs_far, wdown_ref, 0)
    gs, dus = (Chunks(moves, f, b, 1, True, True) for f, b in ((g_far, g_buf), (du_far, du_buf)))
    number = 2 * up.number
    mix = weave(seq)
    cot_there()
    for r in range(rows):
        parted = dot_tn(mix, cot_ref[r]).astype(BF16)
        for i in range(2):
            dm_ref[i * n + r * seq : i * n + (r + 1) * seq] = parted[i * seq : (i + 1) * seq]
    for wait in first:
        wait()
    then = moves.whole(ho_far, ho_ref)
    start_loads(up, down)
    for i, sl in enumerate(halves):
        if i:
            then()
        h1_ref[sl] = dot(o_ref[i], wout_ref[...])
        start_norm(x_ref if i == 0 else ho_ref, h1_ref.at[pl.ds(i * n, n)], n2_ref.at[pl.ds(i * n, n)], gb_ref)
    kept = [moves.whole(*t) for t in ((n2_ref, n2_far), (dm_ref, dm_far))]
    z_ref[...] = jnp.zeros_like(z_ref)
    dn_ref[...] = jnp.zeros_like(dn_ref)

    def step(j, _):
        load_in_turn(j, up, down)

        @pl.when(j >= 2)
        def _():
            gs.wait(j - 2)
            dus.wait(j - 2)

        for sl in halves:
            u = dot(n2_ref[sl], chunk_of(wup_ref, j, 1)[...])
            dg = dot_nt(dm_ref[sl], chunk_of(wdown_ref, j, 0)[...])
            g, d = gelu_parts(u)
            g = g.astype(BF16)
            du = (dg * d).astype(BF16)
            g_buf[j % 2, sl] = g
            du_buf[j % 2, sl] = du
            z_ref[sl] += dot(g, chunk_of(wdown_ref, j, 0)[...])
            dn_ref[sl] += dot_nt(du, chunk_of(wup_ref, j, 1)[...])
        gs.start(j)
        dus.start(j)
        return 0

    lax.fori_loop(0, number, step, 0)
    for r in range(rows):
        pair = [slice(i * n + r * seq, i * n + (r + 1) * seq) for i in range(2)]
        z = jnp.concatenate([(h1_ref[s] + z_ref[s]).astype(BF16) for s in pair], axis=0)
        cot_ref[r] = dot(mix, z).astype(BF16)
    half = rows // 2
    kept += [moves.whole(cot_ref.at[pl.ds(i * half, half)], far) for i, far in enumerate((outs_far, outs2_far))]
    kept += after_norm_back(
        moves, seq, h1_ref, dn_ref, dm_ref, wout_ref, gb_ref, sums_ref, dp_ref, do_ref, dh1_far, dp_far, do_far
    )
    for wait in kept:
        wait()
    for j in range(number - 2, number):
        gs.wait(j)
        dus.wait(j)


def mlp_second(x, ho, o2, cot, wout, gb, ups, downs, seq):
    n, d = x.shape
    ff = 2 * ups[0].shape[1]
    rows = n // seq
    low, wide, full = sds((2 * n, d), BF16), sds((2 * n, ff), BF16), sds((2 * n, d), F32)
    out = sds((rows // 2, 2 * seq, d), BF16)
    return resident(
        functools.partial(mlp_second_body, rows, seq, len(ups), len(downs)),
        far_of(x, ho, o2, cot, wout) + [gb] + far_of(*ups, *downs),
        far_of(out, out, low, wide, wide, full, low, low) + [sds((2, d), F32)] + far_of(low),
        scratch=near_of(x, ho, o2, cot, wout, sds((d, ff), BF16), sds((ff, d), BF16), low, low, full, full, full, low, low)
        + [pltpu.VMEM((2, 2 * n, CHUNK), BF16)] * 2
        + [pltpu.SemaphoreType.DMA((64,))],
        vmem=60,
        name="mlp_second",
    )


def mlp_back_body(rows, seq, number_up, number_down, dy_far, h1_far, wout_far, gb_ref, d_far, *refs):
    mlp_back_work(rows, seq, dy_far, h1_far, wout_far, gb_ref, d_far, *in_pieces(refs, number_up, number_down))


def mlp_back_work(
    rows, seq, dy_far, h1_far, wout_far, gb_ref, d_far, ups_far, downs_far,
    du_far, dh1_far, dp_far, do_far, sums_ref,
    dy_ref, h1_ref, wout_ref, wup_ref, wdown_ref, d_ref, dm_ref, dn_ref, dp_ref, do_ref, du_buf, sems,
):
    moves = Moves(sems)
    first = moves.whole(dy_far, dy_ref)
    up, down = Weight(moves, ups_far, wup_ref, 1), Weight(moves, downs_far, wdown_ref, 0)
    ds, dus = Chunks(moves, d_far, d_ref, 1), Chunks(moves, du_far, du_buf, 1, True, True)
    number = 2 * up.number
    start_loads(down, up)
    for j in range(2):
        ds.start(j)
    then = [moves.later(*t) for t in ((wout_far, wout_ref), (h1_far, h1_ref))]
    first()
    dm_ref[...] = dy_ref[...].astype(BF16)
    dn_ref[...] = jnp.zeros_like(dn_ref)

    def step(j, _):
        load_in_turn(j, down, up)
        ds.wait(j)

        @pl.when(j + 2 < number)
        def _():
            ds.start(j + 2)

        @pl.when(j + 2 == number)
        def _():
            for start, _ in then:
                start()

        @pl.when(j >= 2)
        def _():
            dus.wait(j - 2)

        dg = dot_nt(dm_ref[...], chunk_of(wdown_ref, j, 0)[...])
        du = (dg * chunk_of(d_ref, j, 1)[...].astype(F32)).astype(BF16)
        du_buf[j % 2] = du
        dus.start(j)
        dn_ref[...] += dot_nt(du, chunk_of(wup_ref, j, 1)[...])
        return 0

    lax.fori_loop(0, number, step, 0)
    for _, wait in then:
        wait()
    kept = after_norm_back(
        moves, seq, h1_ref, dn_ref, dy_ref, wout_ref, gb_ref, sums_ref, dp_ref, do_ref, dh1_far, dp_far, do_far
    )
    for wait in kept:
        wait()
    for j in range(number - 2, number):
        dus.wait(j)


def mlp_back(dy, h1, wout, gb, dgelu, ups, downs, seq):
    n, d = dy.shape
    ff = dgelu.shape[1]
    low = sds((n, d), BF16)
    return resident(
        functools.partial(mlp_back_body, n // seq, seq, len(ups), len(downs)),
        far_of(dy, h1, wout) + [gb] + far_of(dgelu, *ups, *downs),
        far_of(dgelu, h1, low, low) + [sds((2, d), F32)],
        scratch=near_of(dy, h1, wout, sds((d, ff), BF16), sds((ff, d), BF16), dgelu, low, dy, low, low)
        + [pltpu.VMEM((2, n, CHUNK), BF16)]
        + [pltpu.SemaphoreType.DMA((48,))],
        vmem=48,
        name="mlp_back",
    )


def lanes_at(ref, start, size):
    return ref.at[:, pl.ds(pl.multiple_of(start, 128), size)]


def stack_rows(moves, pairs, target, start, size):
    copies, row = [], 0
    for far in pairs:
        copies.append(moves.later(lanes_at(far, start, size), target.at[pl.ds(row, far.shape[0])]))
        row += far.shape[0]
    return (lambda: [s() for s, _ in copies]), (lambda: [w() for _, w in copies])


def all_of(*parts):
    return (lambda: [s() for s, _ in parts]), (lambda: [w() for _, w in parts])


class InTurn:
    def __init__(self, *tiles):
        self.tiles, self.at = tiles, 0
        for start, _ in tiles[:2]:
            start()

    def next(self):
        self.tiles[self.at][1]()
        self.at += 1
        if self.at + 1 < len(self.tiles):
            self.tiles[self.at + 1][0]()


def place_of(quarter, y, me_ref):
    return quarter if y else 4 + (quarter ^ me_ref[1])


def packed(body, me, arrays, shape, scratch, flops, vmem, name):
    smem = pl.BlockSpec(memory_space=pltpu.SMEM)
    out = sds(shape, BF16)
    return resident(
        body,
        [(me, smem)] + far_of(*arrays),
        far_of(out, out),
        scratch=near_of(sds((2,) + shape, BF16)) + scratch + [pltpu.SemaphoreType.DMA((64,))],
        flops=flops,
        vmem=vmem,
        name=name,
    )


def grad_down_body(
    me_ref, g1_far, g2_far, dy_far, dm2_far, keep_far, go_far, out_ref, dy_ref, dm_ref, g_ref, acc_ref, sems
):
    low, group = me_ref[0] % 4, (me_ref[0] // 4) % 2
    ring, n, b = g_ref.shape[0], g1_far.shape[0], g_ref.shape[2]
    moves = Moves(sems)
    first, last = moves.take(2 * ring), moves.take(4)

    def tile(i):
        side, y, h = 1 - i // 4, (i // 2) % 2, i % 2
        quarter = ((me_ref[0] // 8) ^ side) * 2 + h
        at = jnp.where(y == 0, 4 + (quarter ^ me_ref[1]), quarter) * b
        return side, y, h, at

    def loads(i):
        at, slot = tile(i)[3], i % ring
        near = g_ref.at[slot]
        ends = ((g1_far, near.at[pl.ds(0, n)]), (g2_far, near.at[pl.ds(n, 2 * n)]))
        return [pltpu.make_async_copy(lanes_at(f, at, b), t, sems.at[first + 2 * slot + k]) for k, (f, t) in enumerate(ends)]

    def store(far, side, y):
        return pltpu.make_async_copy(out_ref.at[side, y], far.at[y], sems.at[last + side * 2 + y])

    ready = [moves.whole(dy_far, dy_ref), moves.whole(dm2_far, dm_ref.at[pl.ds(n, 2 * n)])]
    for i in range(2):
        for c in loads(i):
            c.start()
    for wait in ready:
        wait()
    dm_ref[:n] = dy_ref[...].astype(BF16)

    def step(i, _):
        side, y, h, _ = tile(i)
        for c in loads(i):
            c.wait()

        @pl.when(i + 2 < 8)
        def _():
            for c in loads(i + 2):
                c.start()

        acc_ref[...] = dot_tn(g_ref[i % ring], dm_ref[...]).reshape(acc_ref.shape)
        for s in range(4):
            out_ref[side, y, (h ^ group) * 4 + s] = acc_ref[s ^ low].astype(BF16)

        @pl.when((h == 1) & (side == 1))
        def _():
            store(go_far, 1, y).start()

        @pl.when((h == 1) & (side == 0))
        def _():
            store(keep_far, 0, y).start()

        return 0

    lax.fori_loop(0, 8, step, 0)
    for y in range(2):
        store(go_far, 1, y).wait()
        store(keep_far, 0, y).wait()


def grad_down(me, g1, g2, dy, dm2):
    n, d = dy.shape
    ff = g1.shape[1]
    b = ff // 8
    return packed(
        grad_down_body,
        me,
        (g1, g2, dy, dm2),
        (2, 8, b // 4, d),
        [
            pltpu.VMEM((n, d), F32),
            pltpu.VMEM((3 * n, d), BF16),
            pltpu.VMEM((3, 3 * n, b), BF16),
            pltpu.VMEM((4, b // 4, d), F32),
        ],
        2 * 3 * n * d * ff,
        40,
        "grad_down",
    )


CUT = 768


def put_slots(out_ref, y, lanes, acc_ref, me):
    for s in range(16):
        out_ref[s // 8, y, s % 8, :, lanes] = acc_ref[s ^ me].astype(BF16)


def grad_up_body(
    me_ref, n1_far, n2_far, du1_far, du2_far, dp1_far, dp2_far, o1_far, o2_far, keep_far, go_far,
    out_ref, n_ref, t_ref, du_ref, dp_ref, o_ref, acc_ref, acc2_ref, sems,
):
    moves = Moves(sems)
    d, f = n_ref.shape[1], o_ref.shape[2]
    ring, c, n = du_ref.shape[0], du_ref.shape[2], du1_far.shape[0]
    first, last = moves.take(4 * ring), moves.take(4)

    def loads(i):
        y, t, slot = i // 2, i % 2, i % ring
        copies = []
        for k in range(2):
            quarter = 2 * t + k
            at = jnp.where(y == 0, 4 + (quarter ^ me_ref[1]), quarter) * f
            near = lanes_at(du_ref.at[slot], k * f, f)
            for far, rows in ((du1_far, pl.ds(0, n)), (du2_far, pl.ds(n, 2 * n))):
                copies.append((lanes_at(far, at, f), near.at[rows]))
        return [pltpu.make_async_copy(a, b, sems.at[first + 4 * slot + k]) for k, (a, b) in enumerate(copies)]

    def stores(y):
        return [
            pltpu.make_async_copy(out_ref.at[i, y], far.at[y], sems.at[last + 2 * y + i])
            for i, far in enumerate((keep_far, go_far))
        ]

    ready = stack_rows(moves, (n1_far, n2_far), n_ref, 0, d)
    ready[0]()
    for c0 in loads(0):
        c0.start()
    out_loads = [stack_rows(moves, (dp1_far, dp2_far), dp_ref, 0, d)]
    out_loads += [stack_rows(moves, (o1_far, o2_far), o_ref.at[y], (1 - y) * f, f) for y in range(2)]
    ready[1]()
    for c0 in loads(1):
        c0.start()
    t_ref[...] = n_ref[...].T

    def step(i, _):
        y, t = i // 2, i % 2
        for c0 in loads(i):
            c0.wait()

        @pl.when(i + 2 < 4)
        def _():
            for c0 in loads(i + 2):
                c0.start()

        @pl.when(i == 0)
        def _():
            for start, _ in out_loads:
                start()

        acc_ref[...] = dot(t_ref[...], du_ref[i % ring]).reshape(acc_ref.shape)
        put_slots(out_ref, y, pl.ds(pl.multiple_of(t * c, c), c), acc_ref, jnp.where(t == 0, me_ref[0], me_ref[2]))

        @pl.when(i == 1)
        def _():
            for _, wait in out_loads:
                wait()

        @pl.when(t == 1)
        def _():
            acc2_ref[...] = dot_tn(dp_ref[...], o_ref[y]).reshape(acc2_ref.shape)
            put_slots(out_ref, y, slice(2 * c, 2 * c + f), acc2_ref, me_ref[2])
            for s in stores(y):
                s.start()

        return 0

    lax.fori_loop(0, 4, step, 0)
    for y in range(2):
        for s in stores(y):
            s.wait()


def grad_up(me, n1, n2, du1, du2, dp1, dp2, o1, o2):
    n, d = n1.shape
    ff = du1.shape[1]
    f, c = o1.shape[1] // 2, ff // 4
    return packed(
        grad_up_body,
        me,
        (n1, n2, du1, du2, dp1, dp2, o1, o2),
        (2, 8, d // 16, 2 * c + f),
        [
            pltpu.VMEM((3 * n, d), BF16),
            pltpu.VMEM((d, 3 * n), BF16),
            pltpu.VMEM((3, 3 * n, c), BF16),
            pltpu.VMEM((3 * n, d), BF16),
            pltpu.VMEM((2, 3 * n, f), BF16),
            pltpu.VMEM((16, d // 16, c), F32),
            pltpu.VMEM((16, d // 16, f), F32),
        ],
        2 * 3 * n * d * (ff + d),
        56,
        "grad_up",
    )


def grad_qkv_body(me_ref, ae_far, ao_far, de_far, do_far, keep_far, go_far, out_ref, a_ref, t_ref, d_ref, acc_ref, sems):
    moves = Moves(sems)
    d = a_ref.shape[1]
    f = de_far.shape[2] // 2
    ready = stack_rows(moves, (ae_far, ao_far), a_ref, 0, d)
    tiles = [stack_rows(moves, (de_far.at[j], do_far.at[j]), d_ref.at[j], 0, 2 * f) for j in range(3)]
    ready[0]()
    for start, _ in tiles[:2]:
        start()
    ready[1]()
    tiles[2][0]()
    t_ref[...] = a_ref[...].T
    for _, wait in tiles:
        wait()

    def step(j, _):
        acc_ref[...] = dot(t_ref[...], d_ref[j]).reshape(acc_ref.shape)
        lanes = pl.ds(pl.multiple_of(j * f, f), f)
        for s in range(16):
            block = acc_ref[s ^ me_ref[0]].astype(BF16)
            out_ref[s // 8, 1, s % 8, :, lanes] = block[:, :f]
            out_ref[s // 8, 0, s % 8, :, lanes] = block[:, f:]
        return 0

    lax.fori_loop(0, 3, step, 0)
    sent = [moves.whole(out_ref.at[i], far) for i, far in ((1, go_far), (0, keep_far))]
    for wait in sent:
        wait()


def grad_qkv(me, ae, ao, dqkv_e, dqkv_o):
    n, d = ae.shape
    f = dqkv_e.shape[2] // 2
    return packed(
        grad_qkv_body,
        me,
        (ae, ao, dqkv_e, dqkv_o),
        (2, 8, d // 16, 3 * f),
        [
            pltpu.VMEM((2 * n, d), BF16),
            pltpu.VMEM((d, 2 * n), BF16),
            pltpu.VMEM((3, 2 * n, 2 * f), BF16),
            pltpu.VMEM((16, d // 16, 2 * f), F32),
        ],
        2 * 2 * 3 * n * d * 2 * f,
        40,
        "grad_qkv",
    )


def packed_call(body, grid, me, ins, outs, scratch=(), flops=0, aliases={}, name=None):
    return pl.pallas_call(
        body,
        grid_spec=pltpu.PrefetchScalarGridSpec(
            num_scalar_prefetch=1,
            grid=grid,
            in_specs=[s for _, s in ins],
            out_specs=[s for _, s in outs],
            scratch_shapes=scratch,
        ),
        out_shape=[a for a, _ in outs],
        input_output_aliases=aliases,
        compiler_params=pltpu.CompilerParams(
            dimension_semantics=("arbitrary",) * len(grid), vmem_limit_bytes=VMEM_LIMIT
        ),
        cost_estimate=pl.CostEstimate(flops=int(flops) // 16, bytes_accessed=0, transcendentals=0),
        name=name,
    )(me, *[a for a, _ in ins])


def unpack_body(kind, me_ref, part_ref, *refs):
    low = me_ref[0] % 8
    rows, width = part_ref.shape[1:]
    first = refs[-2] if kind == "up" else refs[-1]
    if kind == "up":
        first, second, wide = refs[-3:]
    for s in range(8):
        sl = slice(s * rows, (s + 1) * rows)
        if kind == "down":
            first[sl] = part_ref[s ^ low].astype(F32)
        elif kind == "up":
            f = first.shape[1]
            other = s ^ (me_ref[2] % 8)
            first[sl, :CUT] = part_ref[s ^ low, :, :CUT].astype(F32)
            first[sl, CUT:] = part_ref[other, :, CUT:f].astype(F32)
            wide[sl] = part_ref[other, :, f:].astype(F32)
        else:
            f = width // 3
            for j in range(3):
                first[j, sl] = part_ref[s ^ low, :, j * f : (j + 1) * f].astype(F32)
    if kind == "up":
        second[...] = wide[...].T


def unpack(kind, me, side, part, into=()):
    _, r, w = part.shape
    half = 8 * r
    at = lambda me: (me[0] // 8) ^ side
    scratch = []
    if kind == "down":
        outs = [(sds((2 * half, w), F32), pl.BlockSpec((half, w), lambda i, me: (at(me), 0)))]
    elif kind == "up":
        f = half
        outs = [
            (sds((2 * half, w - f), F32), pl.BlockSpec((half, w - f), lambda i, me: (at(me), 0))),
            (sds((f, 2 * half), F32), pl.BlockSpec((f, half), lambda i, me: (0, at(me)))),
        ]
        scratch = [pltpu.VMEM((half, f), F32)]
    else:
        f = w // 3
        outs = [(sds((3, 2 * half, f), F32), pl.BlockSpec((3, half, f), lambda i, me: (0, at(me), 0)))]
    ins = [(part, pl.BlockSpec(part.shape, lambda i, me: (0, 0, 0)))]
    ins += [(t, pl.BlockSpec(memory_space=pl.ANY)) for t in into]
    return packed_call(
        functools.partial(unpack_body, kind),
        (1,),
        me,
        ins,
        outs,
        scratch=scratch,
        aliases={2 + i: i for i in range(len(into))},
        name="unpack_" + kind,
    )


def fold(*parts):
    return sum(p.astype(F32) for p in parts).astype(BF16)


def after(value, *first):
    return lax.optimization_barrier((value, first))[0]


class Chunk:
    def __init__(self, keep, got):
        self.keep, self.got = keep, got
        self.sent = None

    def wait(self, *also):
        self.got, also = lax.optimization_barrier((self.got, also))
        return also

    def to_partner(self):
        total = fold(self.keep, self.got)
        self.keep, self.sent = total[1], total[0]
        self.got = lax.ppermute(self.sent, "tensor", FLIP)

    def gather_core(self):
        self.got = lax.ppermute(self.keep, "core", FLIP)


class Hops(Chunk):
    def __init__(self, outer, keep, got):
        super().__init__(keep, got)
        self.axes = {"x": ("x", 2, 1), "z": ("o", outer, 1), "w": ("o", outer, 2)}
        self.extra = [("o", outer, 1 << b) for b in range(2, outer.bit_length() - 1)]

    def send(self, *parts):
        self.keep, self.sent, self.got = [], [], []
        for total, way in parts:
            if way == "partner":
                keep, sent = total[1], total[0]
                got = lax.ppermute(sent, "tensor", FLIP)
            else:
                half = total.shape[-3] // 2
                keep, sent = total[..., :half, :, :], total[..., half:, :, :]
                got = flip_bit(sent, *self.axes[way])
            self.keep.append(keep)
            self.sent.append(sent)
            self.got.append(got)

    def folded(self):
        return [fold(k, g) for k, g in zip(self.keep, self.got)]

    def first(self):
        total = fold(self.keep, self.got)
        self.send((total[..., :CUT], "x"), (total[..., CUT:], "z"))

    def hop(self, *ways):
        self.send(*zip(self.folded(), ways))

    def first_hop(self, way):
        self.send((fold(self.keep, self.got), way))

    def last_hop(self):
        self.send((jnp.concatenate(self.folded(), axis=-1), "w"))

    def back(self, *ways):
        self.sent = self.keep
        self.got = [flip_bit(k, *self.axes[w]) for k, w in zip(self.keep, ways)]

    def back_first(self):
        (total,) = self.folded()
        for s in self.extra:
            total = fold(total, flip_bit(total, *s))
        self.keep = [total]
        self.back("w")

    def joined(self, parts=1):
        self.keep = [jnp.concatenate([k, g], axis=0) for k, g in zip(self.keep, self.got)]
        if parts == 2:
            (total,) = self.keep
            self.keep = [total[..., :CUT], total[..., CUT:]]

    def back_core(self):
        self.joined()
        self.keep = self.sent = jnp.concatenate(self.keep, axis=-1)
        self.gather_core()


def mask_biases(seg):
    seq = seg.shape[1]
    place = jnp.arange(seq, dtype=jnp.int32)
    same = seg[:, :, None] == seg[:, None, :]
    below = (place[:, None] < place[None, :])[None]
    incl = (place[:, None] <= place[None, :])[None]
    bias = lambda m: jnp.where(same & m, 0.0, NEG).astype(F32)
    return bias(incl), bias(below)


def sync(*values):
    return lax.optimization_barrier(values)


class Link:
    def __init__(self, outer, w_qkv, w_out, w_up, w_down):
        self.outer = outer
        self.own = (w_qkv, w_out, w_up, w_down)
        self.core_at, self.x_at, o = (lax.axis_index(a) for a in ("core", "x", "o"))
        bits = {"x": self.x_at, "z": o % 2, "w": (o // 2) % 2}
        self.fetch_bits = self.core_at * 2 + self.x_at
        slots = []
        for order in ("xzw", "zxw"):
            slot = self.core_at
            for name in order:
                slot = slot * 2 + bits[name]
            slots.append(slot)
        self.me = jnp.stack([slots[0], self.fetch_bits, slots[1]]).astype(jnp.int32)
        self.me_z = self.me[2:0:-1]

    def quarter(self, own):
        flat = own.reshape(-1, own.shape[-1])
        return take_half(take_half(flat, self.core_at), self.x_at)

    def over_x(self, t):
        return lax.ppermute(t, "x", FLIP)

    def fetch(self, own_work):
        own = self.own
        size = own[2].shape[1] // 4
        part = lambda t, axis, bits: lax.dynamic_slice_in_dim(t, bits * size, size, axis)
        pieces = [
            self.quarter(own[1]),
            part(own[2], 1, self.fetch_bits),
            jnp.concatenate([part(own[3], 0, self.fetch_bits), part(own[3], 0, self.fetch_bits ^ 1)], axis=0),
        ]
        qkv = self.partner(self.quarter(own[0]))
        up, out, down = (self.partner(pieces[i]) for i in (1, 0, 2))
        qkv, own_work = sync(qkv, own_work)
        qkv, out, up = sync(ordered(self.x_at, qkv, self.over_x(qkv)).reshape(-1, qkv.shape[-1]), out, up)
        qkv_core, out_x, up_x = self.core(qkv), self.over_x(out), self.over_x(up)
        qkv = ordered(self.core_at, qkv, qkv_core).reshape(own[0].shape)

        def join_out(*work):
            nonlocal out, out_x
            work, out, out_x = sync(work, out, out_x)
            out = ordered(self.x_at, out, out_x).reshape(-1, out.shape[-1])
            out = ordered(self.core_at, out, self.core(out)).reshape(own[1].shape)
            return work, jnp.concatenate([own[1], out], axis=0)

        def pieces_of(*work):
            up_there, down_there, work = sync(up_x, down, work)
            ups = (own[2], up, up_there, self.core(up), self.core(up_there))
            return ups, (own[3], down_there, self.core(down_there)), work

        return own_work, own[0], qkv, jnp.concatenate([own[0], qkv], axis=2), join_out, pieces_of

    def partner(self, t):
        return lax.ppermute(t, "tensor", FLIP)

    def core(self, t):
        return lax.ppermute(t, "core", FLIP)

    def chunk(self, keep, got):
        return Chunk(keep, got)

    def hops(self, keep, got):
        return Hops(self.outer, keep, got)

    def small_steps(self):
        return [("core", 2, 1), ("tensor", 2, 1)] + steps_of(self.outer)

    def flip(self, t, step):
        return flip_bit(t, *step)


def local_part(x, seg, cot, gb, link):
    rows, seq = seg.shape
    n, width = x.shape
    me, me_z = link.me, link.me_z
    incl, strict = mask_biases(seg)
    normal, _ = norm_stats(x.astype(F32))
    a_e = (normal * gb[0] + gb[2]).astype(BF16)
    first = attend_first(a_e, link.own[0], incl)
    (a_e, first, cot), wq_own, fetched, wqkv, join_out, pieces_of = link.fetch((a_e, first, cot))
    second = attend_first(a_e, fetched, incl)
    qkv_e, o1 = (jnp.concatenate([s, t], axis=-1) for s, t in zip(first[:2], second[:2]))
    lse1 = jnp.concatenate([first[2], second[2]], axis=0).reshape(-1, GROUP // HD, n)
    (qkv_e, o1, lse1, wqkv), wout = join_out(qkv_e, o1, lse1, wqkv)
    h1, n2_1, g1, d1, part_one = mlp_own(x, o1, wout, gb, link.own[2], link.own[3])
    ups, downs, (n2_1, part_one) = pieces_of(n2_1, part_one)
    g1, d1, ho, a_o = mlp_other(n2_1, part_one, g1, d1, gb, ups[1:], downs[1:])
    qkv_o, o2, lse2 = attend_second(a_o, wqkv, incl, strict, qkv_e, o1, lse1)
    out, out_two, n2_2, g2, du2, dh1_2, dp2, do2, sums2, dm2 = mlp_second(x, ho, o2, cot, wout, gb, ups, downs, seq)
    out_got = link.partner(out)
    dqkv_o, part, dy, sums_o = attend_back(wqkv, incl, strict, qkv_e, qkv_o, o2, lse2, do2, dh1_2, ho, gb)
    o2_flat = o2.reshape(2 * n, width)

    out_got, dy = sync(out_got, dy)
    out_last = link.partner(after(out_two, out_got))
    down_keep, down_go = grad_down(me_z, g1, g2, dy, dm2)
    down_keep, down_go, out_last = sync(down_keep, down_go, out_last)
    down = link.hops(down_keep, link.core(down_go))
    dy = after(dy, down_go)
    du1, dh1_1, dp1, do1, sums1 = mlp_back(dy, h1, wout, gb, d1, ups, downs, seq)
    du1, dp1, do1 = down.wait(du1, dp1, do1)
    down.to_partner()
    up_keep, up_go = grad_up(me, n2_1, n2_2, after(du1, down.sent), du2, dp1, dp2, o1, o2_flat)
    do1 = after(do1, up_go)
    dqkv_e, gt, sums_e = attend_back_even(wqkv, incl, qkv_e, o1, lse1, do1, o2, lse2, do2, part, dh1_1, dh1_2, x, gb)
    dqkv_e, gt, sums_e, up_go = down.wait(dqkv_e, gt, sums_e, up_go)
    up = link.hops(up_keep, link.core(up_go))
    down.first_hop("z")
    small = jnp.stack([sums_e[0] + sums_o[0], sums1[0] + sums2[0], sums_e[1] + sums_o[1], sums1[1] + sums2[1], sums_o[2]])
    qkv_keep, qkv_go = grad_qkv(me_z, a_e, a_o, after(dqkv_e, *down.sent), dqkv_o)
    qkv_keep, qkv_go, down.got = up.wait(qkv_keep, qkv_go, down.got)
    qkv = link.hops(qkv_keep, link.core(qkv_go))
    small_steps = iter(link.small_steps())
    small_got = link.flip(after(small, qkv_go), next(small_steps))

    def wait_all(with_down=True):
        nonlocal small, small_got
        (qkv.got, small_got, *rest) = up.wait(qkv.got, small_got, *([down.got] if with_down else []))
        if rest:
            (down.got,) = rest
        if small_got is not None:
            small = small + small_got
            step = next(small_steps, None)
            small_got = None if step is None else link.flip(small, step)

    wait_all(False)
    up.first()
    qkv.first_hop("partner")
    down.hop("x")
    wait_all()
    up.hop("partner", "x")
    qkv.hop("z")
    down.hop("w")
    wait_all()
    up.hop("z", "partner")
    qkv.hop("x")
    down.back_first()
    half = gt.shape[0] // 2
    gt_got = [link.partner(after(gt[:half], *up.sent))]
    wait_all()
    up.last_hop()
    qkv.hop("w")
    down.joined()
    down.back("x")
    gt_got.append(link.partner(after(gt[half:], *up.sent)))
    (gt_got[0],) = up.wait(gt_got[0])
    wait_all()
    up.back_first()
    qkv.back_first()
    down.joined()
    down.back("z")
    (gt_got[1],) = up.wait(gt_got[1])
    wait_all()
    while small_got is not None:
        wait_all()
    up.joined(2)
    up.back("z", "x")
    qkv.joined()
    qkv.back("x")
    down.back_core()
    out, gt, *_ = link.finish(jnp.concatenate([out, out_two], axis=0), jnp.concatenate([out_got, out_last], axis=0), gt, jnp.concatenate(gt_got, axis=0))
    out, gt = up.wait(out, gt)
    wait_all()
    up.joined()
    up.back("x", "z")
    qkv.joined()
    qkv.back("z")
    (g_down,) = unpack("down", me_z, 0, after(down.keep, up.sent, qkv.sent))
    (g_down,) = unpack("down", me_z, 1, down.got, (g_down,))
    g_down, qkv.got = up.wait(g_down, qkv.got)
    up.back_core()
    qkv.back_core()
    g_up = unpack("up", me, 0, after(up.keep, qkv.sent))
    (g_qkv,) = unpack("qkv", me_z, 0, after(qkv.keep, g_up))
    (g_qkv,) = up.wait(g_qkv)
    g_up, g_out = unpack("up", me, 1, up.got, g_up)
    qkv.wait(g_up)
    (g_qkv,) = unpack("qkv", me_z, 1, qkv.got, (g_qkv,))
    return out, gt, (g_qkv, g_out, g_up, g_down), small


def shards(outer, tokens, segments, pass_embed, w_qkv, w_out, w_up, w_down, gain, bias, cotangent):
    ty = lax.axis_index("tensor")
    rows = tokens.shape[0] // 2
    width = tokens.shape[2]
    mine = lambda t: lax.dynamic_slice_in_dim(t, ty * rows, rows, 0)
    x = mine(tokens).reshape(-1, width)
    gb = jnp.concatenate([gain, bias, pass_embed[None]], axis=0)
    link = Link(outer, w_qkv, w_out, w_up, w_down)
    link.finish = lambda out, out_got, gt, gt_got: (
        ordered(ty, out, out_got).reshape(cotangent.shape),
        ordered(ty, gt, gt_got).reshape(tokens.shape).astype(F32),
    )
    out, gt, grads, small = local_part(x, mine(segments), mine(cotangent), gb, link)
    return out, gt, *grads, small[0:2], small[2:4], small[4]


def solution(mesh):
    outer = mesh.shape["dp"] // 4
    fine = Mesh(mesh.devices.reshape(outer, 2, 2, mesh.shape["tensor"]), ("o", "x", "core", "tensor"))
    rows = ROWS_OVER
    placed = (
        P(rows, None, None),
        P(rows, None),
        P(),
        P(None, None, "tensor"),
        P("tensor", None),
        P(None, "tensor"),
        P("tensor", None),
        P(),
        P(),
        P(rows, None, None),
    )

    def body(*args):
        return shards(outer, *args)

    return jax.shard_map(
        body,
        mesh=fine,
        in_specs=placed,
        out_specs=(
            P(rows, None, None),
            P(rows, None, None),
            P(None, None, "tensor"),
            P("tensor", None),
            P(None, "tensor"),
            P("tensor", None),
            P(),
            P(),
            P(),
        ),
        check_vma=False,
    )
```

profile of v0, /device:TPU:0, one launch (start us, length us, event | category | flops | bytes accessed | tf_op | source)
XLA Modules:
  0.0 384.9 jit_solution(5696669441335623860)
XLA Ops:
  0.7 2.0 constant_dynamic-slice_fusion.7
  2.7 3.0 collective-permute-start
  10.0 2.4 attend_first.2
  16.2 1.7 collective-permute-start.1
  17.9 1.9 constant_dynamic-slice_fusion.2
  19.8 1.5 collective-permute-start.3
  22.9 5.0 %collective-permute-done.1 = bf16[576,384]{1,0:T(8,128)(2,1)} collective-permute-done((bf16[576,384]{1,0:T(8,128)(2,1)}, bf16[576,384]{1,0:T(8,128)(2,1)}, u32[]{:S(2)}, u32[]{:S(2)}) %collective-permute-start.1) | collective-permute-done | bytes 442400 | tf_op jit(solution)/shard_map/ppermute | solution.py:1545
  30.1 7.1 %collective-permute-done.2 = bf16[96,768]{1,0:T(8,128)(2,1)} collective-permute-done((bf16[96,768]{1,0:T(8,128)(2,1)S(1)}, bf16[96,768]{1,0:T(8,128)(2,1)}, u32[]{:S(2)}, u32[]{:S(2)}) %collective-permute-start.2) | collective-permute-done | bytes 147488 | tf_op jit(solution)/shard_map/ppermute | solution.py:1578
  38.4 1.5 collective-permute-start.5
  40.5 1.6 select_bitcast_fusion.1
  43.6 2.1 pad_maximum_fusion.w_far
  45.7 2.4 attend_first.3
  48.1 1.6 pad_maximum_fusion.2.qkve_far
  51.9 1.5 collective-permute-start.4
  54.7 9.0 %mlp_own.1 = (f32[512,768]{1,0:T(8,128)}, bf16[512,768]{1,0:T(8,128)(2,1)}, bf16[512,3072]{1,0:T(8,128)(2,1)}, bf16[512,3072]{1,0:T(8,128)(2,1)}, f32[512,768]{1,0:T(8,128)}) custom-call(bf16[512,768]{1,0:T(8,128)(2,1)} %bitcast.78, bf16[512,768]{1,0:T(8,128)(2,1)} %pad_maximum_fusion.12.o_far.o1_far, bf16[768,768]{1,0:T(8,128)(2,1)} %pad_maximum_fusion.8.wout_far, ...), custom_call_target="tpu_custom_call" | custom-call | tf_op jit(solution)/shard_map/mlp_own/pallas_call | solution.py:112
  63.7 3.4 collective-permute-done.5.refs_4_.refs_6_
  68.2 2.8 collective-permute-done.9.refs_2_.refs_3_
  73.5 8.8 %mlp_other.1 = (bf16[512,3072]{1,0:T(8,128)(2,1)}, bf16[512,3072]{1,0:T(8,128)(2,1)}, f32[512,768]{1,0:T(8,128)}, bf16[512,768]{1,0:T(8,128)(2,1)}) custom-call(bf16[512,768]{1,0:T(8,128)(2,1)} %get-tuple-element.170.n2_far.n1_far, f32[512,768]{1,0:T(8,128)} %get-tuple-element.171.part_far, ...), custom_call_target="tpu_custom_call", output_to_operand_aliasing={{0}: (2, {}), {1}: (3, {})} | custom-call | tf_op jit(solution)/shard_map/mlp_other/pallas_call | solution.py:112
  82.3 13.8 %attend_second.1 = (bf16[3,512,768]{2,1,0:T(8,128)(2,1)}, bf16[2,512,768]{2,1,0:T(8,128)(2,1)}, f32[2,3,4,512]{3,2,1,0:T(4,128)S(1)}) custom-call(bf16[512,768]{1,0:T(8,128)(2,1)} %get-tuple-element.177.a_far.ao_far, bf16[3,768,768]{2,1,0:T(8,128)(2,1)} %pad_maximum_fusion.w_far, f32[2,256,256]{2,1,0:T(8,128)} %copy-done.2, ...), custom_call_target="tpu_custom_call" | custom-call | flops 415236096 | tf_op jit(solution)/shard_map/attend_second/pallas_call | solution.py:112
  96.1 37.4 %mlp_second.1 = (bf16[1,512,768]{2,1,0:T(8,128)(2,1)}, bf16[1,512,768]{2,1,0:T(8,128)(2,1)}, bf16[1024,768]{1,0:T(8,128)(2,1)}, bf16[1024,3072]{1,0:T(8,128)(2,1...) custom-call(bf16[512,768]{1,0:T(8,128)(2,1)} %bitcast.79, ...), custom_call_target="tpu_custom_call" | custom-call | tf_op jit(solution)/shard_map/mlp_second/pallas_call | solution.py:112
  134.5 18.6 %attend_back.1 = (bf16[3,512,768]{2,1,0:T(8,128)(2,1)}, bf16[3,512,768]{2,1,0:T(8,128)(2,1)}, f32[512,768]{1,0:T(8,128)}, f32[3,768]{1,0:T(4,128)S(1)}) custom-call(bf16[3,768,768]{2,1,0:T(8,128)(2,1)} %pad_maximum_fusion.w_far, f32[2,256,256]{2,1,0:T(8,128)} %copy-done.2, f32[2,256,256]{2,1,0:T(8,128)} %get-tuple-element.318.strict_far, ...), custom_call_target="tpu_custom_call" | custom-call | flops 868220928 | tf_op jit(solution)/shard_map/attend_back/pallas_call | solution.py:112
  154.5 14.1 %grad_down.1 = (bf16[2,8,96,768]{3,2,1,0:T(8,128)(2,1)}, bf16[2,8,96,768]{3,2,1,0:T(8,128)(2,1)}) custom-call(s32[2]{0:T(128)S(1)} %rev.3.me_ref, bf16[512,3072]{1,0:T(8,128)(2,1)} %get-tuple-element.184.g1_far, bf16[1024,3072]{1,0:T(8,128)(2,1)} %get-tuple-element.185.g2_far, f32[512,768]{1,0:T(8,128)} %get-tuple-element.200.dy_far, ...), custom_call_target="tpu_custom_call" | custom-call | flops 452984832 | tf_op jit(solution)/shard_map/grad_down/pallas_call | solution.py:112
  168.6 4.0 %collective-permute-done.13 = bf16[1,512,768]{2,1,0:T(8,128)(2,1)S(1)} collective-permute-done((bf16[1,512,768]{2,1,0:T(8,128)(2,1)S(1)}, bf16[1,512,768]{2,1,0:T(8,128)(2,1)S(1)}, u32[]{:S(2)}, u32[]{:S(2)}) %collective-permute-start.13) | collective-permute-done | bytes 786464 | tf_op jit(solution)/shard_map/ppermute | solution.py:1578
  172.6 13.4 %mlp_back.1 = (bf16[512,3072]{1,0:T(8,128)(2,1)}, f32[512,768]{1,0:T(8,128)}, bf16[512,768]{1,0:T(8,128)(2,1)}, bf16[512,768]{1,0:T(8,128)(2,1)}, f32[2,768]{1,0:T(2,128)S(1)}) custom-call(f32[512,768]{1,0:T(8,128)} %get-tuple-element.200.dy_far, f32[512,768]{1,0:T(8,128)} %get-tuple-element.201.h1_far, bf16[768,768]{1,0:T(8,128)(2,1)} %pad_maximum_fusion.8.wout_far, ...), custom_call_target="tpu_custom_call" | custom-call | tf_op jit(solution)/shard_map/mlp_back/pallas_call | solution.py:112
  186.7 1.5 copy-done.16
  189.9 16.7 %grad_up.1 = (bf16[2,8,48,1920]{3,2,1,0:T(8,128)(2,1)}, bf16[2,8,48,1920]{3,2,1,0:T(8,128)(2,1)}) custom-call(s32[3]{0:T(128)} %pad_add_fusion.me_ref, bf16[512,768]{1,0:T(8,128)(2,1)} %get-tuple-element.170.n2_far.n1_far, bf16[1024,768]{1,0:T(8,128)(2,1)} %get-tuple-element.183.n2_far, bf16[512,3072]{1,0:T(8,128)(2,1)} %get-tuple-element.209.du1_far, ...), custom_call_target="tpu_custom_call" | custom-call | flops 566231040 | tf_op jit(solution)/shard_map/grad_up/pallas_call | solution.py:112
  206.6 12.0 %attend_back_even.1 = (bf16[3,512,768]{2,1,0:T(8,128)(2,1)}, bf16[512,768]{1,0:T(8,128)(2,1)S(1)}, f32[2,768]{1,0:T(2,128)S(1)}) custom-call(bf16[3,768,768]{2,1,0:T(8,128)(2,1)} %pad_maximum_fusion.w_far, f32[2,256,256]{2,1,0:T(8,128)} %copy-done.2, bf16[3,512,768]{2,1,0:T(8,128)(2,1)} %pad_maximum_fusion.2.qkve_far, ...), custom_call_target="tpu_custom_call" | custom-call | flops 364904448 | tf_op jit(solution)/shard_map/attend_back_even/pallas_call | solution.py:112
  218.7 1.6 fusion
  220.3 1.6 collective-permute-start.17
  222.0 10.7 %grad_qkv.1 = (bf16[2,8,48,1152]{3,2,1,0:T(8,128)(2,1)}, bf16[2,8,48,1152]{3,2,1,0:T(8,128)(2,1)}) custom-call(s32[2]{0:T(128)S(1)} %rev.3.me_ref, bf16[512,768]{1,0:T(8,128)(2,1)} %copy-done.4, bf16[512,768]{1,0:T(8,128)(2,1)} %get-tuple-element.177.a_far.ao_far, bf16[3,512,768]{2,1,0:T(8,128)(2,1)} %get-tuple-element.225.de_far, ...), custom_call_target="tpu_custom_call" | custom-call | flops 226492416 | tf_op jit(solution)/shard_map/grad_qkv/pallas_call | solution.py:112
  232.7 3.5 collective-permute-done.17
  236.2 1.5 copy-done.31
  237.9 2.0 collective-permute-done.19
  240.2 2.6 add_convert_fusion.2
  244.8 1.6 collective-permute-start.21
  250.9 17.8 %collective-permute-done.24 = bf16[2,96,768]{2,1,0:T(8,128)(2,1)S(1)} collective-permute-done((bf16[2,96,768]{2,1,0:T(8,128)(2,1)S(1)}, bf16[2,96,768]{2,1,0:T(8,128)(2,1)S(1)}, u32[]{:S(2)}, u32[]{:S(2)}) %collective-permute-start.24) | collective-permute-done | bytes 294944 | tf_op jit(solution)/shard_map/ppermute | solution.py:32
  275.5 2.6 collective-permute-start.29
  278.6 4.1 %collective-permute-done.28 = f32[5,768]{1,0:T(8,128)S(1)} collective-permute-done((f32[5,768]{1,0:T(8,128)S(1)}, f32[5,768]{1,0:T(8,128)S(1)}, u32[]{:S(2)}, u32[]{:S(2)}) %collective-permute-start.28) | collective-permute-done | bytes 15392 | tf_op jit(solution)/shard_map/ppermute | solution.py:32
  283.3 2.0 collective-permute-done.27
  287.7 3.3 collective-permute-start.33
  292.0 1.5 collective-permute-start.32
  295.6 2.2 collective-permute-done.30
  298.8 2.8 collective-permute-done.31
  301.8 2.4 collective-permute-start.38
  305.3 2.5 collective-permute-start.35
  309.2 6.8 %collective-permute-done.35 = bf16[1,48,1920]{2,1,0:T(8,128)(2,1)S(1)} collective-permute-done((bf16[1,48,1920]{2,1,0:T(8,128)(2,1)S(1)}, bf16[1,48,1920]{2,1,0:T(8,128)(2,1)S(1)}, u32[]{:S(2)}, u32[]{:S(2)}) %collective-permute-start.35) | collective-permute-done | bytes 184352 | tf_op jit(solution)/shard_map/ppermute | solution.py:32
  317.1 3.1 collective-permute-start.42
  320.3 1.9 pad_maximum_fusion.1
  322.2 7.1 %collective-permute-done.40 = bf16[1,48,1920]{2,1,0:T(8,128)(2,1)S(1)} collective-permute-done((bf16[1,48,1920]{2,1,0:T(8,128)(2,1)S(1)}, bf16[1,48,1920]{2,1,0:T(8,128)(2,1)S(1)}, u32[]{:S(2)}, u32[]{:S(2)}) %collective-permute-start.40) | collective-permute-done | bytes 184352 | tf_op jit(solution)/shard_map/ppermute | solution.py:32
  329.4 1.9 collective-permute-done.43
  334.6 1.5 collective-permute-start.44
  336.2 1.9 convert.9
  338.2 1.6 collective-permute-done.44
  339.8 4.5 %collective-permute-done.45 = bf16[2,48,1152]{2,1,0:T(8,128)(2,1)S(1)} collective-permute-done((bf16[2,48,1152]{2,1,0:T(8,128)(2,1)S(1)}, bf16[2,48,1152]{2,1,0:T(8,128)(2,1)S(1)}, u32[]{:S(2)}, u32[]{:S(2)}) %collective-permute-start.45) | collective-permute-done | bytes 221216 | tf_op jit(solution)/shard_map/ppermute | solution.py:32
  345.4 1.5 collective-permute-start.49
  348.4 3.5 unpack_down.2.refs_0_
  351.9 3.5 unpack_down.3
  355.4 3.2 collective-permute-done.49
  358.6 7.4 %collective-permute-done.50 = bf16[4,48,1152]{2,1,0:T(8,128)(2,1)} collective-permute-done((bf16[4,48,1152]{2,1,0:T(8,128)(2,1)S(1)}, bf16[4,48,1152]{2,1,0:T(8,128)(2,1)}, u32[]{:S(2)}, u32[]{:S(2)}) %collective-permute-start.50) | collective-permute-done | bytes 442400 | tf_op jit(solution)/shard_map/ppermute | solution.py:32
  366.2 1.4 pad_maximum_fusion.11.part_ref
  369.2 3.9 %unpack_up.2 = (f32[768,1536]{1,0:T(8,128)}, f32[384,768]{1,0:T(8,128)}) custom-call(s32[3]{0:T(128)} %pad_add_fusion.me_ref, bf16[8,48,1920]{2,1,0:T(8,128)(2,1)} %copy-done.18), custom_call_target="tpu_custom_call" | custom-call | tf_op jit(solution)/shard_map/unpack_up/pallas_call | solution.py:1351
  373.0 3.2 unpack_qkv.2.refs_0_
  376.2 3.9 %unpack_up.3 = (f32[768,1536]{1,0:T(8,128)}, f32[384,768]{1,0:T(8,128)}) custom-call(s32[3]{0:T(128)} %pad_add_fusion.me_ref, bf16[8,48,1920]{2,1,0:T(8,128)(2,1)} %collective-permute-done.52.part_ref, f32[768,1536]{1,0:T(8,128)} %get-tuple-element.283.refs_0_, f32[384,768]{1,0:T(8,128)} %get-tuple-element.284.refs_1_), custom_call_target="tpu_custom_call", output_to_operand_aliasing={{0}: (2, {}), {1}: (3, {})} | custom-call | tf_op jit(solution)/shard_map/unpack_up/pallas_call | solution.py:1351
  381.0 3.4 unpack_qkv.3
  (268 shorter events, 60.4 us)
Async XLA Ops:
  0.6 13.7 %copy-start = (bf16[4,512,768]{2,1,0:T(8,128)(2,1)S(1)}, bf16[4,512,768]{2,1,0:T(8,128)(2,1)}, u32[]{:S(2)}) copy-start(bf16[4,512,768]{2,1,0:T(8,128)(2,1)} %param.19) | copy-start | bytes 9437188
  2.7 13.4 %collective-permute-start = (bf16[576,384]{1,0:T(8,128)(2,1)}, bf16[576,384]{1,0:T(8,128)(2,1)}, u32[]{:S(2)}, u32[]{:S(2)}) collective-permute-start(bf16[576,384]{1,0:T(8,128)(2,1)} %constant_dynamic-slice_fusion.7), channel_id=1, source_target_pairs={{0,1},{1,0},{2,3},{3,2},{4,5},{5,4},{6,7},{7,6},{8,9},{9,8},{10,11... | collective-permute-start | bytes 1327112 | tf_op jit(solution)/shard_map/ppermute | solution.py:1578
  16.2 11.7 %collective-permute-start.1 = (bf16[576,384]{1,0:T(8,128)(2,1)}, bf16[576,384]{1,0:T(8,128)(2,1)}, u32[]{:S(2)}, u32[]{:S(2)}) collective-permute-start(bf16[576,384]{1,0:T(8,128)(2,1)} %collective-permute-done), channel_id=1, source_target_pairs={{0,4},{4,0},{1,5},{5,1},{2,6},{6,2},{3,7},{7,3},{8,12},{12,8},{9,1... | collective-permute-start | bytes 1327112 | tf_op jit(solution)/shard_map/ppermute | solution.py:1545
  19.8 17.4 %collective-permute-start.3 = (bf16[768,384]{1,0:T(8,128)(2,1)}, bf16[768,384]{1,0:T(8,128)(2,1)S(1)}, u32[]{:S(2)}, u32[]{:S(2)}) collective-permute-start(bf16[768,384]{1,0:T(8,128)(2,1)} %constant_dynamic-slice_fusion.2), channel_id=1, source_target_pairs={{0,1},{1,0},{2,3},{3,2},{4,5},{5,4},{6,7},{7,6},{8,9},{9,8},{10,11... | collective-permute-start | bytes 1769480 | tf_op jit(solution)/shard_map/ppermute | solution.py:1578
  22.3 14.9 %collective-permute-start.2 = (bf16[96,768]{1,0:T(8,128)(2,1)S(1)}, bf16[96,768]{1,0:T(8,128)(2,1)}, u32[]{:S(2)}, u32[]{:S(2)}) collective-permute-start(bf16[96,768]{1,0:T(8,128)(2,1)S(1)} %constant_dynamic-slice_fusion.3), channel_id=1, source_target_pairs={{0,1},{1,0},{2,3},{3,2},{4,5},{5,4},{6,7},{7,6},{8,9},{9,8},{10,11... | collective-permute-start | bytes 442376 | tf_op jit(solution)/shard_map/ppermute | solution.py:1578
  22.9 14.4 %copy-start.13 = (bf16[1536,768]{1,0:T(8,128)(2,1)S(1)}, bf16[1536,768]{1,0:T(8,128)(2,1)}, u32[]{:S(2)}) copy-start(bf16[1536,768]{1,0:T(8,128)(2,1)} %refs_5_.3) | copy-start | bytes 7077892
  37.2 3.3 collective-permute-start.6
  38.4 28.6 %collective-permute-start.5 = (bf16[768,768]{1,0:T(8,128)(2,1)}, bf16[768,768]{1,0:T(8,128)(2,1)}, u32[]{:S(2)}, u32[]{:S(2)}) collective-permute-start(bf16[768,768]{1,0:T(8,128)(2,1)} %pad_maximum_fusion.7), channel_id=1, source_target_pairs={{0,1},{1,0},{2,3},{3,2},{4,5},{5,4},{6,7},{7,6},{8,9},{9,8},{10,11... | collective-permute-start | bytes 3538952 | tf_op jit(solution)/shard_map/ppermute | solution.py:1578
  40.0 10.7 %collective-permute-start.7 = (bf16[96,768]{1,0:T(8,128)(2,1)}, bf16[96,768]{1,0:T(8,128)(2,1)}, u32[]{:S(2)}, u32[]{:S(2)}) collective-permute-start(bf16[96,768]{1,0:T(8,128)(2,1)} %collective-permute-done.2), channel_id=1, source_target_pairs={{0,4},{4,0},{1,5},{5,1},{2,6},{6,2},{3,7},{7,3},{8,12},{12,8},{9,1... | collective-permute-start | bytes 442376 | tf_op jit(solution)/shard_map/ppermute | solution.py:1545
  51.8 1.7 collective-permute-start.8
  51.9 15.8 %collective-permute-start.4 = (bf16[768,384]{1,0:T(8,128)(2,1)S(1)}, bf16[768,384]{1,0:T(8,128)(2,1)S(1)}, u32[]{:S(2)}, u32[]{:S(2)}) collective-permute-start(bf16[768,384]{1,0:T(8,128)(2,1)S(1)} %copy-done.20), channel_id=1, source_target_pairs={{0,4},{4,0},{1,5},{5,1},{2,6},{6,2},{3,7},{7,3},{8,12},{12,8},{9,1... | collective-permute-start | bytes 1769480 | tf_op jit(solution)/shard_map/ppermute | solution.py:1545
  53.5 18.9 %copy-start.8 = (f32[5,768]{1,0:T(8,128)}, f32[5,768]{1,0:T(8,128)S(1)}, u32[]{:S(2)}) copy-start(f32[5,768]{1,0:T(8,128)S(1)} %pad_maximum_fusion.25.gb_ref) | copy-start | bytes 46084
  67.7 4.7 %collective-permute-start.11 = (bf16[768,768]{1,0:T(8,128)(2,1)}, bf16[768,768]{1,0:T(8,128)(2,1)S(1)}, u32[]{:S(2)}, u32[]{:S(2)}) collective-permute-start(bf16[768,768]{1,0:T(8,128)(2,1)} %collective-permute-done.5.refs_4_.refs_6_), channel_id=1, source_target_pairs={{0,2},{2,0},{1,3},{3,1},{4,6},{6,4},{5,7},{7,5},{8,10},{10,8},{9,1... | collective-permute-start | bytes 3538952 | tf_op jit(solution)/shard_map/ppermute | solution.py:1581
  67.7 3.3 collective-permute-start.9
  68.2 4.0 %collective-permute-start.10 = (bf16[768,384]{1,0:T(8,128)(2,1)S(1)}, bf16[768,384]{1,0:T(8,128)(2,1)S(1)}, u32[]{:S(2)}, u32[]{:S(2)}) collective-permute-start(bf16[768,384]{1,0:T(8,128)(2,1)S(1)} %collective-permute-done.4.refs_1_.refs_2_), channel_id=1, source_target_pairs={{0,2},{2,0},{1,3},{3,1},{4,6},{6,4},{5,7},{7,5},{8,10},{10,8},{9,1... | collective-permute-start | bytes 1769480 | tf_op jit(solution)/shard_map/ppermute | solution.py:1581
  96.1 38.4 %copy-start.9 = (f32[5,768]{1,0:T(8,128)S(1)}, f32[5,768]{1,0:T(8,128)}, u32[]{:S(2)}) copy-start(f32[5,768]{1,0:T(8,128)} %copy-done.8) | copy-start | bytes 46084
  133.5 19.8 %collective-permute-start.12 = (bf16[1,512,768]{2,1,0:T(8,128)(2,1)}, bf16[1,512,768]{2,1,0:T(8,128)(2,1)S(1)}, u32[]{:S(2)}, u32[]{:S(2)}) collective-permute-start(bf16[1,512,768]{2,1,0:T(8,128)(2,1)} %get-tuple-element.186), channel_id=1, source_target_pairs={{0,1},{1,0},{2,3},{3,2},{4,5},{5,4},{6,7},{7,6},{8,9},{9,8},{10,11... | collective-permute-start | bytes 2359304 | tf_op jit(solution)/shard_map/ppermute | solution.py:1578
  134.5 18.8 %copy-start.40 = (bf16[1,512,768]{2,1,0:T(8,128)(2,1)S(1)}, bf16[1,512,768]{2,1,0:T(8,128)(2,1)}, u32[]{:S(2)}) copy-start(bf16[1,512,768]{2,1,0:T(8,128)(2,1)} %get-tuple-element.198) | copy-start | bytes 2359300
  153.3 19.2 %collective-permute-start.13 = (bf16[1,512,768]{2,1,0:T(8,128)(2,1)S(1)}, bf16[1,512,768]{2,1,0:T(8,128)(2,1)S(1)}, u32[]{:S(2)}, u32[]{:S(2)}) collective-permute-start(bf16[1,512,768]{2,1,0:T(8,128)(2,1)S(1)} %copy-done.40), channel_id=1, source_target_pairs={{0,1},{1,0},{2,3},{3,2},{4,5},{5,4},{6,7},{7,6},{8,9},{9,8},{10,11... | collective-permute-start | bytes 2359304 | tf_op jit(solution)/shard_map/ppermute | solution.py:1578
  154.5 67.5 %copy-start.12 = (s32[2]{0:T(128)}, s32[2]{0:T(128)S(1)}, u32[]{:S(2)}) copy-start(s32[2]{0:T(128)S(1)} %rev.3.me_ref) | copy-start | bytes 28
  172.6 13.4 %collective-permute-start.14 = (bf16[2,8,96,768]{3,2,1,0:T(8,128)(2,1)}, bf16[2,8,96,768]{3,2,1,0:T(8,128)(2,1)S(1)}, u32[]{:S(2)}, u32[]{:S(2)}) collective-permute-start(bf16[2,8,96,768]{3,2,1,0:T(8,128)(2,1)} %get-tuple-element.199), channel_id=1, source_target_pairs={{0,2},{2,0},{1,3},{3,1},{4,6},{6,4},{5,7},{7,5},{8,10},{10,8},{9,1... | collective-permute-start | bytes 7077896 | tf_op jit(solution)/shard_map/ppermute | solution.py:1581
  172.6 13.4 %copy-start.33 = (bf16[2,8,96,768]{3,2,1,0:T(8,128)(2,1)S(1)}, bf16[2,8,96,768]{3,2,1,0:T(8,128)(2,1)}, u32[]{:S(2)}) copy-start(bf16[2,8,96,768]{3,2,1,0:T(8,128)(2,1)} %get-tuple-element.207) | copy-start | bytes 7077892
  188.2 30.4 %collective-permute-start.15 = (bf16[8,96,768]{2,1,0:T(8,128)(2,1)S(1)}, bf16[8,96,768]{2,1,0:T(8,128)(2,1)}, u32[]{:S(2)}, u32[]{:S(2)}) collective-permute-start(bf16[8,96,768]{2,1,0:T(8,128)(2,1)S(1)} %slice_bitcast_fusion.1), channel_id=1, source_target_pairs={{0,1},{1,0},{2,3},{3,2},{4,5},{5,4},{6,7},{7,6},{8,9},{9,8},{10,11... | collective-permute-start | bytes 3538952 | tf_op jit(solution)/shard_map/ppermute | solution.py:1445
  218.6 17.5 %collective-permute-start.16 = (bf16[2,8,48,1920]{3,2,1,0:T(8,128)(2,1)S(1)}, bf16[2,8,48,1920]{3,2,1,0:T(8,128)(2,1)S(1)}, u32[]{:S(2)}, u32[]{:S(2)}) collective-permute-start(bf16[2,8,48,1920]{3,2,1,0:T(8,128)(2,1)S(1)} %copy-done.54), channel_id=1, source_target_pairs={{0,2},{2,0},{1,3},{3,1},{4,6},{6,4},{5,7},{7,5},{8,10},{10,8},{9,1... | collective-permute-start | bytes 8847368 | tf_op jit(solution)/shard_map/ppermute | solution.py:1581
  220.3 15.8 %collective-permute-start.17 = (bf16[4,96,768]{2,1,0:T(8,128)(2,1)S(1)}, bf16[4,96,768]{2,1,0:T(8,128)(2,1)S(1)}, u32[]{:S(2)}, u32[]{:S(2)}) collective-permute-start(bf16[4,96,768]{2,1,0:T(8,128)(2,1)S(1)} %slice.202), channel_id=1, source_target_pairs={{0,8},{8,0},{16,24},{24,16},{1,9},{9,1},{17,25},{25,17},{2,10},{10... | collective-permute-start | bytes 1769480 | tf_op jit(solution)/shard_map/ppermute | solution.py:32
  222.0 14.2 %copy-start.52 = (f32[2,768]{1,0:T(2,128)S(1)}, f32[2,768]{1,0:T(2,128)}, u32[]{:S(2)}) copy-start(f32[2,768]{1,0:T(2,128)} %get-tuple-element.234) | copy-start | bytes 18436
  236.1 4.0 %collective-permute-start.18 = (bf16[2,8,48,1152]{3,2,1,0:T(8,128)(2,1)}, bf16[2,8,48,1152]{3,2,1,0:T(8,128)(2,1)}, u32[]{:S(2)}, u32[]{:S(2)}) collective-permute-start(bf16[2,8,48,1152]{3,2,1,0:T(8,128)(2,1)} %get-tuple-element.230), channel_id=1, source_target_pairs={{0,2},{2,0},{1,3},{3,1},{4,6},{6,4},{5,7},{7,5},{8,10},{10,8},{9,1... | collective-permute-start | bytes 5308424 | tf_op jit(solution)/shard_map/ppermute | solution.py:1581
  237.8 2.1 collective-permute-start.19
  244.8 23.9 %collective-permute-start.21 = (bf16[2,4,48,1152]{3,2,1,0:T(8,128)(2,1)S(1)}, bf16[2,4,48,1152]{3,2,1,0:T(8,128)(2,1)S(1)}, u32[]{:S(2)}, u32[]{:S(2)}) collective-permute-start(bf16[2,4,48,1152]{3,2,1,0:T(8,128)(2,1)S(1)} %slice.205), channel_id=1, source_target_pairs={{0,8},{8,0},{16,24},{24,16},{1,9},{9,1},{17,25},{25,17},{2,10},{10... | collective-permute-start | bytes 2654216 | tf_op jit(solution)/shard_map/ppermute | solution.py:32
  246.5 22.2 %collective-permute-start.22 = (bf16[8,48,1152]{2,1,0:T(8,128)(2,1)S(1)}, bf16[8,48,1152]{2,1,0:T(8,128)(2,1)S(1)}, u32[]{:S(2)}, u32[]{:S(2)}) collective-permute-start(bf16[8,48,1152]{2,1,0:T(8,128)(2,1)S(1)} %slice_bitcast_fusion.3), channel_id=1, source_target_pairs={{0,1},{1,0},{2,3},{3,2},{4,5},{5,4},{6,7},{7,6},{8,9},{9,8},{10,11... | collective-permute-start | bytes 2654216 | tf_op jit(solution)/shard_map/ppermute | solution.py:1462
  247.5 21.2 %collective-permute-start.20 = (bf16[2,4,48,768]{3,2,1,0:T(8,128)(2,1)S(1)}, bf16[2,4,48,768]{3,2,1,0:T(8,128)(2,1)S(1)}, u32[]{:S(2)}, u32[]{:S(2)}) collective-permute-start(bf16[2,4,48,768]{3,2,1,0:T(8,128)(2,1)S(1)} %slice.204), channel_id=1, source_target_pairs={{0,4},{4,0},{1,5},{5,1},{2,6},{6,2},{3,7},{7,3},{8,12},{12,8},{9,1... | collective-permute-start | bytes 1769480 | tf_op jit(solution)/shard_map/ppermute | solution.py:32
  248.7 20.0 %collective-permute-start.24 = (bf16[2,96,768]{2,1,0:T(8,128)(2,1)S(1)}, bf16[2,96,768]{2,1,0:T(8,128)(2,1)S(1)}, u32[]{:S(2)}, u32[]{:S(2)}) collective-permute-start(bf16[2,96,768]{2,1,0:T(8,128)(2,1)S(1)} %slice.208), channel_id=1, source_target_pairs={{0,4},{4,0},{1,5},{5,1},{2,6},{6,2},{3,7},{7,3},{8,12},{12,8},{9,1... | collective-permute-start | bytes 884744 | tf_op jit(solution)/shard_map/ppermute | solution.py:32
  249.8 18.9 %collective-permute-start.23 = (f32[5,768]{1,0:T(8,128)S(1)}, f32[5,768]{1,0:T(8,128)S(1)}, u32[]{:S(2)}, u32[]{:S(2)}) collective-permute-start(f32[5,768]{1,0:T(8,128)S(1)} %add.190), channel_id=1, source_target_pairs={{0,1},{1,0},{2,3},{3,2},{4,5},{5,4},{6,7},{7,6},{8,9},{9,8},{10,11... | collective-permute-start | bytes 46088 | tf_op jit(solution)/shard_map/ppermute | solution.py:32
  271.0 14.3 %copy-start.29 = (bf16[8,48,1152]{2,1,0:T(8,128)(2,1)S(1)}, bf16[8,48,1152]{2,1,0:T(8,128)(2,1)}, u32[]{:S(2)}) copy-start(bf16[8,48,1152]{2,1,0:T(8,128)(2,1)} %copy-done.28) | copy-start | bytes 2654212
  271.0 14.2 %collective-permute-start.27 = (bf16[4,48,1152]{2,1,0:T(8,128)(2,1)}, bf16[4,48,1152]{2,1,0:T(8,128)(2,1)}, u32[]{:S(2)}, u32[]{:S(2)}) collective-permute-start(bf16[4,48,1152]{2,1,0:T(8,128)(2,1)} %slice.214), channel_id=1, source_target_pairs={{0,8},{8,0},{16,24},{24,16},{1,9},{9,1},{17,25},{25,17},{2,10},{10... | collective-permute-start | bytes 1327112 | tf_op jit(solution)/shard_map/ppermute | solution.py:32
  271.5 13.8 %collective-permute-start.26 = (bf16[2,2,48,1152]{3,2,1,0:T(8,128)(2,1)}, bf16[2,2,48,1152]{3,2,1,0:T(8,128)(2,1)}, u32[]{:S(2)}, u32[]{:S(2)}) collective-permute-start(bf16[2,2,48,1152]{3,2,1,0:T(8,128)(2,1)} %slice.212), channel_id=1, source_target_pairs={{0,4},{4,0},{1,5},{5,1},{2,6},{6,2},{3,7},{7,3},{8,12},{12,8},{9,1... | collective-permute-start | bytes 1327112 | tf_op jit(solution)/shard_map/ppermute | solution.py:32
  273.4 9.9 %collective-permute-start.25 = (bf16[4,48,768]{2,1,0:T(8,128)(2,1)}, bf16[4,48,768]{2,1,0:T(8,128)(2,1)S(1)}, u32[]{:S(2)}, u32[]{:S(2)}) collective-permute-start(bf16[4,48,768]{2,1,0:T(8,128)(2,1)} %slice_bitcast_fusion.4), channel_id=1, source_target_pairs={{0,1},{1,0},{2,3},{3,2},{4,5},{5,4},{6,7},{7,6},{8,9},{9,8},{10,11... | collective-permute-start | bytes 884744 | tf_op jit(solution)/shard_map/ppermute | solution.py:1462
  275.5 7.8 %collective-permute-start.29 = (bf16[1,96,768]{2,1,0:T(8,128)(2,1)}, bf16[1,96,768]{2,1,0:T(8,128)(2,1)S(1)}, u32[]{:S(2)}, u32[]{:S(2)}) collective-permute-start(bf16[1,96,768]{2,1,0:T(8,128)(2,1)} %slice.216), channel_id=1, source_target_pairs={{0,16},{8,24},{16,0},{24,8},{1,17},{9,25},{17,1},{25,9},{2,18},{10... | collective-permute-start | bytes 442376 | tf_op jit(solution)/shard_map/ppermute | solution.py:32
  278.1 4.6 %collective-permute-start.28 = (f32[5,768]{1,0:T(8,128)S(1)}, f32[5,768]{1,0:T(8,128)S(1)}, u32[]{:S(2)}, u32[]{:S(2)}) collective-permute-start(f32[5,768]{1,0:T(8,128)S(1)} %add.195), channel_id=1, source_target_pairs={{0,4},{4,0},{1,5},{5,1},{2,6},{6,2},{3,7},{7,3},{8,12},{12,8},{9,1... | collective-permute-start | bytes 46088 | tf_op jit(solution)/shard_map/ppermute | solution.py:32
  287.7 6.8 %collective-permute-start.33 = (f32[5,768]{1,0:T(8,128)S(1)}, f32[5,768]{1,0:T(8,128)S(1)}, u32[]{:S(2)}, u32[]{:S(2)}) collective-permute-start(f32[5,768]{1,0:T(8,128)S(1)} %add.200), channel_id=1, source_target_pairs={{0,8},{8,0},{16,24},{24,16},{1,9},{9,1},{17,25},{25,17},{2,10},{10... | collective-permute-start | bytes 46088 | tf_op jit(solution)/shard_map/ppermute | solution.py:32
  291.0 6.9 %collective-permute-start.30 = (bf16[2,48,768]{2,1,0:T(8,128)(2,1)S(1)}, bf16[2,48,768]{2,1,0:T(8,128)(2,1)S(1)}, u32[]{:S(2)}, u32[]{:S(2)}) collective-permute-start(bf16[2,48,768]{2,1,0:T(8,128)(2,1)S(1)} %slice.218), channel_id=1, source_target_pairs={{0,8},{8,0},{16,24},{24,16},{1,9},{9,1},{17,25},{25,17},{2,10},{10... | collective-permute-start | bytes 442376 | tf_op jit(solution)/shard_map/ppermute | solution.py:32
  291.1 7.7 %collective-permute-start.34 = (bf16[1,96,768]{2,1,0:T(8,128)(2,1)S(1)}, bf16[1,96,768]{2,1,0:T(8,128)(2,1)S(1)}, u32[]{:S(2)}, u32[]{:S(2)}) collective-permute-start(bf16[1,96,768]{2,1,0:T(8,128)(2,1)S(1)} %add_convert_fusion.13), channel_id=1, source_target_pairs={{0,16},{8,24},{16,0},{24,8},{1,17},{9,25},{17,1},{25,9},{2,18},{10... | collective-permute-start | bytes 442376 | tf_op jit(solution)/shard_map/ppermute | solution.py:32
  292.0 6.8 %collective-permute-start.32 = (bf16[2,48,1152]{2,1,0:T(8,128)(2,1)S(1)}, bf16[2,48,1152]{2,1,0:T(8,128)(2,1)S(1)}, u32[]{:S(2)}, u32[]{:S(2)}) collective-permute-start(bf16[2,48,1152]{2,1,0:T(8,128)(2,1)S(1)} %slice.222), channel_id=1, source_target_pairs={{0,4},{4,0},{1,5},{5,1},{2,6},{6,2},{3,7},{7,3},{8,12},{12,8},{9,1... | collective-permute-start | bytes 663560 | tf_op jit(solution)/shard_map/ppermute | solution.py:32
  293.4 8.2 %collective-permute-start.31 = (bf16[2,48,1152]{2,1,0:T(8,128)(2,1)S(1)}, bf16[2,48,1152]{2,1,0:T(8,128)(2,1)S(1)}, u32[]{:S(2)}, u32[]{:S(2)}) collective-permute-start(bf16[2,48,1152]{2,1,0:T(8,128)(2,1)S(1)} %slice_bitcast_fusion.7), channel_id=1, source_target_pairs={{0,1},{1,0},{2,3},{3,2},{4,5},{5,4},{6,7},{7,6},{8,9},{9,8},{10,11... | collective-permute-start | bytes 663560 | tf_op jit(solution)/shard_map/ppermute | solution.py:1462
  294.5 13.4 %copy-start.39 = (bf16[1,512,768]{2,1,0:T(8,128)(2,1)S(1)}, bf16[1,512,768]{2,1,0:T(8,128)(2,1)}, u32[]{:S(2)}) copy-start(bf16[1,512,768]{2,1,0:T(8,128)(2,1)} %get-tuple-element.186) | copy-start | bytes 2359300
  294.5 13.4 %copy-start.41 = (bf16[1,512,768]{2,1,0:T(8,128)(2,1)S(1)}, bf16[1,512,768]{2,1,0:T(8,128)(2,1)}, u32[]{:S(2)}) copy-start(bf16[1,512,768]{2,1,0:T(8,128)(2,1)} %get-tuple-element.198) | copy-start | bytes 2359300
  294.5 13.7 %collective-permute-start.36 = (bf16[256,768]{1,0:T(8,128)(2,1)S(1)}, bf16[256,768]{1,0:T(8,128)(2,1)S(1)}, u32[]{:S(2)}, u32[]{:S(2)}) collective-permute-start(bf16[256,768]{1,0:T(8,128)(2,1)S(1)} %get-tuple-element.254), channel_id=1, source_target_pairs={{0,1},{1,0},{2,3},{3,2},{4,5},{5,4},{6,7},{7,6},{8,9},{9,8},{10,11... | collective-permute-start | bytes 1179656 | tf_op jit(solution)/shard_map/ppermute | solution.py:1578
  301.8 14.2 %collective-permute-start.38 = (f32[5,768]{1,0:T(8,128)S(1)}, f32[5,768]{1,0:T(8,128)S(1)}, u32[]{:S(2)}, u32[]{:S(2)}) collective-permute-start(f32[5,768]{1,0:T(8,128)S(1)} %add.205), channel_id=1, source_target_pairs={{0,16},{8,24},{16,0},{24,8},{1,17},{9,25},{17,1},{25,9},{2,18},{10... | collective-permute-start | bytes 46088 | tf_op jit(solution)/shard_map/ppermute | solution.py:32
  304.3 11.7 %collective-permute-start.37 = (bf16[1,48,1152]{2,1,0:T(8,128)(2,1)S(1)}, bf16[1,48,1152]{2,1,0:T(8,128)(2,1)S(1)}, u32[]{:S(2)}, u32[]{:S(2)}) collective-permute-start(bf16[1,48,1152]{2,1,0:T(8,128)(2,1)S(1)} %slice.228), channel_id=1, source_target_pairs={{0,16},{8,24},{16,0},{24,8},{1,17},{9,25},{17,1},{25,9},{2,18},{10... | collective-permute-start | bytes 331784 | tf_op jit(solution)/shard_map/ppermute | solution.py:32
  304.9 11.1 %collective-permute-start.39 = (bf16[2,96,768]{2,1,0:T(8,128)(2,1)S(1)}, bf16[2,96,768]{2,1,0:T(8,128)(2,1)S(1)}, u32[]{:S(2)}, u32[]{:S(2)}) collective-permute-start(bf16[2,96,768]{2,1,0:T(8,128)(2,1)S(1)} %pad_maximum_fusion.18), channel_id=1, source_target_pairs={{0,4},{4,0},{1,5},{5,1},{2,6},{6,2},{3,7},{7,3},{8,12},{12,8},{9,1... | collective-permute-start | bytes 884744 | tf_op jit(solution)/shard_map/ppermute | solution.py:32
  305.3 10.6 %collective-permute-start.35 = (bf16[1,48,1920]{2,1,0:T(8,128)(2,1)S(1)}, bf16[1,48,1920]{2,1,0:T(8,128)(2,1)S(1)}, u32[]{:S(2)}, u32[]{:S(2)}) collective-permute-start(bf16[1,48,1920]{2,1,0:T(8,128)(2,1)S(1)} %pad_maximum_fusion.22), channel_id=1, source_target_pairs={{0,16},{8,24},{16,0},{24,8},{1,17},{9,25},{17,1},{25,9},{2,18},{10... | collective-permute-start | bytes 552968 | tf_op jit(solution)/shard_map/ppermute | solution.py:32
  308.2 14.0 %collective-permute-start.41 = (bf16[256,768]{1,0:T(8,128)(2,1)S(1)}, bf16[256,768]{1,0:T(8,128)(2,1)S(1)}, u32[]{:S(2)}, u32[]{:S(2)}) collective-permute-start(bf16[256,768]{1,0:T(8,128)(2,1)S(1)} %get-tuple-element.260), channel_id=1, source_target_pairs={{0,1},{1,0},{2,3},{3,2},{4,5},{5,4},{6,7},{7,6},{8,9},{9,8},{10,11... | collective-permute-start | bytes 1179656 | tf_op jit(solution)/shard_map/ppermute | solution.py:1578
  316.1 15.1 %collective-permute-start.43 = (bf16[4,96,768]{2,1,0:T(8,128)(2,1)S(1)}, bf16[4,96,768]{2,1,0:T(8,128)(2,1)S(1)}, u32[]{:S(2)}, u32[]{:S(2)}) collective-permute-start(bf16[4,96,768]{2,1,0:T(8,128)(2,1)S(1)} %pad_maximum_fusion.14), channel_id=1, source_target_pairs={{0,8},{8,0},{16,24},{24,16},{1,9},{9,1},{17,25},{25,17},{2,10},{10... | collective-permute-start | bytes 1769480 | tf_op jit(solution)/shard_map/ppermute | solution.py:32
  317.1 12.2 %collective-permute-start.42 = (bf16[1,48,1152]{2,1,0:T(8,128)(2,1)S(1)}, bf16[1,48,1152]{2,1,0:T(8,128)(2,1)S(1)}, u32[]{:S(2)}, u32[]{:S(2)}) collective-permute-start(bf16[1,48,1152]{2,1,0:T(8,128)(2,1)S(1)} %add_convert_fusion.14), channel_id=1, source_target_pairs={{0,16},{8,24},{16,0},{24,8},{1,17},{9,25},{17,1},{25,9},{2,18},{10... | collective-permute-start | bytes 331784 | tf_op jit(solution)/shard_map/ppermute | solution.py:32
  320.2 9.2 %collective-permute-start.40 = (bf16[1,48,1920]{2,1,0:T(8,128)(2,1)S(1)}, bf16[1,48,1920]{2,1,0:T(8,128)(2,1)S(1)}, u32[]{:S(2)}, u32[]{:S(2)}) collective-permute-start(bf16[1,48,1920]{2,1,0:T(8,128)(2,1)S(1)} %add_convert_fusion.11), channel_id=1, source_target_pairs={{0,16},{8,24},{16,0},{24,8},{1,17},{9,25},{17,1},{25,9},{2,18},{10... | collective-permute-start | bytes 552968 | tf_op jit(solution)/shard_map/ppermute | solution.py:32
  331.3 12.9 %collective-permute-start.47 = (bf16[8,96,768]{2,1,0:T(8,128)(2,1)S(1)}, bf16[8,96,768]{2,1,0:T(8,128)(2,1)S(1)}, u32[]{:S(2)}, u32[]{:S(2)}) collective-permute-start(bf16[8,96,768]{2,1,0:T(8,128)(2,1)S(1)} %pad_maximum_fusion.9.part_ref), channel_id=1, source_target_pairs={{0,2},{2,0},{1,3},{3,1},{4,6},{6,4},{5,7},{7,5},{8,10},{10,8},{9,1... | collective-permute-start | bytes 3538952 | tf_op jit(solution)/shard_map/ppermute | solution.py:1448
  332.4 11.9 %collective-permute-start.46 = (bf16[2,48,1152]{2,1,0:T(8,128)(2,1)S(1)}, bf16[2,48,1152]{2,1,0:T(8,128)(2,1)S(1)}, u32[]{:S(2)}, u32[]{:S(2)}) collective-permute-start(bf16[2,48,1152]{2,1,0:T(8,128)(2,1)S(1)} %pad_maximum_fusion.21), channel_id=1, source_target_pairs={{0,4},{4,0},{1,5},{5,1},{2,6},{6,2},{3,7},{7,3},{8,12},{12,8},{9,1... | collective-permute-start | bytes 663560 | tf_op jit(solution)/shard_map/ppermute | solution.py:32
  333.2 11.1 %collective-permute-start.45 = (bf16[2,48,1152]{2,1,0:T(8,128)(2,1)S(1)}, bf16[2,48,1152]{2,1,0:T(8,128)(2,1)S(1)}, u32[]{:S(2)}, u32[]{:S(2)}) collective-permute-start(bf16[2,48,1152]{2,1,0:T(8,128)(2,1)S(1)} %pad_maximum_fusion.20), channel_id=1, source_target_pairs={{0,4},{4,0},{1,5},{5,1},{2,6},{6,2},{3,7},{7,3},{8,12},{12,8},{9,1... | collective-permute-start | bytes 663560 | tf_op jit(solution)/shard_map/ppermute | solution.py:32
  334.6 5.2 %collective-permute-start.44 = (bf16[2,48,768]{2,1,0:T(8,128)(2,1)S(1)}, bf16[2,48,768]{2,1,0:T(8,128)(2,1)S(1)}, u32[]{:S(2)}, u32[]{:S(2)}) collective-permute-start(bf16[2,48,768]{2,1,0:T(8,128)(2,1)S(1)} %pad_maximum_fusion.23), channel_id=1, source_target_pairs={{0,8},{8,0},{16,24},{24,16},{1,9},{9,1},{17,25},{25,17},{2,10},{10... | collective-permute-start | bytes 442376 | tf_op jit(solution)/shard_map/ppermute | solution.py:32
  345.4 13.2 %collective-permute-start.49 = (bf16[4,48,1152]{2,1,0:T(8,128)(2,1)S(1)}, bf16[4,48,1152]{2,1,0:T(8,128)(2,1)S(1)}, u32[]{:S(2)}, u32[]{:S(2)}) collective-permute-start(bf16[4,48,1152]{2,1,0:T(8,128)(2,1)S(1)} %pad_maximum_fusion.15), channel_id=1, source_target_pairs={{0,8},{8,0},{16,24},{24,16},{1,9},{9,1},{17,25},{25,17},{2,10},{10... | collective-permute-start | bytes 1327112 | tf_op jit(solution)/shard_map/ppermute | solution.py:32
  346.9 19.1 %collective-permute-start.50 = (bf16[4,48,1152]{2,1,0:T(8,128)(2,1)S(1)}, bf16[4,48,1152]{2,1,0:T(8,128)(2,1)}, u32[]{:S(2)}, u32[]{:S(2)}) collective-permute-start(bf16[4,48,1152]{2,1,0:T(8,128)(2,1)S(1)} %pad_maximum_fusion.16), channel_id=1, source_target_pairs={{0,8},{8,0},{16,24},{24,16},{1,9},{9,1},{17,25},{25,17},{2,10},{10... | collective-permute-start | bytes 1327112 | tf_op jit(solution)/shard_map/ppermute | solution.py:32
  347.5 7.8 %collective-permute-start.48 = (bf16[4,48,768]{2,1,0:T(8,128)(2,1)S(1)}, bf16[4,48,768]{2,1,0:T(8,128)(2,1)S(1)}, u32[]{:S(2)}, u32[]{:S(2)}) collective-permute-start(bf16[4,48,768]{2,1,0:T(8,128)(2,1)S(1)} %pad_maximum_fusion.19), channel_id=1, source_target_pairs={{0,4},{4,0},{1,5},{5,1},{2,6},{6,2},{3,7},{7,3},{8,12},{12,8},{9,1... | collective-permute-start | bytes 884744 | tf_op jit(solution)/shard_map/ppermute | solution.py:32
  366.2 10.0 %collective-permute-start.52 = (bf16[8,48,1920]{2,1,0:T(8,128)(2,1)S(1)}, bf16[8,48,1920]{2,1,0:T(8,128)(2,1)}, u32[]{:S(2)}, u32[]{:S(2)}) collective-permute-start(bf16[8,48,1920]{2,1,0:T(8,128)(2,1)S(1)} %maximum_maximum_fusion.part_ref), channel_id=1, source_target_pairs={{0,2},{2,0},{1,3},{3,1},{4,6},{6,4},{5,7},{7,5},{8,10},{10,8},{9,1... | collective-permute-start | bytes 4423688 | tf_op jit(solution)/shard_map/ppermute | solution.py:1448
  367.7 12.4 %collective-permute-start.51 = (bf16[8,48,1152]{2,1,0:T(8,128)(2,1)S(1)}, bf16[8,48,1152]{2,1,0:T(8,128)(2,1)S(1)}, u32[]{:S(2)}, u32[]{:S(2)}) collective-permute-start(bf16[8,48,1152]{2,1,0:T(8,128)(2,1)S(1)} %pad_maximum_fusion.11.part_ref), channel_id=1, source_target_pairs={{0,2},{2,0},{1,3},{3,1},{4,6},{6,4},{5,7},{7,5},{8,10},{10,8},{9,1... | collective-permute-start | bytes 2654216 | tf_op jit(solution)/shard_map/ppermute | solution.py:1448
  (44 other events, 166.6 us)
where the time goes:
time: 392 us; the launch traced here: 385 us
  Pallas kernels  181 us (46%)
  waiting for transfers between devices  93.8 us (24%)
  starting transfers between devices  53.7 us (14%)
  other arithmetic  31.3 us (8%)
  local copies, waits for them, and re-layouts  23.6 us (6%)
    pallas_call x12, Pallas kernels, resident(): pl.pallas_call(body, in_specs=[s for _, s in ins], out_specs=[s for _, s...  159 us
    ppermute x27, waiting for transfers between devices, flip_bit(): return lax.ppermute(array, axis, [(i, i ^ bit) for i in range(size)])  65.7 us
    ppermute x27, starting transfers between devices, flip_bit(): return lax.ppermute(array, axis, [(i, i ^ bit) for i in range(size)])  33.7 us
    pallas_call x6, Pallas kernels, packed_call(): pl.pallas_call(body, grid_spec=pltpu.PrefetchScalarGridSpec(num_scalar_pr...  21.3 us
    ppermute x8, waiting for transfers between devices, partner(): return lax.ppermute(t, 'tensor', FLIP)  15.1 us
    unnamed x113, local copies, waits for them, and re-layouts  11.7 us
    ppermute x8, starting transfers between devices, partner(): return lax.ppermute(t, 'tensor', FLIP)  10.6 us
    convert_element_type x18, other arithmetic, fold(): return sum((p.astype(F32) for p in parts)).astype(BF16)  9 us
  transfers between devices with their start and end apart: 53, of which 27 were waited for; matrix products, arithmetic and copies ran while one was open for 8% of the time, Pallas kernels for 30%

commit v1 on v0

--- a/solution.py
+++ b/solution.py
@@ -15,7 +15,7 @@
 BF16 = jnp.bfloat16
 ROWS_OVER = ("o", "x", "core")
 FLIP = ((0, 1), (1, 0))
-VMEM_LIMIT = 60 * 1024 * 1024
+VMEM_LIMIT = 16 * 1024 * 1024
 
 
 def ordered(flag, mine, theirs):
@@ -343,7 +343,7 @@
         functools.partial(attend_second_body, rows, seq),
         [(t, FAR) for t in (a, w, incl, strict, qkve, o1)] + [lse1],
         [(qkv, FAR), (o2, FAR), sds((2, *lse1.shape), F32)],
-        scratch=[pltpu.VMEM(t.shape, t.dtype) for t in near] + [pltpu.SemaphoreType.DMA((32,))],
+        scratch=[pltpu.VMEM(t.shape, t.dtype) for t in near] + [pltpu.SemaphoreType.DMA((64,))],
         flops=6 * n * d * f + 48 * n * seq * f,
         vmem=32,
         name="attend_second",
@@ -501,7 +501,7 @@
         + [(t, FAR) for t in (do, dh1, ho)]
         + [gb],
         [(qkv, FAR), (qkv, FAR), (sds((n, d), F32), FAR), sds((3, d), F32)],
-        scratch=[pltpu.VMEM(t.shape, t.dtype) for t in near + (sds((n, d), F32),)] + [pltpu.SemaphoreType.DMA((32,))],
+        scratch=[pltpu.VMEM(t.shape, t.dtype) for t in near + (sds((n, d), F32),)] + [pltpu.SemaphoreType.DMA((64,))],
         flops=6 * n * d * f + 120 * n * seq * f,
         vmem=44,
         name="attend_back",
@@ -628,7 +628,7 @@
         + far(do2.reshape(2, n, f), part, dh1, dh2, x)
         + [gb],
         [(qkv, FAR), sds((n, d), BF16), sds((2, d), F32)],
-        scratch=[pltpu.VMEM(t.shape, t.dtype) for t in near] + [pltpu.SemaphoreType.DMA((32,))],
+        scratch=[pltpu.VMEM(t.shape, t.dtype) for t in near] + [pltpu.SemaphoreType.DMA((64,))],
         flops=6 * n * d * f + 40 * n * seq * f,
         vmem=40,
         name="attend_back_even",
@@ -1191,6 +1191,11 @@
 
 
 CUT = 768
+CUT_BACK = 1536
+
+
+def swapped(s):
+    return ((s >> 1) % 2) * 4 + ((s >> 2) % 2) * 2 + s % 2
 
 
 def put_slots(out_ref, y, lanes, acc_ref, me):
@@ -1302,17 +1307,26 @@
     d = a_ref.shape[1]
     f = de_far.shape[2] // 2
     ready = stack_rows(moves, (ae_far, ao_far), a_ref, 0, d)
-    tiles = [stack_rows(moves, (de_far.at[j], do_far.at[j]), d_ref.at[j], 0, 2 * f) for j in range(3)]
+    n, first = ae_far.shape[0], moves.take(6)
+
+    def loads(j):
+        return [
+            pltpu.make_async_copy(far.at[j], d_ref.at[j, pl.ds(k * n, n)], sems.at[first + 2 * j + k])
+            for k, far in enumerate((de_far, do_far))
+        ]
+
     ready[0]()
-    for start, _ in tiles[:2]:
-        start()
+    for c in loads(0):
+        c.start()
     ready[1]()
-    tiles[2][0]()
+    for j in (1, 2):
+        for c in loads(j):
+            c.start()
     t_ref[...] = a_ref[...].T
-    for _, wait in tiles:
-        wait()
 
     def step(j, _):
+        for c in loads(j):
+            c.wait()
         acc_ref[...] = dot(t_ref[...], d_ref[j]).reshape(acc_ref.shape)
         lanes = pl.ds(pl.multiple_of(j * f, f), f)
         for s in range(16):
@@ -1367,58 +1381,72 @@
     )(me, *[a for a, _ in ins])
 
 
-def unpack_body(kind, me_ref, part_ref, *refs):
-    low = me_ref[0] % 8
-    rows, width = part_ref.shape[1:]
-    first = refs[-2] if kind == "up" else refs[-1]
-    if kind == "up":
-        first, second, wide = refs[-3:]
-    for s in range(8):
-        sl = slice(s * rows, (s + 1) * rows)
-        if kind == "down":
-            first[sl] = part_ref[s ^ low].astype(F32)
-        elif kind == "up":
-            f = first.shape[1]
-            other = s ^ (me_ref[2] % 8)
-            first[sl, :CUT] = part_ref[s ^ low, :, :CUT].astype(F32)
-            first[sl, CUT:] = part_ref[other, :, CUT:f].astype(F32)
-            wide[sl] = part_ref[other, :, f:].astype(F32)
-        else:
-            f = width // 3
-            for j in range(3):
-                first[j, sl] = part_ref[s ^ low, :, j * f : (j + 1) * f].astype(F32)
-    if kind == "up":
-        second[...] = wide[...].T
-
-
-def unpack(kind, me, side, part, into=()):
+def unpack_down_body(me_ref, part_ref, *refs):
+    low, rows = me_ref[0] % 8, part_ref.shape[1]
+    for b in range(8):
+        refs[-1][b * rows : (b + 1) * rows] = part_ref[b ^ low].astype(F32)
+
+
+def unpack_down(me, side, part, into=()):
     _, r, w = part.shape
     half = 8 * r
     at = lambda me: (me[0] // 8) ^ side
-    scratch = []
-    if kind == "down":
-        outs = [(sds((2 * half, w), F32), pl.BlockSpec((half, w), lambda i, me: (at(me), 0)))]
-    elif kind == "up":
-        f = half
-        outs = [
-            (sds((2 * half, w - f), F32), pl.BlockSpec((half, w - f), lambda i, me: (at(me), 0))),
-            (sds((f, 2 * half), F32), pl.BlockSpec((f, half), lambda i, me: (0, at(me)))),
-        ]
-        scratch = [pltpu.VMEM((half, f), F32)]
-    else:
-        f = w // 3
-        outs = [(sds((3, 2 * half, f), F32), pl.BlockSpec((3, half, f), lambda i, me: (0, at(me), 0)))]
     ins = [(part, pl.BlockSpec(part.shape, lambda i, me: (0, 0, 0)))]
     ins += [(t, pl.BlockSpec(memory_space=pl.ANY)) for t in into]
     return packed_call(
-        functools.partial(unpack_body, kind),
+        unpack_down_body,
         (1,),
         me,
         ins,
-        outs,
-        scratch=scratch,
+        [(sds((2 * half, w), F32), pl.BlockSpec((half, w), lambda i, me: (at(me), 0)))],
         aliases={2 + i: i for i in range(len(into))},
-        name="unpack_" + kind,
+        name="unpack_down",
+    )[0]
+
+
+def unpack_rest_body(side, me_ref, part_ref, *refs):
+    up_far, out_far, qkv_far, up_st, wide, out_st, qkv_st, sems = refs[-8:]
+    moves = Moves(sems)
+    left, right = me_ref[0] % 8, me_ref[2] % 8
+    rows, half = part_ref.shape[1], 8 * part_ref.shape[1]
+    d, f = up_st.shape[1], wide.shape[1]
+    base = ((me_ref[0] // 8) ^ side) * half
+    sent = []
+    for b in range(8):
+        sl = slice(b * rows, (b + 1) * rows)
+        up_st[sl, :CUT] = part_ref[b ^ left, :, :CUT].astype(F32)
+        up_st[sl, CUT:] = part_ref[swapped(b ^ right), :, CUT:d].astype(F32)
+        wide[sl] = part_ref[b ^ right, :, d : d + f].astype(F32)
+        if b % 4 == 3:
+            start, size = (b - 3) * rows, 4 * rows
+            at = pl.ds(pl.multiple_of(base + start, 8), size)
+            sent.append(moves.whole(up_st.at[pl.ds(start, size)], up_far.at[at]))
+    out_st[...] = wide[...].T
+    sent.append(moves.whole(out_st, lanes_at(out_far, base, half)))
+    for j in range(3):
+        for b in range(8):
+            sl = slice(b * rows, (b + 1) * rows)
+            qkv_st[j, sl] = part_ref[b ^ right, :, d + (j + 1) * f : d + (j + 2) * f].astype(F32)
+        sent.append(moves.whole(qkv_st.at[j], qkv_far.at[j, pl.ds(pl.multiple_of(base, 8), half)]))
+    for wait in sent:
+        wait()
+
+
+def unpack_rest(me, side, part, into=()):
+    _, r, w = part.shape
+    half = 8 * r
+    d, f = CUT_BACK, (w - CUT_BACK) // 4
+    smem = pl.BlockSpec(memory_space=pltpu.SMEM)
+    outs = [sds((2 * half, d), F32), sds((f, 2 * half), F32), sds((3, 2 * half, f), F32)]
+    stages = [sds((half, d), F32), sds((half, f), F32), sds((f, half), F32), sds((3, half, f), F32)]
+    return resident(
+        functools.partial(unpack_rest_body, side),
+        [(me, smem), part] + far_of(*into),
+        far_of(*outs),
+        scratch=near_of(*stages) + [pltpu.SemaphoreType.DMA((8,))],
+        vmem=24,
+        aliases={2 + i: i for i in range(len(into))},
+        name="unpack_rest",
     )
 
 
@@ -1446,6 +1474,82 @@
 
     def gather_core(self):
         self.got = lax.ppermute(self.keep, "core", FLIP)
+
+
+def add(k, g):
+    return (k.astype(F32) + g.astype(F32)).astype(BF16)
+
+
+def phase_shapes(mode, parts):
+    shapes = [p[0].shape for p in parts]
+    s = shapes[0]
+    if mode == "half":
+        out = s[:-3] + (s[-3] // 2,) + s[-2:]
+        return [out, out]
+    if mode == "partner":
+        return [s[1:], s[1:]]
+    if mode == "last":
+        out = (s[0] // 2, s[1], sum(t[2] for t in shapes))
+        return [out, out]
+    if mode == "sum":
+        return [s]
+    if mode == "split":
+        return [(2 * s[0], s[1], CUT_BACK), (2 * s[0], s[1], s[2] - CUT_BACK)]
+    return [(2 * s[0], s[1], sum(t[2] for t in shapes))]
+
+
+def phase_part(mode, parts, outs):
+    if mode == "half":
+        (k, g), n = parts[0], outs[0].shape[-3]
+        lead = (slice(None),) * (len(k.shape) - 3)
+        for i, out in enumerate(outs):
+            at = lead + (slice(i * n, (i + 1) * n),)
+            out[...] = add(k[at], g[at])
+    elif mode == "partner":
+        k, g = parts[0]
+        for i, out in zip((1, 0), outs):
+            out[...] = add(k[i], g[i])
+    elif mode == "last":
+        n, lane = outs[0].shape[0], 0
+        for k, g in parts:
+            for i, out in enumerate(outs):
+                at = slice(i * n, (i + 1) * n)
+                out[:, :, lane : lane + k.shape[2]] = add(k[at], g[at])
+            lane += k.shape[2]
+    elif mode == "sum":
+        outs[0][...] = add(parts[0][0][...], parts[0][1][...])
+    elif mode == "split":
+        for i, ref in enumerate(parts[0]):
+            at = slice(i * ref.shape[0], (i + 1) * ref.shape[0])
+            outs[0][at] = ref[:, :, :CUT_BACK]
+            outs[1][at] = ref[:, :, CUT_BACK:]
+    else:
+        lane = 0
+        for pair in parts:
+            for i, ref in enumerate(pair):
+                outs[0][i * ref.shape[0] : (i + 1) * ref.shape[0], :, lane : lane + ref.shape[2]] = ref[...]
+            lane += pair[0].shape[2]
+
+
+def phase(*items):
+    shapes = [phase_shapes(*t) for t in items]
+
+    def body(*refs):
+        at = sum(2 * len(parts) for _, parts in items)
+        ins, outs = list(refs[:at]), list(refs[at:])
+        for (mode, parts), made in zip(items, shapes):
+            mine = [(ins.pop(0), ins.pop(0)) for _ in parts]
+            phase_part(mode, mine, [outs.pop(0) for _ in made])
+
+    flat = resident(
+        body,
+        [t for _, parts in items for pair in parts for t in pair],
+        [sds(s, BF16) for made in shapes for s in made],
+        vmem=16,
+        name="phase",
+    )
+    flat = list(flat)
+    return [[flat.pop(0) for _ in made] for made in shapes]
 
 
 class Hops(Chunk):
@@ -1454,57 +1558,87 @@
         self.axes = {"x": ("x", 2, 1), "z": ("o", outer, 1), "w": ("o", outer, 2)}
         self.extra = [("o", outer, 1 << b) for b in range(2, outer.bit_length() - 1)]
 
+    def over(self, way, t):
+        return lax.ppermute(t, "tensor", FLIP) if way == "partner" else flip_bit(t, *self.axes[way])
+
     def send(self, *parts):
         self.keep, self.sent, self.got = [], [], []
         for total, way in parts:
             if way == "partner":
                 keep, sent = total[1], total[0]
-                got = lax.ppermute(sent, "tensor", FLIP)
             else:
                 half = total.shape[-3] // 2
                 keep, sent = total[..., :half, :, :], total[..., half:, :, :]
-                got = flip_bit(sent, *self.axes[way])
             self.keep.append(keep)
             self.sent.append(sent)
-            self.got.append(got)
-
-    def folded(self):
-        return [fold(k, g) for k, g in zip(self.keep, self.got)]
+            self.got.append(self.over(way, sent))
 
     def first(self):
         total = fold(self.keep, self.got)
         self.send((total[..., :CUT], "x"), (total[..., CUT:], "z"))
 
-    def hop(self, *ways):
-        self.send(*zip(self.folded(), ways))
-
     def first_hop(self, way):
         self.send((fold(self.keep, self.got), way))
 
+    def parts(self):
+        return list(zip(self.keep, self.got))
+
+    def hop(self, *ways):
+        items = [("partner" if w == "partner" else "half", [p]) for w, p in zip(ways, self.parts())]
+
+        def then(made):
+            self.keep, self.sent = [m[0] for m in made], [m[1] for m in made]
+            self.got = [self.over(w, s) for w, s in zip(ways, self.sent)]
+
+        return items, then
+
+    def absorb(self, other):
+        self.keep, self.got = self.keep + other.keep, self.got + other.got
+
     def last_hop(self):
-        self.send((jnp.concatenate(self.folded(), axis=-1), "w"))
+        def then(made):
+            ((keep, sent),) = made
+            self.keep, self.sent = [keep], [sent]
+            self.got = [self.over("w", sent)]
+
+        return [("last", self.parts())], then
+
+    def back_first(self):
+        def then(made):
+            ((total,),) = made
+            for s in self.extra:
+                total = fold(total, flip_bit(total, *s))
+            self.keep = self.sent = [total]
+            self.got = [self.over("w", total)]
+
+        return [("sum", self.parts())], then
 
     def back(self, *ways):
-        self.sent = self.keep
-        self.got = [flip_bit(k, *self.axes[w]) for k, w in zip(self.keep, ways)]
-
-    def back_first(self):
-        (total,) = self.folded()
-        for s in self.extra:
-            total = fold(total, flip_bit(total, *s))
-        self.keep = [total]
-        self.back("w")
-
-    def joined(self, parts=1):
-        self.keep = [jnp.concatenate([k, g], axis=0) for k, g in zip(self.keep, self.got)]
-        if parts == 2:
-            (total,) = self.keep
-            self.keep = [total[..., :CUT], total[..., CUT:]]
+        if len(ways) == 2 and len(self.keep) == 1:
+            items = [("split", self.parts())]
+        else:
+            items = [("join", [p]) for p in self.parts()]
+
+        def then(made):
+            self.keep = self.sent = [t for m in made for t in m]
+            self.got = [self.over(w, t) for w, t in zip(ways, self.keep)]
+
+        return items, then
 
     def back_core(self):
-        self.joined()
-        self.keep = self.sent = jnp.concatenate(self.keep, axis=-1)
-        self.gather_core()
+        def then(made):
+            ((self.keep,),) = made
+            self.sent = self.keep
+            self.gather_core()
+
+        return [("join", self.parts())], then
+
+
+def all_steps(*steps):
+    made = phase(*[item for items, _ in steps for item in items])
+    for items, then in steps:
+        then(made[: len(items)])
+        made = made[len(items) :]
 
 
 def mask_biases(seg):
@@ -1629,77 +1763,65 @@
     dqkv_e, gt, sums_e = attend_back_even(wqkv, incl, qkv_e, o1, lse1, do1, o2, lse2, do2, part, dh1_1, dh1_2, x, gb)
     dqkv_e, gt, sums_e, up_go = down.wait(dqkv_e, gt, sums_e, up_go)
     up = link.hops(up_keep, link.core(up_go))
-    down.first_hop("z")
+    down.keep, down.got = [down.keep], [down.got]
+    all_steps(down.hop("z"))
     small = jnp.stack([sums_e[0] + sums_o[0], sums1[0] + sums2[0], sums_e[1] + sums_o[1], sums1[1] + sums2[1], sums_o[2]])
     qkv_keep, qkv_go = grad_qkv(me_z, a_e, a_o, after(dqkv_e, *down.sent), dqkv_o)
-    qkv_keep, qkv_go, down.got = up.wait(qkv_keep, qkv_go, down.got)
+    out = link.finish(
+        jnp.concatenate([out, out_two], axis=0), jnp.concatenate([out_got, after(out_last, dqkv_e)], axis=0), link.out_shape
+    )
+    qkv_keep, qkv_go, down.got, out = up.wait(qkv_keep, qkv_go, down.got, out)
     qkv = link.hops(qkv_keep, link.core(qkv_go))
     small_steps = iter(link.small_steps())
     small_got = link.flip(after(small, qkv_go), next(small_steps))
 
-    def wait_all(with_down=True):
+    chunks = [up, qkv]
+
+    def wait_all():
         nonlocal small, small_got
-        (qkv.got, small_got, *rest) = up.wait(qkv.got, small_got, *([down.got] if with_down else []))
-        if rest:
-            (down.got,) = rest
+        got, small_got = sync([c.got for c in chunks], small_got)
+        for c, g in zip(chunks, got):
+            c.got = g
         if small_got is not None:
             small = small + small_got
             step = next(small_steps, None)
             small_got = None if step is None else link.flip(small, step)
 
-    wait_all(False)
+    wait_all()
+    chunks.append(down)
     up.first()
     qkv.first_hop("partner")
-    down.hop("x")
+    all_steps(down.hop("x"))
     wait_all()
-    up.hop("partner", "x")
-    qkv.hop("z")
-    down.hop("w")
+    all_steps(up.hop("partner", "x"), qkv.hop("z"), down.hop("w"))
     wait_all()
-    up.hop("z", "partner")
-    qkv.hop("x")
-    down.back_first()
+    all_steps(up.hop("z", "partner"), qkv.hop("x"), down.back_first())
     half = gt.shape[0] // 2
     gt_got = [link.partner(after(gt[:half], *up.sent))]
     wait_all()
-    up.last_hop()
-    qkv.hop("w")
-    down.joined()
-    down.back("x")
+    up.absorb(qkv)
+    chunks.remove(qkv)
+    all_steps(up.last_hop(), down.back("x"))
     gt_got.append(link.partner(after(gt[half:], *up.sent)))
     (gt_got[0],) = up.wait(gt_got[0])
     wait_all()
-    up.back_first()
-    qkv.back_first()
-    down.joined()
-    down.back("z")
+    all_steps(up.back_first(), down.back("z"))
     (gt_got[1],) = up.wait(gt_got[1])
     wait_all()
     while small_got is not None:
         wait_all()
-    up.joined(2)
-    up.back("z", "x")
-    qkv.joined()
-    qkv.back("x")
-    down.back_core()
-    out, gt, *_ = link.finish(jnp.concatenate([out, out_two], axis=0), jnp.concatenate([out_got, out_last], axis=0), gt, jnp.concatenate(gt_got, axis=0))
-    out, gt = up.wait(out, gt)
+    all_steps(up.back("z", "x"), down.back_core())
     wait_all()
-    up.joined()
-    up.back("x", "z")
-    qkv.joined()
-    qkv.back("z")
-    (g_down,) = unpack("down", me_z, 0, after(down.keep, up.sent, qkv.sent))
-    (g_down,) = unpack("down", me_z, 1, down.got, (g_down,))
-    g_down, qkv.got = up.wait(g_down, qkv.got)
-    up.back_core()
-    qkv.back_core()
-    g_up = unpack("up", me, 0, after(up.keep, qkv.sent))
-    (g_qkv,) = unpack("qkv", me_z, 0, after(qkv.keep, g_up))
-    (g_qkv,) = up.wait(g_qkv)
-    g_up, g_out = unpack("up", me, 1, up.got, g_up)
-    qkv.wait(g_up)
-    (g_qkv,) = unpack("qkv", me_z, 1, qkv.got, (g_qkv,))
+    all_steps(up.back("x", "z"))
+    g_down = unpack_down(me_z, 0, after(down.keep, *up.sent))
+    g_down = unpack_down(me_z, 1, down.got, (g_down,))
+    gt = link.finish(gt, jnp.concatenate(gt_got, axis=0), link.tokens_shape).astype(F32)
+    small = (small[0:2], small[2:4], small[4])
+    g_down, gt, small = up.wait(g_down, gt, small)
+    all_steps(up.back_core())
+    g_rest = unpack_rest(me, 0, up.keep)
+    g_rest = up.wait(*g_rest)
+    g_up, g_out, g_qkv = unpack_rest(me, 1, up.got, g_rest)
     return out, gt, (g_qkv, g_out, g_up, g_down), small
 
 
@@ -1711,12 +1833,10 @@
     x = mine(tokens).reshape(-1, width)
     gb = jnp.concatenate([gain, bias, pass_embed[None]], axis=0)
     link = Link(outer, w_qkv, w_out, w_up, w_down)
-    link.finish = lambda out, out_got, gt, gt_got: (
-        ordered(ty, out, out_got).reshape(cotangent.shape),
-        ordered(ty, gt, gt_got).reshape(tokens.shape).astype(F32),
-    )
+    link.out_shape, link.tokens_shape = cotangent.shape, tokens.shape
+    link.finish = lambda mine, theirs, shape: ordered(ty, mine, theirs).reshape(shape)
     out, gt, grads, small = local_part(x, mine(segments), mine(cotangent), gb, link)
-    return out, gt, *grads, small[0:2], small[2:4], small[4]
+    return out, gt, *grads, *small
 
 
 def solution(mesh):

time: 392 us -> 369 us (0.941)
  starting transfers between devices: 53.7 us -> 43.5 us
  waiting for transfers between devices: 93.8 us -> 103 us
  Pallas kernels: 181 us -> 172 us
  local copies, waits for them, and re-layouts: 23.6 us -> 16.1 us
  other arithmetic: 31.3 us -> 25.6 us
    pallas_call x6 -> x2, Pallas kernels: 21.3 us -> 4.21 us  [packed_call(): pl.pallas_call(body, grid_spec=pltpu.PrefetchScalarGridSpec(num_scalar_pr...]
    pallas_call x12 -> x23, Pallas kernels: 159 us -> 168 us  [resident(): pl.pallas_call(body, in_specs=[s for _, s in ins], out_specs=[s for _, s...]
    ppermute x27 -> x23, starting transfers between devices: 33.7 us -> 25.6 us  [flip_bit(): return lax.ppermute(array, axis, [(i, i ^ bit) for i in range(size)])]
    ppermute x27 -> x23, waiting for transfers between devices: 65.7 us -> 72.4 us  [flip_bit(): return lax.ppermute(array, axis, [(i, i ^ bit) for i in range(size)])]
    unnamed x113 -> x91, local copies, waits for them, and re-layouts: 11.7 us -> 5.76 us
    ppermute x8, waiting for transfers between devices: 15.1 us -> 19.2 us  [partner(): return lax.ppermute(t, 'tensor', FLIP)]
    convert_element_type x18 -> x3, other arithmetic: 9 us -> 5.22 us  [fold(): return sum((p.astype(F32) for p in parts)).astype(BF16)]
  transfers between devices with their start and end apart: 53 -> 48, of which waited for: 27 -> 29; matrix products, arithmetic and copies ran while one was open for 8% -> 8% of each run, Pallas kernels for 30% -> 30%
where the time goes in v1:
time: 369 us; the launch traced here: 362 us
  Pallas kernels  172 us (47%)
  waiting for transfers between devices  103 us (28%)
  starting transfers between devices  43.5 us (12%)
  other arithmetic  25.6 us (7%)
  local copies, waits for them, and re-layouts  16.1 us (4%)
    pallas_call x23, Pallas kernels, resident(): pl.pallas_call(body, in_specs=[s for _, s in ins], out_specs=[s for _, s...  168 us
    ppermute x23, waiting for transfers between devices, flip_bit(): return lax.ppermute(array, axis, [(i, i ^ bit) for i in range(size)])  72.4 us
    ppermute x23, starting transfers between devices, flip_bit(): return lax.ppermute(array, axis, [(i, i ^ bit) for i in range(size)])  25.6 us
    ppermute x8, waiting for transfers between devices, partner(): return lax.ppermute(t, 'tensor', FLIP)  19.2 us
    ppermute x8, starting transfers between devices, partner(): return lax.ppermute(t, 'tensor', FLIP)  9.74 us
    another operation x11, other arithmetic, ordered(): jnp.stack([jnp.where(first, mine, theirs), jnp.where(first, theirs, mine)])  7.46 us
  transfers between devices with their start and end apart: 48, of which 29 were waited for; matrix products, arithmetic and copies ran while one was open for 8% of the time, Pallas kernels for 30%

profile of v1, /device:TPU:0, one launch (start us, length us, event | category | flops | bytes accessed | tf_op | source)
XLA Modules:
  0.0 362.3 jit_solution(15327230566794400491)
XLA Ops:
  0.7 2.0 constant_dynamic-slice_fusion.7
  2.7 3.0 collective-permute-start
  6.4 1.3 convert_reduce_fusion
  10.0 2.4 attend_first.2
  14.4 1.2 constant_dynamic-slice_fusion.4.cot_far
  16.2 1.7 collective-permute-start.1
  17.9 1.9 constant_dynamic-slice_fusion.2
  19.8 1.5 collective-permute-start.3
  22.9 5.0 %collective-permute-done.1 = bf16[576,384]{1,0:T(8,128)(2,1)} collective-permute-done((bf16[576,384]{1,0:T(8,128)(2,1)}, bf16[576,384]{1,0:T(8,128)(2,1)}, u32[]{:S(2)}, u32[]{:S(2)}) %collective-permute-start.1) | collective-permute-done | bytes 442400 | tf_op jit(solution)/shard_map/ppermute | solution.py:1679
  27.8 1.2 select_bitcast_fusion.5
  30.1 7.1 %collective-permute-done.2 = bf16[96,768]{1,0:T(8,128)(2,1)} collective-permute-done((bf16[96,768]{1,0:T(8,128)(2,1)S(1)}, bf16[96,768]{1,0:T(8,128)(2,1)}, u32[]{:S(2)}, u32[]{:S(2)}) %collective-permute-start.2) | collective-permute-done | bytes 147488 | tf_op jit(solution)/shard_map/ppermute | solution.py:1712
  38.4 1.5 collective-permute-start.5
  40.5 1.6 select_bitcast_fusion.1
  42.3 1.3 copy-done.7
  43.6 2.1 pad_maximum_fusion.w_far
  45.7 2.4 attend_first.3
  48.1 1.6 pad_maximum_fusion.2.qkve_far
  51.9 1.5 collective-permute-start.4
  54.7 9.0 %mlp_own.1 = (f32[512,768]{1,0:T(8,128)}, bf16[512,768]{1,0:T(8,128)(2,1)}, bf16[512,3072]{1,0:T(8,128)(2,1)}, bf16[512,3072]{1,0:T(8,128)(2,1)}, f32[512,768]{1,0:T(8,128)}) custom-call(bf16[512,768]{1,0:T(8,128)(2,1)} %bitcast.58, bf16[512,768]{1,0:T(8,128)(2,1)} %pad_maximum_fusion.10.o_far.o1_far, bf16[768,768]{1,0:T(8,128)(2,1)} %pad_maximum_fusion.8.wout_far, ...), custom_call_target="tpu_custom_call" | custom-call | tf_op jit(solution)/shard_map/mlp_own/pallas_call | solution.py:112
  63.7 3.3 collective-permute-done.5.refs_4_.refs_6_
  68.2 2.8 collective-permute-done.9.refs_2_.refs_3_
  73.4 8.8 %mlp_other.1 = (bf16[512,3072]{1,0:T(8,128)(2,1)}, bf16[512,3072]{1,0:T(8,128)(2,1)}, f32[512,768]{1,0:T(8,128)}, bf16[512,768]{1,0:T(8,128)(2,1)}) custom-call(bf16[512,768]{1,0:T(8,128)(2,1)} %get-tuple-element.198.n2_far.n1_far, f32[512,768]{1,0:T(8,128)} %get-tuple-element.199.part_far, ...), custom_call_target="tpu_custom_call", output_to_operand_aliasing={{0}: (2, {}), {1}: (3, {})} | custom-call | tf_op jit(solution)/shard_map/mlp_other/pallas_call | solution.py:112
  82.3 14.0 %attend_second.1 = (bf16[3,512,768]{2,1,0:T(8,128)(2,1)}, bf16[2,512,768]{2,1,0:T(8,128)(2,1)}, f32[2,3,4,512]{3,2,1,0:T(4,128)S(1)}) custom-call(bf16[512,768]{1,0:T(8,128)(2,1)} %get-tuple-element.206.a_far.ao_far, bf16[3,768,768]{2,1,0:T(8,128)(2,1)} %pad_maximum_fusion.w_far, f32[2,256,256]{2,1,0:T(8,128)} %copy-done.2, ...), custom_call_target="tpu_custom_call" | custom-call | flops 415236096 | tf_op jit(solution)/shard_map/attend_second/pallas_call | solution.py:112
  96.3 37.4 %mlp_second.1 = (bf16[1,512,768]{2,1,0:T(8,128)(2,1)}, bf16[1,512,768]{2,1,0:T(8,128)(2,1)}, bf16[1024,768]{1,0:T(8,128)(2,1)}, bf16[1024,3072]{1,0:T(8,128)(2,1...) custom-call(bf16[512,768]{1,0:T(8,128)(2,1)} %bitcast.59, ...), custom_call_target="tpu_custom_call" | custom-call | tf_op jit(solution)/shard_map/mlp_second/pallas_call | solution.py:112
  134.7 18.9 %attend_back.1 = (bf16[3,512,768]{2,1,0:T(8,128)(2,1)}, bf16[3,512,768]{2,1,0:T(8,128)(2,1)}, f32[512,768]{1,0:T(8,128)}, f32[3,768]{1,0:T(4,128)S(1)}) custom-call(bf16[3,768,768]{2,1,0:T(8,128)(2,1)} %pad_maximum_fusion.w_far, f32[2,256,256]{2,1,0:T(8,128)} %copy-done.2, f32[2,256,256]{2,1,0:T(8,128)} %get-tuple-element.382.strict_far, ...), custom_call_target="tpu_custom_call" | custom-call | flops 868220928 | tf_op jit(solution)/shard_map/attend_back/pallas_call | solution.py:112
  155.0 14.1 %grad_down.1 = (bf16[2,8,96,768]{3,2,1,0:T(8,128)(2,1)}, bf16[2,8,96,768]{3,2,1,0:T(8,128)(2,1)}) custom-call(s32[2]{0:T(128)S(1)} %rev.3.me_ref, bf16[512,3072]{1,0:T(8,128)(2,1)} %get-tuple-element.204.g1_far, bf16[1024,3072]{1,0:T(8,128)(2,1)} %get-tuple-element.212.g2_far, f32[512,768]{1,0:T(8,128)} %get-tuple-element.228.dy_far, ...), custom_call_target="tpu_custom_call" | custom-call | flops 452984832 | tf_op jit(solution)/shard_map/grad_down/pallas_call | solution.py:112
  169.1 4.0 %collective-permute-done.13 = bf16[1,512,768]{2,1,0:T(8,128)(2,1)S(1)} collective-permute-done((bf16[1,512,768]{2,1,0:T(8,128)(2,1)S(1)}, bf16[1,512,768]{2,1,0:T(8,128)(2,1)S(1)}, u32[]{:S(2)}, u32[]{:S(2)}) %collective-permute-start.13) | collective-permute-done | bytes 786464 | tf_op jit(solution)/shard_map/ppermute | solution.py:1712
  173.1 13.5 %mlp_back.1 = (bf16[512,3072]{1,0:T(8,128)(2,1)}, f32[512,768]{1,0:T(8,128)}, bf16[512,768]{1,0:T(8,128)(2,1)}, bf16[512,768]{1,0:T(8,128)(2,1)}, f32[2,768]{1,0:T(2,128)S(1)}) custom-call(f32[512,768]{1,0:T(8,128)} %get-tuple-element.228.dy_far, f32[512,768]{1,0:T(8,128)} %get-tuple-element.229.h1_far, bf16[768,768]{1,0:T(8,128)(2,1)} %pad_maximum_fusion.8.wout_far, ...), custom_call_target="tpu_custom_call" | custom-call | tf_op jit(solution)/shard_map/mlp_back/pallas_call | solution.py:112
  187.3 1.6 slice_bitcast_fusion
  190.4 16.7 %grad_up.1 = (bf16[2,8,48,1920]{3,2,1,0:T(8,128)(2,1)}, bf16[2,8,48,1920]{3,2,1,0:T(8,128)(2,1)}) custom-call(s32[3]{0:T(128)} %pad_add_fusion.1.me_ref, bf16[512,768]{1,0:T(8,128)(2,1)} %get-tuple-element.198.n2_far.n1_far, bf16[1024,768]{1,0:T(8,128)(2,1)} %get-tuple-element.236.n2_far, bf16[512,3072]{1,0:T(8,128)(2,1)} %get-tuple-element.238.du1_far, ...), custom_call_target="tpu_custom_call" | custom-call | flops 566231040 | tf_op jit(solution)/shard_map/grad_up/pallas_call | solution.py:112
  207.2 12.5 %attend_back_even.1 = (bf16[3,512,768]{2,1,0:T(8,128)(2,1)}, bf16[512,768]{1,0:T(8,128)(2,1)S(1)}, f32[2,768]{1,0:T(2,128)S(1)}) custom-call(bf16[3,768,768]{2,1,0:T(8,128)(2,1)} %pad_maximum_fusion.w_far, f32[2,256,256]{2,1,0:T(8,128)} %copy-done.2, bf16[3,512,768]{2,1,0:T(8,128)(2,1)} %pad_maximum_fusion.2.qkve_far, ...), custom_call_target="tpu_custom_call" | custom-call | flops 364904448 | tf_op jit(solution)/shard_map/attend_back_even/pallas_call | solution.py:112
  220.8 1.6 collective-permute-start.17
  222.4 9.6 %grad_qkv.1 = (bf16[2,8,48,1152]{3,2,1,0:T(8,128)(2,1)}, bf16[2,8,48,1152]{3,2,1,0:T(8,128)(2,1)}) custom-call(s32[2]{0:T(128)S(1)} %rev.3.me_ref, bf16[512,768]{1,0:T(8,128)(2,1)} %copy-done.4, bf16[512,768]{1,0:T(8,128)(2,1)} %get-tuple-element.206.a_far.ao_far, bf16[3,512,768]{2,1,0:T(8,128)(2,1)} %get-tuple-element.253.de_far, ...), custom_call_target="tpu_custom_call" | custom-call | flops 226492416 | tf_op jit(solution)/shard_map/grad_qkv/pallas_call | solution.py:112
  232.4 1.9 pad_maximum_fusion.1
  234.3 2.5 collective-permute-done.17.refs_1_
  237.4 2.7 collective-permute-done.19
  240.7 1.9 add_convert_fusion.2
  244.5 2.6 add_convert_fusion
  247.2 1.7 collective-permute-start.21
  249.0 1.5 collective-permute-start.20
  252.2 18.2 %collective-permute-done.23.refs_7_ = bf16[2,96,768]{2,1,0:T(8,128)(2,1)S(1)} collective-permute-done((bf16[2,96,768]{2,1,0:T(8,128)(2,1)S(1)}, bf16[2,96,768]{2,1,0:T(8,128)(2,1)S(1)}, u32[]{:S(2)}, u32[]{:S(2)}) %collective-permute-start.23) | collective-permute-done | bytes 294944 | tf_op jit(solution)/shard_map/ppermute | solution.py:32
  271.1 1.5 collective-permute-start.26
  273.6 2.6 collective-permute-start.28
  277.2 5.5 %collective-permute-done.29 = f32[5,768]{1,0:T(8,128)S(1)} collective-permute-done((f32[5,768]{1,0:T(8,128)S(1)}, f32[5,768]{1,0:T(8,128)S(1)}, u32[]{:S(2)}, u32[]{:S(2)}) %collective-permute-start.29) | collective-permute-done | bytes 15392 | tf_op jit(solution)/shard_map/ppermute | solution.py:32
  282.7 1.8 collective-permute-done.28.refs_7_
  284.5 2.0 collective-permute-done.27.refs_5_
  286.6 2.9 collective-permute-start.34
  293.1 3.6 %collective-permute-done.30.refs_1_ = bf16[2,48,768]{2,1,0:T(8,128)(2,1)S(1)} collective-permute-done((bf16[2,48,768]{2,1,0:T(8,128)(2,1)S(1)}, bf16[2,48,768]{2,1,0:T(8,128)(2,1)S(1)}, u32[]{:S(2)}, u32[]{:S(2)}) %collective-permute-start.30) | collective-permute-done | bytes 147488 | tf_op jit(solution)/shard_map/ppermute | solution.py:32
  296.8 4.4 %collective-permute-done.33.refs_7_ = bf16[1,96,768]{2,1,0:T(8,128)(2,1)S(1)} collective-permute-done((bf16[1,96,768]{2,1,0:T(8,128)(2,1)S(1)}, bf16[1,96,768]{2,1,0:T(8,128)(2,1)S(1)}, u32[]{:S(2)}, u32[]{:S(2)}) %collective-permute-start.33) | collective-permute-done | bytes 147488 | tf_op jit(solution)/shard_map/ppermute | solution.py:32
  301.6 1.6 collective-permute-start.37
  304.4 9.5 %collective-permute-done.35.refs_1_ = bf16[1,48,3072]{2,1,0:T(8,128)(2,1)S(1)} collective-permute-done((bf16[1,48,3072]{2,1,0:T(8,128)(2,1)S(1)}, bf16[1,48,3072]{2,1,0:T(8,128)(2,1)S(1)}, u32[]{:S(2)}, u32[]{:S(2)}) %collective-permute-start.35) | collective-permute-done | bytes 294944 | tf_op jit(solution)/shard_map/ppermute | solution.py:32
  314.8 3.4 collective-permute-start.39
  318.2 4.2 %collective-permute-done.40 = bf16[256,768]{1,0:T(8,128)(2,1)S(1)} collective-permute-done((bf16[256,768]{1,0:T(8,128)(2,1)S(1)}, bf16[256,768]{1,0:T(8,128)(2,1)S(1)}, u32[]{:S(2)}, u32[]{:S(2)}) %collective-permute-start.40) | collective-permute-done | bytes 393248 | tf_op jit(solution)/shard_map/ppermute | solution.py:1712
  322.4 2.7 collective-permute-done.39.refs_1_
  325.2 4.2 %collective-permute-done.41.refs_3_ = bf16[4,96,768]{2,1,0:T(8,128)(2,1)S(1)} collective-permute-done((bf16[4,96,768]{2,1,0:T(8,128)(2,1)S(1)}, bf16[4,96,768]{2,1,0:T(8,128)(2,1)S(1)}, u32[]{:S(2)}, u32[]{:S(2)}) %collective-permute-start.41) | collective-permute-done | bytes 589856 | tf_op jit(solution)/shard_map/ppermute | solution.py:32
  330.6 8.4 %collective-permute-done.42.refs_1_ = bf16[2,48,1536]{2,1,0:T(8,128)(2,1)S(1)} collective-permute-done((bf16[2,48,1536]{2,1,0:T(8,128)(2,1)S(1)}, bf16[2,48,1536]{2,1,0:T(8,128)(2,1)S(1)}, u32[]{:S(2)}, u32[]{:S(2)}) %collective-permute-start.42) | collective-permute-done | bytes 294944 | tf_op jit(solution)/shard_map/ppermute | solution.py:32
  339.5 1.7 collective-permute-start.46
  342.1 1.9 convert.1
  344.0 2.1 unpack_down.2.refs_0_
  346.1 2.1 unpack_down.3
  348.2 5.9 %collective-permute-done.45.refs_1_ = bf16[4,48,1536]{2,1,0:T(8,128)(2,1)S(1)} collective-permute-done((bf16[4,48,1536]{2,1,0:T(8,128)(2,1)S(1)}, bf16[4,48,1536]{2,1,0:T(8,128)(2,1)S(1)}, u32[]{:S(2)}, u32[]{:S(2)}) %collective-permute-start.45) | collective-permute-done | bytes 589856 | tf_op jit(solution)/shard_map/ppermute | solution.py:32
  354.7 2.9 unpack_rest.2
  357.7 1.2 collective-permute-done.47.part_ref
  358.9 2.9 unpack_rest.3
  (206 shorter events, 39.8 us)
Async XLA Ops:
  0.6 13.8 %copy-start = (bf16[4,512,768]{2,1,0:T(8,128)(2,1)S(1)}, bf16[4,512,768]{2,1,0:T(8,128)(2,1)}, u32[]{:S(2)}) copy-start(bf16[4,512,768]{2,1,0:T(8,128)(2,1)} %param.19) | copy-start | bytes 9437188
  2.7 13.4 %collective-permute-start = (bf16[576,384]{1,0:T(8,128)(2,1)}, bf16[576,384]{1,0:T(8,128)(2,1)}, u32[]{:S(2)}, u32[]{:S(2)}) collective-permute-start(bf16[576,384]{1,0:T(8,128)(2,1)} %constant_dynamic-slice_fusion.7), channel_id=1, source_target_pairs={{0,1},{1,0},{2,3},{3,2},{4,5},{5,4},{6,7},{7,6},{8,9},{9,8},{10,11... | collective-permute-start | bytes 1327112 | tf_op jit(solution)/shard_map/ppermute | solution.py:1712
  16.2 11.7 %collective-permute-start.1 = (bf16[576,384]{1,0:T(8,128)(2,1)}, bf16[576,384]{1,0:T(8,128)(2,1)}, u32[]{:S(2)}, u32[]{:S(2)}) collective-permute-start(bf16[576,384]{1,0:T(8,128)(2,1)} %collective-permute-done), channel_id=1, source_target_pairs={{0,4},{4,0},{1,5},{5,1},{2,6},{6,2},{3,7},{7,3},{8,12},{12,8},{9,1... | collective-permute-start | bytes 1327112 | tf_op jit(solution)/shard_map/ppermute | solution.py:1679
  19.8 17.4 %collective-permute-start.3 = (bf16[768,384]{1,0:T(8,128)(2,1)}, bf16[768,384]{1,0:T(8,128)(2,1)S(1)}, u32[]{:S(2)}, u32[]{:S(2)}) collective-permute-start(bf16[768,384]{1,0:T(8,128)(2,1)} %constant_dynamic-slice_fusion.2), channel_id=1, source_target_pairs={{0,1},{1,0},{2,3},{3,2},{4,5},{5,4},{6,7},{7,6},{8,9},{9,8},{10,11... | collective-permute-start | bytes 1769480 | tf_op jit(solution)/shard_map/ppermute | solution.py:1712
  22.3 14.9 %collective-permute-start.2 = (bf16[96,768]{1,0:T(8,128)(2,1)S(1)}, bf16[96,768]{1,0:T(8,128)(2,1)}, u32[]{:S(2)}, u32[]{:S(2)}) collective-permute-start(bf16[96,768]{1,0:T(8,128)(2,1)S(1)} %constant_dynamic-slice_fusion.3), channel_id=1, source_target_pairs={{0,1},{1,0},{2,3},{3,2},{4,5},{5,4},{6,7},{7,6},{8,9},{9,8},{10,11... | collective-permute-start | bytes 442376 | tf_op jit(solution)/shard_map/ppermute | solution.py:1712
  22.9 14.4 %copy-start.20 = (bf16[1536,768]{1,0:T(8,128)(2,1)S(1)}, bf16[1536,768]{1,0:T(8,128)(2,1)}, u32[]{:S(2)}) copy-start(bf16[1536,768]{1,0:T(8,128)(2,1)} %refs_5_.3) | copy-start | bytes 7077892
  37.2 3.3 collective-permute-start.6
  38.4 28.6 %collective-permute-start.5 = (bf16[768,768]{1,0:T(8,128)(2,1)}, bf16[768,768]{1,0:T(8,128)(2,1)}, u32[]{:S(2)}, u32[]{:S(2)}) collective-permute-start(bf16[768,768]{1,0:T(8,128)(2,1)} %pad_maximum_fusion.7), channel_id=1, source_target_pairs={{0,1},{1,0},{2,3},{3,2},{4,5},{5,4},{6,7},{7,6},{8,9},{9,8},{10,11... | collective-permute-start | bytes 3538952 | tf_op jit(solution)/shard_map/ppermute | solution.py:1712
  40.0 10.7 %collective-permute-start.7 = (bf16[96,768]{1,0:T(8,128)(2,1)}, bf16[96,768]{1,0:T(8,128)(2,1)}, u32[]{:S(2)}, u32[]{:S(2)}) collective-permute-start(bf16[96,768]{1,0:T(8,128)(2,1)} %collective-permute-done.2), channel_id=1, source_target_pairs={{0,4},{4,0},{1,5},{5,1},{2,6},{6,2},{3,7},{7,3},{8,12},{12,8},{9,1... | collective-permute-start | bytes 442376 | tf_op jit(solution)/shard_map/ppermute | solution.py:1679
  51.8 1.7 collective-permute-start.8
  51.9 15.8 %collective-permute-start.4 = (bf16[768,384]{1,0:T(8,128)(2,1)S(1)}, bf16[768,384]{1,0:T(8,128)(2,1)S(1)}, u32[]{:S(2)}, u32[]{:S(2)}) collective-permute-start(bf16[768,384]{1,0:T(8,128)(2,1)S(1)} %copy-done.24), channel_id=1, source_target_pairs={{0,4},{4,0},{1,5},{5,1},{2,6},{6,2},{3,7},{7,3},{8,12},{12,8},{9,1... | collective-permute-start | bytes 1769480 | tf_op jit(solution)/shard_map/ppermute | solution.py:1679
  53.5 18.9 %copy-start.11 = (f32[5,768]{1,0:T(8,128)}, f32[5,768]{1,0:T(8,128)S(1)}, u32[]{:S(2)}) copy-start(f32[5,768]{1,0:T(8,128)S(1)} %pad_maximum_fusion.14.gb_ref) | copy-start | bytes 46084
  67.7 4.7 %collective-permute-start.11 = (bf16[768,768]{1,0:T(8,128)(2,1)}, bf16[768,768]{1,0:T(8,128)(2,1)S(1)}, u32[]{:S(2)}, u32[]{:S(2)}) collective-permute-start(bf16[768,768]{1,0:T(8,128)(2,1)} %collective-permute-done.5.refs_4_.refs_6_), channel_id=1, source_target_pairs={{0,2},{2,0},{1,3},{3,1},{4,6},{6,4},{5,7},{7,5},{8,10},{10,8},{9,1... | collective-permute-start | bytes 3538952 | tf_op jit(solution)/shard_map/ppermute | solution.py:1715
  67.7 3.3 collective-permute-start.9
  68.2 4.0 %collective-permute-start.10 = (bf16[768,384]{1,0:T(8,128)(2,1)S(1)}, bf16[768,384]{1,0:T(8,128)(2,1)S(1)}, u32[]{:S(2)}, u32[]{:S(2)}) collective-permute-start(bf16[768,384]{1,0:T(8,128)(2,1)S(1)} %collective-permute-done.4.refs_1_.refs_2_), channel_id=1, source_target_pairs={{0,2},{2,0},{1,3},{3,1},{4,6},{6,4},{5,7},{7,5},{8,10},{10,8},{9,1... | collective-permute-start | bytes 1769480 | tf_op jit(solution)/shard_map/ppermute | solution.py:1715
  96.3 38.5 %copy-start.12 = (f32[5,768]{1,0:T(8,128)S(1)}, f32[5,768]{1,0:T(8,128)}, u32[]{:S(2)}) copy-start(f32[5,768]{1,0:T(8,128)} %copy-done.11) | copy-start | bytes 46084
  133.7 20.0 %collective-permute-start.12 = (bf16[1,512,768]{2,1,0:T(8,128)(2,1)}, bf16[1,512,768]{2,1,0:T(8,128)(2,1)S(1)}, u32[]{:S(2)}, u32[]{:S(2)}) collective-permute-start(bf16[1,512,768]{2,1,0:T(8,128)(2,1)} %get-tuple-element.213), channel_id=1, source_target_pairs={{0,1},{1,0},{2,3},{3,2},{4,5},{5,4},{6,7},{7,6},{8,9},{9,8},{10,11... | collective-permute-start | bytes 2359304 | tf_op jit(solution)/shard_map/ppermute | solution.py:1712
  134.7 18.9 %copy-start.32 = (bf16[1,512,768]{2,1,0:T(8,128)(2,1)S(1)}, bf16[1,512,768]{2,1,0:T(8,128)(2,1)}, u32[]{:S(2)}) copy-start(bf16[1,512,768]{2,1,0:T(8,128)(2,1)} %get-tuple-element.225) | copy-start | bytes 2359300
  153.6 15.4 %copy-start.34 = (bf16[1,512,768]{2,1,0:T(8,128)(2,1)}, bf16[1,512,768]{2,1,0:T(8,128)(2,1)S(1)}, u32[]{:S(2)}) copy-start(bf16[1,512,768]{2,1,0:T(8,128)(2,1)S(1)} %collective-permute-done.12) | copy-start | bytes 2359300
  153.7 19.4 %collective-permute-start.13 = (bf16[1,512,768]{2,1,0:T(8,128)(2,1)S(1)}, bf16[1,512,768]{2,1,0:T(8,128)(2,1)S(1)}, u32[]{:S(2)}, u32[]{:S(2)}) collective-permute-start(bf16[1,512,768]{2,1,0:T(8,128)(2,1)S(1)} %copy-done.32), channel_id=1, source_target_pairs={{0,1},{1,0},{2,3},{3,2},{4,5},{5,4},{6,7},{7,6},{8,9},{9,8},{10,11... | collective-permute-start | bytes 2359304 | tf_op jit(solution)/shard_map/ppermute | solution.py:1712
  173.1 13.5 %copy-start.36 = (bf16[1,512,768]{2,1,0:T(8,128)(2,1)}, bf16[1,512,768]{2,1,0:T(8,128)(2,1)S(1)}, u32[]{:S(2)}) copy-start(bf16[1,512,768]{2,1,0:T(8,128)(2,1)S(1)} %collective-permute-done.13) | copy-start | bytes 2359300
  173.1 13.5 %collective-permute-start.14 = (bf16[2,8,96,768]{3,2,1,0:T(8,128)(2,1)}, bf16[2,8,96,768]{3,2,1,0:T(8,128)(2,1)S(1)}, u32[]{:S(2)}, u32[]{:S(2)}) collective-permute-start(bf16[2,8,96,768]{3,2,1,0:T(8,128)(2,1)} %get-tuple-element.227), channel_id=1, source_target_pairs={{0,2},{2,0},{1,3},{3,1},{4,6},{6,4},{5,7},{7,5},{8,10},{10,8},{9,1... | collective-permute-start | bytes 7077896 | tf_op jit(solution)/shard_map/ppermute | solution.py:1715
  173.1 13.5 %copy-start.29 = (bf16[2,8,96,768]{3,2,1,0:T(8,128)(2,1)S(1)}, bf16[2,8,96,768]{3,2,1,0:T(8,128)(2,1)}, u32[]{:S(2)}) copy-start(bf16[2,8,96,768]{3,2,1,0:T(8,128)(2,1)} %get-tuple-element.226) | copy-start | bytes 7077892
  188.8 30.9 %collective-permute-start.15 = (bf16[8,96,768]{2,1,0:T(8,128)(2,1)}, bf16[8,96,768]{2,1,0:T(8,128)(2,1)S(1)}, u32[]{:S(2)}, u32[]{:S(2)}) collective-permute-start(bf16[8,96,768]{2,1,0:T(8,128)(2,1)} %get-tuple-element.358), channel_id=1, source_target_pairs={{0,1},{1,0},{2,3},{3,2},{4,5},{5,4},{6,7},{7,6},{8,9},{9,8},{10,11... | collective-permute-start | bytes 3538952 | tf_op jit(solution)/shard_map/ppermute | solution.py:1473
  207.2 12.6 %copy-start.8 = (bf16[8,96,768]{2,1,0:T(8,128)(2,1)S(1)}, bf16[8,96,768]{2,1,0:T(8,128)(2,1)}, u32[]{:S(2)}) copy-start(bf16[8,96,768]{2,1,0:T(8,128)(2,1)} %get-tuple-element.357.refs_0_) | copy-start | bytes 3538948
  219.7 17.0 %collective-permute-start.16 = (bf16[2,8,48,1920]{3,2,1,0:T(8,128)(2,1)}, bf16[2,8,48,1920]{3,2,1,0:T(8,128)(2,1)}, u32[]{:S(2)}, u32[]{:S(2)}) collective-permute-start(bf16[2,8,48,1920]{3,2,1,0:T(8,128)(2,1)} %get-tuple-element.249), channel_id=1, source_target_pairs={{0,2},{2,0},{1,3},{3,1},{4,6},{6,4},{5,7},{7,5},{8,10},{10,8},{9,1... | collective-permute-start | bytes 8847368 | tf_op jit(solution)/shard_map/ppermute | solution.py:1715
  220.8 11.2 %copy-start.15 = (bf16[4,96,768]{2,1,0:T(8,128)(2,1)}, bf16[4,96,768]{2,1,0:T(8,128)(2,1)S(1)}, u32[]{:S(2)}) copy-start(bf16[4,96,768]{2,1,0:T(8,128)(2,1)S(1)} %get-tuple-element.271.refs_0_) | copy-start | bytes 1769476
  220.8 15.9 %collective-permute-start.17 = (bf16[4,96,768]{2,1,0:T(8,128)(2,1)}, bf16[4,96,768]{2,1,0:T(8,128)(2,1)S(1)}, u32[]{:S(2)}, u32[]{:S(2)}) collective-permute-start(bf16[4,96,768]{2,1,0:T(8,128)(2,1)} %get-tuple-element.252), channel_id=1, source_target_pairs={{0,8},{8,0},{16,24},{24,16},{1,9},{9,1},{17,25},{25,17},{2,10},{10... | collective-permute-start | bytes 1769480 | tf_op jit(solution)/shard_map/ppermute | solution.py:32
  222.4 9.6 %copy-start.31 = (bf16[1,512,768]{2,1,0:T(8,128)(2,1)S(1)}, bf16[1,512,768]{2,1,0:T(8,128)(2,1)}, u32[]{:S(2)}) copy-start(bf16[1,512,768]{2,1,0:T(8,128)(2,1)} %get-tuple-element.213) | copy-start | bytes 2359300
  222.4 9.6 %copy-start.33 = (bf16[1,512,768]{2,1,0:T(8,128)(2,1)S(1)}, bf16[1,512,768]{2,1,0:T(8,128)(2,1)}, u32[]{:S(2)}) copy-start(bf16[1,512,768]{2,1,0:T(8,128)(2,1)} %get-tuple-element.225) | copy-start | bytes 2359300
  222.4 9.6 %copy-start.35 = (bf16[1,512,768]{2,1,0:T(8,128)(2,1)S(1)}, bf16[1,512,768]{2,1,0:T(8,128)(2,1)}, u32[]{:S(2)}) copy-start(bf16[1,512,768]{2,1,0:T(8,128)(2,1)} %copy-done.34) | copy-start | bytes 2359300
  222.4 9.6 %copy-start.37 = (bf16[1,512,768]{2,1,0:T(8,128)(2,1)S(1)}, bf16[1,512,768]{2,1,0:T(8,128)(2,1)}, u32[]{:S(2)}) copy-start(bf16[1,512,768]{2,1,0:T(8,128)(2,1)} %copy-done.36) | copy-start | bytes 2359300
  236.7 5.9 %copy-start.17 = (bf16[4,96,768]{2,1,0:T(8,128)(2,1)}, bf16[4,96,768]{2,1,0:T(8,128)(2,1)S(1)}, u32[]{:S(2)}) copy-start(bf16[4,96,768]{2,1,0:T(8,128)(2,1)S(1)} %collective-permute-done.17.refs_1_) | copy-start | bytes 1769476
  236.7 3.9 %collective-permute-start.18 = (bf16[2,8,48,1152]{3,2,1,0:T(8,128)(2,1)}, bf16[2,8,48,1152]{3,2,1,0:T(8,128)(2,1)S(1)}, u32[]{:S(2)}, u32[]{:S(2)}) collective-permute-start(bf16[2,8,48,1152]{3,2,1,0:T(8,128)(2,1)} %get-tuple-element.262), channel_id=1, source_target_pairs={{0,2},{2,0},{1,3},{3,1},{4,6},{6,4},{5,7},{7,5},{8,10},{10,8},{9,1... | collective-permute-start | bytes 5308424 | tf_op jit(solution)/shard_map/ppermute | solution.py:1715
  236.8 3.3 collective-permute-start.19
  242.8 27.7 %collective-permute-start.22 = (bf16[8,48,1152]{2,1,0:T(8,128)(2,1)S(1)}, bf16[8,48,1152]{2,1,0:T(8,128)(2,1)S(1)}, u32[]{:S(2)}, u32[]{:S(2)}) collective-permute-start(bf16[8,48,1152]{2,1,0:T(8,128)(2,1)S(1)} %get-tuple-element.362), channel_id=1, source_target_pairs={{0,1},{1,0},{2,3},{3,2},{4,5},{5,4},{6,7},{7,6},{8,9},{9,8},{10,11... | collective-permute-start | bytes 2654216 | tf_op jit(solution)/shard_map/ppermute | solution.py:1562
  247.2 23.2 %collective-permute-start.21 = (bf16[2,4,48,1152]{3,2,1,0:T(8,128)(2,1)S(1)}, bf16[2,4,48,1152]{3,2,1,0:T(8,128)(2,1)S(1)}, u32[]{:S(2)}, u32[]{:S(2)}) collective-permute-start(bf16[2,4,48,1152]{3,2,1,0:T(8,128)(2,1)S(1)} %get-tuple-element.354), channel_id=1, source_target_pairs={{0,8},{8,0},{16,24},{24,16},{1,9},{9,1},{17,25},{25,17},{2,10},{10... | collective-permute-start | bytes 2654216 | tf_op jit(solution)/shard_map/ppermute | solution.py:32
  249.0 21.5 %collective-permute-start.20 = (bf16[2,4,48,768]{3,2,1,0:T(8,128)(2,1)S(1)}, bf16[2,4,48,768]{3,2,1,0:T(8,128)(2,1)S(1)}, u32[]{:S(2)}, u32[]{:S(2)}) collective-permute-start(bf16[2,4,48,768]{3,2,1,0:T(8,128)(2,1)S(1)} %get-tuple-element.355), channel_id=1, source_target_pairs={{0,4},{4,0},{1,5},{5,1},{2,6},{6,2},{3,7},{7,3},{8,12},{12,8},{9,1... | collective-permute-start | bytes 1769480 | tf_op jit(solution)/shard_map/ppermute | solution.py:32
  250.7 19.8 %collective-permute-start.23 = (bf16[2,96,768]{2,1,0:T(8,128)(2,1)S(1)}, bf16[2,96,768]{2,1,0:T(8,128)(2,1)S(1)}, u32[]{:S(2)}, u32[]{:S(2)}) collective-permute-start(bf16[2,96,768]{2,1,0:T(8,128)(2,1)S(1)} %get-tuple-element.273), channel_id=1, source_target_pairs={{0,4},{4,0},{1,5},{5,1},{2,6},{6,2},{3,7},{7,3},{8,12},{12,8},{9,1... | collective-permute-start | bytes 884744 | tf_op jit(solution)/shard_map/ppermute | solution.py:32
  251.3 19.2 %collective-permute-start.24 = (f32[5,768]{1,0:T(8,128)S(1)}, f32[5,768]{1,0:T(8,128)S(1)}, u32[]{:S(2)}, u32[]{:S(2)}) collective-permute-start(f32[5,768]{1,0:T(8,128)S(1)} %add.144), channel_id=1, source_target_pairs={{0,1},{1,0},{2,3},{3,2},{4,5},{5,4},{6,7},{7,6},{8,9},{9,8},{10,11... | collective-permute-start | bytes 46088 | tf_op jit(solution)/shard_map/ppermute | solution.py:32
  271.1 20.9 %copy-start.10 = (bf16[512,768]{1,0:T(8,128)(2,1)S(1)}, bf16[512,768]{1,0:T(8,128)(2,1)}, u32[]{:S(2)}) copy-start(bf16[512,768]{1,0:T(8,128)(2,1)} %copy-done.9) | copy-start | bytes 2359300
  271.1 13.4 %collective-permute-start.26 = (bf16[2,2,48,1152]{3,2,1,0:T(8,128)(2,1)S(1)}, bf16[2,2,48,1152]{3,2,1,0:T(8,128)(2,1)S(1)}, u32[]{:S(2)}, u32[]{:S(2)}) collective-permute-start(bf16[2,2,48,1152]{3,2,1,0:T(8,128)(2,1)S(1)} %get-tuple-element.282), channel_id=1, source_target_pairs={{0,4},{4,0},{1,5},{5,1},{2,6},{6,2},{3,7},{7,3},{8,12},{12,8},{9,1... | collective-permute-start | bytes 1327112 | tf_op jit(solution)/shard_map/ppermute | solution.py:32
  272.6 13.9 %collective-permute-start.27 = (bf16[4,48,1152]{2,1,0:T(8,128)(2,1)S(1)}, bf16[4,48,1152]{2,1,0:T(8,128)(2,1)S(1)}, u32[]{:S(2)}, u32[]{:S(2)}) collective-permute-start(bf16[4,48,1152]{2,1,0:T(8,128)(2,1)S(1)} %get-tuple-element.283), channel_id=1, source_target_pairs={{0,8},{8,0},{16,24},{24,16},{1,9},{9,1},{17,25},{25,17},{2,10},{10... | collective-permute-start | bytes 1327112 | tf_op jit(solution)/shard_map/ppermute | solution.py:32
  273.1 11.5 %collective-permute-start.25 = (bf16[4,48,768]{2,1,0:T(8,128)(2,1)S(1)}, bf16[4,48,768]{2,1,0:T(8,128)(2,1)S(1)}, u32[]{:S(2)}, u32[]{:S(2)}) collective-permute-start(bf16[4,48,768]{2,1,0:T(8,128)(2,1)S(1)} %get-tuple-element.281), channel_id=1, source_target_pairs={{0,1},{1,0},{2,3},{3,2},{4,5},{5,4},{6,7},{7,6},{8,9},{9,8},{10,11... | collective-permute-start | bytes 884744 | tf_op jit(solution)/shard_map/ppermute | solution.py:1562
  273.6 11.0 %collective-permute-start.28 = (bf16[1,96,768]{2,1,0:T(8,128)(2,1)S(1)}, bf16[1,96,768]{2,1,0:T(8,128)(2,1)S(1)}, u32[]{:S(2)}, u32[]{:S(2)}) collective-permute-start(bf16[1,96,768]{2,1,0:T(8,128)(2,1)S(1)} %get-tuple-element.284), channel_id=1, source_target_pairs={{0,16},{8,24},{16,0},{24,8},{1,17},{9,25},{17,1},{25,9},{2,18},{10... | collective-permute-start | bytes 442376 | tf_op jit(solution)/shard_map/ppermute | solution.py:32
  276.2 6.6 %collective-permute-start.29 = (f32[5,768]{1,0:T(8,128)S(1)}, f32[5,768]{1,0:T(8,128)S(1)}, u32[]{:S(2)}, u32[]{:S(2)}) collective-permute-start(f32[5,768]{1,0:T(8,128)S(1)} %add.145), channel_id=1, source_target_pairs={{0,4},{4,0},{1,5},{5,1},{2,6},{6,2},{3,7},{7,3},{8,12},{12,8},{9,1... | collective-permute-start | bytes 46088 | tf_op jit(solution)/shard_map/ppermute | solution.py:32
  286.6 5.7 %collective-permute-start.34 = (f32[5,768]{1,0:T(8,128)S(1)}, f32[5,768]{1,0:T(8,128)S(1)}, u32[]{:S(2)}, u32[]{:S(2)}) collective-permute-start(f32[5,768]{1,0:T(8,128)S(1)} %add.146), channel_id=1, source_target_pairs={{0,8},{8,0},{16,24},{24,16},{1,9},{9,1},{17,25},{25,17},{2,10},{10... | collective-permute-start | bytes 46088 | tf_op jit(solution)/shard_map/ppermute | solution.py:32
  289.8 6.9 %collective-permute-start.30 = (bf16[2,48,768]{2,1,0:T(8,128)(2,1)S(1)}, bf16[2,48,768]{2,1,0:T(8,128)(2,1)S(1)}, u32[]{:S(2)}, u32[]{:S(2)}) collective-permute-start(bf16[2,48,768]{2,1,0:T(8,128)(2,1)S(1)} %get-tuple-element.294), channel_id=1, source_target_pairs={{0,8},{8,0},{16,24},{24,16},{1,9},{9,1},{17,25},{25,17},{2,10},{10... | collective-permute-start | bytes 442376 | tf_op jit(solution)/shard_map/ppermute | solution.py:32
  289.9 11.2 %collective-permute-start.33 = (bf16[1,96,768]{2,1,0:T(8,128)(2,1)S(1)}, bf16[1,96,768]{2,1,0:T(8,128)(2,1)S(1)}, u32[]{:S(2)}, u32[]{:S(2)}) collective-permute-start(bf16[1,96,768]{2,1,0:T(8,128)(2,1)S(1)} %get-tuple-element.297.refs_6_), channel_id=1, source_target_pairs={{0,16},{8,24},{16,0},{24,8},{1,17},{9,25},{17,1},{25,9},{2,18},{10... | collective-permute-start | bytes 442376 | tf_op jit(solution)/shard_map/ppermute | solution.py:32
  290.4 10.7 %collective-permute-start.32 = (bf16[2,48,1152]{2,1,0:T(8,128)(2,1)S(1)}, bf16[2,48,1152]{2,1,0:T(8,128)(2,1)S(1)}, u32[]{:S(2)}, u32[]{:S(2)}) collective-permute-start(bf16[2,48,1152]{2,1,0:T(8,128)(2,1)S(1)} %get-tuple-element.296), channel_id=1, source_target_pairs={{0,4},{4,0},{1,5},{5,1},{2,6},{6,2},{3,7},{7,3},{8,12},{12,8},{9,1... | collective-permute-start | bytes 663560 | tf_op jit(solution)/shard_map/ppermute | solution.py:32
  291.0 10.2 %collective-permute-start.31 = (bf16[2,48,1152]{2,1,0:T(8,128)(2,1)S(1)}, bf16[2,48,1152]{2,1,0:T(8,128)(2,1)S(1)}, u32[]{:S(2)}, u32[]{:S(2)}) collective-permute-start(bf16[2,48,1152]{2,1,0:T(8,128)(2,1)S(1)} %get-tuple-element.295), channel_id=1, source_target_pairs={{0,1},{1,0},{2,3},{3,2},{4,5},{5,4},{6,7},{7,6},{8,9},{9,8},{10,11... | collective-permute-start | bytes 663560 | tf_op jit(solution)/shard_map/ppermute | solution.py:1562
  292.3 12.1 %collective-permute-start.36 = (bf16[256,768]{1,0:T(8,128)(2,1)S(1)}, bf16[256,768]{1,0:T(8,128)(2,1)S(1)}, u32[]{:S(2)}, u32[]{:S(2)}) collective-permute-start(bf16[256,768]{1,0:T(8,128)(2,1)S(1)} %get-tuple-element.308), channel_id=1, source_target_pairs={{0,1},{1,0},{2,3},{3,2},{4,5},{5,4},{6,7},{7,6},{8,9},{9,8},{10,11... | collective-permute-start | bytes 1179656 | tf_op jit(solution)/shard_map/ppermute | solution.py:1712
  301.3 12.6 %collective-permute-start.35 = (bf16[1,48,3072]{2,1,0:T(8,128)(2,1)S(1)}, bf16[1,48,3072]{2,1,0:T(8,128)(2,1)S(1)}, u32[]{:S(2)}, u32[]{:S(2)}) collective-permute-start(bf16[1,48,3072]{2,1,0:T(8,128)(2,1)S(1)} %get-tuple-element.306), channel_id=1, source_target_pairs={{0,16},{8,24},{16,0},{24,8},{1,17},{9,25},{17,1},{25,9},{2,18},{10... | collective-permute-start | bytes 884744 | tf_op jit(solution)/shard_map/ppermute | solution.py:32
  301.6 12.8 %collective-permute-start.37 = (bf16[2,96,768]{2,1,0:T(8,128)(2,1)S(1)}, bf16[2,96,768]{2,1,0:T(8,128)(2,1)S(1)}, u32[]{:S(2)}, u32[]{:S(2)}) collective-permute-start(bf16[2,96,768]{2,1,0:T(8,128)(2,1)S(1)} %get-tuple-element.310.refs_2_), channel_id=1, source_target_pairs={{0,4},{4,0},{1,5},{5,1},{2,6},{6,2},{3,7},{7,3},{8,12},{12,8},{9,1... | collective-permute-start | bytes 884744 | tf_op jit(solution)/shard_map/ppermute | solution.py:32
  303.2 11.2 %collective-permute-start.38 = (f32[5,768]{1,0:T(8,128)S(1)}, f32[5,768]{1,0:T(8,128)S(1)}, u32[]{:S(2)}, u32[]{:S(2)}) collective-permute-start(f32[5,768]{1,0:T(8,128)S(1)} %add.147), channel_id=1, source_target_pairs={{0,16},{8,24},{16,0},{24,8},{1,17},{9,25},{17,1},{25,9},{2,18},{10... | collective-permute-start | bytes 46088 | tf_op jit(solution)/shard_map/ppermute | solution.py:32
  314.5 14.8 %collective-permute-start.41 = (bf16[4,96,768]{2,1,0:T(8,128)(2,1)S(1)}, bf16[4,96,768]{2,1,0:T(8,128)(2,1)S(1)}, u32[]{:S(2)}, u32[]{:S(2)}) collective-permute-start(bf16[4,96,768]{2,1,0:T(8,128)(2,1)S(1)} %get-tuple-element.317.refs_2_), channel_id=1, source_target_pairs={{0,8},{8,0},{16,24},{24,16},{1,9},{9,1},{17,25},{25,17},{2,10},{10... | collective-permute-start | bytes 1769480 | tf_op jit(solution)/shard_map/ppermute | solution.py:32
  314.6 7.8 %collective-permute-start.40 = (bf16[256,768]{1,0:T(8,128)(2,1)S(1)}, bf16[256,768]{1,0:T(8,128)(2,1)S(1)}, u32[]{:S(2)}, u32[]{:S(2)}) collective-permute-start(bf16[256,768]{1,0:T(8,128)(2,1)S(1)} %get-tuple-element.315), channel_id=1, source_target_pairs={{0,1},{1,0},{2,3},{3,2},{4,5},{5,4},{6,7},{7,6},{8,9},{9,8},{10,11... | collective-permute-start | bytes 1179656 | tf_op jit(solution)/shard_map/ppermute | solution.py:1712
  314.8 10.4 %collective-permute-start.39 = (bf16[1,48,3072]{2,1,0:T(8,128)(2,1)S(1)}, bf16[1,48,3072]{2,1,0:T(8,128)(2,1)S(1)}, u32[]{:S(2)}, u32[]{:S(2)}) collective-permute-start(bf16[1,48,3072]{2,1,0:T(8,128)(2,1)S(1)} %get-tuple-element.314.refs_0_), channel_id=1, source_target_pairs={{0,16},{8,24},{16,0},{24,8},{1,17},{9,25},{17,1},{25,9},{2,18},{10... | collective-permute-start | bytes 884744 | tf_op jit(solution)/shard_map/ppermute | solution.py:32
  329.5 9.6 %collective-permute-start.44 = (bf16[8,96,768]{2,1,0:T(8,128)(2,1)S(1)}, bf16[8,96,768]{2,1,0:T(8,128)(2,1)S(1)}, u32[]{:S(2)}, u32[]{:S(2)}) collective-permute-start(bf16[8,96,768]{2,1,0:T(8,128)(2,1)S(1)} %get-tuple-element.328.part_ref), channel_id=1, source_target_pairs={{0,2},{2,0},{1,3},{3,1},{4,6},{6,4},{5,7},{7,5},{8,10},{10,8},{9,1... | collective-permute-start | bytes 3538952 | tf_op jit(solution)/shard_map/ppermute | solution.py:1476
  329.6 9.4 %collective-permute-start.42 = (bf16[2,48,1536]{2,1,0:T(8,128)(2,1)S(1)}, bf16[2,48,1536]{2,1,0:T(8,128)(2,1)S(1)}, u32[]{:S(2)}, u32[]{:S(2)}) collective-permute-start(bf16[2,48,1536]{2,1,0:T(8,128)(2,1)S(1)} %get-tuple-element.320.refs_0_), channel_id=1, source_target_pairs={{0,8},{8,0},{16,24},{24,16},{1,9},{9,1},{17,25},{25,17},{2,10},{10... | collective-permute-start | bytes 884744 | tf_op jit(solution)/shard_map/ppermute | solution.py:32
  329.6 9.4 %collective-permute-start.43 = (bf16[2,48,1536]{2,1,0:T(8,128)(2,1)S(1)}, bf16[2,48,1536]{2,1,0:T(8,128)(2,1)S(1)}, u32[]{:S(2)}, u32[]{:S(2)}) collective-permute-start(bf16[2,48,1536]{2,1,0:T(8,128)(2,1)S(1)} %get-tuple-element.321.refs_2_), channel_id=1, source_target_pairs={{0,4},{4,0},{1,5},{5,1},{2,6},{6,2},{3,7},{7,3},{8,12},{12,8},{9,1... | collective-permute-start | bytes 884744 | tf_op jit(solution)/shard_map/ppermute | solution.py:32
  339.1 14.9 %collective-permute-start.45 = (bf16[4,48,1536]{2,1,0:T(8,128)(2,1)S(1)}, bf16[4,48,1536]{2,1,0:T(8,128)(2,1)S(1)}, u32[]{:S(2)}, u32[]{:S(2)}) collective-permute-start(bf16[4,48,1536]{2,1,0:T(8,128)(2,1)S(1)} %get-tuple-element.325.refs_0_), channel_id=1, source_target_pairs={{0,4},{4,0},{1,5},{5,1},{2,6},{6,2},{3,7},{7,3},{8,12},{12,8},{9,1... | collective-permute-start | bytes 1769480 | tf_op jit(solution)/shard_map/ppermute | solution.py:32
  339.5 14.7 %collective-permute-start.46 = (bf16[4,48,1536]{2,1,0:T(8,128)(2,1)S(1)}, bf16[4,48,1536]{2,1,0:T(8,128)(2,1)S(1)}, u32[]{:S(2)}, u32[]{:S(2)}) collective-permute-start(bf16[4,48,1536]{2,1,0:T(8,128)(2,1)S(1)} %get-tuple-element.326.refs_2_), channel_id=1, source_target_pairs={{0,8},{8,0},{16,24},{24,16},{1,9},{9,1},{17,25},{25,17},{2,10},{10... | collective-permute-start | bytes 1769480 | tf_op jit(solution)/shard_map/ppermute | solution.py:32
  354.3 4.6 %collective-permute-start.47 = (bf16[8,48,3072]{2,1,0:T(8,128)(2,1)S(1)}, bf16[8,48,3072]{2,1,0:T(8,128)(2,1)S(1)}, u32[]{:S(2)}, u32[]{:S(2)}) collective-permute-start(bf16[8,48,3072]{2,1,0:T(8,128)(2,1)S(1)} %phase.17.part_ref), channel_id=1, source_target_pairs={{0,2},{2,0},{1,3},{3,1},{4,6},{6,4},{5,7},{7,5},{8,10},{10,8},{9,1... | collective-permute-start | bytes 7077896 | tf_op jit(solution)/shard_map/ppermute | solution.py:1476
  (28 other events, 62.2 us)

commit v2 on v1

--- a/solution.py
+++ b/solution.py
@@ -1384,7 +1384,7 @@
 def unpack_down_body(me_ref, part_ref, *refs):
     low, rows = me_ref[0] % 8, part_ref.shape[1]
     for b in range(8):
-        refs[-1][b * rows : (b + 1) * rows] = part_ref[b ^ low].astype(F32)
+        refs[-1][b * rows : (b + 1) * rows] = part_ref[swapped(b ^ low)].astype(F32)
 
 
 def unpack_down(me, side, part, into=()):
@@ -1750,13 +1750,15 @@
     o2_flat = o2.reshape(2 * n, width)
 
     out_got, dy = sync(out_got, dy)
-    out_last = link.partner(after(out_two, out_got))
+    quarter = out_two.shape[1] // 2
+    out_last = [link.partner(after(out_two[:, :quarter], out_got))]
     down_keep, down_go = grad_down(me_z, g1, g2, dy, dm2)
-    down_keep, down_go, out_last = sync(down_keep, down_go, out_last)
+    down_keep, down_go, out_last[0] = sync(down_keep, down_go, out_last[0])
+    out_last.append(link.partner(after(out_two[:, quarter:], down_go)))
     down = link.hops(down_keep, link.core(down_go))
     dy = after(dy, down_go)
     du1, dh1_1, dp1, do1, sums1 = mlp_back(dy, h1, wout, gb, d1, ups, downs, seq)
-    du1, dp1, do1 = down.wait(du1, dp1, do1)
+    du1, dp1, do1, out_last[1] = down.wait(du1, dp1, do1, out_last[1])
     down.to_partner()
     up_keep, up_go = grad_up(me, n2_1, n2_2, after(du1, down.sent), du2, dp1, dp2, o1, o2_flat)
     do1 = after(do1, up_go)
@@ -1768,7 +1770,7 @@
     small = jnp.stack([sums_e[0] + sums_o[0], sums1[0] + sums2[0], sums_e[1] + sums_o[1], sums1[1] + sums2[1], sums_o[2]])
     qkv_keep, qkv_go = grad_qkv(me_z, a_e, a_o, after(dqkv_e, *down.sent), dqkv_o)
     out = link.finish(
-        jnp.concatenate([out, out_two], axis=0), jnp.concatenate([out_got, after(out_last, dqkv_e)], axis=0), link.out_shape
+        jnp.concatenate([out, out_two], axis=0), jnp.concatenate([out_got, jnp.concatenate(after(out_last, dqkv_e), axis=1)], axis=0), link.out_shape
     )
     qkv_keep, qkv_go, down.got, out = up.wait(qkv_keep, qkv_go, down.got, out)
     qkv = link.hops(qkv_keep, link.core(qkv_go))
@@ -1801,11 +1803,11 @@
     wait_all()
     up.absorb(qkv)
     chunks.remove(qkv)
-    all_steps(up.last_hop(), down.back("x"))
+    all_steps(up.last_hop(), down.back("z"))
     gt_got.append(link.partner(after(gt[half:], *up.sent)))
     (gt_got[0],) = up.wait(gt_got[0])
     wait_all()
-    all_steps(up.back_first(), down.back("z"))
+    all_steps(up.back_first(), down.back("x"))
     (gt_got[1],) = up.wait(gt_got[1])
     wait_all()
     while small_got is not None:

time: 369 us -> 366 us (level)
  waiting for transfers between devices: 103 us -> 91.9 us
  starting transfers between devices: 43.5 us -> 50.5 us
    ppermute x23, waiting for transfers between devices: 72.4 us -> 59.2 us  [flip_bit(): return lax.ppermute(array, axis, [(i, i ^ bit) for i in range(size)])]
    ppermute x23, starting transfers between devices: 25.6 us -> 29.6 us  [flip_bit(): return lax.ppermute(array, axis, [(i, i ^ bit) for i in range(size)])]
    ppermute x8 -> x9, starting transfers between devices: 9.74 us -> 11.7 us  [partner(): return lax.ppermute(t, 'tensor', FLIP)]
    ppermute x8 -> x9, waiting for transfers between devices: 19.2 us -> 21.2 us  [partner(): return lax.ppermute(t, 'tensor', FLIP)]
  transfers between devices with their start and end apart: 48 -> 49, of which waited for: 29 -> 27; matrix products, arithmetic and copies ran while one was open for 8% -> 8% of each run, Pallas kernels for 30% -> 30%
where the time goes in v2:
time: 366 us; the launch traced here: 359 us
  Pallas kernels  172 us (47%)
  waiting for transfers between devices  91.9 us (25%)
  starting transfers between devices  50.5 us (14%)
  other arithmetic  27.1 us (7%)
  local copies, waits for them, and re-layouts  16.2 us (4%)
    pallas_call x23, Pallas kernels, resident(): pl.pallas_call(body, in_specs=[s for _, s in ins], out_specs=[s for _, s...  167 us
    ppermute x23, waiting for transfers between devices, flip_bit(): return lax.ppermute(array, axis, [(i, i ^ bit) for i in range(size)])  59.2 us
    ppermute x23, starting transfers between devices, flip_bit(): return lax.ppermute(array, axis, [(i, i ^ bit) for i in range(size)])  29.6 us
    ppermute x9, waiting for transfers between devices, partner(): return lax.ppermute(t, 'tensor', FLIP)  21.2 us
    ppermute x9, starting transfers between devices, partner(): return lax.ppermute(t, 'tensor', FLIP)  11.7 us
    another operation x11, other arithmetic, ordered(): jnp.stack([jnp.where(first, mine, theirs), jnp.where(first, theirs, mine)])  7.46 us
  transfers between devices with their start and end apart: 49, of which 27 were waited for; matrix products, arithmetic and copies ran while one was open for 8% of the time, Pallas kernels for 30%

profile of v2, /device:TPU:0, one launch (start us, length us, event | category | flops | bytes accessed | tf_op | source)
XLA Modules:
  0.0 359.3 jit_solution(16185203788162529511)
XLA Ops:
  0.7 2.0 constant_dynamic-slice_fusion.7
  2.7 3.0 collective-permute-start
  5.8 1.3 convert_reduce_fusion
  9.4 2.4 attend_first.2
  13.7 1.3 constant_dynamic-slice_fusion.4.cot_far
  16.2 1.7 collective-permute-start.1
  17.9 1.9 constant_dynamic-slice_fusion.2
  19.8 1.5 collective-permute-start.3
  22.9 5.0 %collective-permute-done.1 = bf16[576,384]{1,0:T(8,128)(2,1)} collective-permute-done((bf16[576,384]{1,0:T(8,128)(2,1)}, bf16[576,384]{1,0:T(8,128)(2,1)}, u32[]{:S(2)}, u32[]{:S(2)}) %collective-permute-start.1) | collective-permute-done | bytes 442400 | tf_op jit(solution)/shard_map/ppermute | solution.py:1679
  30.1 7.1 %collective-permute-done.2 = bf16[96,768]{1,0:T(8,128)(2,1)} collective-permute-done((bf16[96,768]{1,0:T(8,128)(2,1)S(1)}, bf16[96,768]{1,0:T(8,128)(2,1)}, u32[]{:S(2)}, u32[]{:S(2)}) %collective-permute-start.2) | collective-permute-done | bytes 147488 | tf_op jit(solution)/shard_map/ppermute | solution.py:1712
  38.5 1.5 collective-permute-start.5
  40.5 1.6 select_bitcast_fusion.1
  43.6 2.1 pad_maximum_fusion.w_far
  45.7 2.4 attend_first.3
  48.1 1.6 pad_maximum_fusion.2.qkve_far
  51.9 1.6 collective-permute-start.4
  54.7 9.0 %mlp_own.1 = (f32[512,768]{1,0:T(8,128)}, bf16[512,768]{1,0:T(8,128)(2,1)}, bf16[512,3072]{1,0:T(8,128)(2,1)}, bf16[512,3072]{1,0:T(8,128)(2,1)}, f32[512,768]{1,0:T(8,128)}) custom-call(bf16[512,768]{1,0:T(8,128)(2,1)} %bitcast.59, bf16[512,768]{1,0:T(8,128)(2,1)} %pad_maximum_fusion.10.o_far.o1_far, bf16[768,768]{1,0:T(8,128)(2,1)} %pad_maximum_fusion.8.wout_far, ...), custom_call_target="tpu_custom_call" | custom-call | tf_op jit(solution)/shard_map/mlp_own/pallas_call | solution.py:112
  63.7 3.4 collective-permute-done.5.refs_4_.refs_6_
  68.2 2.8 collective-permute-done.9.refs_2_.refs_3_
  73.5 8.8 %mlp_other.1 = (bf16[512,3072]{1,0:T(8,128)(2,1)}, bf16[512,3072]{1,0:T(8,128)(2,1)}, f32[512,768]{1,0:T(8,128)}, bf16[512,768]{1,0:T(8,128)(2,1)}) custom-call(bf16[512,768]{1,0:T(8,128)(2,1)} %get-tuple-element.201.n2_far.n1_far, f32[512,768]{1,0:T(8,128)} %get-tuple-element.202.part_far, ...), custom_call_target="tpu_custom_call", output_to_operand_aliasing={{0}: (2, {}), {1}: (3, {})} | custom-call | tf_op jit(solution)/shard_map/mlp_other/pallas_call | solution.py:112
  82.3 14.1 %attend_second.1 = (bf16[3,512,768]{2,1,0:T(8,128)(2,1)}, bf16[2,512,768]{2,1,0:T(8,128)(2,1)}, f32[2,3,4,512]{3,2,1,0:T(4,128)S(1)}) custom-call(bf16[512,768]{1,0:T(8,128)(2,1)} %get-tuple-element.209.a_far.ao_far, bf16[3,768,768]{2,1,0:T(8,128)(2,1)} %pad_maximum_fusion.w_far, f32[2,256,256]{2,1,0:T(8,128)} %copy-done.2, ...), custom_call_target="tpu_custom_call" | custom-call | flops 415236096 | tf_op jit(solution)/shard_map/attend_second/pallas_call | solution.py:112
  96.4 37.4 %mlp_second.1 = (bf16[1,512,768]{2,1,0:T(8,128)(2,1)}, bf16[1,512,768]{2,1,0:T(8,128)(2,1)}, bf16[1024,768]{1,0:T(8,128)(2,1)}, bf16[1024,3072]{1,0:T(8,128)(2,1...) custom-call(bf16[512,768]{1,0:T(8,128)(2,1)} %bitcast.60, ...), custom_call_target="tpu_custom_call" | custom-call | tf_op jit(solution)/shard_map/mlp_second/pallas_call | solution.py:112
  134.8 18.9 %attend_back.1 = (bf16[3,512,768]{2,1,0:T(8,128)(2,1)}, bf16[3,512,768]{2,1,0:T(8,128)(2,1)}, f32[512,768]{1,0:T(8,128)}, f32[3,768]{1,0:T(4,128)S(1)}) custom-call(bf16[3,768,768]{2,1,0:T(8,128)(2,1)} %pad_maximum_fusion.w_far, f32[2,256,256]{2,1,0:T(8,128)} %copy-done.2, f32[2,256,256]{2,1,0:T(8,128)} %get-tuple-element.390.strict_far, ...), custom_call_target="tpu_custom_call" | custom-call | flops 868220928 | tf_op jit(solution)/shard_map/attend_back/pallas_call | solution.py:112
  155.1 14.1 %grad_down.1 = (bf16[2,8,96,768]{3,2,1,0:T(8,128)(2,1)}, bf16[2,8,96,768]{3,2,1,0:T(8,128)(2,1)}) custom-call(s32[2]{0:T(128)S(1)} %rev.3.me_ref, bf16[512,3072]{1,0:T(8,128)(2,1)} %get-tuple-element.207.g1_far, bf16[1024,3072]{1,0:T(8,128)(2,1)} %get-tuple-element.215.g2_far, f32[512,768]{1,0:T(8,128)} %get-tuple-element.231.dy_far, ...), custom_call_target="tpu_custom_call" | custom-call | flops 452984832 | tf_op jit(solution)/shard_map/grad_down/pallas_call | solution.py:112
  170.4 13.2 %mlp_back.1 = (bf16[512,3072]{1,0:T(8,128)(2,1)}, f32[512,768]{1,0:T(8,128)}, bf16[512,768]{1,0:T(8,128)(2,1)}, bf16[512,768]{1,0:T(8,128)(2,1)}, f32[2,768]{1,0:T(2,128)S(1)}) custom-call(f32[512,768]{1,0:T(8,128)} %get-tuple-element.231.dy_far, f32[512,768]{1,0:T(8,128)} %get-tuple-element.232.h1_far, bf16[768,768]{1,0:T(8,128)(2,1)} %pad_maximum_fusion.8.wout_far, ...), custom_call_target="tpu_custom_call" | custom-call | tf_op jit(solution)/shard_map/mlp_back/pallas_call | solution.py:112
  184.3 1.6 slice_bitcast_fusion
  187.5 16.7 %grad_up.1 = (bf16[2,8,48,1920]{3,2,1,0:T(8,128)(2,1)}, bf16[2,8,48,1920]{3,2,1,0:T(8,128)(2,1)}) custom-call(s32[3]{0:T(128)} %pad_add_fusion.1.me_ref, bf16[512,768]{1,0:T(8,128)(2,1)} %get-tuple-element.201.n2_far.n1_far, bf16[1024,768]{1,0:T(8,128)(2,1)} %get-tuple-element.240.n2_far, bf16[512,3072]{1,0:T(8,128)(2,1)} %get-tuple-element.242.du1_far, ...), custom_call_target="tpu_custom_call" | custom-call | flops 566231040 | tf_op jit(solution)/shard_map/grad_up/pallas_call | solution.py:112
  204.3 12.5 %attend_back_even.1 = (bf16[3,512,768]{2,1,0:T(8,128)(2,1)}, bf16[512,768]{1,0:T(8,128)(2,1)S(1)}, f32[2,768]{1,0:T(2,128)S(1)}) custom-call(bf16[3,768,768]{2,1,0:T(8,128)(2,1)} %pad_maximum_fusion.w_far, f32[2,256,256]{2,1,0:T(8,128)} %copy-done.2, bf16[3,512,768]{2,1,0:T(8,128)(2,1)} %pad_maximum_fusion.2.qkve_far, ...), custom_call_target="tpu_custom_call" | custom-call | flops 364904448 | tf_op jit(solution)/shard_map/attend_back_even/pallas_call | solution.py:112
  217.9 1.6 collective-permute-start.18
  219.4 9.3 %grad_qkv.1 = (bf16[2,8,48,1152]{3,2,1,0:T(8,128)(2,1)}, bf16[2,8,48,1152]{3,2,1,0:T(8,128)(2,1)}) custom-call(s32[2]{0:T(128)S(1)} %rev.3.me_ref, bf16[512,768]{1,0:T(8,128)(2,1)} %copy-done.4, bf16[512,768]{1,0:T(8,128)(2,1)} %get-tuple-element.209.a_far.ao_far, bf16[3,512,768]{2,1,0:T(8,128)(2,1)} %get-tuple-element.257.de_far, ...), custom_call_target="tpu_custom_call" | custom-call | flops 226492416 | tf_op jit(solution)/shard_map/grad_qkv/pallas_call | solution.py:112
  230.5 1.9 pad_maximum_fusion.1
  232.4 1.4 collective-permute-done.18.refs_1_
  234.5 2.7 collective-permute-done.20
  237.8 4.0 %add_convert_fusion = bf16[2,8,48,1920]{3,2,1,0:T(8,128)(2,1)S(1)} fusion(bf16[2,8,48,1920]{3,2,1,0:T(8,128)(2,1)} %collective-permute-done.17, bf16[2,8,48,1920]{3,2,1,0:T(8,128)(2,1)} %get-tuple-element.266), kind=kLoop, calls=%fused_computation | loop fusion | flops 5898240 | bytes 8847360 | tf_op jit(solution)/shard_map/convert_element_type | solution.py:1454
  242.0 1.6 collective-permute-start.22
  243.6 1.9 add_convert_fusion.2
  246.9 1.3 collective-permute-start.21
  250.2 17.8 %collective-permute-done.24.refs_7_ = bf16[2,96,768]{2,1,0:T(8,128)(2,1)S(1)} collective-permute-done((bf16[2,96,768]{2,1,0:T(8,128)(2,1)S(1)}, bf16[2,96,768]{2,1,0:T(8,128)(2,1)S(1)}, u32[]{:S(2)}, u32[]{:S(2)}) %collective-permute-start.24) | collective-permute-done | bytes 294944 | tf_op jit(solution)/shard_map/ppermute | solution.py:32
  268.7 1.3 collective-permute-start.27
  270.0 1.5 collective-permute-start.28
  271.5 1.3 collective-permute-start.26
  272.8 2.6 collective-permute-start.29
  276.0 4.1 %collective-permute-done.30 = f32[5,768]{1,0:T(8,128)S(1)} collective-permute-done((f32[5,768]{1,0:T(8,128)S(1)}, f32[5,768]{1,0:T(8,128)S(1)}, u32[]{:S(2)}, u32[]{:S(2)}) %collective-permute-start.30) | collective-permute-done | bytes 15392 | tf_op jit(solution)/shard_map/ppermute | solution.py:32
  280.0 3.2 collective-permute-done.29.refs_7_
  284.3 2.7 collective-permute-start.31
  288.5 1.7 collective-permute-start.34
  290.7 3.4 collective-permute-done.35
  296.6 2.1 collective-permute-start.38
  299.9 3.2 collective-permute-done.37
  303.1 5.9 %collective-permute-done.36.refs_1_ = bf16[1,48,3072]{2,1,0:T(8,128)(2,1)S(1)} collective-permute-done((bf16[1,48,3072]{2,1,0:T(8,128)(2,1)S(1)}, bf16[1,48,3072]{2,1,0:T(8,128)(2,1)S(1)}, u32[]{:S(2)}, u32[]{:S(2)}) %collective-permute-start.36) | collective-permute-done | bytes 294944 | tf_op jit(solution)/shard_map/ppermute | solution.py:32
  309.3 1.5 collective-permute-start.42
  311.7 1.5 collective-permute-start.40
  313.2 6.3 %collective-permute-done.41 = bf16[256,768]{1,0:T(8,128)(2,1)S(1)} collective-permute-done((bf16[256,768]{1,0:T(8,128)(2,1)S(1)}, bf16[256,768]{1,0:T(8,128)(2,1)S(1)}, u32[]{:S(2)}, u32[]{:S(2)}) %collective-permute-start.41) | collective-permute-done | bytes 393248 | tf_op jit(solution)/shard_map/ppermute | solution.py:1712
  319.5 5.8 %collective-permute-done.40.refs_1_ = bf16[1,48,3072]{2,1,0:T(8,128)(2,1)S(1)} collective-permute-done((bf16[1,48,3072]{2,1,0:T(8,128)(2,1)S(1)}, bf16[1,48,3072]{2,1,0:T(8,128)(2,1)S(1)}, u32[]{:S(2)}, u32[]{:S(2)}) %collective-permute-start.40) | collective-permute-done | bytes 294944 | tf_op jit(solution)/shard_map/ppermute | solution.py:32
  325.7 1.4 collective-permute-start.44
  327.7 7.3 %collective-permute-done.43.refs_1_ = bf16[2,48,1536]{2,1,0:T(8,128)(2,1)S(1)} collective-permute-done((bf16[2,48,1536]{2,1,0:T(8,128)(2,1)S(1)}, bf16[2,48,1536]{2,1,0:T(8,128)(2,1)S(1)}, u32[]{:S(2)}, u32[]{:S(2)}) %collective-permute-start.43) | collective-permute-done | bytes 294944 | tf_op jit(solution)/shard_map/ppermute | solution.py:32
  335.2 1.4 collective-permute-start.46
  336.5 1.7 collective-permute-start.47
  339.1 1.9 convert.1
  341.0 2.1 unpack_down.2.refs_0_
  343.2 2.1 unpack_down.3
  345.3 4.8 %collective-permute-done.46.refs_1_ = bf16[4,48,1536]{2,1,0:T(8,128)(2,1)S(1)} collective-permute-done((bf16[4,48,1536]{2,1,0:T(8,128)(2,1)S(1)}, bf16[4,48,1536]{2,1,0:T(8,128)(2,1)S(1)}, u32[]{:S(2)}, u32[]{:S(2)}) %collective-permute-start.46) | collective-permute-done | bytes 589856 | tf_op jit(solution)/shard_map/ppermute | solution.py:32
  351.7 2.9 unpack_rest.2
  355.9 2.9 unpack_rest.3
  (214 shorter events, 46.5 us)
Async XLA Ops:
  0.6 13.1 %copy-start = (bf16[4,512,768]{2,1,0:T(8,128)(2,1)S(1)}, bf16[4,512,768]{2,1,0:T(8,128)(2,1)}, u32[]{:S(2)}) copy-start(bf16[4,512,768]{2,1,0:T(8,128)(2,1)} %param.19) | copy-start | bytes 9437188
  0.7 6.8 %copy-start.45 = (s32[4,256]{1,0:T(4,128)S(1)}, s32[4,256]{1,0:T(4,128)}, u32[]{:S(2)}) copy-start(s32[4,256]{1,0:T(4,128)} %param.11) | copy-start | bytes 12292
  2.7 13.4 %collective-permute-start = (bf16[576,384]{1,0:T(8,128)(2,1)}, bf16[576,384]{1,0:T(8,128)(2,1)}, u32[]{:S(2)}, u32[]{:S(2)}) collective-permute-start(bf16[576,384]{1,0:T(8,128)(2,1)} %constant_dynamic-slice_fusion.7), channel_id=1, source_target_pairs={{0,1},{1,0},{2,3},{3,2},{4,5},{5,4},{6,7},{7,6},{8,9},{9,8},{10,11... | collective-permute-start | bytes 1327112 | tf_op jit(solution)/shard_map/ppermute | solution.py:1712
  16.2 11.7 %collective-permute-start.1 = (bf16[576,384]{1,0:T(8,128)(2,1)}, bf16[576,384]{1,0:T(8,128)(2,1)}, u32[]{:S(2)}, u32[]{:S(2)}) collective-permute-start(bf16[576,384]{1,0:T(8,128)(2,1)} %collective-permute-done), channel_id=1, source_target_pairs={{0,4},{4,0},{1,5},{5,1},{2,6},{6,2},{3,7},{7,3},{8,12},{12,8},{9,1... | collective-permute-start | bytes 1327112 | tf_op jit(solution)/shard_map/ppermute | solution.py:1679
  19.8 17.4 %collective-permute-start.3 = (bf16[768,384]{1,0:T(8,128)(2,1)}, bf16[768,384]{1,0:T(8,128)(2,1)S(1)}, u32[]{:S(2)}, u32[]{:S(2)}) collective-permute-start(bf16[768,384]{1,0:T(8,128)(2,1)} %constant_dynamic-slice_fusion.2), channel_id=1, source_target_pairs={{0,1},{1,0},{2,3},{3,2},{4,5},{5,4},{6,7},{7,6},{8,9},{9,8},{10,11... | collective-permute-start | bytes 1769480 | tf_op jit(solution)/shard_map/ppermute | solution.py:1712
  22.3 14.9 %collective-permute-start.2 = (bf16[96,768]{1,0:T(8,128)(2,1)S(1)}, bf16[96,768]{1,0:T(8,128)(2,1)}, u32[]{:S(2)}, u32[]{:S(2)}) collective-permute-start(bf16[96,768]{1,0:T(8,128)(2,1)S(1)} %constant_dynamic-slice_fusion.3), channel_id=1, source_target_pairs={{0,1},{1,0},{2,3},{3,2},{4,5},{5,4},{6,7},{7,6},{8,9},{9,8},{10,11... | collective-permute-start | bytes 442376 | tf_op jit(solution)/shard_map/ppermute | solution.py:1712
  22.9 14.4 %copy-start.20 = (bf16[1536,768]{1,0:T(8,128)(2,1)S(1)}, bf16[1536,768]{1,0:T(8,128)(2,1)}, u32[]{:S(2)}) copy-start(bf16[1536,768]{1,0:T(8,128)(2,1)} %refs_5_.3) | copy-start | bytes 7077892
  37.2 3.3 collective-permute-start.6
  38.5 28.6 %collective-permute-start.5 = (bf16[768,768]{1,0:T(8,128)(2,1)}, bf16[768,768]{1,0:T(8,128)(2,1)}, u32[]{:S(2)}, u32[]{:S(2)}) collective-permute-start(bf16[768,768]{1,0:T(8,128)(2,1)} %pad_maximum_fusion.7), channel_id=1, source_target_pairs={{0,1},{1,0},{2,3},{3,2},{4,5},{5,4},{6,7},{7,6},{8,9},{9,8},{10,11... | collective-permute-start | bytes 3538952 | tf_op jit(solution)/shard_map/ppermute | solution.py:1712
  40.0 10.7 %collective-permute-start.7 = (bf16[96,768]{1,0:T(8,128)(2,1)}, bf16[96,768]{1,0:T(8,128)(2,1)}, u32[]{:S(2)}, u32[]{:S(2)}) collective-permute-start(bf16[96,768]{1,0:T(8,128)(2,1)} %collective-permute-done.2), channel_id=1, source_target_pairs={{0,4},{4,0},{1,5},{5,1},{2,6},{6,2},{3,7},{7,3},{8,12},{12,8},{9,1... | collective-permute-start | bytes 442376 | tf_op jit(solution)/shard_map/ppermute | solution.py:1679
  51.8 1.7 collective-permute-start.8
  51.9 15.8 %collective-permute-start.4 = (bf16[768,384]{1,0:T(8,128)(2,1)S(1)}, bf16[768,384]{1,0:T(8,128)(2,1)S(1)}, u32[]{:S(2)}, u32[]{:S(2)}) collective-permute-start(bf16[768,384]{1,0:T(8,128)(2,1)S(1)} %copy-done.24), channel_id=1, source_target_pairs={{0,4},{4,0},{1,5},{5,1},{2,6},{6,2},{3,7},{7,3},{8,12},{12,8},{9,1... | collective-permute-start | bytes 1769480 | tf_op jit(solution)/shard_map/ppermute | solution.py:1679
  53.5 18.9 %copy-start.11 = (f32[5,768]{1,0:T(8,128)}, f32[5,768]{1,0:T(8,128)S(1)}, u32[]{:S(2)}) copy-start(f32[5,768]{1,0:T(8,128)S(1)} %pad_maximum_fusion.14.gb_ref) | copy-start | bytes 46084
  67.7 4.7 %copy-start.25 = (bf16[768,384]{1,0:T(8,128)(2,1)}, bf16[768,384]{1,0:T(8,128)(2,1)S(1)}, u32[]{:S(2)}) copy-start(bf16[768,384]{1,0:T(8,128)(2,1)S(1)} %collective-permute-done.4.refs_1_.refs_2_) | copy-start | bytes 1769476
  67.7 4.7 %collective-permute-start.11 = (bf16[768,768]{1,0:T(8,128)(2,1)}, bf16[768,768]{1,0:T(8,128)(2,1)S(1)}, u32[]{:S(2)}, u32[]{:S(2)}) collective-permute-start(bf16[768,768]{1,0:T(8,128)(2,1)} %collective-permute-done.5.refs_4_.refs_6_), channel_id=1, source_target_pairs={{0,2},{2,0},{1,3},{3,1},{4,6},{6,4},{5,7},{7,5},{8,10},{10,8},{9,1... | collective-permute-start | bytes 3538952 | tf_op jit(solution)/shard_map/ppermute | solution.py:1715
  67.7 3.3 collective-permute-start.9
  68.2 4.0 %collective-permute-start.10 = (bf16[768,384]{1,0:T(8,128)(2,1)S(1)}, bf16[768,384]{1,0:T(8,128)(2,1)S(1)}, u32[]{:S(2)}, u32[]{:S(2)}) collective-permute-start(bf16[768,384]{1,0:T(8,128)(2,1)S(1)} %collective-permute-done.4.refs_1_.refs_2_), channel_id=1, source_target_pairs={{0,2},{2,0},{1,3},{3,1},{4,6},{6,4},{5,7},{7,5},{8,10},{10,8},{9,1... | collective-permute-start | bytes 1769480 | tf_op jit(solution)/shard_map/ppermute | solution.py:1715
  96.4 38.4 %copy-start.12 = (f32[5,768]{1,0:T(8,128)S(1)}, f32[5,768]{1,0:T(8,128)}, u32[]{:S(2)}) copy-start(f32[5,768]{1,0:T(8,128)} %copy-done.11) | copy-start | bytes 46084
  133.8 20.0 %collective-permute-start.12 = (bf16[1,512,768]{2,1,0:T(8,128)(2,1)}, bf16[1,512,768]{2,1,0:T(8,128)(2,1)S(1)}, u32[]{:S(2)}, u32[]{:S(2)}) collective-permute-start(bf16[1,512,768]{2,1,0:T(8,128)(2,1)} %get-tuple-element.216), channel_id=1, source_target_pairs={{0,1},{1,0},{2,3},{3,2},{4,5},{5,4},{6,7},{7,6},{8,9},{9,8},{10,11... | collective-permute-start | bytes 2359304 | tf_op jit(solution)/shard_map/ppermute | solution.py:1712
  134.8 18.9 %copy-start.28 = (bf16[1,512,768]{2,1,0:T(8,128)(2,1)S(1)}, bf16[1,512,768]{2,1,0:T(8,128)(2,1)}, u32[]{:S(2)}) copy-start(bf16[1,512,768]{2,1,0:T(8,128)(2,1)} %get-tuple-element.226) | copy-start | bytes 2359300
  153.8 15.4 %copy-start.35 = (bf16[1,512,768]{2,1,0:T(8,128)(2,1)}, bf16[1,512,768]{2,1,0:T(8,128)(2,1)S(1)}, u32[]{:S(2)}) copy-start(bf16[1,512,768]{2,1,0:T(8,128)(2,1)S(1)} %collective-permute-done.12) | copy-start | bytes 2359300
  153.8 15.4 %collective-permute-start.13 = (bf16[1,256,768]{2,1,0:T(8,128)(2,1)S(1)}, bf16[1,256,768]{2,1,0:T(8,128)(2,1)S(1)}, u32[]{:S(2)}, u32[]{:S(2)}) collective-permute-start(bf16[1,256,768]{2,1,0:T(8,128)(2,1)S(1)} %get-tuple-element.228), channel_id=1, source_target_pairs={{0,1},{1,0},{2,3},{3,2},{4,5},{5,4},{6,7},{7,6},{8,9},{9,8},{10,11... | collective-permute-start | bytes 1179656 | tf_op jit(solution)/shard_map/ppermute | solution.py:1712
  169.2 14.3 %collective-permute-start.14 = (bf16[2,8,96,768]{3,2,1,0:T(8,128)(2,1)}, bf16[2,8,96,768]{3,2,1,0:T(8,128)(2,1)S(1)}, u32[]{:S(2)}, u32[]{:S(2)}) collective-permute-start(bf16[2,8,96,768]{3,2,1,0:T(8,128)(2,1)} %get-tuple-element.230), channel_id=1, source_target_pairs={{0,2},{2,0},{1,3},{3,1},{4,6},{6,4},{5,7},{7,5},{8,10},{10,8},{9,1... | collective-permute-start | bytes 7077896 | tf_op jit(solution)/shard_map/ppermute | solution.py:1715
  169.3 14.2 %collective-permute-start.15 = (bf16[1,256,768]{2,1,0:T(8,128)(2,1)S(1)}, bf16[1,256,768]{2,1,0:T(8,128)(2,1)S(1)}, u32[]{:S(2)}, u32[]{:S(2)}) collective-permute-start(bf16[1,256,768]{2,1,0:T(8,128)(2,1)S(1)} %get-tuple-element.237), channel_id=1, source_target_pairs={{0,1},{1,0},{2,3},{3,2},{4,5},{5,4},{6,7},{7,6},{8,9},{9,8},{10,11... | collective-permute-start | bytes 1179656 | tf_op jit(solution)/shard_map/ppermute | solution.py:1712
  170.4 13.2 %copy-start.30 = (bf16[2,8,96,768]{3,2,1,0:T(8,128)(2,1)S(1)}, bf16[2,8,96,768]{3,2,1,0:T(8,128)(2,1)}, u32[]{:S(2)}) copy-start(bf16[2,8,96,768]{3,2,1,0:T(8,128)(2,1)} %get-tuple-element.229) | copy-start | bytes 7077892
  185.9 30.9 %collective-permute-start.16 = (bf16[8,96,768]{2,1,0:T(8,128)(2,1)}, bf16[8,96,768]{2,1,0:T(8,128)(2,1)S(1)}, u32[]{:S(2)}, u32[]{:S(2)}) collective-permute-start(bf16[8,96,768]{2,1,0:T(8,128)(2,1)} %get-tuple-element.364), channel_id=1, source_target_pairs={{0,1},{1,0},{2,3},{3,2},{4,5},{5,4},{6,7},{7,6},{8,9},{9,8},{10,11... | collective-permute-start | bytes 3538952 | tf_op jit(solution)/shard_map/ppermute | solution.py:1473
  204.2 12.6 %copy-start.8 = (bf16[8,96,768]{2,1,0:T(8,128)(2,1)S(1)}, bf16[8,96,768]{2,1,0:T(8,128)(2,1)}, u32[]{:S(2)}) copy-start(bf16[8,96,768]{2,1,0:T(8,128)(2,1)} %get-tuple-element.363.refs_0_) | copy-start | bytes 3538948
  216.8 17.0 %collective-permute-start.17 = (bf16[2,8,48,1920]{3,2,1,0:T(8,128)(2,1)}, bf16[2,8,48,1920]{3,2,1,0:T(8,128)(2,1)}, u32[]{:S(2)}, u32[]{:S(2)}) collective-permute-start(bf16[2,8,48,1920]{3,2,1,0:T(8,128)(2,1)} %get-tuple-element.253), channel_id=1, source_target_pairs={{0,2},{2,0},{1,3},{3,1},{4,6},{6,4},{5,7},{7,5},{8,10},{10,8},{9,1... | collective-permute-start | bytes 8847368 | tf_op jit(solution)/shard_map/ppermute | solution.py:1715
  217.9 10.9 %copy-start.15 = (bf16[4,96,768]{2,1,0:T(8,128)(2,1)}, bf16[4,96,768]{2,1,0:T(8,128)(2,1)S(1)}, u32[]{:S(2)}) copy-start(bf16[4,96,768]{2,1,0:T(8,128)(2,1)S(1)} %get-tuple-element.277.refs_0_) | copy-start | bytes 1769476
  217.9 15.9 %collective-permute-start.18 = (bf16[4,96,768]{2,1,0:T(8,128)(2,1)}, bf16[4,96,768]{2,1,0:T(8,128)(2,1)S(1)}, u32[]{:S(2)}, u32[]{:S(2)}) collective-permute-start(bf16[4,96,768]{2,1,0:T(8,128)(2,1)} %get-tuple-element.256), channel_id=1, source_target_pairs={{0,8},{8,0},{16,24},{24,16},{1,9},{9,1},{17,25},{25,17},{2,10},{10... | collective-permute-start | bytes 1769480 | tf_op jit(solution)/shard_map/ppermute | solution.py:32
  219.4 9.3 %copy-start.38 = (bf16[1,256,768]{2,1,0:T(8,128)(2,1)S(1)}, bf16[1,256,768]{2,1,0:T(8,128)(2,1)}, u32[]{:S(2)}) copy-start(bf16[1,256,768]{2,1,0:T(8,128)(2,1)} %copy-done.37) | copy-start | bytes 1179652
  219.4 9.4 %copy-start.36 = (bf16[1,512,768]{2,1,0:T(8,128)(2,1)S(1)}, bf16[1,512,768]{2,1,0:T(8,128)(2,1)}, u32[]{:S(2)}) copy-start(bf16[1,512,768]{2,1,0:T(8,128)(2,1)} %copy-done.35) | copy-start | bytes 2359300
  233.8 8.0 %copy-start.17 = (bf16[4,96,768]{2,1,0:T(8,128)(2,1)}, bf16[4,96,768]{2,1,0:T(8,128)(2,1)S(1)}, u32[]{:S(2)}) copy-start(bf16[4,96,768]{2,1,0:T(8,128)(2,1)S(1)} %collective-permute-done.18.refs_1_) | copy-start | bytes 1769476
  233.8 3.9 %collective-permute-start.19 = (bf16[2,8,48,1152]{3,2,1,0:T(8,128)(2,1)}, bf16[2,8,48,1152]{3,2,1,0:T(8,128)(2,1)S(1)}, u32[]{:S(2)}, u32[]{:S(2)}) collective-permute-start(bf16[2,8,48,1152]{3,2,1,0:T(8,128)(2,1)} %get-tuple-element.268), channel_id=1, source_target_pairs={{0,2},{2,0},{1,3},{3,1},{4,6},{6,4},{5,7},{7,5},{8,10},{10,8},{9,1... | collective-permute-start | bytes 5308424 | tf_op jit(solution)/shard_map/ppermute | solution.py:1715
  233.9 3.3 collective-permute-start.20
  242.0 26.1 %collective-permute-start.22 = (bf16[2,4,48,1152]{3,2,1,0:T(8,128)(2,1)S(1)}, bf16[2,4,48,1152]{3,2,1,0:T(8,128)(2,1)S(1)}, u32[]{:S(2)}, u32[]{:S(2)}) collective-permute-start(bf16[2,4,48,1152]{3,2,1,0:T(8,128)(2,1)S(1)} %get-tuple-element.360), channel_id=1, source_target_pairs={{0,8},{8,0},{16,24},{24,16},{1,9},{9,1},{17,25},{25,17},{2,10},{10... | collective-permute-start | bytes 2654216 | tf_op jit(solution)/shard_map/ppermute | solution.py:32
  245.7 22.3 %collective-permute-start.23 = (bf16[8,48,1152]{2,1,0:T(8,128)(2,1)S(1)}, bf16[8,48,1152]{2,1,0:T(8,128)(2,1)S(1)}, u32[]{:S(2)}, u32[]{:S(2)}) collective-permute-start(bf16[8,48,1152]{2,1,0:T(8,128)(2,1)S(1)} %get-tuple-element.368), channel_id=1, source_target_pairs={{0,1},{1,0},{2,3},{3,2},{4,5},{5,4},{6,7},{7,6},{8,9},{9,8},{10,11... | collective-permute-start | bytes 2654216 | tf_op jit(solution)/shard_map/ppermute | solution.py:1562
  246.9 21.2 %collective-permute-start.21 = (bf16[2,4,48,768]{3,2,1,0:T(8,128)(2,1)S(1)}, bf16[2,4,48,768]{3,2,1,0:T(8,128)(2,1)S(1)}, u32[]{:S(2)}, u32[]{:S(2)}) collective-permute-start(bf16[2,4,48,768]{3,2,1,0:T(8,128)(2,1)S(1)} %get-tuple-element.361), channel_id=1, source_target_pairs={{0,4},{4,0},{1,5},{5,1},{2,6},{6,2},{3,7},{7,3},{8,12},{12,8},{9,1... | collective-permute-start | bytes 1769480 | tf_op jit(solution)/shard_map/ppermute | solution.py:32
  248.3 19.8 %collective-permute-start.24 = (bf16[2,96,768]{2,1,0:T(8,128)(2,1)S(1)}, bf16[2,96,768]{2,1,0:T(8,128)(2,1)S(1)}, u32[]{:S(2)}, u32[]{:S(2)}) collective-permute-start(bf16[2,96,768]{2,1,0:T(8,128)(2,1)S(1)} %get-tuple-element.279), channel_id=1, source_target_pairs={{0,4},{4,0},{1,5},{5,1},{2,6},{6,2},{3,7},{7,3},{8,12},{12,8},{9,1... | collective-permute-start | bytes 884744 | tf_op jit(solution)/shard_map/ppermute | solution.py:32
  249.2 18.9 %collective-permute-start.25 = (f32[5,768]{1,0:T(8,128)S(1)}, f32[5,768]{1,0:T(8,128)S(1)}, u32[]{:S(2)}, u32[]{:S(2)}) collective-permute-start(f32[5,768]{1,0:T(8,128)S(1)} %add.144), channel_id=1, source_target_pairs={{0,1},{1,0},{2,3},{3,2},{4,5},{5,4},{6,7},{7,6},{8,9},{9,8},{10,11... | collective-permute-start | bytes 46088 | tf_op jit(solution)/shard_map/ppermute | solution.py:32
  268.7 21.9 %copy-start.10 = (bf16[512,768]{1,0:T(8,128)(2,1)S(1)}, bf16[512,768]{1,0:T(8,128)(2,1)}, u32[]{:S(2)}) copy-start(bf16[512,768]{1,0:T(8,128)(2,1)} %copy-done.9) | copy-start | bytes 2359300
  268.7 14.5 %collective-permute-start.27 = (bf16[2,2,48,1152]{3,2,1,0:T(8,128)(2,1)S(1)}, bf16[2,2,48,1152]{3,2,1,0:T(8,128)(2,1)S(1)}, u32[]{:S(2)}, u32[]{:S(2)}) collective-permute-start(bf16[2,2,48,1152]{3,2,1,0:T(8,128)(2,1)S(1)} %get-tuple-element.288), channel_id=1, source_target_pairs={{0,4},{4,0},{1,5},{5,1},{2,6},{6,2},{3,7},{7,3},{8,12},{12,8},{9,1... | collective-permute-start | bytes 1327112 | tf_op jit(solution)/shard_map/ppermute | solution.py:32
  270.0 14.0 %collective-permute-start.28 = (bf16[4,48,1152]{2,1,0:T(8,128)(2,1)S(1)}, bf16[4,48,1152]{2,1,0:T(8,128)(2,1)S(1)}, u32[]{:S(2)}, u32[]{:S(2)}) collective-permute-start(bf16[4,48,1152]{2,1,0:T(8,128)(2,1)S(1)} %get-tuple-element.289), channel_id=1, source_target_pairs={{0,8},{8,0},{16,24},{24,16},{1,9},{9,1},{17,25},{25,17},{2,10},{10... | collective-permute-start | bytes 1327112 | tf_op jit(solution)/shard_map/ppermute | solution.py:32
  271.5 11.7 %collective-permute-start.26 = (bf16[4,48,768]{2,1,0:T(8,128)(2,1)S(1)}, bf16[4,48,768]{2,1,0:T(8,128)(2,1)S(1)}, u32[]{:S(2)}, u32[]{:S(2)}) collective-permute-start(bf16[4,48,768]{2,1,0:T(8,128)(2,1)S(1)} %get-tuple-element.287), channel_id=1, source_target_pairs={{0,1},{1,0},{2,3},{3,2},{4,5},{5,4},{6,7},{7,6},{8,9},{9,8},{10,11... | collective-permute-start | bytes 884744 | tf_op jit(solution)/shard_map/ppermute | solution.py:1562
  272.8 10.4 %collective-permute-start.29 = (bf16[1,96,768]{2,1,0:T(8,128)(2,1)S(1)}, bf16[1,96,768]{2,1,0:T(8,128)(2,1)S(1)}, u32[]{:S(2)}, u32[]{:S(2)}) collective-permute-start(bf16[1,96,768]{2,1,0:T(8,128)(2,1)S(1)} %get-tuple-element.290), channel_id=1, source_target_pairs={{0,16},{8,24},{16,0},{24,8},{1,17},{9,25},{17,1},{25,9},{2,18},{10... | collective-permute-start | bytes 442376 | tf_op jit(solution)/shard_map/ppermute | solution.py:32
  275.4 4.6 %collective-permute-start.30 = (f32[5,768]{1,0:T(8,128)S(1)}, f32[5,768]{1,0:T(8,128)S(1)}, u32[]{:S(2)}, u32[]{:S(2)}) collective-permute-start(f32[5,768]{1,0:T(8,128)S(1)} %add.145), channel_id=1, source_target_pairs={{0,4},{4,0},{1,5},{5,1},{2,6},{6,2},{3,7},{7,3},{8,12},{12,8},{9,1... | collective-permute-start | bytes 46088 | tf_op jit(solution)/shard_map/ppermute | solution.py:32
  284.3 10.8 %collective-permute-start.31 = (bf16[2,48,768]{2,1,0:T(8,128)(2,1)S(1)}, bf16[2,48,768]{2,1,0:T(8,128)(2,1)S(1)}, u32[]{:S(2)}, u32[]{:S(2)}) collective-permute-start(bf16[2,48,768]{2,1,0:T(8,128)(2,1)S(1)} %get-tuple-element.300), channel_id=1, source_target_pairs={{0,8},{8,0},{16,24},{24,16},{1,9},{9,1},{17,25},{25,17},{2,10},{10... | collective-permute-start | bytes 442376 | tf_op jit(solution)/shard_map/ppermute | solution.py:32
  287.0 8.7 %collective-permute-start.32 = (bf16[2,48,1152]{2,1,0:T(8,128)(2,1)S(1)}, bf16[2,48,1152]{2,1,0:T(8,128)(2,1)S(1)}, u32[]{:S(2)}, u32[]{:S(2)}) collective-permute-start(bf16[2,48,1152]{2,1,0:T(8,128)(2,1)S(1)} %get-tuple-element.301), channel_id=1, source_target_pairs={{0,1},{1,0},{2,3},{3,2},{4,5},{5,4},{6,7},{7,6},{8,9},{9,8},{10,11... | collective-permute-start | bytes 663560 | tf_op jit(solution)/shard_map/ppermute | solution.py:1562
  288.0 7.7 %collective-permute-start.33 = (bf16[2,48,1152]{2,1,0:T(8,128)(2,1)S(1)}, bf16[2,48,1152]{2,1,0:T(8,128)(2,1)S(1)}, u32[]{:S(2)}, u32[]{:S(2)}) collective-permute-start(bf16[2,48,1152]{2,1,0:T(8,128)(2,1)S(1)} %get-tuple-element.302), channel_id=1, source_target_pairs={{0,4},{4,0},{1,5},{5,1},{2,6},{6,2},{3,7},{7,3},{8,12},{12,8},{9,1... | collective-permute-start | bytes 663560 | tf_op jit(solution)/shard_map/ppermute | solution.py:32
  288.5 7.1 %collective-permute-start.34 = (bf16[1,96,768]{2,1,0:T(8,128)(2,1)S(1)}, bf16[1,96,768]{2,1,0:T(8,128)(2,1)S(1)}, u32[]{:S(2)}, u32[]{:S(2)}) collective-permute-start(bf16[1,96,768]{2,1,0:T(8,128)(2,1)S(1)} %get-tuple-element.303.refs_6_), channel_id=1, source_target_pairs={{0,16},{8,24},{16,0},{24,8},{1,17},{9,25},{17,1},{25,9},{2,18},{10... | collective-permute-start | bytes 442376 | tf_op jit(solution)/shard_map/ppermute | solution.py:32
  290.3 3.8 %collective-permute-start.35 = (f32[5,768]{1,0:T(8,128)S(1)}, f32[5,768]{1,0:T(8,128)S(1)}, u32[]{:S(2)}, u32[]{:S(2)}) collective-permute-start(f32[5,768]{1,0:T(8,128)S(1)} %add.146), channel_id=1, source_target_pairs={{0,8},{8,0},{16,24},{24,16},{1,9},{9,1},{17,25},{25,17},{2,10},{10... | collective-permute-start | bytes 46088 | tf_op jit(solution)/shard_map/ppermute | solution.py:32
  294.1 8.9 %collective-permute-start.37 = (bf16[256,768]{1,0:T(8,128)(2,1)S(1)}, bf16[256,768]{1,0:T(8,128)(2,1)S(1)}, u32[]{:S(2)}, u32[]{:S(2)}) collective-permute-start(bf16[256,768]{1,0:T(8,128)(2,1)S(1)} %get-tuple-element.314), channel_id=1, source_target_pairs={{0,1},{1,0},{2,3},{3,2},{4,5},{5,4},{6,7},{7,6},{8,9},{9,8},{10,11... | collective-permute-start | bytes 1179656 | tf_op jit(solution)/shard_map/ppermute | solution.py:1712
  295.8 13.1 %collective-permute-start.36 = (bf16[1,48,3072]{2,1,0:T(8,128)(2,1)S(1)}, bf16[1,48,3072]{2,1,0:T(8,128)(2,1)S(1)}, u32[]{:S(2)}, u32[]{:S(2)}) collective-permute-start(bf16[1,48,3072]{2,1,0:T(8,128)(2,1)S(1)} %get-tuple-element.312), channel_id=1, source_target_pairs={{0,16},{8,24},{16,0},{24,8},{1,17},{9,25},{17,1},{25,9},{2,18},{10... | collective-permute-start | bytes 884744 | tf_op jit(solution)/shard_map/ppermute | solution.py:32
  296.6 12.6 %collective-permute-start.38 = (bf16[2,96,768]{2,1,0:T(8,128)(2,1)S(1)}, bf16[2,96,768]{2,1,0:T(8,128)(2,1)S(1)}, u32[]{:S(2)}, u32[]{:S(2)}) collective-permute-start(bf16[2,96,768]{2,1,0:T(8,128)(2,1)S(1)} %get-tuple-element.316.refs_2_), channel_id=1, source_target_pairs={{0,8},{8,0},{16,24},{24,16},{1,9},{9,1},{17,25},{25,17},{2,10},{10... | collective-permute-start | bytes 884744 | tf_op jit(solution)/shard_map/ppermute | solution.py:32
  298.8 10.4 %collective-permute-start.39 = (f32[5,768]{1,0:T(8,128)S(1)}, f32[5,768]{1,0:T(8,128)S(1)}, u32[]{:S(2)}, u32[]{:S(2)}) collective-permute-start(f32[5,768]{1,0:T(8,128)S(1)} %add.147), channel_id=1, source_target_pairs={{0,16},{8,24},{16,0},{24,8},{1,17},{9,25},{17,1},{25,9},{2,18},{10... | collective-permute-start | bytes 46088 | tf_op jit(solution)/shard_map/ppermute | solution.py:32
  309.3 16.1 %collective-permute-start.42 = (bf16[4,96,768]{2,1,0:T(8,128)(2,1)S(1)}, bf16[4,96,768]{2,1,0:T(8,128)(2,1)S(1)}, u32[]{:S(2)}, u32[]{:S(2)}) collective-permute-start(bf16[4,96,768]{2,1,0:T(8,128)(2,1)S(1)} %get-tuple-element.323.refs_2_), channel_id=1, source_target_pairs={{0,4},{4,0},{1,5},{5,1},{2,6},{6,2},{3,7},{7,3},{8,12},{12,8},{9,1... | collective-permute-start | bytes 1769480 | tf_op jit(solution)/shard_map/ppermute | solution.py:32
  310.8 8.8 %collective-permute-start.41 = (bf16[256,768]{1,0:T(8,128)(2,1)S(1)}, bf16[256,768]{1,0:T(8,128)(2,1)S(1)}, u32[]{:S(2)}, u32[]{:S(2)}) collective-permute-start(bf16[256,768]{1,0:T(8,128)(2,1)S(1)} %get-tuple-element.321), channel_id=1, source_target_pairs={{0,1},{1,0},{2,3},{3,2},{4,5},{5,4},{6,7},{7,6},{8,9},{9,8},{10,11... | collective-permute-start | bytes 1179656 | tf_op jit(solution)/shard_map/ppermute | solution.py:1712
  311.7 13.6 %collective-permute-start.40 = (bf16[1,48,3072]{2,1,0:T(8,128)(2,1)S(1)}, bf16[1,48,3072]{2,1,0:T(8,128)(2,1)S(1)}, u32[]{:S(2)}, u32[]{:S(2)}) collective-permute-start(bf16[1,48,3072]{2,1,0:T(8,128)(2,1)S(1)} %get-tuple-element.320.refs_0_), channel_id=1, source_target_pairs={{0,16},{8,24},{16,0},{24,8},{1,17},{9,25},{17,1},{25,9},{2,18},{10... | collective-permute-start | bytes 884744 | tf_op jit(solution)/shard_map/ppermute | solution.py:32
  325.5 9.6 %collective-permute-start.45 = (bf16[8,96,768]{2,1,0:T(8,128)(2,1)S(1)}, bf16[8,96,768]{2,1,0:T(8,128)(2,1)S(1)}, u32[]{:S(2)}, u32[]{:S(2)}) collective-permute-start(bf16[8,96,768]{2,1,0:T(8,128)(2,1)S(1)} %get-tuple-element.334.part_ref), channel_id=1, source_target_pairs={{0,2},{2,0},{1,3},{3,1},{4,6},{6,4},{5,7},{7,5},{8,10},{10,8},{9,1... | collective-permute-start | bytes 3538952 | tf_op jit(solution)/shard_map/ppermute | solution.py:1476
  325.6 9.4 %collective-permute-start.43 = (bf16[2,48,1536]{2,1,0:T(8,128)(2,1)S(1)}, bf16[2,48,1536]{2,1,0:T(8,128)(2,1)S(1)}, u32[]{:S(2)}, u32[]{:S(2)}) collective-permute-start(bf16[2,48,1536]{2,1,0:T(8,128)(2,1)S(1)} %get-tuple-element.326.refs_0_), channel_id=1, source_target_pairs={{0,8},{8,0},{16,24},{24,16},{1,9},{9,1},{17,25},{25,17},{2,10},{10... | collective-permute-start | bytes 884744 | tf_op jit(solution)/shard_map/ppermute | solution.py:32
  325.7 9.4 %collective-permute-start.44 = (bf16[2,48,1536]{2,1,0:T(8,128)(2,1)S(1)}, bf16[2,48,1536]{2,1,0:T(8,128)(2,1)S(1)}, u32[]{:S(2)}, u32[]{:S(2)}) collective-permute-start(bf16[2,48,1536]{2,1,0:T(8,128)(2,1)S(1)} %get-tuple-element.327.refs_2_), channel_id=1, source_target_pairs={{0,4},{4,0},{1,5},{5,1},{2,6},{6,2},{3,7},{7,3},{8,12},{12,8},{9,1... | collective-permute-start | bytes 884744 | tf_op jit(solution)/shard_map/ppermute | solution.py:32
  335.2 14.9 %collective-permute-start.46 = (bf16[4,48,1536]{2,1,0:T(8,128)(2,1)S(1)}, bf16[4,48,1536]{2,1,0:T(8,128)(2,1)S(1)}, u32[]{:S(2)}, u32[]{:S(2)}) collective-permute-start(bf16[4,48,1536]{2,1,0:T(8,128)(2,1)S(1)} %get-tuple-element.331.refs_0_), channel_id=1, source_target_pairs={{0,4},{4,0},{1,5},{5,1},{2,6},{6,2},{3,7},{7,3},{8,12},{12,8},{9,1... | collective-permute-start | bytes 1769480 | tf_op jit(solution)/shard_map/ppermute | solution.py:32
  336.5 14.6 %collective-permute-start.47 = (bf16[4,48,1536]{2,1,0:T(8,128)(2,1)S(1)}, bf16[4,48,1536]{2,1,0:T(8,128)(2,1)S(1)}, u32[]{:S(2)}, u32[]{:S(2)}) collective-permute-start(bf16[4,48,1536]{2,1,0:T(8,128)(2,1)S(1)} %get-tuple-element.332.refs_2_), channel_id=1, source_target_pairs={{0,8},{8,0},{16,24},{24,16},{1,9},{9,1},{17,25},{25,17},{2,10},{10... | collective-permute-start | bytes 1769480 | tf_op jit(solution)/shard_map/ppermute | solution.py:32
  351.3 4.6 %collective-permute-start.48 = (bf16[8,48,3072]{2,1,0:T(8,128)(2,1)S(1)}, bf16[8,48,3072]{2,1,0:T(8,128)(2,1)S(1)}, u32[]{:S(2)}, u32[]{:S(2)}) collective-permute-start(bf16[8,48,3072]{2,1,0:T(8,128)(2,1)S(1)} %phase.17.part_ref), channel_id=1, source_target_pairs={{0,2},{2,0},{1,3},{3,1},{4,6},{6,4},{5,7},{7,5},{8,10},{10,8},{9,1... | collective-permute-start | bytes 7077896 | tf_op jit(solution)/shard_map/ppermute | solution.py:1476
  (31 other events, 62.3 us)

commit v3 on v2

--- a/solution.py
+++ b/solution.py
@@ -250,24 +250,34 @@
 ):
     groups = lse1_ref.shape[0]
     moves = Moves(sems)
-    ready = [moves.whole(a_far, a_ref), moves.whole(w_far.at[0], w_ref.at[0])]
+    first = moves.take(6)
+
+    def weight(j):
+        return pltpu.make_async_copy(w_far.at[j], w_ref.at[j], sems.at[first + j])
+
+    def projected(j):
+        return pltpu.make_async_copy(qkvo_ref.at[j], qkvo_far.at[j], sems.at[first + 3 + j])
+
+    a_there = moves.whole(a_far, a_ref)
+    weight(0).start()
     arrive = [moves.groups(*t) for t in ((qkve_far, qkve_ref), (o1_far, o1_ref))]
     leave = moves.groups(o2_ref, o2_far)
-    for wait in ready:
-        wait()
-    ready = [moves.whole(w_far.at[j], w_ref.at[j]) for j in (1, 2)]
-    a = a_ref[...]
-    sent = []
-    for j in range(3):
-        if j:
-            ready[j - 1]()
-        if j == 1:
-            masks = [moves.whole(*t) for t in ((incl_far, incl_ref), (strict_far, strict_ref))]
-            for g in range(2):
-                for start, _ in arrive:
-                    start(g)
-        qkvo_ref[j] = dot(a, w_ref[j]).astype(BF16)
-        sent.append(moves.whole(qkvo_ref.at[j], qkvo_far.at[j]))
+    a_there()
+    weight(0).wait()
+    weight(1).start()
+    weight(2).start()
+    masks = [moves.whole(*t) for t in ((incl_far, incl_ref), (strict_far, strict_ref))]
+    for g in range(2):
+        for start, _ in arrive:
+            start(g)
+
+    def project(j, _):
+        pl.when(j > 0)(lambda: weight(j).wait())
+        qkvo_ref[j] = dot(a_ref[...], w_ref[j]).astype(BF16)
+        projected(j).start()
+        return 0
+
+    lax.fori_loop(0, 3, project, 0)
     for wait in masks:
         wait()
 
@@ -327,8 +337,8 @@
         return 0
 
     lax.fori_loop(0, rows * groups, row, 0)
-    for wait in sent:
-        wait()
+    for j in range(3):
+        projected(j).wait()
     for g in range(groups):
         leave[1](g)
 
@@ -590,10 +600,13 @@
     lax.fori_loop(0, rows * groups, row, 0)
     for _, wait in late:
         wait()
-    da = dot_nt(dqkv_ref[0], w_ref[0])
-    da += dot_nt(dqkv_ref[1], w_ref[1])
-    da += dot_nt(dqkv_ref[2], w_ref[2])
-    da_ref[...] = da
+    da_ref[...] = jnp.zeros_like(da_ref)
+
+    def project_back(j, _):
+        da_ref[...] += dot_nt(dqkv_ref[j], w_ref[j])
+        return 0
+
+    lax.fori_loop(0, 3, project_back, 0)
     sums_ref[...] = jnp.zeros_like(sums_ref)
 
     def finish(i, _):
@@ -731,15 +744,18 @@
         ho_ref[i * half : (i + 1) * half] += dot(g, chunk_of(wdown_ref, j, 0)[...])
 
 
-def start_norm(x_ref, h1_ref, n2_ref, gb_ref, ho_ref=None):
+def start_norm(x_ref, h1_ref, n2_ref, gb_ref, ho_ref=None, normal_ref=None, inverse_ref=None):
     def part(k, _):
         sl = pl.ds(pl.multiple_of(k * ROWS_AT_ONCE, ROWS_AT_ONCE), ROWS_AT_ONCE)
         h1 = x_ref[sl].astype(F32) + h1_ref[sl]
         h1_ref[sl] = h1
-        normal, _ = norm_stats(h1)
+        normal, inverse = norm_stats(h1)
         n2_ref[sl] = (normal * gb_ref[1:2] + gb_ref[3:4]).astype(BF16)
         if ho_ref is not None:
             ho_ref[sl] = h1 + gb_ref[4:5]
+        if normal_ref is not None:
+            normal_ref[sl] = normal
+            inverse_ref[sl] = jnp.broadcast_to(inverse, (ROWS_AT_ONCE, inverse_ref.shape[1]))
         return 0
 
     lax.fori_loop(0, h1_ref.shape[0] // ROWS_AT_ONCE, part, 0)
@@ -787,19 +803,34 @@
     up = Weight(moves, (None,) + ups_far, wup_ref, 1)
     down = Weight(moves, (None,) + downs_far, wdown_ref, 0)
     gs, ds = (Chunks(moves, f, b, 1, True, True) for f, b in ((g_far, g_buf), (d_far, d_buf)))
-    ready = [moves.whole(*t) for t in ((n2_far, n2_ref), (part_far, ho_ref))]
+    n2_there = moves.whole(n2_far, n2_ref)
     up.start_others()
     down.start_others()
-    for wait in ready:
-        wait()
+    part_there = moves.whole(part_far, ho_ref)
+    number, half = up.number, n2_ref.shape[0] // 2
+    n2_there()
     up.wait_others()
+
+    def rise(i, _):
+        j = number + i
+        for sl in (slice(0, half), slice(half, 2 * half)):
+            g, d = gelu_parts(dot(n2_ref[sl], chunk_of(wup_ref, j, 1)[...]))
+            g_buf[j % number, sl] = g.astype(BF16)
+            d_buf[j % number, sl] = d.astype(BF16)
+        gs.start(j)
+        ds.start(j)
+        return 0
+
+    lax.fori_loop(0, number, rise, 0)
     down.wait_others()
-
-    def step(i, _):
-        feed_chunk(n2_ref, wup_ref, wdown_ref, up.number + i, g_buf, d_buf, ho_ref, gs, ds, i)
+    part_there()
+
+    def fall(i, _):
+        j = number + i
+        ho_ref[...] += dot(g_buf[j % number], chunk_of(wdown_ref, j, 0)[...])
         return 0
 
-    lax.fori_loop(0, up.number, step, 0)
+    lax.fori_loop(0, number, fall, 0)
     sent = moves.whole(ho_ref, ho_far)
 
     def norm(k, _):
@@ -811,7 +842,7 @@
     lax.fori_loop(0, ho_ref.shape[0] // ROWS_AT_ONCE, norm, 0)
     moves.whole(ao_ref, ao_far)()
     sent()
-    for j in range(2 * up.number - 2, 2 * up.number):
+    for j in range(number, 2 * number):
         gs.wait(j)
         ds.wait(j)
 
@@ -848,7 +879,7 @@
         far_of(n2, part, g, dgelu) + [gb] + far_of(*ups, *downs),
         far_of(sds(g.shape, BF16), sds(g.shape, BF16), sds(part.shape, F32), sds(n2.shape, BF16)),
         scratch=near_of(n2, sds((d, ff), BF16), sds((ff, d), BF16), part, n2)
-        + [pltpu.VMEM((2, n, CHUNK), BF16)] * 2
+        + [pltpu.VMEM((ff // CHUNK // 2, n, CHUNK), BF16)] * 2
         + [pltpu.SemaphoreType.DMA((40,))],
         vmem=40,
         aliases={2: 0, 3: 1},
@@ -864,14 +895,18 @@
 
 
 def after_norm_back(
-    moves, size, h1_ref, dn_ref, db_ref, wout_ref, gb_ref, sums_ref, dp_ref, do_ref, dh1_far, dp_far, do_far
+    moves, size, h1_ref, dn_ref, db_ref, wout_ref, gb_ref, sums_ref, dp_ref, do_ref, dh1_far, dp_far, do_far,
+    inverse_ref=None,
 ):
     gain_sum = jnp.zeros_like(gb_ref[0:1])
     bias_sum = jnp.zeros_like(gb_ref[0:1])
     waits = []
     for i in range(h1_ref.shape[0] // size):
         sl = slice(i * size, (i + 1) * size)
-        normal, inverse = norm_stats(h1_ref[sl])
+        if inverse_ref is None:
+            normal, inverse = norm_stats(h1_ref[sl])
+        else:
+            normal, inverse = h1_ref[sl], inverse_ref[sl, :1]
         dn = dn_ref[sl]
         gain_sum += jnp.sum(dn * normal, axis=0, keepdims=True)
         bias_sum += jnp.sum(dn, axis=0, keepdims=True)
@@ -901,7 +936,7 @@
     rows, seq, x_far, ho_far, o_far, cot_far, wout_far, gb_ref, ups_far, downs_far,
     outs_far, outs2_far, n2_far, g_far, du_far, dh1_far, dp_far, do_far, sums_ref, dm_far,
     x_ref, ho_ref, o_ref, cot_ref, wout_ref, wup_ref, wdown_ref, n2_ref, dm_ref,
-    h1_ref, z_ref, dn_ref, dp_ref, do_ref, g_buf, du_buf, sems,
+    normal_ref, z_ref, dn_ref, dp_ref, do_ref, inverse_ref, g_buf, du_buf, sems,
 ):
     n = rows * seq
     moves = Moves(sems)
@@ -924,10 +959,10 @@
     for i, sl in enumerate(halves):
         if i:
             then()
-        h1_ref[sl] = dot(o_ref[i], wout_ref[...])
-        start_norm(x_ref if i == 0 else ho_ref, h1_ref.at[pl.ds(i * n, n)], n2_ref.at[pl.ds(i * n, n)], gb_ref)
+        z_ref[sl] = dot(o_ref[i], wout_ref[...])
+        z_at, n2_at, normal_at, inverse_at = (t.at[pl.ds(i * n, n)] for t in (z_ref, n2_ref, normal_ref, inverse_ref))
+        start_norm(x_ref if i == 0 else ho_ref, z_at, n2_at, gb_ref, None, normal_at, inverse_at)
     kept = [moves.whole(*t) for t in ((n2_ref, n2_far), (dm_ref, dm_far))]
-    z_ref[...] = jnp.zeros_like(z_ref)
     dn_ref[...] = jnp.zeros_like(dn_ref)
 
     def step(j, _):
@@ -938,7 +973,7 @@
             gs.wait(j - 2)
             dus.wait(j - 2)
 
-        for sl in halves:
+        for sl in (slice(0, 2 * n),):
             u = dot(n2_ref[sl], chunk_of(wup_ref, j, 1)[...])
             dg = dot_nt(dm_ref[sl], chunk_of(wdown_ref, j, 0)[...])
             g, d = gelu_parts(u)
@@ -955,12 +990,13 @@
     lax.fori_loop(0, number, step, 0)
     for r in range(rows):
         pair = [slice(i * n + r * seq, i * n + (r + 1) * seq) for i in range(2)]
-        z = jnp.concatenate([(h1_ref[s] + z_ref[s]).astype(BF16) for s in pair], axis=0)
+        z = jnp.concatenate([z_ref[s].astype(BF16) for s in pair], axis=0)
         cot_ref[r] = dot(mix, z).astype(BF16)
     half = rows // 2
     kept += [moves.whole(cot_ref.at[pl.ds(i * half, half)], far) for i, far in enumerate((outs_far, outs2_far))]
     kept += after_norm_back(
-        moves, seq, h1_ref, dn_ref, dm_ref, wout_ref, gb_ref, sums_ref, dp_ref, do_ref, dh1_far, dp_far, do_far
+        moves, seq, normal_ref, dn_ref, dm_ref, wout_ref, gb_ref, sums_ref, dp_ref, do_ref, dh1_far, dp_far, do_far,
+        inverse_ref,
     )
     for wait in kept:
         wait()
@@ -979,7 +1015,7 @@
         functools.partial(mlp_second_body, rows, seq, len(ups), len(downs)),
         far_of(x, ho, o2, cot, wout) + [gb] + far_of(*ups, *downs),
         far_of(out, out, low, wide, wide, full, low, low) + [sds((2, d), F32)] + far_of(low),
-        scratch=near_of(x, ho, o2, cot, wout, sds((d, ff), BF16), sds((ff, d), BF16), low, low, full, full, full, low, low)
+        scratch=near_of(x, ho, o2, cot, wout, sds((d, ff), BF16), sds((ff, d), BF16), low, low, full, full, full, low, low, sds((2 * n, 128), F32))
         + [pltpu.VMEM((2, 2 * n, CHUNK), BF16)] * 2
         + [pltpu.SemaphoreType.DMA((64,))],
         vmem=60,
@@ -1573,9 +1609,14 @@
             self.sent.append(sent)
             self.got.append(self.over(way, sent))
 
-    def first(self):
+    def fold_first(self):
         total = fold(self.keep, self.got)
-        self.send((total[..., :CUT], "x"), (total[..., CUT:], "z"))
+        half = total.shape[1] // 2
+        return [part for lanes in (total[..., :CUT], total[..., CUT:]) for part in (lanes[:, :half], lanes[:, half:])]
+
+    def first(self, parts):
+        self.keep, self.sent = [parts[0], parts[2]], [parts[1], parts[3]]
+        self.got = [self.over("x", parts[1]), self.over("z", parts[3])]
 
     def first_hop(self, way):
         self.send((fold(self.keep, self.got), way))
@@ -1769,10 +1810,13 @@
     all_steps(down.hop("z"))
     small = jnp.stack([sums_e[0] + sums_o[0], sums1[0] + sums2[0], sums_e[1] + sums_o[1], sums1[1] + sums2[1], sums_o[2]])
     qkv_keep, qkv_go = grad_qkv(me_z, a_e, a_o, after(dqkv_e, *down.sent), dqkv_o)
+    up_parts = up.fold_first()
+    qkv_keep, qkv_go, down.got, up_parts = sync(qkv_keep, qkv_go, down.got, up_parts)
     out = link.finish(
-        jnp.concatenate([out, out_two], axis=0), jnp.concatenate([out_got, jnp.concatenate(after(out_last, dqkv_e), axis=1)], axis=0), link.out_shape
+        jnp.concatenate([out, out_two], axis=0),
+        jnp.concatenate([out_got, jnp.concatenate(after(out_last, up_parts), axis=1)], axis=0),
+        link.out_shape,
     )
-    qkv_keep, qkv_go, down.got, out = up.wait(qkv_keep, qkv_go, down.got, out)
     qkv = link.hops(qkv_keep, link.core(qkv_go))
     small_steps = iter(link.small_steps())
     small_got = link.flip(after(small, qkv_go), next(small_steps))
@@ -1789,11 +1833,13 @@
             step = next(small_steps, None)
             small_got = None if step is None else link.flip(small, step)
 
+    chunks.remove(up)
     wait_all()
-    chunks.append(down)
-    up.first()
+    up.first(up_parts)
     qkv.first_hop("partner")
     all_steps(down.hop("x"))
+    chunks += [up, down]
+    (out,) = up.wait(out)
     wait_all()
     all_steps(up.hop("partner", "x"), qkv.hop("z"), down.hop("w"))
     wait_all()

time: 366 us -> 361 us (0.986)
  waiting for transfers between devices: 91.9 us -> 84.6 us
  local copies, waits for them, and re-layouts: 16.2 us -> 20 us
    ppermute x23, waiting for transfers between devices: 59.2 us -> 52 us  [flip_bit(): return lax.ppermute(array, axis, [(i, i ^ bit) for i in range(size)])]
  transfers between devices with their start and end apart: 49 -> 49, of which waited for: 27 -> 28; matrix products, arithmetic and copies ran while one was open for 8% -> 10% of each run, Pallas kernels for 30% -> 30%
where the time goes in v3:
time: 361 us; the launch traced here: 354 us
  Pallas kernels  171 us (47%)
  waiting for transfers between devices  84.6 us (23%)
  starting transfers between devices  50.2 us (14%)
  other arithmetic  26.4 us (7%)
  local copies, waits for them, and re-layouts  20 us (6%)
    pallas_call x23, Pallas kernels, resident(): pl.pallas_call(body, in_specs=[s for _, s in ins], out_specs=[s for _, s...  167 us
    ppermute x23, waiting for transfers between devices, flip_bit(): return lax.ppermute(array, axis, [(i, i ^ bit) for i in range(size)])  52 us
    ppermute x23, starting transfers between devices, flip_bit(): return lax.ppermute(array, axis, [(i, i ^ bit) for i in range(size)])  29.5 us
    ppermute x9, waiting for transfers between devices, partner(): return lax.ppermute(t, 'tensor', FLIP)  21 us
    ppermute x9, starting transfers between devices, partner(): return lax.ppermute(t, 'tensor', FLIP)  11.9 us
    another operation x11, other arithmetic, ordered(): jnp.stack([jnp.where(first, mine, theirs), jnp.where(first, theirs, mine)])  7.45 us
  transfers between devices with their start and end apart: 49, of which 28 were waited for; matrix products, arithmetic and copies ran while one was open for 10% of the time, Pallas kernels for 30%

profile of v3, /device:TPU:0, one launch (start us, length us, event | category | flops | bytes accessed | tf_op | source)
XLA Modules:
  0.0 354.4 jit_solution(16704787932363013974)
XLA Ops:
  0.7 2.0 constant_dynamic-slice_fusion.7
  2.7 3.0 collective-permute-start
  5.8 1.3 convert_reduce_fusion
  9.4 2.4 attend_first.2
  13.7 1.3 constant_dynamic-slice_fusion.4.cot_far
  16.2 1.7 collective-permute-start.1
  17.9 1.9 constant_dynamic-slice_fusion.2
  19.8 1.5 collective-permute-start.3
  22.9 5.0 %collective-permute-done.1 = bf16[576,384]{1,0:T(8,128)(2,1)} collective-permute-done((bf16[576,384]{1,0:T(8,128)(2,1)}, bf16[576,384]{1,0:T(8,128)(2,1)}, u32[]{:S(2)}, u32[]{:S(2)}) %collective-permute-start.1) | collective-permute-done | bytes 442400 | tf_op jit(solution)/shard_map/ppermute | solution.py:1720
  30.1 7.1 %collective-permute-done.2 = bf16[96,768]{1,0:T(8,128)(2,1)} collective-permute-done((bf16[96,768]{1,0:T(8,128)(2,1)S(1)}, bf16[96,768]{1,0:T(8,128)(2,1)}, u32[]{:S(2)}, u32[]{:S(2)}) %collective-permute-start.2) | collective-permute-done | bytes 147488 | tf_op jit(solution)/shard_map/ppermute | solution.py:1753
  38.5 1.5 collective-permute-start.5
  40.5 1.6 select_bitcast_fusion.1
  42.3 1.3 copy-done.7
  43.6 2.1 pad_maximum_fusion.w_far
  45.7 2.4 attend_first.3
  48.2 1.6 pad_maximum_fusion.2.qkve_far
  51.9 1.5 collective-permute-start.4
  54.8 9.0 %mlp_own.1 = (f32[512,768]{1,0:T(8,128)}, bf16[512,768]{1,0:T(8,128)(2,1)}, bf16[512,3072]{1,0:T(8,128)(2,1)}, bf16[512,3072]{1,0:T(8,128)(2,1)}, f32[512,768]{1,0:T(8,128)}) custom-call(bf16[512,768]{1,0:T(8,128)(2,1)} %bitcast.59, bf16[512,768]{1,0:T(8,128)(2,1)} %pad_maximum_fusion.10.o_far.o1_far, bf16[768,768]{1,0:T(8,128)(2,1)} %pad_maximum_fusion.8.wout_far, ...), custom_call_target="tpu_custom_call" | custom-call | tf_op jit(solution)/shard_map/mlp_own/pallas_call | solution.py:112
  63.8 3.3 collective-permute-done.5.refs_4_.refs_6_
  68.2 2.8 collective-permute-done.9.refs_2_.refs_3_
  73.5 8.4 %mlp_other.1 = (bf16[512,3072]{1,0:T(8,128)(2,1)}, bf16[512,3072]{1,0:T(8,128)(2,1)}, f32[512,768]{1,0:T(8,128)}, bf16[512,768]{1,0:T(8,128)(2,1)}) custom-call(bf16[512,768]{1,0:T(8,128)(2,1)} %get-tuple-element.205.n2_far.n1_far, f32[512,768]{1,0:T(8,128)} %get-tuple-element.206.part_far, ...), custom_call_target="tpu_custom_call", output_to_operand_aliasing={{0}: (2, {}), {1}: (3, {})} | custom-call | tf_op jit(solution)/shard_map/mlp_other/pallas_call | solution.py:112
  81.9 13.6 %attend_second.1 = (bf16[3,512,768]{2,1,0:T(8,128)(2,1)}, bf16[2,512,768]{2,1,0:T(8,128)(2,1)}, f32[2,3,4,512]{3,2,1,0:T(4,128)S(1)}) custom-call(bf16[512,768]{1,0:T(8,128)(2,1)} %get-tuple-element.211.a_far.ao_far, bf16[3,768,768]{2,1,0:T(8,128)(2,1)} %pad_maximum_fusion.w_far, f32[2,256,256]{2,1,0:T(8,128)} %copy-done.2, ...), custom_call_target="tpu_custom_call" | custom-call | flops 415236096 | tf_op jit(solution)/shard_map/attend_second/pallas_call | solution.py:112
  95.5 35.9 %mlp_second.1 = (bf16[1,512,768]{2,1,0:T(8,128)(2,1)}, bf16[1,512,768]{2,1,0:T(8,128)(2,1)}, bf16[1024,768]{1,0:T(8,128)(2,1)}, bf16[1024,3072]{1,0:T(8,128)(2,1...) custom-call(bf16[512,768]{1,0:T(8,128)(2,1)} %bitcast.60, ...), custom_call_target="tpu_custom_call" | custom-call | tf_op jit(solution)/shard_map/mlp_second/pallas_call | solution.py:112
  132.5 18.9 %attend_back.1 = (bf16[3,512,768]{2,1,0:T(8,128)(2,1)}, bf16[3,512,768]{2,1,0:T(8,128)(2,1)}, f32[512,768]{1,0:T(8,128)}, f32[3,768]{1,0:T(4,128)S(1)}) custom-call(bf16[3,768,768]{2,1,0:T(8,128)(2,1)} %pad_maximum_fusion.w_far, f32[2,256,256]{2,1,0:T(8,128)} %copy-done.2, f32[2,256,256]{2,1,0:T(8,128)} %get-tuple-element.398.strict_far, ...), custom_call_target="tpu_custom_call" | custom-call | flops 868220928 | tf_op jit(solution)/shard_map/attend_back/pallas_call | solution.py:112
  153.5 14.1 %grad_down.1 = (bf16[2,8,96,768]{3,2,1,0:T(8,128)(2,1)}, bf16[2,8,96,768]{3,2,1,0:T(8,128)(2,1)}) custom-call(s32[2]{0:T(128)S(1)} %rev.3.me_ref, bf16[512,3072]{1,0:T(8,128)(2,1)} %get-tuple-element.212.g1_far, bf16[1024,3072]{1,0:T(8,128)(2,1)} %get-tuple-element.219.g2_far, f32[512,768]{1,0:T(8,128)} %get-tuple-element.235.dy_far, ...), custom_call_target="tpu_custom_call" | custom-call | flops 452984832 | tf_op jit(solution)/shard_map/grad_down/pallas_call | solution.py:112
  168.8 13.4 %mlp_back.1 = (bf16[512,3072]{1,0:T(8,128)(2,1)}, f32[512,768]{1,0:T(8,128)}, bf16[512,768]{1,0:T(8,128)(2,1)}, bf16[512,768]{1,0:T(8,128)(2,1)}, f32[2,768]{1,0:T(2,128)S(1)}) custom-call(f32[512,768]{1,0:T(8,128)} %get-tuple-element.235.dy_far, f32[512,768]{1,0:T(8,128)} %get-tuple-element.236.h1_far, bf16[768,768]{1,0:T(8,128)(2,1)} %pad_maximum_fusion.8.wout_far, ...), custom_call_target="tpu_custom_call" | custom-call | tf_op jit(solution)/shard_map/mlp_back/pallas_call | solution.py:112
  183.0 1.6 slice_bitcast_fusion
  186.2 16.7 %grad_up.1 = (bf16[2,8,48,1920]{3,2,1,0:T(8,128)(2,1)}, bf16[2,8,48,1920]{3,2,1,0:T(8,128)(2,1)}) custom-call(s32[3]{0:T(128)} %pad_add_fusion.1.me_ref, bf16[512,768]{1,0:T(8,128)(2,1)} %get-tuple-element.205.n2_far.n1_far, bf16[1024,768]{1,0:T(8,128)(2,1)} %get-tuple-element.244.n2_far, bf16[512,3072]{1,0:T(8,128)(2,1)} %get-tuple-element.246.du1_far, ...), custom_call_target="tpu_custom_call" | custom-call | flops 566231040 | tf_op jit(solution)/shard_map/grad_up/pallas_call | solution.py:112
  202.9 12.8 %attend_back_even.1 = (bf16[3,512,768]{2,1,0:T(8,128)(2,1)}, bf16[512,768]{1,0:T(8,128)(2,1)S(1)}, f32[2,768]{1,0:T(2,128)S(1)}) custom-call(bf16[3,768,768]{2,1,0:T(8,128)(2,1)} %pad_maximum_fusion.w_far, f32[2,256,256]{2,1,0:T(8,128)} %copy-done.2, bf16[3,512,768]{2,1,0:T(8,128)(2,1)} %pad_maximum_fusion.2.qkve_far, ...), custom_call_target="tpu_custom_call" | custom-call | flops 364904448 | tf_op jit(solution)/shard_map/attend_back_even/pallas_call | solution.py:112
  216.6 1.6 collective-permute-start.17
  218.2 9.8 %grad_qkv.1 = (bf16[2,8,48,1152]{3,2,1,0:T(8,128)(2,1)}, bf16[2,8,48,1152]{3,2,1,0:T(8,128)(2,1)}) custom-call(s32[2]{0:T(128)S(1)} %rev.3.me_ref, bf16[512,768]{1,0:T(8,128)(2,1)} %copy-done.4, bf16[512,768]{1,0:T(8,128)(2,1)} %get-tuple-element.211.a_far.ao_far, bf16[3,512,768]{2,1,0:T(8,128)(2,1)} %get-tuple-element.260.de_far, ...), custom_call_target="tpu_custom_call" | custom-call | flops 226492416 | tf_op jit(solution)/shard_map/grad_qkv/pallas_call | solution.py:112
  229.8 1.3 fusion.5
  233.3 1.6 collective-permute-start.20
  236.6 1.9 add_convert_fusion.2
  243.9 2.0 broadcast_select_fusion.1
  247.0 1.9 pad_maximum_fusion.1
  248.9 8.2 %collective-permute-done.19.refs_1_ = bf16[2,4,48,768]{3,2,1,0:T(8,128)(2,1)} collective-permute-done((bf16[2,4,48,768]{3,2,1,0:T(8,128)(2,1)}, bf16[2,4,48,768]{3,2,1,0:T(8,128)(2,1)}, u32[]{:S(2)}, u32[]{:S(2)}) %collective-permute-start.19) | collective-permute-done | bytes 589856 | tf_op jit(solution)/shard_map/ppermute | solution.py:32
  257.1 5.1 %collective-permute-done.24.refs_7_ = bf16[2,96,768]{2,1,0:T(8,128)(2,1)S(1)} collective-permute-done((bf16[2,96,768]{2,1,0:T(8,128)(2,1)S(1)}, bf16[2,96,768]{2,1,0:T(8,128)(2,1)S(1)}, u32[]{:S(2)}, u32[]{:S(2)}) %collective-permute-start.24) | collective-permute-done | bytes 294944 | tf_op jit(solution)/shard_map/ppermute | solution.py:32
  262.2 2.2 phase.11
  264.5 1.6 collective-permute-start.26
  266.1 1.3 collective-permute-start.28
  268.6 2.6 collective-permute-start.29
  271.8 5.9 %collective-permute-done.30 = f32[5,768]{1,0:T(8,128)S(1)} collective-permute-done((f32[5,768]{1,0:T(8,128)S(1)}, f32[5,768]{1,0:T(8,128)S(1)}, u32[]{:S(2)}, u32[]{:S(2)}) %collective-permute-start.30) | collective-permute-done | bytes 15392 | tf_op jit(solution)/shard_map/ppermute | solution.py:32
  279.3 1.5 collective-permute-start.31
  280.9 2.6 collective-permute-start.32
  284.4 1.6 collective-permute-start.34
  286.4 3.4 collective-permute-done.35
  292.5 1.7 collective-permute-start.38
  294.2 1.6 collective-permute-start.39
  295.8 2.0 collective-permute-done.37
  297.8 7.1 %collective-permute-done.36.refs_1_ = bf16[1,48,3072]{2,1,0:T(8,128)(2,1)S(1)} collective-permute-done((bf16[1,48,3072]{2,1,0:T(8,128)(2,1)S(1)}, bf16[1,48,3072]{2,1,0:T(8,128)(2,1)S(1)}, u32[]{:S(2)}, u32[]{:S(2)}) %collective-permute-start.36) | collective-permute-done | bytes 294944 | tf_op jit(solution)/shard_map/ppermute | solution.py:32
  308.1 7.3 %collective-permute-done.41 = bf16[256,768]{1,0:T(8,128)(2,1)S(1)} collective-permute-done((bf16[256,768]{1,0:T(8,128)(2,1)S(1)}, bf16[256,768]{1,0:T(8,128)(2,1)S(1)}, u32[]{:S(2)}, u32[]{:S(2)}) %collective-permute-start.41) | collective-permute-done | bytes 393248 | tf_op jit(solution)/shard_map/ppermute | solution.py:1753
  315.4 4.9 %collective-permute-done.40.refs_1_ = bf16[1,48,3072]{2,1,0:T(8,128)(2,1)S(1)} collective-permute-done((bf16[1,48,3072]{2,1,0:T(8,128)(2,1)S(1)}, bf16[1,48,3072]{2,1,0:T(8,128)(2,1)S(1)}, u32[]{:S(2)}, u32[]{:S(2)}) %collective-permute-start.40) | collective-permute-done | bytes 294944 | tf_op jit(solution)/shard_map/ppermute | solution.py:32
  320.5 1.6 collective-permute-start.44
  322.7 7.1 %collective-permute-done.43.refs_1_ = bf16[2,48,1536]{2,1,0:T(8,128)(2,1)S(1)} collective-permute-done((bf16[2,48,1536]{2,1,0:T(8,128)(2,1)S(1)}, bf16[2,48,1536]{2,1,0:T(8,128)(2,1)S(1)}, u32[]{:S(2)}, u32[]{:S(2)}) %collective-permute-start.43) | collective-permute-done | bytes 294944 | tf_op jit(solution)/shard_map/ppermute | solution.py:32
  330.0 1.6 collective-permute-start.46
  331.6 1.7 collective-permute-start.47
  334.2 1.9 convert.1
  336.1 2.1 unpack_down.2.refs_0_
  338.2 2.1 unpack_down.3
  340.3 4.6 %collective-permute-done.46.refs_1_ = bf16[4,48,1536]{2,1,0:T(8,128)(2,1)S(1)} collective-permute-done((bf16[4,48,1536]{2,1,0:T(8,128)(2,1)S(1)}, bf16[4,48,1536]{2,1,0:T(8,128)(2,1)S(1)}, u32[]{:S(2)}, u32[]{:S(2)}) %collective-permute-start.46) | collective-permute-done | bytes 589856 | tf_op jit(solution)/shard_map/ppermute | solution.py:32
  344.9 1.2 collective-permute-done.47.refs_3_
  346.8 2.9 unpack_rest.2
  350.9 2.9 unpack_rest.3
  (212 shorter events, 52.0 us)
Async XLA Ops:
  0.6 13.1 %copy-start = (bf16[4,512,768]{2,1,0:T(8,128)(2,1)S(1)}, bf16[4,512,768]{2,1,0:T(8,128)(2,1)}, u32[]{:S(2)}) copy-start(bf16[4,512,768]{2,1,0:T(8,128)(2,1)} %param.19) | copy-start | bytes 9437188
  2.7 13.4 %collective-permute-start = (bf16[576,384]{1,0:T(8,128)(2,1)}, bf16[576,384]{1,0:T(8,128)(2,1)}, u32[]{:S(2)}, u32[]{:S(2)}) collective-permute-start(bf16[576,384]{1,0:T(8,128)(2,1)} %constant_dynamic-slice_fusion.7), channel_id=1, source_target_pairs={{0,1},{1,0},{2,3},{3,2},{4,5},{5,4},{6,7},{7,6},{8,9},{9,8},{10,11... | collective-permute-start | bytes 1327112 | tf_op jit(solution)/shard_map/ppermute | solution.py:1753
  16.2 11.7 %collective-permute-start.1 = (bf16[576,384]{1,0:T(8,128)(2,1)}, bf16[576,384]{1,0:T(8,128)(2,1)}, u32[]{:S(2)}, u32[]{:S(2)}) collective-permute-start(bf16[576,384]{1,0:T(8,128)(2,1)} %collective-permute-done), channel_id=1, source_target_pairs={{0,4},{4,0},{1,5},{5,1},{2,6},{6,2},{3,7},{7,3},{8,12},{12,8},{9,1... | collective-permute-start | bytes 1327112 | tf_op jit(solution)/shard_map/ppermute | solution.py:1720
  19.8 17.4 %collective-permute-start.3 = (bf16[768,384]{1,0:T(8,128)(2,1)}, bf16[768,384]{1,0:T(8,128)(2,1)S(1)}, u32[]{:S(2)}, u32[]{:S(2)}) collective-permute-start(bf16[768,384]{1,0:T(8,128)(2,1)} %constant_dynamic-slice_fusion.2), channel_id=1, source_target_pairs={{0,1},{1,0},{2,3},{3,2},{4,5},{5,4},{6,7},{7,6},{8,9},{9,8},{10,11... | collective-permute-start | bytes 1769480 | tf_op jit(solution)/shard_map/ppermute | solution.py:1753
  22.3 14.9 %collective-permute-start.2 = (bf16[96,768]{1,0:T(8,128)(2,1)S(1)}, bf16[96,768]{1,0:T(8,128)(2,1)}, u32[]{:S(2)}, u32[]{:S(2)}) collective-permute-start(bf16[96,768]{1,0:T(8,128)(2,1)S(1)} %constant_dynamic-slice_fusion.3), channel_id=1, source_target_pairs={{0,1},{1,0},{2,3},{3,2},{4,5},{5,4},{6,7},{7,6},{8,9},{9,8},{10,11... | collective-permute-start | bytes 442376 | tf_op jit(solution)/shard_map/ppermute | solution.py:1753
  22.9 14.4 %copy-start.22 = (bf16[1536,768]{1,0:T(8,128)(2,1)S(1)}, bf16[1536,768]{1,0:T(8,128)(2,1)}, u32[]{:S(2)}) copy-start(bf16[1536,768]{1,0:T(8,128)(2,1)} %refs_5_.3) | copy-start | bytes 7077892
  37.2 3.3 collective-permute-start.6
  38.5 28.6 %collective-permute-start.5 = (bf16[768,768]{1,0:T(8,128)(2,1)}, bf16[768,768]{1,0:T(8,128)(2,1)}, u32[]{:S(2)}, u32[]{:S(2)}) collective-permute-start(bf16[768,768]{1,0:T(8,128)(2,1)} %pad_maximum_fusion.7), channel_id=1, source_target_pairs={{0,1},{1,0},{2,3},{3,2},{4,5},{5,4},{6,7},{7,6},{8,9},{9,8},{10,11... | collective-permute-start | bytes 3538952 | tf_op jit(solution)/shard_map/ppermute | solution.py:1753
  40.0 10.7 %collective-permute-start.7 = (bf16[96,768]{1,0:T(8,128)(2,1)}, bf16[96,768]{1,0:T(8,128)(2,1)}, u32[]{:S(2)}, u32[]{:S(2)}) collective-permute-start(bf16[96,768]{1,0:T(8,128)(2,1)} %collective-permute-done.2), channel_id=1, source_target_pairs={{0,4},{4,0},{1,5},{5,1},{2,6},{6,2},{3,7},{7,3},{8,12},{12,8},{9,1... | collective-permute-start | bytes 442376 | tf_op jit(solution)/shard_map/ppermute | solution.py:1720
  51.8 1.7 collective-permute-start.8
  51.9 15.8 %collective-permute-start.4 = (bf16[768,384]{1,0:T(8,128)(2,1)S(1)}, bf16[768,384]{1,0:T(8,128)(2,1)S(1)}, u32[]{:S(2)}, u32[]{:S(2)}) collective-permute-start(bf16[768,384]{1,0:T(8,128)(2,1)S(1)} %copy-done.26), channel_id=1, source_target_pairs={{0,4},{4,0},{1,5},{5,1},{2,6},{6,2},{3,7},{7,3},{8,12},{12,8},{9,1... | collective-permute-start | bytes 1769480 | tf_op jit(solution)/shard_map/ppermute | solution.py:1720
  53.5 18.9 %copy-start.13 = (f32[5,768]{1,0:T(8,128)}, f32[5,768]{1,0:T(8,128)S(1)}, u32[]{:S(2)}) copy-start(f32[5,768]{1,0:T(8,128)S(1)} %pad_maximum_fusion.14.gb_ref) | copy-start | bytes 46084
  67.7 4.7 %collective-permute-start.11 = (bf16[768,768]{1,0:T(8,128)(2,1)}, bf16[768,768]{1,0:T(8,128)(2,1)S(1)}, u32[]{:S(2)}, u32[]{:S(2)}) collective-permute-start(bf16[768,768]{1,0:T(8,128)(2,1)} %collective-permute-done.5.refs_4_.refs_6_), channel_id=1, source_target_pairs={{0,2},{2,0},{1,3},{3,1},{4,6},{6,4},{5,7},{7,5},{8,10},{10,8},{9,1... | collective-permute-start | bytes 3538952 | tf_op jit(solution)/shard_map/ppermute | solution.py:1756
  67.7 3.3 collective-permute-start.9
  68.2 4.0 %collective-permute-start.10 = (bf16[768,384]{1,0:T(8,128)(2,1)S(1)}, bf16[768,384]{1,0:T(8,128)(2,1)S(1)}, u32[]{:S(2)}, u32[]{:S(2)}) collective-permute-start(bf16[768,384]{1,0:T(8,128)(2,1)S(1)} %collective-permute-done.4.refs_1_.refs_2_), channel_id=1, source_target_pairs={{0,2},{2,0},{1,3},{3,1},{4,6},{6,4},{5,7},{7,5},{8,10},{10,8},{9,1... | collective-permute-start | bytes 1769480 | tf_op jit(solution)/shard_map/ppermute | solution.py:1756
  95.5 37.0 %copy-start.14 = (f32[5,768]{1,0:T(8,128)S(1)}, f32[5,768]{1,0:T(8,128)}, u32[]{:S(2)}) copy-start(f32[5,768]{1,0:T(8,128)} %copy-done.13) | copy-start | bytes 46084
  131.5 20.8 %collective-permute-start.12 = (bf16[1,512,768]{2,1,0:T(8,128)(2,1)}, bf16[1,512,768]{2,1,0:T(8,128)(2,1)S(1)}, u32[]{:S(2)}, u32[]{:S(2)}) collective-permute-start(bf16[1,512,768]{2,1,0:T(8,128)(2,1)} %get-tuple-element.220), channel_id=1, source_target_pairs={{0,1},{1,0},{2,3},{3,2},{4,5},{5,4},{6,7},{7,6},{8,9},{9,8},{10,11... | collective-permute-start | bytes 2359304 | tf_op jit(solution)/shard_map/ppermute | solution.py:1753
  132.5 18.9 %copy-start.30 = (bf16[1,512,768]{2,1,0:T(8,128)(2,1)S(1)}, bf16[1,512,768]{2,1,0:T(8,128)(2,1)}, u32[]{:S(2)}) copy-start(bf16[1,512,768]{2,1,0:T(8,128)(2,1)} %get-tuple-element.230) | copy-start | bytes 2359300
  152.3 15.3 %copy-start.34 = (bf16[1,512,768]{2,1,0:T(8,128)(2,1)}, bf16[1,512,768]{2,1,0:T(8,128)(2,1)S(1)}, u32[]{:S(2)}) copy-start(bf16[1,512,768]{2,1,0:T(8,128)(2,1)S(1)} %collective-permute-done.12) | copy-start | bytes 2359300
  152.3 15.3 %collective-permute-start.13 = (bf16[1,256,768]{2,1,0:T(8,128)(2,1)S(1)}, bf16[1,256,768]{2,1,0:T(8,128)(2,1)S(1)}, u32[]{:S(2)}, u32[]{:S(2)}) collective-permute-start(bf16[1,256,768]{2,1,0:T(8,128)(2,1)S(1)} %get-tuple-element.232), channel_id=1, source_target_pairs={{0,1},{1,0},{2,3},{3,2},{4,5},{5,4},{6,7},{7,6},{8,9},{9,8},{10,11... | collective-permute-start | bytes 1179656 | tf_op jit(solution)/shard_map/ppermute | solution.py:1753
  153.5 14.2 %copy-start.36 = (bf16[1,256,768]{2,1,0:T(8,128)(2,1)S(1)}, bf16[1,256,768]{2,1,0:T(8,128)(2,1)}, u32[]{:S(2)}) copy-start(bf16[1,256,768]{2,1,0:T(8,128)(2,1)} %get-tuple-element.241) | copy-start | bytes 1179652
  167.6 14.6 %collective-permute-start.14 = (bf16[2,8,96,768]{3,2,1,0:T(8,128)(2,1)}, bf16[2,8,96,768]{3,2,1,0:T(8,128)(2,1)S(1)}, u32[]{:S(2)}, u32[]{:S(2)}) collective-permute-start(bf16[2,8,96,768]{3,2,1,0:T(8,128)(2,1)} %get-tuple-element.234), channel_id=1, source_target_pairs={{0,2},{2,0},{1,3},{3,1},{4,6},{6,4},{5,7},{7,5},{8,10},{10,8},{9,1... | collective-permute-start | bytes 7077896 | tf_op jit(solution)/shard_map/ppermute | solution.py:1756
  167.7 14.5 %collective-permute-start.15 = (bf16[1,256,768]{2,1,0:T(8,128)(2,1)S(1)}, bf16[1,256,768]{2,1,0:T(8,128)(2,1)S(1)}, u32[]{:S(2)}, u32[]{:S(2)}) collective-permute-start(bf16[1,256,768]{2,1,0:T(8,128)(2,1)S(1)} %copy-done.36), channel_id=1, source_target_pairs={{0,1},{1,0},{2,3},{3,2},{4,5},{5,4},{6,7},{7,6},{8,9},{9,8},{10,11... | collective-permute-start | bytes 1179656 | tf_op jit(solution)/shard_map/ppermute | solution.py:1753
  168.8 13.5 %copy-start.32 = (bf16[2,8,96,768]{3,2,1,0:T(8,128)(2,1)S(1)}, bf16[2,8,96,768]{3,2,1,0:T(8,128)(2,1)}, u32[]{:S(2)}) copy-start(bf16[2,8,96,768]{3,2,1,0:T(8,128)(2,1)} %get-tuple-element.233) | copy-start | bytes 7077892
  184.5 31.2 %collective-permute-start.16 = (bf16[8,96,768]{2,1,0:T(8,128)(2,1)}, bf16[8,96,768]{2,1,0:T(8,128)(2,1)S(1)}, u32[]{:S(2)}, u32[]{:S(2)}) collective-permute-start(bf16[8,96,768]{2,1,0:T(8,128)(2,1)} %get-tuple-element.372), channel_id=1, source_target_pairs={{0,1},{1,0},{2,3},{3,2},{4,5},{5,4},{6,7},{7,6},{8,9},{9,8},{10,11... | collective-permute-start | bytes 3538952 | tf_op jit(solution)/shard_map/ppermute | solution.py:1509
  202.9 12.8 %copy-start.44 = (bf16[2,8,48,1920]{3,2,1,0:T(8,128)(2,1)S(1)}, bf16[2,8,48,1920]{3,2,1,0:T(8,128)(2,1)}, u32[]{:S(2)}) copy-start(bf16[2,8,48,1920]{3,2,1,0:T(8,128)(2,1)} %get-tuple-element.265) | copy-start | bytes 8847364
  202.9 12.9 %copy-start.8 = (bf16[8,96,768]{2,1,0:T(8,128)(2,1)S(1)}, bf16[8,96,768]{2,1,0:T(8,128)(2,1)}, u32[]{:S(2)}) copy-start(bf16[8,96,768]{2,1,0:T(8,128)(2,1)} %get-tuple-element.371.refs_0_) | copy-start | bytes 3538948
  215.7 12.3 %collective-permute-start.18 = (bf16[2,8,48,1920]{3,2,1,0:T(8,128)(2,1)S(1)}, bf16[2,8,48,1920]{3,2,1,0:T(8,128)(2,1)S(1)}, u32[]{:S(2)}, u32[]{:S(2)}) collective-permute-start(bf16[2,8,48,1920]{3,2,1,0:T(8,128)(2,1)S(1)} %copy-done.44), channel_id=1, source_target_pairs={{0,2},{2,0},{1,3},{3,1},{4,6},{6,4},{5,7},{7,5},{8,10},{10,8},{9,1... | collective-permute-start | bytes 8847368 | tf_op jit(solution)/shard_map/ppermute | solution.py:1756
  216.6 11.4 %copy-start.17 = (bf16[4,96,768]{2,1,0:T(8,128)(2,1)}, bf16[4,96,768]{2,1,0:T(8,128)(2,1)S(1)}, u32[]{:S(2)}) copy-start(bf16[4,96,768]{2,1,0:T(8,128)(2,1)S(1)} %get-tuple-element.285.refs_0_) | copy-start | bytes 1769476
  216.6 15.3 %collective-permute-start.17 = (bf16[4,96,768]{2,1,0:T(8,128)(2,1)S(1)}, bf16[4,96,768]{2,1,0:T(8,128)(2,1)S(1)}, u32[]{:S(2)}, u32[]{:S(2)}) collective-permute-start(bf16[4,96,768]{2,1,0:T(8,128)(2,1)S(1)} %get-tuple-element.259), channel_id=1, source_target_pairs={{0,8},{8,0},{16,24},{24,16},{1,9},{9,1},{17,25},{25,17},{2,10},{10... | collective-permute-start | bytes 1769480 | tf_op jit(solution)/shard_map/ppermute | solution.py:32
  218.2 9.9 %copy-start.31 = (bf16[2,8,48,1920]{3,2,1,0:T(8,128)(2,1)S(1)}, bf16[2,8,48,1920]{3,2,1,0:T(8,128)(2,1)}, u32[]{:S(2)}) copy-start(bf16[2,8,48,1920]{3,2,1,0:T(8,128)(2,1)} %get-tuple-element.264) | copy-start | bytes 8847364
  232.7 3.9 %collective-permute-start.21 = (bf16[2,8,48,1152]{3,2,1,0:T(8,128)(2,1)}, bf16[2,8,48,1152]{3,2,1,0:T(8,128)(2,1)S(1)}, u32[]{:S(2)}, u32[]{:S(2)}) collective-permute-start(bf16[2,8,48,1152]{3,2,1,0:T(8,128)(2,1)} %get-tuple-element.276), channel_id=1, source_target_pairs={{0,2},{2,0},{1,3},{3,1},{4,6},{6,4},{5,7},{7,5},{8,10},{10,8},{9,1... | collective-permute-start | bytes 5308424 | tf_op jit(solution)/shard_map/ppermute | solution.py:1756
  232.8 3.3 collective-permute-start.22
  233.3 23.8 %collective-permute-start.20 = (bf16[2,4,48,1152]{3,2,1,0:T(8,128)(2,1)}, bf16[2,4,48,1152]{3,2,1,0:T(8,128)(2,1)}, u32[]{:S(2)}, u32[]{:S(2)}) collective-permute-start(bf16[2,4,48,1152]{3,2,1,0:T(8,128)(2,1)} %get-tuple-element.267), channel_id=1, source_target_pairs={{0,8},{8,0},{16,24},{24,16},{1,9},{9,1},{17,25},{25,17},{2,10},{10... | collective-permute-start | bytes 2654216 | tf_op jit(solution)/shard_map/ppermute | solution.py:32
  239.6 22.6 %collective-permute-start.23 = (bf16[8,48,1152]{2,1,0:T(8,128)(2,1)}, bf16[8,48,1152]{2,1,0:T(8,128)(2,1)}, u32[]{:S(2)}, u32[]{:S(2)}) collective-permute-start(bf16[8,48,1152]{2,1,0:T(8,128)(2,1)} %get-tuple-element.376), channel_id=1, source_target_pairs={{0,1},{1,0},{2,3},{3,2},{4,5},{5,4},{6,7},{7,6},{8,9},{9,8},{10,11... | collective-permute-start | bytes 2654216 | tf_op jit(solution)/shard_map/ppermute | solution.py:1598
  240.6 16.5 %collective-permute-start.19 = (bf16[2,4,48,768]{3,2,1,0:T(8,128)(2,1)}, bf16[2,4,48,768]{3,2,1,0:T(8,128)(2,1)}, u32[]{:S(2)}, u32[]{:S(2)}) collective-permute-start(bf16[2,4,48,768]{3,2,1,0:T(8,128)(2,1)} %get-tuple-element.266), channel_id=1, source_target_pairs={{0,4},{4,0},{1,5},{5,1},{2,6},{6,2},{3,7},{7,3},{8,12},{12,8},{9,1... | collective-permute-start | bytes 1769480 | tf_op jit(solution)/shard_map/ppermute | solution.py:32
  241.7 20.5 %collective-permute-start.24 = (bf16[2,96,768]{2,1,0:T(8,128)(2,1)S(1)}, bf16[2,96,768]{2,1,0:T(8,128)(2,1)S(1)}, u32[]{:S(2)}, u32[]{:S(2)}) collective-permute-start(bf16[2,96,768]{2,1,0:T(8,128)(2,1)S(1)} %get-tuple-element.287), channel_id=1, source_target_pairs={{0,4},{4,0},{1,5},{5,1},{2,6},{6,2},{3,7},{7,3},{8,12},{12,8},{9,1... | collective-permute-start | bytes 884744 | tf_op jit(solution)/shard_map/ppermute | solution.py:32
  245.8 16.4 %collective-permute-start.25 = (f32[5,768]{1,0:T(8,128)S(1)}, f32[5,768]{1,0:T(8,128)S(1)}, u32[]{:S(2)}, u32[]{:S(2)}) collective-permute-start(f32[5,768]{1,0:T(8,128)S(1)} %add.144), channel_id=1, source_target_pairs={{0,1},{1,0},{2,3},{3,2},{4,5},{5,4},{6,7},{7,6},{8,9},{9,8},{10,11... | collective-permute-start | bytes 46088 | tf_op jit(solution)/shard_map/ppermute | solution.py:32
  247.0 15.3 %copy-start.9 = (bf16[2,4,48,1152]{3,2,1,0:T(8,128)(2,1)S(1)}, bf16[2,4,48,1152]{3,2,1,0:T(8,128)(2,1)}, u32[]{:S(2)}) copy-start(bf16[2,4,48,1152]{3,2,1,0:T(8,128)(2,1)} %get-tuple-element.271.refs_2_) | copy-start | bytes 2654212
  247.0 15.3 %copy-start.12 = (bf16[2,4,48,768]{3,2,1,0:T(8,128)(2,1)S(1)}, bf16[2,4,48,768]{3,2,1,0:T(8,128)(2,1)}, u32[]{:S(2)}) copy-start(bf16[2,4,48,768]{3,2,1,0:T(8,128)(2,1)} %get-tuple-element.270.refs_0_) | copy-start | bytes 1769476
  264.5 21.8 %copy-start.11 = (bf16[512,768]{1,0:T(8,128)(2,1)S(1)}, bf16[512,768]{1,0:T(8,128)(2,1)}, u32[]{:S(2)}) copy-start(bf16[512,768]{1,0:T(8,128)(2,1)} %copy-done.10) | copy-start | bytes 2359300
  264.5 14.5 %collective-permute-start.26 = (bf16[4,48,1152]{2,1,0:T(8,128)(2,1)S(1)}, bf16[4,48,1152]{2,1,0:T(8,128)(2,1)S(1)}, u32[]{:S(2)}, u32[]{:S(2)}) collective-permute-start(bf16[4,48,1152]{2,1,0:T(8,128)(2,1)S(1)} %get-tuple-element.295), channel_id=1, source_target_pairs={{0,8},{8,0},{16,24},{24,16},{1,9},{9,1},{17,25},{25,17},{2,10},{10... | collective-permute-start | bytes 1327112 | tf_op jit(solution)/shard_map/ppermute | solution.py:32
  266.1 12.9 %collective-permute-start.28 = (bf16[2,2,48,1152]{3,2,1,0:T(8,128)(2,1)S(1)}, bf16[2,2,48,1152]{3,2,1,0:T(8,128)(2,1)S(1)}, u32[]{:S(2)}, u32[]{:S(2)}) collective-permute-start(bf16[2,2,48,1152]{3,2,1,0:T(8,128)(2,1)S(1)} %get-tuple-element.297), channel_id=1, source_target_pairs={{0,4},{4,0},{1,5},{5,1},{2,6},{6,2},{3,7},{7,3},{8,12},{12,8},{9,1... | collective-permute-start | bytes 1327112 | tf_op jit(solution)/shard_map/ppermute | solution.py:32
  267.4 10.7 %collective-permute-start.27 = (bf16[4,48,768]{2,1,0:T(8,128)(2,1)S(1)}, bf16[4,48,768]{2,1,0:T(8,128)(2,1)S(1)}, u32[]{:S(2)}, u32[]{:S(2)}) collective-permute-start(bf16[4,48,768]{2,1,0:T(8,128)(2,1)S(1)} %get-tuple-element.296), channel_id=1, source_target_pairs={{0,1},{1,0},{2,3},{3,2},{4,5},{5,4},{6,7},{7,6},{8,9},{9,8},{10,11... | collective-permute-start | bytes 884744 | tf_op jit(solution)/shard_map/ppermute | solution.py:1598
  268.6 9.4 %collective-permute-start.29 = (bf16[1,96,768]{2,1,0:T(8,128)(2,1)S(1)}, bf16[1,96,768]{2,1,0:T(8,128)(2,1)S(1)}, u32[]{:S(2)}, u32[]{:S(2)}) collective-permute-start(bf16[1,96,768]{2,1,0:T(8,128)(2,1)S(1)} %get-tuple-element.298), channel_id=1, source_target_pairs={{0,16},{8,24},{16,0},{24,8},{1,17},{9,25},{17,1},{25,9},{2,18},{10... | collective-permute-start | bytes 442376 | tf_op jit(solution)/shard_map/ppermute | solution.py:32
  271.2 6.4 %collective-permute-start.30 = (f32[5,768]{1,0:T(8,128)S(1)}, f32[5,768]{1,0:T(8,128)S(1)}, u32[]{:S(2)}, u32[]{:S(2)}) collective-permute-start(f32[5,768]{1,0:T(8,128)S(1)} %add.145), channel_id=1, source_target_pairs={{0,4},{4,0},{1,5},{5,1},{2,6},{6,2},{3,7},{7,3},{8,12},{12,8},{9,1... | collective-permute-start | bytes 46088 | tf_op jit(solution)/shard_map/ppermute | solution.py:32
  279.3 12.4 %collective-permute-start.31 = (bf16[2,48,1152]{2,1,0:T(8,128)(2,1)S(1)}, bf16[2,48,1152]{2,1,0:T(8,128)(2,1)S(1)}, u32[]{:S(2)}, u32[]{:S(2)}) collective-permute-start(bf16[2,48,1152]{2,1,0:T(8,128)(2,1)S(1)} %get-tuple-element.308), channel_id=1, source_target_pairs={{0,4},{4,0},{1,5},{5,1},{2,6},{6,2},{3,7},{7,3},{8,12},{12,8},{9,1... | collective-permute-start | bytes 663560 | tf_op jit(solution)/shard_map/ppermute | solution.py:32
  280.9 10.1 %collective-permute-start.32 = (bf16[2,48,768]{2,1,0:T(8,128)(2,1)S(1)}, bf16[2,48,768]{2,1,0:T(8,128)(2,1)S(1)}, u32[]{:S(2)}, u32[]{:S(2)}) collective-permute-start(bf16[2,48,768]{2,1,0:T(8,128)(2,1)S(1)} %get-tuple-element.309), channel_id=1, source_target_pairs={{0,8},{8,0},{16,24},{24,16},{1,9},{9,1},{17,25},{25,17},{2,10},{10... | collective-permute-start | bytes 442376 | tf_op jit(solution)/shard_map/ppermute | solution.py:32
  283.5 8.3 %collective-permute-start.33 = (bf16[2,48,1152]{2,1,0:T(8,128)(2,1)S(1)}, bf16[2,48,1152]{2,1,0:T(8,128)(2,1)S(1)}, u32[]{:S(2)}, u32[]{:S(2)}) collective-permute-start(bf16[2,48,1152]{2,1,0:T(8,128)(2,1)S(1)} %get-tuple-element.310), channel_id=1, source_target_pairs={{0,1},{1,0},{2,3},{3,2},{4,5},{5,4},{6,7},{7,6},{8,9},{9,8},{10,11... | collective-permute-start | bytes 663560 | tf_op jit(solution)/shard_map/ppermute | solution.py:1598
  284.4 7.4 %collective-permute-start.34 = (bf16[1,96,768]{2,1,0:T(8,128)(2,1)S(1)}, bf16[1,96,768]{2,1,0:T(8,128)(2,1)S(1)}, u32[]{:S(2)}, u32[]{:S(2)}) collective-permute-start(bf16[1,96,768]{2,1,0:T(8,128)(2,1)S(1)} %get-tuple-element.311.refs_6_), channel_id=1, source_target_pairs={{0,16},{8,24},{16,0},{24,8},{1,17},{9,25},{17,1},{25,9},{2,18},{10... | collective-permute-start | bytes 442376 | tf_op jit(solution)/shard_map/ppermute | solution.py:32
  286.0 3.9 %collective-permute-start.35 = (f32[5,768]{1,0:T(8,128)S(1)}, f32[5,768]{1,0:T(8,128)S(1)}, u32[]{:S(2)}, u32[]{:S(2)}) collective-permute-start(f32[5,768]{1,0:T(8,128)S(1)} %add.146), channel_id=1, source_target_pairs={{0,8},{8,0},{16,24},{24,16},{1,9},{9,1},{17,25},{25,17},{2,10},{10... | collective-permute-start | bytes 46088 | tf_op jit(solution)/shard_map/ppermute | solution.py:32
  289.8 8.0 %collective-permute-start.37 = (bf16[256,768]{1,0:T(8,128)(2,1)S(1)}, bf16[256,768]{1,0:T(8,128)(2,1)S(1)}, u32[]{:S(2)}, u32[]{:S(2)}) collective-permute-start(bf16[256,768]{1,0:T(8,128)(2,1)S(1)} %get-tuple-element.322), channel_id=1, source_target_pairs={{0,1},{1,0},{2,3},{3,2},{4,5},{5,4},{6,7},{7,6},{8,9},{9,8},{10,11... | collective-permute-start | bytes 1179656 | tf_op jit(solution)/shard_map/ppermute | solution.py:1753
  291.9 13.0 %collective-permute-start.36 = (bf16[1,48,3072]{2,1,0:T(8,128)(2,1)S(1)}, bf16[1,48,3072]{2,1,0:T(8,128)(2,1)S(1)}, u32[]{:S(2)}, u32[]{:S(2)}) collective-permute-start(bf16[1,48,3072]{2,1,0:T(8,128)(2,1)S(1)} %get-tuple-element.320), channel_id=1, source_target_pairs={{0,16},{8,24},{16,0},{24,8},{1,17},{9,25},{17,1},{25,9},{2,18},{10... | collective-permute-start | bytes 884744 | tf_op jit(solution)/shard_map/ppermute | solution.py:32
  292.5 12.7 %collective-permute-start.38 = (bf16[2,96,768]{2,1,0:T(8,128)(2,1)S(1)}, bf16[2,96,768]{2,1,0:T(8,128)(2,1)S(1)}, u32[]{:S(2)}, u32[]{:S(2)}) collective-permute-start(bf16[2,96,768]{2,1,0:T(8,128)(2,1)S(1)} %get-tuple-element.324.refs_2_), channel_id=1, source_target_pairs={{0,8},{8,0},{16,24},{24,16},{1,9},{9,1},{17,25},{25,17},{2,10},{10... | collective-permute-start | bytes 884744 | tf_op jit(solution)/shard_map/ppermute | solution.py:32
  294.2 11.0 %collective-permute-start.39 = (f32[5,768]{1,0:T(8,128)S(1)}, f32[5,768]{1,0:T(8,128)S(1)}, u32[]{:S(2)}, u32[]{:S(2)}) collective-permute-start(f32[5,768]{1,0:T(8,128)S(1)} %add.147), channel_id=1, source_target_pairs={{0,16},{8,24},{16,0},{24,8},{1,17},{9,25},{17,1},{25,9},{2,18},{10... | collective-permute-start | bytes 46088 | tf_op jit(solution)/shard_map/ppermute | solution.py:32
  305.3 14.9 %collective-permute-start.42 = (bf16[4,96,768]{2,1,0:T(8,128)(2,1)S(1)}, bf16[4,96,768]{2,1,0:T(8,128)(2,1)S(1)}, u32[]{:S(2)}, u32[]{:S(2)}) collective-permute-start(bf16[4,96,768]{2,1,0:T(8,128)(2,1)S(1)} %get-tuple-element.331.refs_2_), channel_id=1, source_target_pairs={{0,4},{4,0},{1,5},{5,1},{2,6},{6,2},{3,7},{7,3},{8,12},{12,8},{9,1... | collective-permute-start | bytes 1769480 | tf_op jit(solution)/shard_map/ppermute | solution.py:32
  305.9 9.5 %collective-permute-start.41 = (bf16[256,768]{1,0:T(8,128)(2,1)S(1)}, bf16[256,768]{1,0:T(8,128)(2,1)S(1)}, u32[]{:S(2)}, u32[]{:S(2)}) collective-permute-start(bf16[256,768]{1,0:T(8,128)(2,1)S(1)} %get-tuple-element.329), channel_id=1, source_target_pairs={{0,1},{1,0},{2,3},{3,2},{4,5},{5,4},{6,7},{7,6},{8,9},{9,8},{10,11... | collective-permute-start | bytes 1179656 | tf_op jit(solution)/shard_map/ppermute | solution.py:1753
  307.0 13.3 %collective-permute-start.40 = (bf16[1,48,3072]{2,1,0:T(8,128)(2,1)S(1)}, bf16[1,48,3072]{2,1,0:T(8,128)(2,1)S(1)}, u32[]{:S(2)}, u32[]{:S(2)}) collective-permute-start(bf16[1,48,3072]{2,1,0:T(8,128)(2,1)S(1)} %get-tuple-element.328.refs_0_), channel_id=1, source_target_pairs={{0,16},{8,24},{16,0},{24,8},{1,17},{9,25},{17,1},{25,9},{2,18},{10... | collective-permute-start | bytes 884744 | tf_op jit(solution)/shard_map/ppermute | solution.py:32
  320.3 9.6 %collective-permute-start.45 = (bf16[8,96,768]{2,1,0:T(8,128)(2,1)S(1)}, bf16[8,96,768]{2,1,0:T(8,128)(2,1)S(1)}, u32[]{:S(2)}, u32[]{:S(2)}) collective-permute-start(bf16[8,96,768]{2,1,0:T(8,128)(2,1)S(1)} %get-tuple-element.342.part_ref), channel_id=1, source_target_pairs={{0,2},{2,0},{1,3},{3,1},{4,6},{6,4},{5,7},{7,5},{8,10},{10,8},{9,1... | collective-permute-start | bytes 3538952 | tf_op jit(solution)/shard_map/ppermute | solution.py:1512
  320.4 9.4 %collective-permute-start.43 = (bf16[2,48,1536]{2,1,0:T(8,128)(2,1)S(1)}, bf16[2,48,1536]{2,1,0:T(8,128)(2,1)S(1)}, u32[]{:S(2)}, u32[]{:S(2)}) collective-permute-start(bf16[2,48,1536]{2,1,0:T(8,128)(2,1)S(1)} %get-tuple-element.334.refs_0_), channel_id=1, source_target_pairs={{0,8},{8,0},{16,24},{24,16},{1,9},{9,1},{17,25},{25,17},{2,10},{10... | collective-permute-start | bytes 884744 | tf_op jit(solution)/shard_map/ppermute | solution.py:32
  320.5 9.4 %collective-permute-start.44 = (bf16[2,48,1536]{2,1,0:T(8,128)(2,1)S(1)}, bf16[2,48,1536]{2,1,0:T(8,128)(2,1)S(1)}, u32[]{:S(2)}, u32[]{:S(2)}) collective-permute-start(bf16[2,48,1536]{2,1,0:T(8,128)(2,1)S(1)} %get-tuple-element.335.refs_2_), channel_id=1, source_target_pairs={{0,4},{4,0},{1,5},{5,1},{2,6},{6,2},{3,7},{7,3},{8,12},{12,8},{9,1... | collective-permute-start | bytes 884744 | tf_op jit(solution)/shard_map/ppermute | solution.py:32
  330.0 14.9 %collective-permute-start.46 = (bf16[4,48,1536]{2,1,0:T(8,128)(2,1)S(1)}, bf16[4,48,1536]{2,1,0:T(8,128)(2,1)S(1)}, u32[]{:S(2)}, u32[]{:S(2)}) collective-permute-start(bf16[4,48,1536]{2,1,0:T(8,128)(2,1)S(1)} %get-tuple-element.339.refs_0_), channel_id=1, source_target_pairs={{0,4},{4,0},{1,5},{5,1},{2,6},{6,2},{3,7},{7,3},{8,12},{12,8},{9,1... | collective-permute-start | bytes 1769480 | tf_op jit(solution)/shard_map/ppermute | solution.py:32
  331.6 14.6 %collective-permute-start.47 = (bf16[4,48,1536]{2,1,0:T(8,128)(2,1)S(1)}, bf16[4,48,1536]{2,1,0:T(8,128)(2,1)S(1)}, u32[]{:S(2)}, u32[]{:S(2)}) collective-permute-start(bf16[4,48,1536]{2,1,0:T(8,128)(2,1)S(1)} %get-tuple-element.340.refs_2_), channel_id=1, source_target_pairs={{0,8},{8,0},{16,24},{24,16},{1,9},{9,1},{17,25},{25,17},{2,10},{10... | collective-permute-start | bytes 1769480 | tf_op jit(solution)/shard_map/ppermute | solution.py:32
  346.3 4.6 %collective-permute-start.48 = (bf16[8,48,3072]{2,1,0:T(8,128)(2,1)S(1)}, bf16[8,48,3072]{2,1,0:T(8,128)(2,1)S(1)}, u32[]{:S(2)}, u32[]{:S(2)}) collective-permute-start(bf16[8,48,3072]{2,1,0:T(8,128)(2,1)S(1)} %phase.17.part_ref), channel_id=1, source_target_pairs={{0,2},{2,0},{1,3},{3,1},{4,6},{6,4},{5,7},{7,5},{8,10},{10,8},{9,1... | collective-permute-start | bytes 7077896 | tf_op jit(solution)/shard_map/ppermute | solution.py:1512
  (30 other events, 66.7 us)

commit v4 on v3

--- a/solution.py
+++ b/solution.py
@@ -761,10 +761,17 @@
     lax.fori_loop(0, h1_ref.shape[0] // ROWS_AT_ONCE, part, 0)
 
 
+def weave(seq):
+    i = lax.broadcasted_iota(jnp.int32, (2 * seq, 2 * seq), 0)
+    k = lax.broadcasted_iota(jnp.int32, (2 * seq, 2 * seq), 1)
+    place = jnp.where(k < seq, 2 * k, 2 * (k - seq) + 1)
+    return jnp.where(i == place, 1.0, 0.0).astype(BF16)
+
+
 def mlp_own_body(
-    x_far, o_far, wout_far, gb_ref, wup_far, wdown_far,
-    h1_far, n2_far, g_far, d_far, ho_far,
-    x_ref, o_ref, wout_ref, wup_ref, wdown_ref, h1_ref, n2_ref, ho_ref, g_buf, d_buf, sems,
+    x_far, o_far, wout_far, gb_ref, wup_far, wdown_far, cot_far,
+    h1_far, n2_far, g_far, d_far, ho_far, dm_far,
+    x_ref, o_ref, wout_ref, wup_ref, wdown_ref, h1_ref, n2_ref, ho_ref, cot_ref, dm_ref, g_buf, d_buf, sems,
 ):
     moves = Moves(sems)
     first = [moves.whole(*t) for t in ((o_far, o_ref), (wout_far, wout_ref), (x_far, x_ref))]
@@ -776,6 +783,7 @@
     for j in range(number):
         ups.start(j)
         downs.start(j)
+    cot_there = moves.whole(cot_far, cot_ref)
     h1_ref[...] = dot(o_ref[...], wout_ref[...])
     start_norm(x_ref, h1_ref, n2_ref, gb_ref, ho_ref)
     kept = [moves.whole(*t) for t in ((h1_ref, h1_far), (n2_ref, n2_far))]
@@ -788,6 +796,15 @@
 
     lax.fori_loop(0, number, step, 0)
     kept.append(moves.whole(ho_ref, ho_far))
+    cot_there()
+    rows, seq = cot_ref.shape[0], cot_ref.shape[1] // 2
+    mix = weave(seq)
+    for r in range(rows):
+        parted = dot_tn(mix, cot_ref[r]).astype(BF16)
+        for i in range(2):
+            at = (i * rows + r) * seq
+            dm_ref[at : at + seq] = parted[i * seq : (i + 1) * seq]
+    kept.append(moves.whole(dm_ref, dm_far))
     for wait in kept:
         wait()
     for j in range(number - 2, number):
@@ -855,18 +872,18 @@
     return [(t, FAR) for t in arrays]
 
 
-def mlp_own(x, o, wout, gb, wup, wdown):
+def mlp_own(x, o, wout, gb, wup, wdown, cot):
     n, d = x.shape
     ff = 2 * wup.shape[1]
     h1, low, wide = sds((n, d), F32), sds((n, d), BF16), sds((n, ff), BF16)
     return resident(
         mlp_own_body,
-        far_of(x, o, wout) + [gb] + far_of(wup, wdown),
-        far_of(h1, low, wide, wide, h1),
-        scratch=near_of(x, o, wout, wup, wdown, h1, low, h1)
+        far_of(x, o, wout) + [gb] + far_of(wup, wdown, cot),
+        far_of(h1, low, wide, wide, h1, sds((2 * n, d), BF16)),
+        scratch=near_of(x, o, wout, wup, wdown, h1, low, h1, cot, sds((2 * n, d), BF16))
         + [pltpu.VMEM((2, n, CHUNK), BF16)] * 2
         + [pltpu.SemaphoreType.DMA((40,))],
-        vmem=36,
+        vmem=44,
         name="mlp_own",
     )
 
@@ -885,13 +902,6 @@
         aliases={2: 0, 3: 1},
         name="mlp_other",
     )
-
-
-def weave(seq):
-    i = lax.broadcasted_iota(jnp.int32, (2 * seq, 2 * seq), 0)
-    k = lax.broadcasted_iota(jnp.int32, (2 * seq, 2 * seq), 1)
-    place = jnp.where(k < seq, 2 * k, 2 * (k - seq) + 1)
-    return jnp.where(i == place, 1.0, 0.0).astype(BF16)
 
 
 def after_norm_back(
@@ -913,15 +923,19 @@
         dh1 = db_ref[sl].astype(F32) + norm_back(dn, normal, inverse, gb_ref[1:2])
         dn_ref[sl] = dh1
         dp_ref[sl] = dh1.astype(BF16)
+        at = pl.ds(i * size, size)
+        waits += [moves.whole(a.at[at], b.at[at]) for a, b in ((dn_ref, dh1_far), (dp_ref, dp_far))]
+        if i % 2:
+            both = pl.ds((i - 1) * size, 2 * size)
+            do_ref[both] = dot_nt(dp_ref[both], wout_ref[...]).astype(BF16)
+            waits.append(moves.whole(do_ref.at[both], do_far.at[both]))
     sums_ref[0:1] = gain_sum
     sums_ref[1:2] = bias_sum
-    waits += [moves.whole(dn_ref, dh1_far), moves.whole(dp_ref, dp_far)]
-    do_ref[...] = dot_nt(dp_ref[...], wout_ref[...]).astype(BF16)
-    return waits + [moves.whole(do_ref, do_far)]
-
-
-def mlp_second_body(rows, seq, number_up, number_down, x_far, ho_far, o_far, cot_far, wout_far, gb_ref, *refs):
-    mlp_second_work(rows, seq, x_far, ho_far, o_far, cot_far, wout_far, gb_ref, *in_pieces(refs, number_up, number_down))
+    return waits
+
+
+def mlp_second_body(rows, seq, number_up, number_down, x_far, ho_far, o_far, dm_far, wout_far, gb_ref, *refs):
+    mlp_second_work(rows, seq, x_far, ho_far, o_far, dm_far, wout_far, gb_ref, *in_pieces(refs, number_up, number_down))
 
 
 def in_pieces(refs, *numbers):
@@ -933,36 +947,36 @@
 
 
 def mlp_second_work(
-    rows, seq, x_far, ho_far, o_far, cot_far, wout_far, gb_ref, ups_far, downs_far,
-    outs_far, outs2_far, n2_far, g_far, du_far, dh1_far, dp_far, do_far, sums_ref, dm_far,
+    rows, seq, x_far, ho_far, o_far, dm_far, wout_far, gb_ref, ups_far, downs_far,
+    outs_far, outs2_far, n2_far, g_far, du_far, dh1_far, dp_far, do_far, sums_ref,
     x_ref, ho_ref, o_ref, cot_ref, wout_ref, wup_ref, wdown_ref, n2_ref, dm_ref,
     normal_ref, z_ref, dn_ref, dp_ref, do_ref, inverse_ref, g_buf, du_buf, sems,
 ):
     n = rows * seq
     moves = Moves(sems)
     halves = (slice(0, n), slice(n, 2 * n))
-    cot_there = moves.whole(cot_far, cot_ref)
-    first = [moves.whole(*t) for t in ((o_far, o_ref), (wout_far, wout_ref), (x_far, x_ref))]
+    first = [moves.whole(*t) for t in ((o_far.at[0], o_ref.at[0]), (wout_far, wout_ref))]
     up, down = Weight(moves, ups_far, wup_ref, 1), Weight(moves, downs_far, wdown_ref, 0)
     gs, dus = (Chunks(moves, f, b, 1, True, True) for f, b in ((g_far, g_buf), (du_far, du_buf)))
     number = 2 * up.number
-    mix = weave(seq)
-    cot_there()
-    for r in range(rows):
-        parted = dot_tn(mix, cot_ref[r]).astype(BF16)
-        for i in range(2):
-            dm_ref[i * n + r * seq : i * n + (r + 1) * seq] = parted[i * seq : (i + 1) * seq]
     for wait in first:
         wait()
-    then = moves.whole(ho_far, ho_ref)
+    x_there = moves.whole(x_far, x_ref)
+    then = [moves.whole(*t) for t in ((o_far.at[1], o_ref.at[1]), (ho_far, ho_ref))]
     start_loads(up, down)
+    dm_there = moves.whole(dm_far, dm_ref)
     for i, sl in enumerate(halves):
         if i:
-            then()
+            for wait in then:
+                wait()
         z_ref[sl] = dot(o_ref[i], wout_ref[...])
+        if i == 0:
+            x_there()
         z_at, n2_at, normal_at, inverse_at = (t.at[pl.ds(i * n, n)] for t in (z_ref, n2_ref, normal_ref, inverse_ref))
         start_norm(x_ref if i == 0 else ho_ref, z_at, n2_at, gb_ref, None, normal_at, inverse_at)
-    kept = [moves.whole(*t) for t in ((n2_ref, n2_far), (dm_ref, dm_far))]
+    dm_there()
+    mix = weave(seq)
+    kept = [moves.whole(n2_ref, n2_far)]
     dn_ref[...] = jnp.zeros_like(dn_ref)
 
     def step(j, _):
@@ -1005,7 +1019,7 @@
         dus.wait(j)
 
 
-def mlp_second(x, ho, o2, cot, wout, gb, ups, downs, seq):
+def mlp_second(x, ho, o2, dm, wout, gb, ups, downs, seq):
     n, d = x.shape
     ff = 2 * ups[0].shape[1]
     rows = n // seq
@@ -1013,9 +1027,9 @@
     out = sds((rows // 2, 2 * seq, d), BF16)
     return resident(
         functools.partial(mlp_second_body, rows, seq, len(ups), len(downs)),
-        far_of(x, ho, o2, cot, wout) + [gb] + far_of(*ups, *downs),
-        far_of(out, out, low, wide, wide, full, low, low) + [sds((2, d), F32)] + far_of(low),
-        scratch=near_of(x, ho, o2, cot, wout, sds((d, ff), BF16), sds((ff, d), BF16), low, low, full, full, full, low, low, sds((2 * n, 128), F32))
+        far_of(x, ho, o2, dm, wout) + [gb] + far_of(*ups, *downs),
+        far_of(out, out, low, wide, wide, full, low, low) + [sds((2, d), F32)],
+        scratch=near_of(x, ho, o2, sds((rows, 2 * seq, d), BF16), wout, sds((d, ff), BF16), sds((ff, d), BF16), low, low, full, full, full, low, low, sds((2 * n, 128), F32))
         + [pltpu.VMEM((2, 2 * n, CHUNK), BF16)] * 2
         + [pltpu.SemaphoreType.DMA((64,))],
         vmem=60,
@@ -1776,16 +1790,16 @@
     normal, _ = norm_stats(x.astype(F32))
     a_e = (normal * gb[0] + gb[2]).astype(BF16)
     first = attend_first(a_e, link.own[0], incl)
-    (a_e, first, cot), wq_own, fetched, wqkv, join_out, pieces_of = link.fetch((a_e, first, cot))
+    (a_e, first, cot, me, me_z), wq_own, fetched, wqkv, join_out, pieces_of = link.fetch((a_e, first, cot, me, me_z))
     second = attend_first(a_e, fetched, incl)
     qkv_e, o1 = (jnp.concatenate([s, t], axis=-1) for s, t in zip(first[:2], second[:2]))
     lse1 = jnp.concatenate([first[2], second[2]], axis=0).reshape(-1, GROUP // HD, n)
     (qkv_e, o1, lse1, wqkv), wout = join_out(qkv_e, o1, lse1, wqkv)
-    h1, n2_1, g1, d1, part_one = mlp_own(x, o1, wout, gb, link.own[2], link.own[3])
+    h1, n2_1, g1, d1, part_one, dm2 = mlp_own(x, o1, wout, gb, link.own[2], link.own[3], cot)
     ups, downs, (n2_1, part_one) = pieces_of(n2_1, part_one)
     g1, d1, ho, a_o = mlp_other(n2_1, part_one, g1, d1, gb, ups[1:], downs[1:])
     qkv_o, o2, lse2 = attend_second(a_o, wqkv, incl, strict, qkv_e, o1, lse1)
-    out, out_two, n2_2, g2, du2, dh1_2, dp2, do2, sums2, dm2 = mlp_second(x, ho, o2, cot, wout, gb, ups, downs, seq)
+    out, out_two, n2_2, g2, du2, dh1_2, dp2, do2, sums2 = mlp_second(x, ho, o2, dm2, wout, gb, ups, downs, seq)
     out_got = link.partner(out)
     dqkv_o, part, dy, sums_o = attend_back(wqkv, incl, strict, qkv_e, qkv_o, o2, lse2, do2, dh1_2, ho, gb)
     o2_flat = o2.reshape(2 * n, width)

time: 361 us -> 359 us (level)
  transfers between devices with their start and end apart: 49 -> 49, of which waited for: 28 -> 29; matrix products, arithmetic and copies ran while one was open for 10% -> 10% of each run, Pallas kernels for 30% -> 31%
where the time goes in v4:
time: 359 us; the launch traced here: 352 us
  Pallas kernels  171 us (48%)
  waiting for transfers between devices  84.4 us (24%)
  starting transfers between devices  48.6 us (14%)
  other arithmetic  27.7 us (8%)
  local copies, waits for them, and re-layouts  18.8 us (5%)
    pallas_call x23, Pallas kernels, resident(): pl.pallas_call(body, in_specs=[s for _, s in ins], out_specs=[s for _, s...  167 us
    ppermute x23, waiting for transfers between devices, flip_bit(): return lax.ppermute(array, axis, [(i, i ^ bit) for i in range(size)])  51.7 us
    ppermute x23, starting transfers between devices, flip_bit(): return lax.ppermute(array, axis, [(i, i ^ bit) for i in range(size)])  30.2 us
    ppermute x9, waiting for transfers between devices, partner(): return lax.ppermute(t, 'tensor', FLIP)  19.8 us
    ppermute x9, starting transfers between devices, partner(): return lax.ppermute(t, 'tensor', FLIP)  10.7 us
    another operation x11, other arithmetic, ordered(): jnp.stack([jnp.where(first, mine, theirs), jnp.where(first, theirs, mine)])  7.45 us
  transfers between devices with their start and end apart: 49, of which 29 were waited for; matrix products, arithmetic and copies ran while one was open for 10% of the time, Pallas kernels for 31%

profile of v4, /device:TPU:0, one launch (start us, length us, event | category | flops | bytes accessed | tf_op | source)
XLA Modules:
  0.0 352.3 jit_solution(15842369880751315520)
XLA Ops:
  0.7 2.0 constant_dynamic-slice_fusion.7
  2.8 3.0 collective-permute-start
  5.8 1.3 convert_reduce_fusion
  9.2 1.6 add_convert_fusion.3.a_ref.ae_far
  11.9 2.4 attend_first.2
  16.7 1.2 constant_dynamic-slice_fusion.4.cot_far
  18.0 1.5 collective-permute-start.1
  19.5 1.9 constant_dynamic-slice_fusion.2
  22.9 1.6 collective-permute-start.2
  24.5 5.5 %collective-permute-done.1 = bf16[576,384]{1,0:T(8,128)(2,1)} collective-permute-done((bf16[576,384]{1,0:T(8,128)(2,1)}, bf16[576,384]{1,0:T(8,128)(2,1)}, u32[]{:S(2)}, u32[]{:S(2)}) %collective-permute-start.1) | collective-permute-done | bytes 442400 | tf_op jit(solution)/shard_map/ppermute | solution.py:1734
  29.9 1.2 select_bitcast_fusion.5
  32.2 7.2 %collective-permute-done.2 = bf16[96,768]{1,0:T(8,128)(2,1)} collective-permute-done((bf16[96,768]{1,0:T(8,128)(2,1)S(1)}, bf16[96,768]{1,0:T(8,128)(2,1)}, u32[]{:S(2)}, u32[]{:S(2)}) %collective-permute-start.2) | collective-permute-done | bytes 147488 | tf_op jit(solution)/shard_map/ppermute | solution.py:1767
  42.2 1.6 select_bitcast_fusion.1
  44.0 1.3 copy-done.7
  45.3 2.1 pad_maximum_fusion.w_far
  47.3 2.4 attend_first.3
  49.8 1.6 pad_maximum_fusion.2.qkve_far
  56.4 10.0 %mlp_own.1 = (f32[512,768]{1,0:T(8,128)}, bf16[512,768]{1,0:T(8,128)(2,1)}, bf16[512,3072]{1,0:T(8,128)(2,1)}, bf16[512,3072]{1,0:T(8,128)(2,1)}, f32[512,768]{1,0:T(8,128)}, /*index=5*/bf16[1024,768]{1,0:T(8,128)(2,1)}) custom-call(bf16[512,768]{1,0:T(8,128)(2,1)} %bitcast.59, bf16[512,768]{1,0:T(8,128)(2,1)} %pad_maximum_fusion.10.o_far.o1_far, ...), custom_call_target="tpu_custom_call" | custom-call | tf_op jit(solution)/shard_map/mlp_own/pallas_call | solution.py:112
  66.4 2.9 collective-permute-done.5.refs_4_.refs_6_
  69.9 2.8 collective-permute-done.9.refs_2_.refs_3_
  75.1 8.4 %mlp_other.1 = (bf16[512,3072]{1,0:T(8,128)(2,1)}, bf16[512,3072]{1,0:T(8,128)(2,1)}, f32[512,768]{1,0:T(8,128)}, bf16[512,768]{1,0:T(8,128)(2,1)}) custom-call(bf16[512,768]{1,0:T(8,128)(2,1)} %get-tuple-element.209.n2_far.n1_far, f32[512,768]{1,0:T(8,128)} %get-tuple-element.210.part_far, ...), custom_call_target="tpu_custom_call", output_to_operand_aliasing={{0}: (2, {}), {1}: (3, {})} | custom-call | tf_op jit(solution)/shard_map/mlp_other/pallas_call | solution.py:112
  83.6 13.6 %attend_second.1 = (bf16[3,512,768]{2,1,0:T(8,128)(2,1)}, bf16[2,512,768]{2,1,0:T(8,128)(2,1)}, f32[2,3,4,512]{3,2,1,0:T(4,128)S(1)}) custom-call(bf16[512,768]{1,0:T(8,128)(2,1)} %get-tuple-element.215.a_far.ao_far, bf16[3,768,768]{2,1,0:T(8,128)(2,1)} %pad_maximum_fusion.w_far, f32[2,256,256]{2,1,0:T(8,128)} %copy-done.2, ...), custom_call_target="tpu_custom_call" | custom-call | flops 415236096 | tf_op jit(solution)/shard_map/attend_second/pallas_call | solution.py:112
  97.2 34.7 %mlp_second.1 = (bf16[1,512,768]{2,1,0:T(8,128)(2,1)}, bf16[1,512,768]{2,1,0:T(8,128)(2,1)}, bf16[1024,768]{1,0:T(8,128)(2,1)}, bf16[1024,3072]{1,0:T(8,128)(2,1...) custom-call(bf16[512,768]{1,0:T(8,128)(2,1)} %bitcast.60, ...), custom_call_target="tpu_custom_call" | custom-call | tf_op jit(solution)/shard_map/mlp_second/pallas_call | solution.py:112
  133.0 18.9 %attend_back.1 = (bf16[3,512,768]{2,1,0:T(8,128)(2,1)}, bf16[3,512,768]{2,1,0:T(8,128)(2,1)}, f32[512,768]{1,0:T(8,128)}, f32[3,768]{1,0:T(4,128)S(1)}) custom-call(bf16[3,768,768]{2,1,0:T(8,128)(2,1)} %pad_maximum_fusion.w_far, f32[2,256,256]{2,1,0:T(8,128)} %copy-done.2, f32[2,256,256]{2,1,0:T(8,128)} %get-tuple-element.402.strict_far, ...), custom_call_target="tpu_custom_call" | custom-call | flops 868220928 | tf_op jit(solution)/shard_map/attend_back/pallas_call | solution.py:112
  153.1 14.1 %grad_down.1 = (bf16[2,8,96,768]{3,2,1,0:T(8,128)(2,1)}, bf16[2,8,96,768]{3,2,1,0:T(8,128)(2,1)}) custom-call(s32[2]{0:T(128)S(1)} %copy-done.21, bf16[512,3072]{1,0:T(8,128)(2,1)} %get-tuple-element.216.g1_far, bf16[1024,3072]{1,0:T(8,128)(2,1)} %get-tuple-element.223.g2_far, f32[512,768]{1,0:T(8,128)} %get-tuple-element.238.dy_far, ...), custom_call_target="tpu_custom_call" | custom-call | flops 452984832 | tf_op jit(solution)/shard_map/grad_down/pallas_call | solution.py:112
  168.4 13.2 %mlp_back.1 = (bf16[512,3072]{1,0:T(8,128)(2,1)}, f32[512,768]{1,0:T(8,128)}, bf16[512,768]{1,0:T(8,128)(2,1)}, bf16[512,768]{1,0:T(8,128)(2,1)}, f32[2,768]{1,0:T(2,128)S(1)}) custom-call(f32[512,768]{1,0:T(8,128)} %get-tuple-element.238.dy_far, f32[512,768]{1,0:T(8,128)} %get-tuple-element.239.h1_far, bf16[768,768]{1,0:T(8,128)(2,1)} %pad_maximum_fusion.8.wout_far, ...), custom_call_target="tpu_custom_call" | custom-call | tf_op jit(solution)/shard_map/mlp_back/pallas_call | solution.py:112
  183.6 16.7 %grad_up.1 = (bf16[2,8,48,1920]{3,2,1,0:T(8,128)(2,1)}, bf16[2,8,48,1920]{3,2,1,0:T(8,128)(2,1)}) custom-call(s32[3]{0:T(128)} %pad_add_fusion.me_ref, bf16[512,768]{1,0:T(8,128)(2,1)} %get-tuple-element.209.n2_far.n1_far, bf16[1024,768]{1,0:T(8,128)(2,1)} %get-tuple-element.248.n2_far, bf16[512,3072]{1,0:T(8,128)(2,1)} %get-tuple-element.250.du1_far, ...), custom_call_target="tpu_custom_call" | custom-call | flops 566231040 | tf_op jit(solution)/shard_map/grad_up/pallas_call | solution.py:112
  200.4 12.8 %attend_back_even.1 = (bf16[3,512,768]{2,1,0:T(8,128)(2,1)}, bf16[512,768]{1,0:T(8,128)(2,1)S(1)}, f32[2,768]{1,0:T(2,128)S(1)}) custom-call(bf16[3,768,768]{2,1,0:T(8,128)(2,1)} %pad_maximum_fusion.w_far, f32[2,256,256]{2,1,0:T(8,128)} %copy-done.2, bf16[3,512,768]{2,1,0:T(8,128)(2,1)} %pad_maximum_fusion.2.qkve_far, ...), custom_call_target="tpu_custom_call" | custom-call | flops 364904448 | tf_op jit(solution)/shard_map/attend_back_even/pallas_call | solution.py:112
  214.1 1.6 collective-permute-start.17
  215.6 9.8 %grad_qkv.1 = (bf16[2,8,48,1152]{3,2,1,0:T(8,128)(2,1)}, bf16[2,8,48,1152]{3,2,1,0:T(8,128)(2,1)}) custom-call(s32[2]{0:T(128)S(1)} %copy-done.21, bf16[512,768]{1,0:T(8,128)(2,1)} %copy-done.4, bf16[512,768]{1,0:T(8,128)(2,1)} %get-tuple-element.215.a_far.ao_far, bf16[3,512,768]{2,1,0:T(8,128)(2,1)} %get-tuple-element.264.de_far, ...), custom_call_target="tpu_custom_call" | custom-call | flops 226492416 | tf_op jit(solution)/shard_map/grad_qkv/pallas_call | solution.py:112
  227.3 1.3 fusion.5
  230.8 1.6 collective-permute-start.20
  234.2 1.9 add_convert_fusion.2
  238.2 1.5 collective-permute-start.19
  241.5 2.0 broadcast_select_fusion.1
  244.6 1.9 pad_maximum_fusion.1
  246.5 8.3 %collective-permute-done.19.refs_1_ = bf16[2,4,48,768]{3,2,1,0:T(8,128)(2,1)} collective-permute-done((bf16[2,4,48,768]{3,2,1,0:T(8,128)(2,1)}, bf16[2,4,48,768]{3,2,1,0:T(8,128)(2,1)}, u32[]{:S(2)}, u32[]{:S(2)}) %collective-permute-start.19) | collective-permute-done | bytes 589856 | tf_op jit(solution)/shard_map/ppermute | solution.py:32
  254.8 5.1 %collective-permute-done.24.refs_7_ = bf16[2,96,768]{2,1,0:T(8,128)(2,1)S(1)} collective-permute-done((bf16[2,96,768]{2,1,0:T(8,128)(2,1)S(1)}, bf16[2,96,768]{2,1,0:T(8,128)(2,1)S(1)}, u32[]{:S(2)}, u32[]{:S(2)}) %collective-permute-start.24) | collective-permute-done | bytes 294944 | tf_op jit(solution)/shard_map/ppermute | solution.py:32
  259.9 2.2 phase.11
  262.1 1.7 collective-permute-start.26
  263.8 1.5 collective-permute-start.28
  266.1 2.6 collective-permute-start.29
  269.4 5.9 %collective-permute-done.30 = f32[5,768]{1,0:T(8,128)S(1)} collective-permute-done((f32[5,768]{1,0:T(8,128)S(1)}, f32[5,768]{1,0:T(8,128)S(1)}, u32[]{:S(2)}, u32[]{:S(2)}) %collective-permute-start.30) | collective-permute-done | bytes 15392 | tf_op jit(solution)/shard_map/ppermute | solution.py:32
  276.9 1.5 collective-permute-start.31
  278.4 2.6 collective-permute-start.32
  282.1 1.6 collective-permute-start.34
  284.1 3.4 collective-permute-done.35
  290.2 2.3 collective-permute-start.38
  293.2 2.5 collective-permute-done.37
  295.7 7.0 %collective-permute-done.36.refs_1_ = bf16[1,48,3072]{2,1,0:T(8,128)(2,1)S(1)} collective-permute-done((bf16[1,48,3072]{2,1,0:T(8,128)(2,1)S(1)}, bf16[1,48,3072]{2,1,0:T(8,128)(2,1)S(1)}, u32[]{:S(2)}, u32[]{:S(2)}) %collective-permute-start.36) | collective-permute-done | bytes 294944 | tf_op jit(solution)/shard_map/ppermute | solution.py:32
  304.5 1.3 collective-permute-start.40
  305.8 7.3 %collective-permute-done.41 = bf16[256,768]{1,0:T(8,128)(2,1)S(1)} collective-permute-done((bf16[256,768]{1,0:T(8,128)(2,1)S(1)}, bf16[256,768]{1,0:T(8,128)(2,1)S(1)}, u32[]{:S(2)}, u32[]{:S(2)}) %collective-permute-start.41) | collective-permute-done | bytes 393248 | tf_op jit(solution)/shard_map/ppermute | solution.py:1767
  313.1 4.9 %collective-permute-done.40.refs_1_ = bf16[1,48,3072]{2,1,0:T(8,128)(2,1)S(1)} collective-permute-done((bf16[1,48,3072]{2,1,0:T(8,128)(2,1)S(1)}, bf16[1,48,3072]{2,1,0:T(8,128)(2,1)S(1)}, u32[]{:S(2)}, u32[]{:S(2)}) %collective-permute-start.40) | collective-permute-done | bytes 294944 | tf_op jit(solution)/shard_map/ppermute | solution.py:32
  318.3 1.7 collective-permute-start.44
  320.7 7.0 %collective-permute-done.43.refs_1_ = bf16[2,48,1536]{2,1,0:T(8,128)(2,1)S(1)} collective-permute-done((bf16[2,48,1536]{2,1,0:T(8,128)(2,1)S(1)}, bf16[2,48,1536]{2,1,0:T(8,128)(2,1)S(1)}, u32[]{:S(2)}, u32[]{:S(2)}) %collective-permute-start.43) | collective-permute-done | bytes 294944 | tf_op jit(solution)/shard_map/ppermute | solution.py:32
  327.8 1.7 collective-permute-start.46
  329.5 1.7 collective-permute-start.47
  332.1 1.9 convert.1
  334.0 2.1 unpack_down.2.refs_0_
  336.2 2.1 unpack_down.3
  338.3 4.5 %collective-permute-done.46.refs_1_ = bf16[4,48,1536]{2,1,0:T(8,128)(2,1)S(1)} collective-permute-done((bf16[4,48,1536]{2,1,0:T(8,128)(2,1)S(1)}, bf16[4,48,1536]{2,1,0:T(8,128)(2,1)S(1)}, u32[]{:S(2)}, u32[]{:S(2)}) %collective-permute-start.46) | collective-permute-done | bytes 589856 | tf_op jit(solution)/shard_map/ppermute | solution.py:32
  342.7 1.4 collective-permute-done.47.refs_3_
  344.7 2.9 unpack_rest.2
  348.9 2.9 unpack_rest.3
  (212 shorter events, 49.6 us)
Async XLA Ops:
  0.6 16.1 %copy-start = (bf16[4,512,768]{2,1,0:T(8,128)(2,1)S(1)}, bf16[4,512,768]{2,1,0:T(8,128)(2,1)}, u32[]{:S(2)}) copy-start(bf16[4,512,768]{2,1,0:T(8,128)(2,1)} %param.19) | copy-start | bytes 9437188
  0.7 8.4 %copy-start.37 = (f32[2,768]{1,0:T(2,128)S(1)}, f32[2,768]{1,0:T(2,128)}, u32[]{:S(2)}) copy-start(f32[2,768]{1,0:T(2,128)} %param.18) | copy-start | bytes 18436
  2.8 15.2 %collective-permute-start = (bf16[576,384]{1,0:T(8,128)(2,1)}, bf16[576,384]{1,0:T(8,128)(2,1)}, u32[]{:S(2)}, u32[]{:S(2)}) collective-permute-start(bf16[576,384]{1,0:T(8,128)(2,1)} %constant_dynamic-slice_fusion.7), channel_id=1, source_target_pairs={{0,1},{1,0},{2,3},{3,2},{4,5},{5,4},{6,7},{7,6},{8,9},{9,8},{10,11... | collective-permute-start | bytes 1327112 | tf_op jit(solution)/shard_map/ppermute | solution.py:1767
  18.0 11.9 %collective-permute-start.1 = (bf16[576,384]{1,0:T(8,128)(2,1)}, bf16[576,384]{1,0:T(8,128)(2,1)}, u32[]{:S(2)}, u32[]{:S(2)}) collective-permute-start(bf16[576,384]{1,0:T(8,128)(2,1)} %collective-permute-done), channel_id=1, source_target_pairs={{0,4},{4,0},{1,5},{5,1},{2,6},{6,2},{3,7},{7,3},{8,12},{12,8},{9,1... | collective-permute-start | bytes 1327112 | tf_op jit(solution)/shard_map/ppermute | solution.py:1734
  21.4 18.0 %collective-permute-start.3 = (bf16[768,384]{1,0:T(8,128)(2,1)}, bf16[768,384]{1,0:T(8,128)(2,1)S(1)}, u32[]{:S(2)}, u32[]{:S(2)}) collective-permute-start(bf16[768,384]{1,0:T(8,128)(2,1)} %constant_dynamic-slice_fusion.2), channel_id=1, source_target_pairs={{0,1},{1,0},{2,3},{3,2},{4,5},{5,4},{6,7},{7,6},{8,9},{9,8},{10,11... | collective-permute-start | bytes 1769480 | tf_op jit(solution)/shard_map/ppermute | solution.py:1767
  22.9 16.5 %collective-permute-start.2 = (bf16[96,768]{1,0:T(8,128)(2,1)S(1)}, bf16[96,768]{1,0:T(8,128)(2,1)}, u32[]{:S(2)}, u32[]{:S(2)}) collective-permute-start(bf16[96,768]{1,0:T(8,128)(2,1)S(1)} %constant_dynamic-slice_fusion.3), channel_id=1, source_target_pairs={{0,1},{1,0},{2,3},{3,2},{4,5},{5,4},{6,7},{7,6},{8,9},{9,8},{10,11... | collective-permute-start | bytes 442376 | tf_op jit(solution)/shard_map/ppermute | solution.py:1767
  24.5 15.0 %copy-start.22 = (bf16[1536,768]{1,0:T(8,128)(2,1)S(1)}, bf16[1536,768]{1,0:T(8,128)(2,1)}, u32[]{:S(2)}) copy-start(bf16[1536,768]{1,0:T(8,128)(2,1)} %refs_5_.3) | copy-start | bytes 7077892
  39.4 2.8 collective-permute-start.6
  40.6 28.6 %collective-permute-start.5 = (bf16[768,768]{1,0:T(8,128)(2,1)}, bf16[768,768]{1,0:T(8,128)(2,1)}, u32[]{:S(2)}, u32[]{:S(2)}) collective-permute-start(bf16[768,768]{1,0:T(8,128)(2,1)} %pad_maximum_fusion.7), channel_id=1, source_target_pairs={{0,1},{1,0},{2,3},{3,2},{4,5},{5,4},{6,7},{7,6},{8,9},{9,8},{10,11... | collective-permute-start | bytes 3538952 | tf_op jit(solution)/shard_map/ppermute | solution.py:1767
  41.2 11.2 %collective-permute-start.7 = (bf16[96,768]{1,0:T(8,128)(2,1)}, bf16[96,768]{1,0:T(8,128)(2,1)}, u32[]{:S(2)}, u32[]{:S(2)}) collective-permute-start(bf16[96,768]{1,0:T(8,128)(2,1)} %collective-permute-done.2), channel_id=1, source_target_pairs={{0,4},{4,0},{1,5},{5,1},{2,6},{6,2},{3,7},{7,3},{8,12},{12,8},{9,1... | collective-permute-start | bytes 442376 | tf_op jit(solution)/shard_map/ppermute | solution.py:1734
  53.5 1.6 collective-permute-start.8
  53.7 15.7 %collective-permute-start.4 = (bf16[768,384]{1,0:T(8,128)(2,1)S(1)}, bf16[768,384]{1,0:T(8,128)(2,1)S(1)}, u32[]{:S(2)}, u32[]{:S(2)}) collective-permute-start(bf16[768,384]{1,0:T(8,128)(2,1)S(1)} %copy-done.26), channel_id=1, source_target_pairs={{0,4},{4,0},{1,5},{5,1},{2,6},{6,2},{3,7},{7,3},{8,12},{12,8},{9,1... | collective-permute-start | bytes 1769480 | tf_op jit(solution)/shard_map/ppermute | solution.py:1734
  54.7 19.4 %copy-start.12 = (f32[5,768]{1,0:T(8,128)}, f32[5,768]{1,0:T(8,128)S(1)}, u32[]{:S(2)}) copy-start(f32[5,768]{1,0:T(8,128)S(1)} %pad_maximum_fusion.14.gb_ref) | copy-start | bytes 46084
  69.4 4.7 %collective-permute-start.11 = (bf16[768,768]{1,0:T(8,128)(2,1)}, bf16[768,768]{1,0:T(8,128)(2,1)S(1)}, u32[]{:S(2)}, u32[]{:S(2)}) collective-permute-start(bf16[768,768]{1,0:T(8,128)(2,1)} %collective-permute-done.5.refs_4_.refs_6_), channel_id=1, source_target_pairs={{0,2},{2,0},{1,3},{3,1},{4,6},{6,4},{5,7},{7,5},{8,10},{10,8},{9,1... | collective-permute-start | bytes 3538952 | tf_op jit(solution)/shard_map/ppermute | solution.py:1770
  69.4 3.3 collective-permute-start.9
  69.9 4.0 %collective-permute-start.10 = (bf16[768,384]{1,0:T(8,128)(2,1)S(1)}, bf16[768,384]{1,0:T(8,128)(2,1)S(1)}, u32[]{:S(2)}, u32[]{:S(2)}) collective-permute-start(bf16[768,384]{1,0:T(8,128)(2,1)S(1)} %collective-permute-done.4.refs_1_.refs_2_), channel_id=1, source_target_pairs={{0,2},{2,0},{1,3},{3,1},{4,6},{6,4},{5,7},{7,5},{8,10},{10,8},{9,1... | collective-permute-start | bytes 1769480 | tf_op jit(solution)/shard_map/ppermute | solution.py:1770
  97.2 35.8 %copy-start.13 = (f32[5,768]{1,0:T(8,128)S(1)}, f32[5,768]{1,0:T(8,128)}, u32[]{:S(2)}) copy-start(f32[5,768]{1,0:T(8,128)} %copy-done.12) | copy-start | bytes 46084
  131.9 20.1 %collective-permute-start.12 = (bf16[1,512,768]{2,1,0:T(8,128)(2,1)}, bf16[1,512,768]{2,1,0:T(8,128)(2,1)S(1)}, u32[]{:S(2)}, u32[]{:S(2)}) collective-permute-start(bf16[1,512,768]{2,1,0:T(8,128)(2,1)} %get-tuple-element.224), channel_id=1, source_target_pairs={{0,1},{1,0},{2,3},{3,2},{4,5},{5,4},{6,7},{7,6},{8,9},{9,8},{10,11... | collective-permute-start | bytes 2359304 | tf_op jit(solution)/shard_map/ppermute | solution.py:1767
  133.0 18.9 %copy-start.30 = (bf16[1,512,768]{2,1,0:T(8,128)(2,1)S(1)}, bf16[1,512,768]{2,1,0:T(8,128)(2,1)}, u32[]{:S(2)}) copy-start(bf16[1,512,768]{2,1,0:T(8,128)(2,1)} %get-tuple-element.233) | copy-start | bytes 2359300
  133.0 20.1 %copy-start.21 = (s32[2]{0:T(128)S(1)}, s32[2]{0:T(128)}, u32[]{:S(2)}) copy-start(s32[2]{0:T(128)} %rev.3.me_ref) | copy-start | bytes 28
  152.0 15.2 %copy-start.35 = (bf16[1,512,768]{2,1,0:T(8,128)(2,1)}, bf16[1,512,768]{2,1,0:T(8,128)(2,1)S(1)}, u32[]{:S(2)}) copy-start(bf16[1,512,768]{2,1,0:T(8,128)(2,1)S(1)} %collective-permute-done.12) | copy-start | bytes 2359300
  152.0 15.2 %collective-permute-start.13 = (bf16[1,256,768]{2,1,0:T(8,128)(2,1)S(1)}, bf16[1,256,768]{2,1,0:T(8,128)(2,1)S(1)}, u32[]{:S(2)}, u32[]{:S(2)}) collective-permute-start(bf16[1,256,768]{2,1,0:T(8,128)(2,1)S(1)} %get-tuple-element.235), channel_id=1, source_target_pairs={{0,1},{1,0},{2,3},{3,2},{4,5},{5,4},{6,7},{7,6},{8,9},{9,8},{10,11... | collective-permute-start | bytes 1179656 | tf_op jit(solution)/shard_map/ppermute | solution.py:1767
  167.2 14.5 %collective-permute-start.14 = (bf16[2,8,96,768]{3,2,1,0:T(8,128)(2,1)}, bf16[2,8,96,768]{3,2,1,0:T(8,128)(2,1)S(1)}, u32[]{:S(2)}, u32[]{:S(2)}) collective-permute-start(bf16[2,8,96,768]{3,2,1,0:T(8,128)(2,1)} %get-tuple-element.237), channel_id=1, source_target_pairs={{0,2},{2,0},{1,3},{3,1},{4,6},{6,4},{5,7},{7,5},{8,10},{10,8},{9,1... | collective-permute-start | bytes 7077896 | tf_op jit(solution)/shard_map/ppermute | solution.py:1770
  167.3 14.4 %collective-permute-start.15 = (bf16[1,256,768]{2,1,0:T(8,128)(2,1)S(1)}, bf16[1,256,768]{2,1,0:T(8,128)(2,1)S(1)}, u32[]{:S(2)}, u32[]{:S(2)}) collective-permute-start(bf16[1,256,768]{2,1,0:T(8,128)(2,1)S(1)} %get-tuple-element.244), channel_id=1, source_target_pairs={{0,1},{1,0},{2,3},{3,2},{4,5},{5,4},{6,7},{7,6},{8,9},{9,8},{10,11... | collective-permute-start | bytes 1179656 | tf_op jit(solution)/shard_map/ppermute | solution.py:1767
  168.4 13.3 %copy-start.32 = (bf16[2,8,96,768]{3,2,1,0:T(8,128)(2,1)S(1)}, bf16[2,8,96,768]{3,2,1,0:T(8,128)(2,1)}, u32[]{:S(2)}) copy-start(bf16[2,8,96,768]{3,2,1,0:T(8,128)(2,1)} %get-tuple-element.236) | copy-start | bytes 7077892
  182.6 30.6 %collective-permute-start.16 = (bf16[8,96,768]{2,1,0:T(8,128)(2,1)S(1)}, bf16[8,96,768]{2,1,0:T(8,128)(2,1)S(1)}, u32[]{:S(2)}, u32[]{:S(2)}) collective-permute-start(bf16[8,96,768]{2,1,0:T(8,128)(2,1)S(1)} %get-tuple-element.376), channel_id=1, source_target_pairs={{0,1},{1,0},{2,3},{3,2},{4,5},{5,4},{6,7},{7,6},{8,9},{9,8},{10,11... | collective-permute-start | bytes 3538952 | tf_op jit(solution)/shard_map/ppermute | solution.py:1523
  200.3 12.8 %copy-start.44 = (bf16[2,8,48,1920]{3,2,1,0:T(8,128)(2,1)S(1)}, bf16[2,8,48,1920]{3,2,1,0:T(8,128)(2,1)}, u32[]{:S(2)}) copy-start(bf16[2,8,48,1920]{3,2,1,0:T(8,128)(2,1)} %get-tuple-element.269) | copy-start | bytes 8847364
  213.2 12.3 %collective-permute-start.18 = (bf16[2,8,48,1920]{3,2,1,0:T(8,128)(2,1)S(1)}, bf16[2,8,48,1920]{3,2,1,0:T(8,128)(2,1)S(1)}, u32[]{:S(2)}, u32[]{:S(2)}) collective-permute-start(bf16[2,8,48,1920]{3,2,1,0:T(8,128)(2,1)S(1)} %copy-done.44), channel_id=1, source_target_pairs={{0,2},{2,0},{1,3},{3,1},{4,6},{6,4},{5,7},{7,5},{8,10},{10,8},{9,1... | collective-permute-start | bytes 8847368 | tf_op jit(solution)/shard_map/ppermute | solution.py:1770
  214.1 11.4 %copy-start.16 = (bf16[4,96,768]{2,1,0:T(8,128)(2,1)}, bf16[4,96,768]{2,1,0:T(8,128)(2,1)S(1)}, u32[]{:S(2)}) copy-start(bf16[4,96,768]{2,1,0:T(8,128)(2,1)S(1)} %get-tuple-element.289.refs_0_) | copy-start | bytes 1769476
  214.1 15.3 %collective-permute-start.17 = (bf16[4,96,768]{2,1,0:T(8,128)(2,1)S(1)}, bf16[4,96,768]{2,1,0:T(8,128)(2,1)S(1)}, u32[]{:S(2)}, u32[]{:S(2)}) collective-permute-start(bf16[4,96,768]{2,1,0:T(8,128)(2,1)S(1)} %get-tuple-element.263), channel_id=1, source_target_pairs={{0,8},{8,0},{16,24},{24,16},{1,9},{9,1},{17,25},{25,17},{2,10},{10... | collective-permute-start | bytes 1769480 | tf_op jit(solution)/shard_map/ppermute | solution.py:32
  215.6 9.8 %copy-start.31 = (bf16[2,8,48,1920]{3,2,1,0:T(8,128)(2,1)S(1)}, bf16[2,8,48,1920]{3,2,1,0:T(8,128)(2,1)}, u32[]{:S(2)}) copy-start(bf16[2,8,48,1920]{3,2,1,0:T(8,128)(2,1)} %get-tuple-element.268) | copy-start | bytes 8847364
  230.2 4.1 %collective-permute-start.21 = (bf16[2,8,48,1152]{3,2,1,0:T(8,128)(2,1)}, bf16[2,8,48,1152]{3,2,1,0:T(8,128)(2,1)}, u32[]{:S(2)}, u32[]{:S(2)}) collective-permute-start(bf16[2,8,48,1152]{3,2,1,0:T(8,128)(2,1)} %get-tuple-element.280), channel_id=1, source_target_pairs={{0,2},{2,0},{1,3},{3,1},{4,6},{6,4},{5,7},{7,5},{8,10},{10,8},{9,1... | collective-permute-start | bytes 5308424 | tf_op jit(solution)/shard_map/ppermute | solution.py:1770
  230.2 3.3 collective-permute-start.22
  230.8 24.0 %collective-permute-start.20 = (bf16[2,4,48,1152]{3,2,1,0:T(8,128)(2,1)}, bf16[2,4,48,1152]{3,2,1,0:T(8,128)(2,1)}, u32[]{:S(2)}, u32[]{:S(2)}) collective-permute-start(bf16[2,4,48,1152]{3,2,1,0:T(8,128)(2,1)} %get-tuple-element.271), channel_id=1, source_target_pairs={{0,8},{8,0},{16,24},{24,16},{1,9},{9,1},{17,25},{25,17},{2,10},{10... | collective-permute-start | bytes 2654216 | tf_op jit(solution)/shard_map/ppermute | solution.py:32
  237.2 22.7 %collective-permute-start.23 = (bf16[8,48,1152]{2,1,0:T(8,128)(2,1)}, bf16[8,48,1152]{2,1,0:T(8,128)(2,1)}, u32[]{:S(2)}, u32[]{:S(2)}) collective-permute-start(bf16[8,48,1152]{2,1,0:T(8,128)(2,1)} %get-tuple-element.380), channel_id=1, source_target_pairs={{0,1},{1,0},{2,3},{3,2},{4,5},{5,4},{6,7},{7,6},{8,9},{9,8},{10,11... | collective-permute-start | bytes 2654216 | tf_op jit(solution)/shard_map/ppermute | solution.py:1612
  238.2 16.5 %collective-permute-start.19 = (bf16[2,4,48,768]{3,2,1,0:T(8,128)(2,1)}, bf16[2,4,48,768]{3,2,1,0:T(8,128)(2,1)}, u32[]{:S(2)}, u32[]{:S(2)}) collective-permute-start(bf16[2,4,48,768]{3,2,1,0:T(8,128)(2,1)} %get-tuple-element.270), channel_id=1, source_target_pairs={{0,4},{4,0},{1,5},{5,1},{2,6},{6,2},{3,7},{7,3},{8,12},{12,8},{9,1... | collective-permute-start | bytes 1769480 | tf_op jit(solution)/shard_map/ppermute | solution.py:32
  239.9 20.0 %collective-permute-start.24 = (bf16[2,96,768]{2,1,0:T(8,128)(2,1)S(1)}, bf16[2,96,768]{2,1,0:T(8,128)(2,1)S(1)}, u32[]{:S(2)}, u32[]{:S(2)}) collective-permute-start(bf16[2,96,768]{2,1,0:T(8,128)(2,1)S(1)} %get-tuple-element.291), channel_id=1, source_target_pairs={{0,4},{4,0},{1,5},{5,1},{2,6},{6,2},{3,7},{7,3},{8,12},{12,8},{9,1... | collective-permute-start | bytes 884744 | tf_op jit(solution)/shard_map/ppermute | solution.py:32
  243.5 16.4 %collective-permute-start.25 = (f32[5,768]{1,0:T(8,128)S(1)}, f32[5,768]{1,0:T(8,128)S(1)}, u32[]{:S(2)}, u32[]{:S(2)}) collective-permute-start(f32[5,768]{1,0:T(8,128)S(1)} %add.144), channel_id=1, source_target_pairs={{0,1},{1,0},{2,3},{3,2},{4,5},{5,4},{6,7},{7,6},{8,9},{9,8},{10,11... | collective-permute-start | bytes 46088 | tf_op jit(solution)/shard_map/ppermute | solution.py:32
  244.5 15.3 %copy-start.8 = (bf16[2,4,48,1152]{3,2,1,0:T(8,128)(2,1)S(1)}, bf16[2,4,48,1152]{3,2,1,0:T(8,128)(2,1)}, u32[]{:S(2)}) copy-start(bf16[2,4,48,1152]{3,2,1,0:T(8,128)(2,1)} %get-tuple-element.275.refs_2_) | copy-start | bytes 2654212
  244.6 15.3 %copy-start.11 = (bf16[2,4,48,768]{3,2,1,0:T(8,128)(2,1)S(1)}, bf16[2,4,48,768]{3,2,1,0:T(8,128)(2,1)}, u32[]{:S(2)}) copy-start(bf16[2,4,48,768]{3,2,1,0:T(8,128)(2,1)} %get-tuple-element.274.refs_0_) | copy-start | bytes 1769476
  262.1 21.9 %copy-start.10 = (bf16[512,768]{1,0:T(8,128)(2,1)S(1)}, bf16[512,768]{1,0:T(8,128)(2,1)}, u32[]{:S(2)}) copy-start(bf16[512,768]{1,0:T(8,128)(2,1)} %copy-done.9) | copy-start | bytes 2359300
  262.1 14.5 %collective-permute-start.26 = (bf16[4,48,1152]{2,1,0:T(8,128)(2,1)S(1)}, bf16[4,48,1152]{2,1,0:T(8,128)(2,1)S(1)}, u32[]{:S(2)}, u32[]{:S(2)}) collective-permute-start(bf16[4,48,1152]{2,1,0:T(8,128)(2,1)S(1)} %get-tuple-element.299), channel_id=1, source_target_pairs={{0,8},{8,0},{16,24},{24,16},{1,9},{9,1},{17,25},{25,17},{2,10},{10... | collective-permute-start | bytes 1327112 | tf_op jit(solution)/shard_map/ppermute | solution.py:32
  263.8 12.8 %collective-permute-start.28 = (bf16[2,2,48,1152]{3,2,1,0:T(8,128)(2,1)S(1)}, bf16[2,2,48,1152]{3,2,1,0:T(8,128)(2,1)S(1)}, u32[]{:S(2)}, u32[]{:S(2)}) collective-permute-start(bf16[2,2,48,1152]{3,2,1,0:T(8,128)(2,1)S(1)} %get-tuple-element.301), channel_id=1, source_target_pairs={{0,4},{4,0},{1,5},{5,1},{2,6},{6,2},{3,7},{7,3},{8,12},{12,8},{9,1... | collective-permute-start | bytes 1327112 | tf_op jit(solution)/shard_map/ppermute | solution.py:32
  265.3 10.4 %collective-permute-start.27 = (bf16[4,48,768]{2,1,0:T(8,128)(2,1)S(1)}, bf16[4,48,768]{2,1,0:T(8,128)(2,1)S(1)}, u32[]{:S(2)}, u32[]{:S(2)}) collective-permute-start(bf16[4,48,768]{2,1,0:T(8,128)(2,1)S(1)} %get-tuple-element.300), channel_id=1, source_target_pairs={{0,1},{1,0},{2,3},{3,2},{4,5},{5,4},{6,7},{7,6},{8,9},{9,8},{10,11... | collective-permute-start | bytes 884744 | tf_op jit(solution)/shard_map/ppermute | solution.py:1612
  266.1 9.6 %collective-permute-start.29 = (bf16[1,96,768]{2,1,0:T(8,128)(2,1)S(1)}, bf16[1,96,768]{2,1,0:T(8,128)(2,1)S(1)}, u32[]{:S(2)}, u32[]{:S(2)}) collective-permute-start(bf16[1,96,768]{2,1,0:T(8,128)(2,1)S(1)} %get-tuple-element.302), channel_id=1, source_target_pairs={{0,16},{8,24},{16,0},{24,8},{1,17},{9,25},{17,1},{25,9},{2,18},{10... | collective-permute-start | bytes 442376 | tf_op jit(solution)/shard_map/ppermute | solution.py:32
  268.6 6.6 %collective-permute-start.30 = (f32[5,768]{1,0:T(8,128)S(1)}, f32[5,768]{1,0:T(8,128)S(1)}, u32[]{:S(2)}, u32[]{:S(2)}) collective-permute-start(f32[5,768]{1,0:T(8,128)S(1)} %add.145), channel_id=1, source_target_pairs={{0,4},{4,0},{1,5},{5,1},{2,6},{6,2},{3,7},{7,3},{8,12},{12,8},{9,1... | collective-permute-start | bytes 46088 | tf_op jit(solution)/shard_map/ppermute | solution.py:32
  276.9 12.4 %collective-permute-start.31 = (bf16[2,48,1152]{2,1,0:T(8,128)(2,1)S(1)}, bf16[2,48,1152]{2,1,0:T(8,128)(2,1)S(1)}, u32[]{:S(2)}, u32[]{:S(2)}) collective-permute-start(bf16[2,48,1152]{2,1,0:T(8,128)(2,1)S(1)} %get-tuple-element.312), channel_id=1, source_target_pairs={{0,4},{4,0},{1,5},{5,1},{2,6},{6,2},{3,7},{7,3},{8,12},{12,8},{9,1... | collective-permute-start | bytes 663560 | tf_op jit(solution)/shard_map/ppermute | solution.py:32
  278.4 10.1 %collective-permute-start.32 = (bf16[2,48,768]{2,1,0:T(8,128)(2,1)S(1)}, bf16[2,48,768]{2,1,0:T(8,128)(2,1)S(1)}, u32[]{:S(2)}, u32[]{:S(2)}) collective-permute-start(bf16[2,48,768]{2,1,0:T(8,128)(2,1)S(1)} %get-tuple-element.313), channel_id=1, source_target_pairs={{0,8},{8,0},{16,24},{24,16},{1,9},{9,1},{17,25},{25,17},{2,10},{10... | collective-permute-start | bytes 442376 | tf_op jit(solution)/shard_map/ppermute | solution.py:32
  281.0 8.3 %collective-permute-start.33 = (bf16[2,48,1152]{2,1,0:T(8,128)(2,1)S(1)}, bf16[2,48,1152]{2,1,0:T(8,128)(2,1)S(1)}, u32[]{:S(2)}, u32[]{:S(2)}) collective-permute-start(bf16[2,48,1152]{2,1,0:T(8,128)(2,1)S(1)} %get-tuple-element.314), channel_id=1, source_target_pairs={{0,1},{1,0},{2,3},{3,2},{4,5},{5,4},{6,7},{7,6},{8,9},{9,8},{10,11... | collective-permute-start | bytes 663560 | tf_op jit(solution)/shard_map/ppermute | solution.py:1612
  282.1 7.2 %collective-permute-start.34 = (bf16[1,96,768]{2,1,0:T(8,128)(2,1)S(1)}, bf16[1,96,768]{2,1,0:T(8,128)(2,1)S(1)}, u32[]{:S(2)}, u32[]{:S(2)}) collective-permute-start(bf16[1,96,768]{2,1,0:T(8,128)(2,1)S(1)} %get-tuple-element.315.refs_6_), channel_id=1, source_target_pairs={{0,16},{8,24},{16,0},{24,8},{1,17},{9,25},{17,1},{25,9},{2,18},{10... | collective-permute-start | bytes 442376 | tf_op jit(solution)/shard_map/ppermute | solution.py:32
  283.7 3.9 %collective-permute-start.35 = (f32[5,768]{1,0:T(8,128)S(1)}, f32[5,768]{1,0:T(8,128)S(1)}, u32[]{:S(2)}, u32[]{:S(2)}) collective-permute-start(f32[5,768]{1,0:T(8,128)S(1)} %add.146), channel_id=1, source_target_pairs={{0,8},{8,0},{16,24},{24,16},{1,9},{9,1},{17,25},{25,17},{2,10},{10... | collective-permute-start | bytes 46088 | tf_op jit(solution)/shard_map/ppermute | solution.py:32
  287.6 8.1 %collective-permute-start.37 = (bf16[256,768]{1,0:T(8,128)(2,1)S(1)}, bf16[256,768]{1,0:T(8,128)(2,1)S(1)}, u32[]{:S(2)}, u32[]{:S(2)}) collective-permute-start(bf16[256,768]{1,0:T(8,128)(2,1)S(1)} %get-tuple-element.326), channel_id=1, source_target_pairs={{0,1},{1,0},{2,3},{3,2},{4,5},{5,4},{6,7},{7,6},{8,9},{9,8},{10,11... | collective-permute-start | bytes 1179656 | tf_op jit(solution)/shard_map/ppermute | solution.py:1767
  289.4 13.2 %collective-permute-start.36 = (bf16[1,48,3072]{2,1,0:T(8,128)(2,1)S(1)}, bf16[1,48,3072]{2,1,0:T(8,128)(2,1)S(1)}, u32[]{:S(2)}, u32[]{:S(2)}) collective-permute-start(bf16[1,48,3072]{2,1,0:T(8,128)(2,1)S(1)} %get-tuple-element.324), channel_id=1, source_target_pairs={{0,16},{8,24},{16,0},{24,8},{1,17},{9,25},{17,1},{25,9},{2,18},{10... | collective-permute-start | bytes 884744 | tf_op jit(solution)/shard_map/ppermute | solution.py:32
  290.2 12.8 %collective-permute-start.38 = (bf16[2,96,768]{2,1,0:T(8,128)(2,1)S(1)}, bf16[2,96,768]{2,1,0:T(8,128)(2,1)S(1)}, u32[]{:S(2)}, u32[]{:S(2)}) collective-permute-start(bf16[2,96,768]{2,1,0:T(8,128)(2,1)S(1)} %get-tuple-element.328.refs_2_), channel_id=1, source_target_pairs={{0,8},{8,0},{16,24},{24,16},{1,9},{9,1},{17,25},{25,17},{2,10},{10... | collective-permute-start | bytes 884744 | tf_op jit(solution)/shard_map/ppermute | solution.py:32
  292.5 10.5 %collective-permute-start.39 = (f32[5,768]{1,0:T(8,128)S(1)}, f32[5,768]{1,0:T(8,128)S(1)}, u32[]{:S(2)}, u32[]{:S(2)}) collective-permute-start(f32[5,768]{1,0:T(8,128)S(1)} %add.147), channel_id=1, source_target_pairs={{0,16},{8,24},{16,0},{24,8},{1,17},{9,25},{17,1},{25,9},{2,18},{10... | collective-permute-start | bytes 46088 | tf_op jit(solution)/shard_map/ppermute | solution.py:32
  303.0 15.0 %collective-permute-start.42 = (bf16[4,96,768]{2,1,0:T(8,128)(2,1)S(1)}, bf16[4,96,768]{2,1,0:T(8,128)(2,1)S(1)}, u32[]{:S(2)}, u32[]{:S(2)}) collective-permute-start(bf16[4,96,768]{2,1,0:T(8,128)(2,1)S(1)} %get-tuple-element.335.refs_2_), channel_id=1, source_target_pairs={{0,4},{4,0},{1,5},{5,1},{2,6},{6,2},{3,7},{7,3},{8,12},{12,8},{9,1... | collective-permute-start | bytes 1769480 | tf_op jit(solution)/shard_map/ppermute | solution.py:32
  303.6 9.5 %collective-permute-start.41 = (bf16[256,768]{1,0:T(8,128)(2,1)S(1)}, bf16[256,768]{1,0:T(8,128)(2,1)S(1)}, u32[]{:S(2)}, u32[]{:S(2)}) collective-permute-start(bf16[256,768]{1,0:T(8,128)(2,1)S(1)} %get-tuple-element.333), channel_id=1, source_target_pairs={{0,1},{1,0},{2,3},{3,2},{4,5},{5,4},{6,7},{7,6},{8,9},{9,8},{10,11... | collective-permute-start | bytes 1179656 | tf_op jit(solution)/shard_map/ppermute | solution.py:1767
  304.5 13.5 %collective-permute-start.40 = (bf16[1,48,3072]{2,1,0:T(8,128)(2,1)S(1)}, bf16[1,48,3072]{2,1,0:T(8,128)(2,1)S(1)}, u32[]{:S(2)}, u32[]{:S(2)}) collective-permute-start(bf16[1,48,3072]{2,1,0:T(8,128)(2,1)S(1)} %get-tuple-element.332.refs_0_), channel_id=1, source_target_pairs={{0,16},{8,24},{16,0},{24,8},{1,17},{9,25},{17,1},{25,9},{2,18},{10... | collective-permute-start | bytes 884744 | tf_op jit(solution)/shard_map/ppermute | solution.py:32
  318.1 9.6 %collective-permute-start.45 = (bf16[8,96,768]{2,1,0:T(8,128)(2,1)S(1)}, bf16[8,96,768]{2,1,0:T(8,128)(2,1)S(1)}, u32[]{:S(2)}, u32[]{:S(2)}) collective-permute-start(bf16[8,96,768]{2,1,0:T(8,128)(2,1)S(1)} %get-tuple-element.346.part_ref), channel_id=1, source_target_pairs={{0,2},{2,0},{1,3},{3,1},{4,6},{6,4},{5,7},{7,5},{8,10},{10,8},{9,1... | collective-permute-start | bytes 3538952 | tf_op jit(solution)/shard_map/ppermute | solution.py:1526
  318.2 9.4 %collective-permute-start.43 = (bf16[2,48,1536]{2,1,0:T(8,128)(2,1)S(1)}, bf16[2,48,1536]{2,1,0:T(8,128)(2,1)S(1)}, u32[]{:S(2)}, u32[]{:S(2)}) collective-permute-start(bf16[2,48,1536]{2,1,0:T(8,128)(2,1)S(1)} %get-tuple-element.338.refs_0_), channel_id=1, source_target_pairs={{0,8},{8,0},{16,24},{24,16},{1,9},{9,1},{17,25},{25,17},{2,10},{10... | collective-permute-start | bytes 884744 | tf_op jit(solution)/shard_map/ppermute | solution.py:32
  318.3 9.4 %collective-permute-start.44 = (bf16[2,48,1536]{2,1,0:T(8,128)(2,1)S(1)}, bf16[2,48,1536]{2,1,0:T(8,128)(2,1)S(1)}, u32[]{:S(2)}, u32[]{:S(2)}) collective-permute-start(bf16[2,48,1536]{2,1,0:T(8,128)(2,1)S(1)} %get-tuple-element.339.refs_2_), channel_id=1, source_target_pairs={{0,4},{4,0},{1,5},{5,1},{2,6},{6,2},{3,7},{7,3},{8,12},{12,8},{9,1... | collective-permute-start | bytes 884744 | tf_op jit(solution)/shard_map/ppermute | solution.py:32
  327.8 14.9 %collective-permute-start.46 = (bf16[4,48,1536]{2,1,0:T(8,128)(2,1)S(1)}, bf16[4,48,1536]{2,1,0:T(8,128)(2,1)S(1)}, u32[]{:S(2)}, u32[]{:S(2)}) collective-permute-start(bf16[4,48,1536]{2,1,0:T(8,128)(2,1)S(1)} %get-tuple-element.343.refs_0_), channel_id=1, source_target_pairs={{0,4},{4,0},{1,5},{5,1},{2,6},{6,2},{3,7},{7,3},{8,12},{12,8},{9,1... | collective-permute-start | bytes 1769480 | tf_op jit(solution)/shard_map/ppermute | solution.py:32
  329.5 14.6 %collective-permute-start.47 = (bf16[4,48,1536]{2,1,0:T(8,128)(2,1)S(1)}, bf16[4,48,1536]{2,1,0:T(8,128)(2,1)S(1)}, u32[]{:S(2)}, u32[]{:S(2)}) collective-permute-start(bf16[4,48,1536]{2,1,0:T(8,128)(2,1)S(1)} %get-tuple-element.344.refs_2_), channel_id=1, source_target_pairs={{0,8},{8,0},{16,24},{24,16},{1,9},{9,1},{17,25},{25,17},{2,10},{10... | collective-permute-start | bytes 1769480 | tf_op jit(solution)/shard_map/ppermute | solution.py:32
  344.3 4.6 %collective-permute-start.48 = (bf16[8,48,3072]{2,1,0:T(8,128)(2,1)S(1)}, bf16[8,48,3072]{2,1,0:T(8,128)(2,1)S(1)}, u32[]{:S(2)}, u32[]{:S(2)}) collective-permute-start(bf16[8,48,3072]{2,1,0:T(8,128)(2,1)S(1)} %phase.17.part_ref), channel_id=1, source_target_pairs={{0,2},{2,0},{1,3},{3,1},{4,6},{6,4},{5,7},{7,5},{8,10},{10,8},{9,1... | collective-permute-start | bytes 7077896 | tf_op jit(solution)/shard_map/ppermute | solution.py:1526
  (30 other events, 79.8 us)

commit v5 on v4

--- a/solution.py
+++ b/solution.py
@@ -1476,7 +1476,7 @@
     for j in range(3):
         for b in range(8):
             sl = slice(b * rows, (b + 1) * rows)
-            qkv_st[j, sl] = part_ref[b ^ right, :, d + (j + 1) * f : d + (j + 2) * f].astype(F32)
+            qkv_st[j, sl] = part_ref[swapped(b ^ left), :, d + (j + 1) * f : d + (j + 2) * f].astype(F32)
         sent.append(moves.whole(qkv_st.at[j], qkv_far.at[j, pl.ds(pl.multiple_of(base, 8), half)]))
     for wait in sent:
         wait()
@@ -1823,7 +1823,7 @@
     down.keep, down.got = [down.keep], [down.got]
     all_steps(down.hop("z"))
     small = jnp.stack([sums_e[0] + sums_o[0], sums1[0] + sums2[0], sums_e[1] + sums_o[1], sums1[1] + sums2[1], sums_o[2]])
-    qkv_keep, qkv_go = grad_qkv(me_z, a_e, a_o, after(dqkv_e, *down.sent), dqkv_o)
+    qkv_keep, qkv_go = grad_qkv(me, a_e, a_o, after(dqkv_e, *down.sent), dqkv_o)
     up_parts = up.fold_first()
     qkv_keep, qkv_go, down.got, up_parts = sync(qkv_keep, qkv_go, down.got, up_parts)
     out = link.finish(
@@ -1855,9 +1855,9 @@
     chunks += [up, down]
     (out,) = up.wait(out)
     wait_all()
-    all_steps(up.hop("partner", "x"), qkv.hop("z"), down.hop("w"))
+    all_steps(up.hop("z", "partner"), qkv.hop("x"), down.hop("w"))
     wait_all()
-    all_steps(up.hop("z", "partner"), qkv.hop("x"), down.back_first())
+    all_steps(up.hop("partner", "x"), qkv.hop("z"), down.back_first())
     half = gt.shape[0] // 2
     gt_got = [link.partner(after(gt[:half], *up.sent))]
     wait_all()

time: 359 us -> 357 us (level)
  no operation moved by 1% of the time
where the time goes in v5:
time: 357 us; the launch traced here: 350 us
  Pallas kernels  171 us (48%)
  waiting for transfers between devices  84.4 us (24%)
  starting transfers between devices  46.9 us (13%)
  other arithmetic  27.7 us (8%)
  local copies, waits for them, and re-layouts  18.4 us (5%)
    pallas_call x23, Pallas kernels, resident(): pl.pallas_call(body, in_specs=[s for _, s in ins], out_specs=[s for _, s...  167 us
    ppermute x23, waiting for transfers between devices, flip_bit(): return lax.ppermute(array, axis, [(i, i ^ bit) for i in range(size)])  52.4 us
    ppermute x23, starting transfers between devices, flip_bit(): return lax.ppermute(array, axis, [(i, i ^ bit) for i in range(size)])  28.6 us
    ppermute x9, waiting for transfers between devices, partner(): return lax.ppermute(t, 'tensor', FLIP)  18.9 us
    ppermute x9, starting transfers between devices, partner(): return lax.ppermute(t, 'tensor', FLIP)  10.7 us
    another operation x11, other arithmetic, ordered(): jnp.stack([jnp.where(first, mine, theirs), jnp.where(first, theirs, mine)])  7.45 us
  transfers between devices with their start and end apart: 49, of which 29 were waited for; matrix products, arithmetic and copies ran while one was open for 10% of the time, Pallas kernels for 31%

profile of v5, /device:TPU:0, one launch (start us, length us, event | category | flops | bytes accessed | tf_op | source)
XLA Modules:
  0.0 350.3 jit_solution(8479187574154155610)
XLA Ops:
  0.7 2.0 constant_dynamic-slice_fusion.7
  2.8 3.0 collective-permute-start
  5.8 1.3 convert_reduce_fusion
  9.2 1.6 add_convert_fusion.3.a_ref.ae_far
  11.9 2.4 attend_first.2
  16.7 1.2 constant_dynamic-slice_fusion.4.cot_far
  18.0 1.5 collective-permute-start.1
  19.5 1.9 constant_dynamic-slice_fusion.2
  22.9 1.6 collective-permute-start.2
  24.5 5.5 %collective-permute-done.1 = bf16[576,384]{1,0:T(8,128)(2,1)} collective-permute-done((bf16[576,384]{1,0:T(8,128)(2,1)}, bf16[576,384]{1,0:T(8,128)(2,1)}, u32[]{:S(2)}, u32[]{:S(2)}) %collective-permute-start.1) | collective-permute-done | bytes 442400 | tf_op jit(solution)/shard_map/ppermute | solution.py:1734
  29.9 1.2 select_bitcast_fusion.5
  32.2 7.2 %collective-permute-done.2 = bf16[96,768]{1,0:T(8,128)(2,1)} collective-permute-done((bf16[96,768]{1,0:T(8,128)(2,1)S(1)}, bf16[96,768]{1,0:T(8,128)(2,1)}, u32[]{:S(2)}, u32[]{:S(2)}) %collective-permute-start.2) | collective-permute-done | bytes 147488 | tf_op jit(solution)/shard_map/ppermute | solution.py:1767
  42.2 1.6 select_bitcast_fusion.1
  44.0 1.3 copy-done.7
  45.3 2.1 pad_maximum_fusion.w_far
  47.3 2.4 attend_first.3
  49.8 1.6 pad_maximum_fusion.2.qkve_far
  56.4 10.0 %mlp_own.1 = (f32[512,768]{1,0:T(8,128)}, bf16[512,768]{1,0:T(8,128)(2,1)}, bf16[512,3072]{1,0:T(8,128)(2,1)}, bf16[512,3072]{1,0:T(8,128)(2,1)}, f32[512,768]{1,0:T(8,128)}, /*index=5*/bf16[1024,768]{1,0:T(8,128)(2,1)}) custom-call(bf16[512,768]{1,0:T(8,128)(2,1)} %bitcast.59, bf16[512,768]{1,0:T(8,128)(2,1)} %pad_maximum_fusion.10.o_far.o1_far, ...), custom_call_target="tpu_custom_call" | custom-call | tf_op jit(solution)/shard_map/mlp_own/pallas_call | solution.py:112
  66.4 2.9 collective-permute-done.5.refs_4_.refs_6_
  69.9 2.8 collective-permute-done.9.refs_2_.refs_3_
  72.7 1.2 collective-permute-done.10.refs_3_.refs_4_
  75.1 8.4 %mlp_other.1 = (bf16[512,3072]{1,0:T(8,128)(2,1)}, bf16[512,3072]{1,0:T(8,128)(2,1)}, f32[512,768]{1,0:T(8,128)}, bf16[512,768]{1,0:T(8,128)(2,1)}) custom-call(bf16[512,768]{1,0:T(8,128)(2,1)} %get-tuple-element.209.n2_far.n1_far, f32[512,768]{1,0:T(8,128)} %get-tuple-element.210.part_far, ...), custom_call_target="tpu_custom_call", output_to_operand_aliasing={{0}: (2, {}), {1}: (3, {})} | custom-call | tf_op jit(solution)/shard_map/mlp_other/pallas_call | solution.py:112
  83.6 13.6 %attend_second.1 = (bf16[3,512,768]{2,1,0:T(8,128)(2,1)}, bf16[2,512,768]{2,1,0:T(8,128)(2,1)}, f32[2,3,4,512]{3,2,1,0:T(4,128)S(1)}) custom-call(bf16[512,768]{1,0:T(8,128)(2,1)} %get-tuple-element.215.a_far.ao_far, bf16[3,768,768]{2,1,0:T(8,128)(2,1)} %pad_maximum_fusion.w_far, f32[2,256,256]{2,1,0:T(8,128)} %copy-done.2, ...), custom_call_target="tpu_custom_call" | custom-call | flops 415236096 | tf_op jit(solution)/shard_map/attend_second/pallas_call | solution.py:112
  97.2 34.7 %mlp_second.1 = (bf16[1,512,768]{2,1,0:T(8,128)(2,1)}, bf16[1,512,768]{2,1,0:T(8,128)(2,1)}, bf16[1024,768]{1,0:T(8,128)(2,1)}, bf16[1024,3072]{1,0:T(8,128)(2,1...) custom-call(bf16[512,768]{1,0:T(8,128)(2,1)} %bitcast.60, ...), custom_call_target="tpu_custom_call" | custom-call | tf_op jit(solution)/shard_map/mlp_second/pallas_call | solution.py:112
  133.0 18.9 %attend_back.1 = (bf16[3,512,768]{2,1,0:T(8,128)(2,1)}, bf16[3,512,768]{2,1,0:T(8,128)(2,1)}, f32[512,768]{1,0:T(8,128)}, f32[3,768]{1,0:T(4,128)S(1)}) custom-call(bf16[3,768,768]{2,1,0:T(8,128)(2,1)} %pad_maximum_fusion.w_far, f32[2,256,256]{2,1,0:T(8,128)} %copy-done.2, f32[2,256,256]{2,1,0:T(8,128)} %get-tuple-element.402.strict_far, ...), custom_call_target="tpu_custom_call" | custom-call | flops 868220928 | tf_op jit(solution)/shard_map/attend_back/pallas_call | solution.py:112
  153.1 14.1 %grad_down.1 = (bf16[2,8,96,768]{3,2,1,0:T(8,128)(2,1)}, bf16[2,8,96,768]{3,2,1,0:T(8,128)(2,1)}) custom-call(s32[2]{0:T(128)S(1)} %copy-done.21, bf16[512,3072]{1,0:T(8,128)(2,1)} %get-tuple-element.217.g1_far, bf16[1024,3072]{1,0:T(8,128)(2,1)} %get-tuple-element.224.g2_far, f32[512,768]{1,0:T(8,128)} %get-tuple-element.239.dy_far, ...), custom_call_target="tpu_custom_call" | custom-call | flops 452984832 | tf_op jit(solution)/shard_map/grad_down/pallas_call | solution.py:112
  168.4 13.2 %mlp_back.1 = (bf16[512,3072]{1,0:T(8,128)(2,1)}, f32[512,768]{1,0:T(8,128)}, bf16[512,768]{1,0:T(8,128)(2,1)}, bf16[512,768]{1,0:T(8,128)(2,1)}, f32[2,768]{1,0:T(2,128)S(1)}) custom-call(f32[512,768]{1,0:T(8,128)} %get-tuple-element.239.dy_far, f32[512,768]{1,0:T(8,128)} %get-tuple-element.240.h1_far, bf16[768,768]{1,0:T(8,128)(2,1)} %pad_maximum_fusion.8.wout_far, ...), custom_call_target="tpu_custom_call" | custom-call | tf_op jit(solution)/shard_map/mlp_back/pallas_call | solution.py:112
  183.6 16.7 %grad_up.1 = (bf16[2,8,48,1920]{3,2,1,0:T(8,128)(2,1)}, bf16[2,8,48,1920]{3,2,1,0:T(8,128)(2,1)}) custom-call(s32[3]{0:T(128)} %pad_add_fusion.me_ref, bf16[512,768]{1,0:T(8,128)(2,1)} %get-tuple-element.209.n2_far.n1_far, bf16[1024,768]{1,0:T(8,128)(2,1)} %get-tuple-element.248.n2_far, bf16[512,3072]{1,0:T(8,128)(2,1)} %get-tuple-element.250.du1_far, ...), custom_call_target="tpu_custom_call" | custom-call | flops 566231040 | tf_op jit(solution)/shard_map/grad_up/pallas_call | solution.py:112
  200.4 12.8 %attend_back_even.1 = (bf16[3,512,768]{2,1,0:T(8,128)(2,1)}, bf16[512,768]{1,0:T(8,128)(2,1)S(1)}, f32[2,768]{1,0:T(2,128)S(1)}) custom-call(bf16[3,768,768]{2,1,0:T(8,128)(2,1)} %pad_maximum_fusion.w_far, f32[2,256,256]{2,1,0:T(8,128)} %copy-done.2, bf16[3,512,768]{2,1,0:T(8,128)(2,1)} %pad_maximum_fusion.2.qkve_far, ...), custom_call_target="tpu_custom_call" | custom-call | flops 364904448 | tf_op jit(solution)/shard_map/attend_back_even/pallas_call | solution.py:112
  214.1 1.6 collective-permute-start.17
  215.6 9.8 %grad_qkv.1 = (bf16[2,8,48,1152]{3,2,1,0:T(8,128)(2,1)}, bf16[2,8,48,1152]{3,2,1,0:T(8,128)(2,1)}) custom-call(s32[3]{0:T(128)S(1)} %copy-done.20, bf16[512,768]{1,0:T(8,128)(2,1)} %copy-done.4, bf16[512,768]{1,0:T(8,128)(2,1)} %get-tuple-element.215.a_far.ao_far, bf16[3,512,768]{2,1,0:T(8,128)(2,1)} %get-tuple-element.264.de_far, ...), custom_call_target="tpu_custom_call" | custom-call | flops 226492416 | tf_op jit(solution)/shard_map/grad_qkv/pallas_call | solution.py:112
  227.3 1.3 fusion.5
  230.8 1.6 collective-permute-start.20
  234.2 1.9 add_convert_fusion.2
  238.3 1.5 collective-permute-start.19
  241.5 2.0 broadcast_select_fusion.1
  244.6 1.9 pad_maximum_fusion.1
  246.5 8.3 %collective-permute-done.19.refs_1_ = bf16[2,4,48,768]{3,2,1,0:T(8,128)(2,1)} collective-permute-done((bf16[2,4,48,768]{3,2,1,0:T(8,128)(2,1)}, bf16[2,4,48,768]{3,2,1,0:T(8,128)(2,1)}, u32[]{:S(2)}, u32[]{:S(2)}) %collective-permute-start.19) | collective-permute-done | bytes 589856 | tf_op jit(solution)/shard_map/ppermute | solution.py:32
  254.8 5.1 %collective-permute-done.24.refs_7_ = bf16[2,96,768]{2,1,0:T(8,128)(2,1)S(1)} collective-permute-done((bf16[2,96,768]{2,1,0:T(8,128)(2,1)S(1)}, bf16[2,96,768]{2,1,0:T(8,128)(2,1)S(1)}, u32[]{:S(2)}, u32[]{:S(2)}) %collective-permute-start.24) | collective-permute-done | bytes 294944 | tf_op jit(solution)/shard_map/ppermute | solution.py:32
  259.9 2.2 phase.11
  262.1 1.6 collective-permute-start.26
  264.5 1.6 collective-permute-start.27
  266.1 2.6 collective-permute-start.29
  269.4 4.6 %collective-permute-done.30 = f32[5,768]{1,0:T(8,128)S(1)} collective-permute-done((f32[5,768]{1,0:T(8,128)S(1)}, f32[5,768]{1,0:T(8,128)S(1)}, u32[]{:S(2)}, u32[]{:S(2)}) %collective-permute-start.30) | collective-permute-done | bytes 15392 | tf_op jit(solution)/shard_map/ppermute | solution.py:32
  275.8 2.7 collective-permute-start.31
  279.9 1.6 collective-permute-start.34
  281.9 4.2 %collective-permute-done.35 = f32[5,768]{1,0:T(8,128)S(1)} collective-permute-done((f32[5,768]{1,0:T(8,128)S(1)}, f32[5,768]{1,0:T(8,128)S(1)}, u32[]{:S(2)}, u32[]{:S(2)}) %collective-permute-start.35) | collective-permute-done | bytes 15392 | tf_op jit(solution)/shard_map/ppermute | solution.py:32
  287.9 1.4 collective-permute-start.36
  289.3 1.6 collective-permute-start.38
  292.2 2.3 collective-permute-done.37
  294.5 6.7 %collective-permute-done.36.refs_1_ = bf16[1,48,3072]{2,1,0:T(8,128)(2,1)S(1)} collective-permute-done((bf16[1,48,3072]{2,1,0:T(8,128)(2,1)S(1)}, bf16[1,48,3072]{2,1,0:T(8,128)(2,1)S(1)}, u32[]{:S(2)}, u32[]{:S(2)}) %collective-permute-start.36) | collective-permute-done | bytes 294944 | tf_op jit(solution)/shard_map/ppermute | solution.py:32
  301.5 1.2 collective-permute-start.42
  303.7 1.9 collective-permute-start.40
  305.6 6.5 %collective-permute-done.41 = bf16[256,768]{1,0:T(8,128)(2,1)S(1)} collective-permute-done((bf16[256,768]{1,0:T(8,128)(2,1)S(1)}, bf16[256,768]{1,0:T(8,128)(2,1)S(1)}, u32[]{:S(2)}, u32[]{:S(2)}) %collective-permute-start.41) | collective-permute-done | bytes 393248 | tf_op jit(solution)/shard_map/ppermute | solution.py:1767
  312.1 5.1 %collective-permute-done.40.refs_1_ = bf16[1,48,3072]{2,1,0:T(8,128)(2,1)S(1)} collective-permute-done((bf16[1,48,3072]{2,1,0:T(8,128)(2,1)S(1)}, bf16[1,48,3072]{2,1,0:T(8,128)(2,1)S(1)}, u32[]{:S(2)}, u32[]{:S(2)}) %collective-permute-start.40) | collective-permute-done | bytes 294944 | tf_op jit(solution)/shard_map/ppermute | solution.py:32
  318.6 8.2 %collective-permute-done.43.refs_1_ = bf16[2,48,1536]{2,1,0:T(8,128)(2,1)S(1)} collective-permute-done((bf16[2,48,1536]{2,1,0:T(8,128)(2,1)S(1)}, bf16[2,48,1536]{2,1,0:T(8,128)(2,1)S(1)}, u32[]{:S(2)}, u32[]{:S(2)}) %collective-permute-start.43) | collective-permute-done | bytes 294944 | tf_op jit(solution)/shard_map/ppermute | solution.py:32
  327.5 1.7 collective-permute-start.47
  330.1 1.9 convert.1
  332.0 2.1 unpack_down.2.refs_0_
  334.1 2.1 unpack_down.3
  336.2 5.7 %collective-permute-done.46.refs_1_ = bf16[4,48,1536]{2,1,0:T(8,128)(2,1)S(1)} collective-permute-done((bf16[4,48,1536]{2,1,0:T(8,128)(2,1)S(1)}, bf16[4,48,1536]{2,1,0:T(8,128)(2,1)S(1)}, u32[]{:S(2)}, u32[]{:S(2)}) %collective-permute-start.46) | collective-permute-done | bytes 589856 | tf_op jit(solution)/shard_map/ppermute | solution.py:32
  342.3 3.0 unpack_rest.2
  345.3 1.6 collective-permute-done.48.part_ref
  346.8 2.9 unpack_rest.3
  (212 shorter events, 47.6 us)
Async XLA Ops:
  0.6 16.1 %copy-start = (bf16[4,512,768]{2,1,0:T(8,128)(2,1)S(1)}, bf16[4,512,768]{2,1,0:T(8,128)(2,1)}, u32[]{:S(2)}) copy-start(bf16[4,512,768]{2,1,0:T(8,128)(2,1)} %param.19) | copy-start | bytes 9437188
  0.7 8.4 %copy-start.37 = (f32[2,768]{1,0:T(2,128)S(1)}, f32[2,768]{1,0:T(2,128)}, u32[]{:S(2)}) copy-start(f32[2,768]{1,0:T(2,128)} %param.18) | copy-start | bytes 18436
  2.8 15.2 %collective-permute-start = (bf16[576,384]{1,0:T(8,128)(2,1)}, bf16[576,384]{1,0:T(8,128)(2,1)}, u32[]{:S(2)}, u32[]{:S(2)}) collective-permute-start(bf16[576,384]{1,0:T(8,128)(2,1)} %constant_dynamic-slice_fusion.7), channel_id=1, source_target_pairs={{0,1},{1,0},{2,3},{3,2},{4,5},{5,4},{6,7},{7,6},{8,9},{9,8},{10,11... | collective-permute-start | bytes 1327112 | tf_op jit(solution)/shard_map/ppermute | solution.py:1767
  18.0 11.9 %collective-permute-start.1 = (bf16[576,384]{1,0:T(8,128)(2,1)}, bf16[576,384]{1,0:T(8,128)(2,1)}, u32[]{:S(2)}, u32[]{:S(2)}) collective-permute-start(bf16[576,384]{1,0:T(8,128)(2,1)} %collective-permute-done), channel_id=1, source_target_pairs={{0,4},{4,0},{1,5},{5,1},{2,6},{6,2},{3,7},{7,3},{8,12},{12,8},{9,1... | collective-permute-start | bytes 1327112 | tf_op jit(solution)/shard_map/ppermute | solution.py:1734
  21.4 18.0 %collective-permute-start.3 = (bf16[768,384]{1,0:T(8,128)(2,1)}, bf16[768,384]{1,0:T(8,128)(2,1)S(1)}, u32[]{:S(2)}, u32[]{:S(2)}) collective-permute-start(bf16[768,384]{1,0:T(8,128)(2,1)} %constant_dynamic-slice_fusion.2), channel_id=1, source_target_pairs={{0,1},{1,0},{2,3},{3,2},{4,5},{5,4},{6,7},{7,6},{8,9},{9,8},{10,11... | collective-permute-start | bytes 1769480 | tf_op jit(solution)/shard_map/ppermute | solution.py:1767
  22.9 16.5 %collective-permute-start.2 = (bf16[96,768]{1,0:T(8,128)(2,1)S(1)}, bf16[96,768]{1,0:T(8,128)(2,1)}, u32[]{:S(2)}, u32[]{:S(2)}) collective-permute-start(bf16[96,768]{1,0:T(8,128)(2,1)S(1)} %constant_dynamic-slice_fusion.3), channel_id=1, source_target_pairs={{0,1},{1,0},{2,3},{3,2},{4,5},{5,4},{6,7},{7,6},{8,9},{9,8},{10,11... | collective-permute-start | bytes 442376 | tf_op jit(solution)/shard_map/ppermute | solution.py:1767
  24.5 15.0 %copy-start.22 = (bf16[1536,768]{1,0:T(8,128)(2,1)S(1)}, bf16[1536,768]{1,0:T(8,128)(2,1)}, u32[]{:S(2)}) copy-start(bf16[1536,768]{1,0:T(8,128)(2,1)} %refs_5_.3) | copy-start | bytes 7077892
  39.4 2.8 collective-permute-start.6
  40.6 28.6 %collective-permute-start.5 = (bf16[768,768]{1,0:T(8,128)(2,1)}, bf16[768,768]{1,0:T(8,128)(2,1)}, u32[]{:S(2)}, u32[]{:S(2)}) collective-permute-start(bf16[768,768]{1,0:T(8,128)(2,1)} %pad_maximum_fusion.7), channel_id=1, source_target_pairs={{0,1},{1,0},{2,3},{3,2},{4,5},{5,4},{6,7},{7,6},{8,9},{9,8},{10,11... | collective-permute-start | bytes 3538952 | tf_op jit(solution)/shard_map/ppermute | solution.py:1767
  41.2 11.2 %collective-permute-start.7 = (bf16[96,768]{1,0:T(8,128)(2,1)}, bf16[96,768]{1,0:T(8,128)(2,1)}, u32[]{:S(2)}, u32[]{:S(2)}) collective-permute-start(bf16[96,768]{1,0:T(8,128)(2,1)} %collective-permute-done.2), channel_id=1, source_target_pairs={{0,4},{4,0},{1,5},{5,1},{2,6},{6,2},{3,7},{7,3},{8,12},{12,8},{9,1... | collective-permute-start | bytes 442376 | tf_op jit(solution)/shard_map/ppermute | solution.py:1734
  53.5 1.6 collective-permute-start.8
  53.7 15.7 %collective-permute-start.4 = (bf16[768,384]{1,0:T(8,128)(2,1)S(1)}, bf16[768,384]{1,0:T(8,128)(2,1)S(1)}, u32[]{:S(2)}, u32[]{:S(2)}) collective-permute-start(bf16[768,384]{1,0:T(8,128)(2,1)S(1)} %copy-done.26), channel_id=1, source_target_pairs={{0,4},{4,0},{1,5},{5,1},{2,6},{6,2},{3,7},{7,3},{8,12},{12,8},{9,1... | collective-permute-start | bytes 1769480 | tf_op jit(solution)/shard_map/ppermute | solution.py:1734
  54.7 19.4 %copy-start.12 = (f32[5,768]{1,0:T(8,128)}, f32[5,768]{1,0:T(8,128)S(1)}, u32[]{:S(2)}) copy-start(f32[5,768]{1,0:T(8,128)S(1)} %pad_maximum_fusion.14.gb_ref) | copy-start | bytes 46084
  69.4 4.7 %collective-permute-start.11 = (bf16[768,768]{1,0:T(8,128)(2,1)}, bf16[768,768]{1,0:T(8,128)(2,1)S(1)}, u32[]{:S(2)}, u32[]{:S(2)}) collective-permute-start(bf16[768,768]{1,0:T(8,128)(2,1)} %collective-permute-done.5.refs_4_.refs_6_), channel_id=1, source_target_pairs={{0,2},{2,0},{1,3},{3,1},{4,6},{6,4},{5,7},{7,5},{8,10},{10,8},{9,1... | collective-permute-start | bytes 3538952 | tf_op jit(solution)/shard_map/ppermute | solution.py:1770
  69.4 3.3 collective-permute-start.9
  69.9 4.0 %collective-permute-start.10 = (bf16[768,384]{1,0:T(8,128)(2,1)S(1)}, bf16[768,384]{1,0:T(8,128)(2,1)S(1)}, u32[]{:S(2)}, u32[]{:S(2)}) collective-permute-start(bf16[768,384]{1,0:T(8,128)(2,1)S(1)} %collective-permute-done.4.refs_1_.refs_2_), channel_id=1, source_target_pairs={{0,2},{2,0},{1,3},{3,1},{4,6},{6,4},{5,7},{7,5},{8,10},{10,8},{9,1... | collective-permute-start | bytes 1769480 | tf_op jit(solution)/shard_map/ppermute | solution.py:1770
  97.2 35.8 %copy-start.13 = (f32[5,768]{1,0:T(8,128)S(1)}, f32[5,768]{1,0:T(8,128)}, u32[]{:S(2)}) copy-start(f32[5,768]{1,0:T(8,128)} %copy-done.12) | copy-start | bytes 46084
  131.9 20.1 %collective-permute-start.12 = (bf16[1,512,768]{2,1,0:T(8,128)(2,1)}, bf16[1,512,768]{2,1,0:T(8,128)(2,1)S(1)}, u32[]{:S(2)}, u32[]{:S(2)}) collective-permute-start(bf16[1,512,768]{2,1,0:T(8,128)(2,1)} %get-tuple-element.225), channel_id=1, source_target_pairs={{0,1},{1,0},{2,3},{3,2},{4,5},{5,4},{6,7},{7,6},{8,9},{9,8},{10,11... | collective-permute-start | bytes 2359304 | tf_op jit(solution)/shard_map/ppermute | solution.py:1767
  133.0 18.9 %copy-start.30 = (bf16[1,512,768]{2,1,0:T(8,128)(2,1)S(1)}, bf16[1,512,768]{2,1,0:T(8,128)(2,1)}, u32[]{:S(2)}) copy-start(bf16[1,512,768]{2,1,0:T(8,128)(2,1)} %get-tuple-element.234) | copy-start | bytes 2359300
  133.0 20.1 %copy-start.21 = (s32[2]{0:T(128)S(1)}, s32[2]{0:T(128)}, u32[]{:S(2)}) copy-start(s32[2]{0:T(128)} %rev.3.me_ref) | copy-start | bytes 28
  152.0 15.2 %copy-start.35 = (bf16[1,512,768]{2,1,0:T(8,128)(2,1)}, bf16[1,512,768]{2,1,0:T(8,128)(2,1)S(1)}, u32[]{:S(2)}) copy-start(bf16[1,512,768]{2,1,0:T(8,128)(2,1)S(1)} %collective-permute-done.12) | copy-start | bytes 2359300
  152.0 15.2 %collective-permute-start.13 = (bf16[1,256,768]{2,1,0:T(8,128)(2,1)S(1)}, bf16[1,256,768]{2,1,0:T(8,128)(2,1)S(1)}, u32[]{:S(2)}, u32[]{:S(2)}) collective-permute-start(bf16[1,256,768]{2,1,0:T(8,128)(2,1)S(1)} %get-tuple-element.236), channel_id=1, source_target_pairs={{0,1},{1,0},{2,3},{3,2},{4,5},{5,4},{6,7},{7,6},{8,9},{9,8},{10,11... | collective-permute-start | bytes 1179656 | tf_op jit(solution)/shard_map/ppermute | solution.py:1767
  167.2 14.5 %collective-permute-start.14 = (bf16[2,8,96,768]{3,2,1,0:T(8,128)(2,1)}, bf16[2,8,96,768]{3,2,1,0:T(8,128)(2,1)S(1)}, u32[]{:S(2)}, u32[]{:S(2)}) collective-permute-start(bf16[2,8,96,768]{3,2,1,0:T(8,128)(2,1)} %get-tuple-element.238), channel_id=1, source_target_pairs={{0,2},{2,0},{1,3},{3,1},{4,6},{6,4},{5,7},{7,5},{8,10},{10,8},{9,1... | collective-permute-start | bytes 7077896 | tf_op jit(solution)/shard_map/ppermute | solution.py:1770
  167.3 14.4 %collective-permute-start.15 = (bf16[1,256,768]{2,1,0:T(8,128)(2,1)S(1)}, bf16[1,256,768]{2,1,0:T(8,128)(2,1)S(1)}, u32[]{:S(2)}, u32[]{:S(2)}) collective-permute-start(bf16[1,256,768]{2,1,0:T(8,128)(2,1)S(1)} %get-tuple-element.245), channel_id=1, source_target_pairs={{0,1},{1,0},{2,3},{3,2},{4,5},{5,4},{6,7},{7,6},{8,9},{9,8},{10,11... | collective-permute-start | bytes 1179656 | tf_op jit(solution)/shard_map/ppermute | solution.py:1767
  168.4 13.3 %copy-start.32 = (bf16[2,8,96,768]{3,2,1,0:T(8,128)(2,1)S(1)}, bf16[2,8,96,768]{3,2,1,0:T(8,128)(2,1)}, u32[]{:S(2)}) copy-start(bf16[2,8,96,768]{3,2,1,0:T(8,128)(2,1)} %get-tuple-element.237) | copy-start | bytes 7077892
  182.6 30.6 %collective-permute-start.16 = (bf16[8,96,768]{2,1,0:T(8,128)(2,1)S(1)}, bf16[8,96,768]{2,1,0:T(8,128)(2,1)S(1)}, u32[]{:S(2)}, u32[]{:S(2)}) collective-permute-start(bf16[8,96,768]{2,1,0:T(8,128)(2,1)S(1)} %get-tuple-element.376), channel_id=1, source_target_pairs={{0,1},{1,0},{2,3},{3,2},{4,5},{5,4},{6,7},{7,6},{8,9},{9,8},{10,11... | collective-permute-start | bytes 3538952 | tf_op jit(solution)/shard_map/ppermute | solution.py:1523
  200.3 12.8 %copy-start.44 = (bf16[2,8,48,1920]{3,2,1,0:T(8,128)(2,1)S(1)}, bf16[2,8,48,1920]{3,2,1,0:T(8,128)(2,1)}, u32[]{:S(2)}) copy-start(bf16[2,8,48,1920]{3,2,1,0:T(8,128)(2,1)} %get-tuple-element.269) | copy-start | bytes 8847364
  213.2 12.3 %collective-permute-start.18 = (bf16[2,8,48,1920]{3,2,1,0:T(8,128)(2,1)S(1)}, bf16[2,8,48,1920]{3,2,1,0:T(8,128)(2,1)S(1)}, u32[]{:S(2)}, u32[]{:S(2)}) collective-permute-start(bf16[2,8,48,1920]{3,2,1,0:T(8,128)(2,1)S(1)} %copy-done.44), channel_id=1, source_target_pairs={{0,2},{2,0},{1,3},{3,1},{4,6},{6,4},{5,7},{7,5},{8,10},{10,8},{9,1... | collective-permute-start | bytes 8847368 | tf_op jit(solution)/shard_map/ppermute | solution.py:1770
  214.1 11.4 %copy-start.16 = (bf16[4,96,768]{2,1,0:T(8,128)(2,1)}, bf16[4,96,768]{2,1,0:T(8,128)(2,1)S(1)}, u32[]{:S(2)}) copy-start(bf16[4,96,768]{2,1,0:T(8,128)(2,1)S(1)} %get-tuple-element.289.refs_0_) | copy-start | bytes 1769476
  214.1 15.3 %collective-permute-start.17 = (bf16[4,96,768]{2,1,0:T(8,128)(2,1)S(1)}, bf16[4,96,768]{2,1,0:T(8,128)(2,1)S(1)}, u32[]{:S(2)}, u32[]{:S(2)}) collective-permute-start(bf16[4,96,768]{2,1,0:T(8,128)(2,1)S(1)} %get-tuple-element.263), channel_id=1, source_target_pairs={{0,8},{8,0},{16,24},{24,16},{1,9},{9,1},{17,25},{25,17},{2,10},{10... | collective-permute-start | bytes 1769480 | tf_op jit(solution)/shard_map/ppermute | solution.py:32
  215.6 9.9 %copy-start.31 = (bf16[2,8,48,1920]{3,2,1,0:T(8,128)(2,1)S(1)}, bf16[2,8,48,1920]{3,2,1,0:T(8,128)(2,1)}, u32[]{:S(2)}) copy-start(bf16[2,8,48,1920]{3,2,1,0:T(8,128)(2,1)} %get-tuple-element.268) | copy-start | bytes 8847364
  230.2 4.1 %collective-permute-start.21 = (bf16[2,8,48,1152]{3,2,1,0:T(8,128)(2,1)}, bf16[2,8,48,1152]{3,2,1,0:T(8,128)(2,1)}, u32[]{:S(2)}, u32[]{:S(2)}) collective-permute-start(bf16[2,8,48,1152]{3,2,1,0:T(8,128)(2,1)} %get-tuple-element.280), channel_id=1, source_target_pairs={{0,2},{2,0},{1,3},{3,1},{4,6},{6,4},{5,7},{7,5},{8,10},{10,8},{9,1... | collective-permute-start | bytes 5308424 | tf_op jit(solution)/shard_map/ppermute | solution.py:1770
  230.2 3.3 collective-permute-start.22
  230.8 24.0 %collective-permute-start.20 = (bf16[2,4,48,1152]{3,2,1,0:T(8,128)(2,1)}, bf16[2,4,48,1152]{3,2,1,0:T(8,128)(2,1)}, u32[]{:S(2)}, u32[]{:S(2)}) collective-permute-start(bf16[2,4,48,1152]{3,2,1,0:T(8,128)(2,1)} %get-tuple-element.271), channel_id=1, source_target_pairs={{0,8},{8,0},{16,24},{24,16},{1,9},{9,1},{17,25},{25,17},{2,10},{10... | collective-permute-start | bytes 2654216 | tf_op jit(solution)/shard_map/ppermute | solution.py:32
  237.2 22.7 %collective-permute-start.23 = (bf16[8,48,1152]{2,1,0:T(8,128)(2,1)}, bf16[8,48,1152]{2,1,0:T(8,128)(2,1)}, u32[]{:S(2)}, u32[]{:S(2)}) collective-permute-start(bf16[8,48,1152]{2,1,0:T(8,128)(2,1)} %get-tuple-element.380), channel_id=1, source_target_pairs={{0,1},{1,0},{2,3},{3,2},{4,5},{5,4},{6,7},{7,6},{8,9},{9,8},{10,11... | collective-permute-start | bytes 2654216 | tf_op jit(solution)/shard_map/ppermute | solution.py:1612
  238.3 16.5 %collective-permute-start.19 = (bf16[2,4,48,768]{3,2,1,0:T(8,128)(2,1)}, bf16[2,4,48,768]{3,2,1,0:T(8,128)(2,1)}, u32[]{:S(2)}, u32[]{:S(2)}) collective-permute-start(bf16[2,4,48,768]{3,2,1,0:T(8,128)(2,1)} %get-tuple-element.270), channel_id=1, source_target_pairs={{0,4},{4,0},{1,5},{5,1},{2,6},{6,2},{3,7},{7,3},{8,12},{12,8},{9,1... | collective-permute-start | bytes 1769480 | tf_op jit(solution)/shard_map/ppermute | solution.py:32
  239.9 20.0 %collective-permute-start.24 = (bf16[2,96,768]{2,1,0:T(8,128)(2,1)S(1)}, bf16[2,96,768]{2,1,0:T(8,128)(2,1)S(1)}, u32[]{:S(2)}, u32[]{:S(2)}) collective-permute-start(bf16[2,96,768]{2,1,0:T(8,128)(2,1)S(1)} %get-tuple-element.291), channel_id=1, source_target_pairs={{0,4},{4,0},{1,5},{5,1},{2,6},{6,2},{3,7},{7,3},{8,12},{12,8},{9,1... | collective-permute-start | bytes 884744 | tf_op jit(solution)/shard_map/ppermute | solution.py:32
  243.5 16.4 %collective-permute-start.25 = (f32[5,768]{1,0:T(8,128)S(1)}, f32[5,768]{1,0:T(8,128)S(1)}, u32[]{:S(2)}, u32[]{:S(2)}) collective-permute-start(f32[5,768]{1,0:T(8,128)S(1)} %add.144), channel_id=1, source_target_pairs={{0,1},{1,0},{2,3},{3,2},{4,5},{5,4},{6,7},{7,6},{8,9},{9,8},{10,11... | collective-permute-start | bytes 46088 | tf_op jit(solution)/shard_map/ppermute | solution.py:32
  244.6 15.3 %copy-start.8 = (bf16[2,4,48,1152]{3,2,1,0:T(8,128)(2,1)S(1)}, bf16[2,4,48,1152]{3,2,1,0:T(8,128)(2,1)}, u32[]{:S(2)}) copy-start(bf16[2,4,48,1152]{3,2,1,0:T(8,128)(2,1)} %get-tuple-element.275.refs_2_) | copy-start | bytes 2654212
  244.6 15.3 %copy-start.11 = (bf16[2,4,48,768]{3,2,1,0:T(8,128)(2,1)S(1)}, bf16[2,4,48,768]{3,2,1,0:T(8,128)(2,1)}, u32[]{:S(2)}) copy-start(bf16[2,4,48,768]{3,2,1,0:T(8,128)(2,1)} %get-tuple-element.274.refs_0_) | copy-start | bytes 1769476
  262.1 19.7 %copy-start.10 = (bf16[512,768]{1,0:T(8,128)(2,1)S(1)}, bf16[512,768]{1,0:T(8,128)(2,1)}, u32[]{:S(2)}) copy-start(bf16[512,768]{1,0:T(8,128)(2,1)} %copy-done.9) | copy-start | bytes 2359300
  262.1 13.3 %collective-permute-start.26 = (bf16[4,48,1152]{2,1,0:T(8,128)(2,1)S(1)}, bf16[4,48,1152]{2,1,0:T(8,128)(2,1)S(1)}, u32[]{:S(2)}, u32[]{:S(2)}) collective-permute-start(bf16[4,48,1152]{2,1,0:T(8,128)(2,1)S(1)} %get-tuple-element.299), channel_id=1, source_target_pairs={{0,4},{4,0},{1,5},{5,1},{2,6},{6,2},{3,7},{7,3},{8,12},{12,8},{9,1... | collective-permute-start | bytes 1327112 | tf_op jit(solution)/shard_map/ppermute | solution.py:32
  263.7 11.7 %collective-permute-start.28 = (bf16[4,48,1152]{2,1,0:T(8,128)(2,1)S(1)}, bf16[4,48,1152]{2,1,0:T(8,128)(2,1)S(1)}, u32[]{:S(2)}, u32[]{:S(2)}) collective-permute-start(bf16[4,48,1152]{2,1,0:T(8,128)(2,1)S(1)} %get-tuple-element.301), channel_id=1, source_target_pairs={{0,1},{1,0},{2,3},{3,2},{4,5},{5,4},{6,7},{7,6},{8,9},{9,8},{10,11... | collective-permute-start | bytes 1327112 | tf_op jit(solution)/shard_map/ppermute | solution.py:1612
  264.5 10.9 %collective-permute-start.27 = (bf16[2,2,48,768]{3,2,1,0:T(8,128)(2,1)S(1)}, bf16[2,2,48,768]{3,2,1,0:T(8,128)(2,1)S(1)}, u32[]{:S(2)}, u32[]{:S(2)}) collective-permute-start(bf16[2,2,48,768]{3,2,1,0:T(8,128)(2,1)S(1)} %get-tuple-element.300), channel_id=1, source_target_pairs={{0,8},{8,0},{16,24},{24,16},{1,9},{9,1},{17,25},{25,17},{2,10},{10... | collective-permute-start | bytes 884744 | tf_op jit(solution)/shard_map/ppermute | solution.py:32
  266.1 8.4 %collective-permute-start.29 = (bf16[1,96,768]{2,1,0:T(8,128)(2,1)S(1)}, bf16[1,96,768]{2,1,0:T(8,128)(2,1)S(1)}, u32[]{:S(2)}, u32[]{:S(2)}) collective-permute-start(bf16[1,96,768]{2,1,0:T(8,128)(2,1)S(1)} %get-tuple-element.302), channel_id=1, source_target_pairs={{0,16},{8,24},{16,0},{24,8},{1,17},{9,25},{17,1},{25,9},{2,18},{10... | collective-permute-start | bytes 442376 | tf_op jit(solution)/shard_map/ppermute | solution.py:32
  268.7 5.3 %collective-permute-start.30 = (f32[5,768]{1,0:T(8,128)S(1)}, f32[5,768]{1,0:T(8,128)S(1)}, u32[]{:S(2)}, u32[]{:S(2)}) collective-permute-start(f32[5,768]{1,0:T(8,128)S(1)} %add.145), channel_id=1, source_target_pairs={{0,4},{4,0},{1,5},{5,1},{2,6},{6,2},{3,7},{7,3},{8,12},{12,8},{9,1... | collective-permute-start | bytes 46088 | tf_op jit(solution)/shard_map/ppermute | solution.py:32
  275.8 12.0 %collective-permute-start.31 = (bf16[2,48,1152]{2,1,0:T(8,128)(2,1)S(1)}, bf16[2,48,1152]{2,1,0:T(8,128)(2,1)S(1)}, u32[]{:S(2)}, u32[]{:S(2)}) collective-permute-start(bf16[2,48,1152]{2,1,0:T(8,128)(2,1)S(1)} %get-tuple-element.312), channel_id=1, source_target_pairs={{0,8},{8,0},{16,24},{24,16},{1,9},{9,1},{17,25},{25,17},{2,10},{10... | collective-permute-start | bytes 663560 | tf_op jit(solution)/shard_map/ppermute | solution.py:32
  278.4 8.6 %collective-permute-start.32 = (bf16[2,48,768]{2,1,0:T(8,128)(2,1)S(1)}, bf16[2,48,768]{2,1,0:T(8,128)(2,1)S(1)}, u32[]{:S(2)}, u32[]{:S(2)}) collective-permute-start(bf16[2,48,768]{2,1,0:T(8,128)(2,1)S(1)} %get-tuple-element.313), channel_id=1, source_target_pairs={{0,1},{1,0},{2,3},{3,2},{4,5},{5,4},{6,7},{7,6},{8,9},{9,8},{10,11... | collective-permute-start | bytes 442376 | tf_op jit(solution)/shard_map/ppermute | solution.py:1612
  279.3 8.5 %collective-permute-start.33 = (bf16[2,48,1152]{2,1,0:T(8,128)(2,1)S(1)}, bf16[2,48,1152]{2,1,0:T(8,128)(2,1)S(1)}, u32[]{:S(2)}, u32[]{:S(2)}) collective-permute-start(bf16[2,48,1152]{2,1,0:T(8,128)(2,1)S(1)} %get-tuple-element.314), channel_id=1, source_target_pairs={{0,4},{4,0},{1,5},{5,1},{2,6},{6,2},{3,7},{7,3},{8,12},{12,8},{9,1... | collective-permute-start | bytes 663560 | tf_op jit(solution)/shard_map/ppermute | solution.py:32
  279.9 7.8 %collective-permute-start.34 = (bf16[1,96,768]{2,1,0:T(8,128)(2,1)S(1)}, bf16[1,96,768]{2,1,0:T(8,128)(2,1)S(1)}, u32[]{:S(2)}, u32[]{:S(2)}) collective-permute-start(bf16[1,96,768]{2,1,0:T(8,128)(2,1)S(1)} %get-tuple-element.315.refs_6_), channel_id=1, source_target_pairs={{0,16},{8,24},{16,0},{24,8},{1,17},{9,25},{17,1},{25,9},{2,18},{10... | collective-permute-start | bytes 442376 | tf_op jit(solution)/shard_map/ppermute | solution.py:32
  281.5 4.6 %collective-permute-start.35 = (f32[5,768]{1,0:T(8,128)S(1)}, f32[5,768]{1,0:T(8,128)S(1)}, u32[]{:S(2)}, u32[]{:S(2)}) collective-permute-start(f32[5,768]{1,0:T(8,128)S(1)} %add.146), channel_id=1, source_target_pairs={{0,8},{8,0},{16,24},{24,16},{1,9},{9,1},{17,25},{25,17},{2,10},{10... | collective-permute-start | bytes 46088 | tf_op jit(solution)/shard_map/ppermute | solution.py:32
  286.1 8.4 %collective-permute-start.37 = (bf16[256,768]{1,0:T(8,128)(2,1)S(1)}, bf16[256,768]{1,0:T(8,128)(2,1)S(1)}, u32[]{:S(2)}, u32[]{:S(2)}) collective-permute-start(bf16[256,768]{1,0:T(8,128)(2,1)S(1)} %get-tuple-element.326), channel_id=1, source_target_pairs={{0,1},{1,0},{2,3},{3,2},{4,5},{5,4},{6,7},{7,6},{8,9},{9,8},{10,11... | collective-permute-start | bytes 1179656 | tf_op jit(solution)/shard_map/ppermute | solution.py:1767
  287.9 13.2 %collective-permute-start.36 = (bf16[1,48,3072]{2,1,0:T(8,128)(2,1)S(1)}, bf16[1,48,3072]{2,1,0:T(8,128)(2,1)S(1)}, u32[]{:S(2)}, u32[]{:S(2)}) collective-permute-start(bf16[1,48,3072]{2,1,0:T(8,128)(2,1)S(1)} %get-tuple-element.324), channel_id=1, source_target_pairs={{0,16},{8,24},{16,0},{24,8},{1,17},{9,25},{17,1},{25,9},{2,18},{10... | collective-permute-start | bytes 884744 | tf_op jit(solution)/shard_map/ppermute | solution.py:32
  289.3 12.1 %collective-permute-start.38 = (bf16[2,96,768]{2,1,0:T(8,128)(2,1)S(1)}, bf16[2,96,768]{2,1,0:T(8,128)(2,1)S(1)}, u32[]{:S(2)}, u32[]{:S(2)}) collective-permute-start(bf16[2,96,768]{2,1,0:T(8,128)(2,1)S(1)} %get-tuple-element.328.refs_2_), channel_id=1, source_target_pairs={{0,8},{8,0},{16,24},{24,16},{1,9},{9,1},{17,25},{25,17},{2,10},{10... | collective-permute-start | bytes 884744 | tf_op jit(solution)/shard_map/ppermute | solution.py:32
  291.0 10.4 %collective-permute-start.39 = (f32[5,768]{1,0:T(8,128)S(1)}, f32[5,768]{1,0:T(8,128)S(1)}, u32[]{:S(2)}, u32[]{:S(2)}) collective-permute-start(f32[5,768]{1,0:T(8,128)S(1)} %add.147), channel_id=1, source_target_pairs={{0,16},{8,24},{16,0},{24,8},{1,17},{9,25},{17,1},{25,9},{2,18},{10... | collective-permute-start | bytes 46088 | tf_op jit(solution)/shard_map/ppermute | solution.py:32
  301.5 15.7 %collective-permute-start.42 = (bf16[4,96,768]{2,1,0:T(8,128)(2,1)S(1)}, bf16[4,96,768]{2,1,0:T(8,128)(2,1)S(1)}, u32[]{:S(2)}, u32[]{:S(2)}) collective-permute-start(bf16[4,96,768]{2,1,0:T(8,128)(2,1)S(1)} %get-tuple-element.335.refs_2_), channel_id=1, source_target_pairs={{0,4},{4,0},{1,5},{5,1},{2,6},{6,2},{3,7},{7,3},{8,12},{12,8},{9,1... | collective-permute-start | bytes 1769480 | tf_op jit(solution)/shard_map/ppermute | solution.py:32
  302.7 9.4 %collective-permute-start.41 = (bf16[256,768]{1,0:T(8,128)(2,1)S(1)}, bf16[256,768]{1,0:T(8,128)(2,1)S(1)}, u32[]{:S(2)}, u32[]{:S(2)}) collective-permute-start(bf16[256,768]{1,0:T(8,128)(2,1)S(1)} %get-tuple-element.333), channel_id=1, source_target_pairs={{0,1},{1,0},{2,3},{3,2},{4,5},{5,4},{6,7},{7,6},{8,9},{9,8},{10,11... | collective-permute-start | bytes 1179656 | tf_op jit(solution)/shard_map/ppermute | solution.py:1767
  303.7 13.5 %collective-permute-start.40 = (bf16[1,48,3072]{2,1,0:T(8,128)(2,1)S(1)}, bf16[1,48,3072]{2,1,0:T(8,128)(2,1)S(1)}, u32[]{:S(2)}, u32[]{:S(2)}) collective-permute-start(bf16[1,48,3072]{2,1,0:T(8,128)(2,1)S(1)} %get-tuple-element.332.refs_0_), channel_id=1, source_target_pairs={{0,16},{8,24},{16,0},{24,8},{1,17},{9,25},{17,1},{25,9},{2,18},{10... | collective-permute-start | bytes 884744 | tf_op jit(solution)/shard_map/ppermute | solution.py:32
  317.3 9.6 %collective-permute-start.45 = (bf16[8,96,768]{2,1,0:T(8,128)(2,1)S(1)}, bf16[8,96,768]{2,1,0:T(8,128)(2,1)S(1)}, u32[]{:S(2)}, u32[]{:S(2)}) collective-permute-start(bf16[8,96,768]{2,1,0:T(8,128)(2,1)S(1)} %get-tuple-element.346.part_ref), channel_id=1, source_target_pairs={{0,2},{2,0},{1,3},{3,1},{4,6},{6,4},{5,7},{7,5},{8,10},{10,8},{9,1... | collective-permute-start | bytes 3538952 | tf_op jit(solution)/shard_map/ppermute | solution.py:1526
  317.4 9.4 %collective-permute-start.43 = (bf16[2,48,1536]{2,1,0:T(8,128)(2,1)S(1)}, bf16[2,48,1536]{2,1,0:T(8,128)(2,1)S(1)}, u32[]{:S(2)}, u32[]{:S(2)}) collective-permute-start(bf16[2,48,1536]{2,1,0:T(8,128)(2,1)S(1)} %get-tuple-element.338.refs_0_), channel_id=1, source_target_pairs={{0,8},{8,0},{16,24},{24,16},{1,9},{9,1},{17,25},{25,17},{2,10},{10... | collective-permute-start | bytes 884744 | tf_op jit(solution)/shard_map/ppermute | solution.py:32
  317.5 9.4 %collective-permute-start.44 = (bf16[2,48,1536]{2,1,0:T(8,128)(2,1)S(1)}, bf16[2,48,1536]{2,1,0:T(8,128)(2,1)S(1)}, u32[]{:S(2)}, u32[]{:S(2)}) collective-permute-start(bf16[2,48,1536]{2,1,0:T(8,128)(2,1)S(1)} %get-tuple-element.339.refs_2_), channel_id=1, source_target_pairs={{0,4},{4,0},{1,5},{5,1},{2,6},{6,2},{3,7},{7,3},{8,12},{12,8},{9,1... | collective-permute-start | bytes 884744 | tf_op jit(solution)/shard_map/ppermute | solution.py:32
  327.0 14.9 %collective-permute-start.46 = (bf16[4,48,1536]{2,1,0:T(8,128)(2,1)S(1)}, bf16[4,48,1536]{2,1,0:T(8,128)(2,1)S(1)}, u32[]{:S(2)}, u32[]{:S(2)}) collective-permute-start(bf16[4,48,1536]{2,1,0:T(8,128)(2,1)S(1)} %get-tuple-element.343.refs_0_), channel_id=1, source_target_pairs={{0,4},{4,0},{1,5},{5,1},{2,6},{6,2},{3,7},{7,3},{8,12},{12,8},{9,1... | collective-permute-start | bytes 1769480 | tf_op jit(solution)/shard_map/ppermute | solution.py:32
  327.5 14.6 %collective-permute-start.47 = (bf16[4,48,1536]{2,1,0:T(8,128)(2,1)S(1)}, bf16[4,48,1536]{2,1,0:T(8,128)(2,1)S(1)}, u32[]{:S(2)}, u32[]{:S(2)}) collective-permute-start(bf16[4,48,1536]{2,1,0:T(8,128)(2,1)S(1)} %get-tuple-element.344.refs_2_), channel_id=1, source_target_pairs={{0,8},{8,0},{16,24},{24,16},{1,9},{9,1},{17,25},{25,17},{2,10},{10... | collective-permute-start | bytes 1769480 | tf_op jit(solution)/shard_map/ppermute | solution.py:32
  342.2 4.6 %collective-permute-start.48 = (bf16[8,48,3072]{2,1,0:T(8,128)(2,1)S(1)}, bf16[8,48,3072]{2,1,0:T(8,128)(2,1)S(1)}, u32[]{:S(2)}, u32[]{:S(2)}) collective-permute-start(bf16[8,48,3072]{2,1,0:T(8,128)(2,1)S(1)} %phase.17.part_ref), channel_id=1, source_target_pairs={{0,2},{2,0},{1,3},{3,1},{4,6},{6,4},{5,7},{7,5},{8,10},{10,8},{9,1... | collective-permute-start | bytes 7077896 | tf_op jit(solution)/shard_map/ppermute | solution.py:1526
  (30 other events, 81.7 us)

commit v6 on v5

--- a/solution.py
+++ b/solution.py
@@ -1051,11 +1051,12 @@
     up, down = Weight(moves, ups_far, wup_ref, 1), Weight(moves, downs_far, wdown_ref, 0)
     ds, dus = Chunks(moves, d_far, d_ref, 1), Chunks(moves, du_far, du_buf, 1, True, True)
     number = 2 * up.number
-    start_loads(down, up)
-    for j in range(2):
-        ds.start(j)
+    for chunks in (down.own, ds, up.own):
+        chunks.start(0)
     then = [moves.later(*t) for t in ((wout_far, wout_ref), (h1_far, h1_ref))]
     first()
+    for chunks in (down.own, ds, up.own):
+        chunks.start(1)
     dm_ref[...] = dy_ref[...].astype(BF16)
     dn_ref[...] = jnp.zeros_like(dn_ref)
 
@@ -1182,11 +1183,12 @@
         return pltpu.make_async_copy(out_ref.at[side, y], far.at[y], sems.at[last + side * 2 + y])
 
     ready = [moves.whole(dy_far, dy_ref), moves.whole(dm2_far, dm_ref.at[pl.ds(n, 2 * n)])]
-    for i in range(2):
-        for c in loads(i):
-            c.start()
+    for c in loads(0):
+        c.start()
     for wait in ready:
         wait()
+    for c in loads(1):
+        c.start()
     dm_ref[:n] = dy_ref[...].astype(BF16)
 
     def step(i, _):

time: 357 us -> 357 us (level)
  no operation moved by 1% of the time
where the time goes in v6:
time: 357 us; the launch traced here: 350 us
  Pallas kernels  171 us (48%)
  waiting for transfers between devices  84.4 us (24%)
  starting transfers between devices  46.9 us (13%)
  other arithmetic  27.7 us (8%)
  local copies, waits for them, and re-layouts  18.4 us (5%)
    pallas_call x23, Pallas kernels, resident(): pl.pallas_call(body, in_specs=[s for _, s in ins], out_specs=[s for _, s...  166 us
    ppermute x23, waiting for transfers between devices, flip_bit(): return lax.ppermute(array, axis, [(i, i ^ bit) for i in range(size)])  52.3 us
    ppermute x23, starting transfers between devices, flip_bit(): return lax.ppermute(array, axis, [(i, i ^ bit) for i in range(size)])  28.7 us
    ppermute x9, waiting for transfers between devices, partner(): return lax.ppermute(t, 'tensor', FLIP)  18.9 us
    ppermute x9, starting transfers between devices, partner(): return lax.ppermute(t, 'tensor', FLIP)  10.7 us
    another operation x11, other arithmetic, ordered(): jnp.stack([jnp.where(first, mine, theirs), jnp.where(first, theirs, mine)])  7.45 us
  transfers between devices with their start and end apart: 49, of which 29 were waited for; matrix products, arithmetic and copies ran while one was open for 10% of the time, Pallas kernels for 31%

profile of v6, /device:TPU:0, one launch (start us, length us, event | category | flops | bytes accessed | tf_op | source)
XLA Modules:
  0.0 349.9 jit_solution(5965170175345345946)
XLA Ops:
  0.7 2.0 constant_dynamic-slice_fusion.7
  2.8 3.0 collective-permute-start
  5.8 1.3 convert_reduce_fusion
  9.2 1.6 add_convert_fusion.3.a_ref.ae_far
  11.9 2.4 attend_first.2
  16.7 1.2 constant_dynamic-slice_fusion.4.cot_far
  18.0 1.5 collective-permute-start.1
  19.5 1.9 constant_dynamic-slice_fusion.2
  22.9 1.6 collective-permute-start.2
  24.5 5.5 %collective-permute-done.1 = bf16[576,384]{1,0:T(8,128)(2,1)} collective-permute-done((bf16[576,384]{1,0:T(8,128)(2,1)}, bf16[576,384]{1,0:T(8,128)(2,1)}, u32[]{:S(2)}, u32[]{:S(2)}) %collective-permute-start.1) | collective-permute-done | bytes 442400 | tf_op jit(solution)/shard_map/ppermute | solution.py:1736
  29.9 1.2 select_bitcast_fusion.5
  32.2 7.2 %collective-permute-done.2 = bf16[96,768]{1,0:T(8,128)(2,1)} collective-permute-done((bf16[96,768]{1,0:T(8,128)(2,1)S(1)}, bf16[96,768]{1,0:T(8,128)(2,1)}, u32[]{:S(2)}, u32[]{:S(2)}) %collective-permute-start.2) | collective-permute-done | bytes 147488 | tf_op jit(solution)/shard_map/ppermute | solution.py:1769
  42.2 1.6 select_bitcast_fusion.1
  44.0 1.3 copy-done.7
  45.3 2.1 pad_maximum_fusion.w_far
  47.3 2.4 attend_first.3
  49.8 1.6 pad_maximum_fusion.2.qkve_far
  56.4 10.0 %mlp_own.1 = (f32[512,768]{1,0:T(8,128)}, bf16[512,768]{1,0:T(8,128)(2,1)}, bf16[512,3072]{1,0:T(8,128)(2,1)}, bf16[512,3072]{1,0:T(8,128)(2,1)}, f32[512,768]{1,0:T(8,128)}, /*index=5*/bf16[1024,768]{1,0:T(8,128)(2,1)}) custom-call(bf16[512,768]{1,0:T(8,128)(2,1)} %bitcast.59, bf16[512,768]{1,0:T(8,128)(2,1)} %pad_maximum_fusion.10.o_far.o1_far, ...), custom_call_target="tpu_custom_call" | custom-call | tf_op jit(solution)/shard_map/mlp_own/pallas_call | solution.py:112
  66.4 2.9 collective-permute-done.5.refs_4_.refs_6_
  69.9 2.8 collective-permute-done.9.refs_2_.refs_3_
  72.7 1.2 collective-permute-done.10.refs_3_.refs_4_
  75.1 8.4 %mlp_other.1 = (bf16[512,3072]{1,0:T(8,128)(2,1)}, bf16[512,3072]{1,0:T(8,128)(2,1)}, f32[512,768]{1,0:T(8,128)}, bf16[512,768]{1,0:T(8,128)(2,1)}) custom-call(bf16[512,768]{1,0:T(8,128)(2,1)} %get-tuple-element.209.n2_far.n1_far, f32[512,768]{1,0:T(8,128)} %get-tuple-element.210.part_far, ...), custom_call_target="tpu_custom_call", output_to_operand_aliasing={{0}: (2, {}), {1}: (3, {})} | custom-call | tf_op jit(solution)/shard_map/mlp_other/pallas_call | solution.py:112
  83.6 13.6 %attend_second.1 = (bf16[3,512,768]{2,1,0:T(8,128)(2,1)}, bf16[2,512,768]{2,1,0:T(8,128)(2,1)}, f32[2,3,4,512]{3,2,1,0:T(4,128)S(1)}) custom-call(bf16[512,768]{1,0:T(8,128)(2,1)} %get-tuple-element.215.a_far.ao_far, bf16[3,768,768]{2,1,0:T(8,128)(2,1)} %pad_maximum_fusion.w_far, f32[2,256,256]{2,1,0:T(8,128)} %copy-done.2, ...), custom_call_target="tpu_custom_call" | custom-call | flops 415236096 | tf_op jit(solution)/shard_map/attend_second/pallas_call | solution.py:112
  97.2 34.7 %mlp_second.1 = (bf16[1,512,768]{2,1,0:T(8,128)(2,1)}, bf16[1,512,768]{2,1,0:T(8,128)(2,1)}, bf16[1024,768]{1,0:T(8,128)(2,1)}, bf16[1024,3072]{1,0:T(8,128)(2,1...) custom-call(bf16[512,768]{1,0:T(8,128)(2,1)} %bitcast.60, ...), custom_call_target="tpu_custom_call" | custom-call | tf_op jit(solution)/shard_map/mlp_second/pallas_call | solution.py:112
  133.0 18.9 %attend_back.1 = (bf16[3,512,768]{2,1,0:T(8,128)(2,1)}, bf16[3,512,768]{2,1,0:T(8,128)(2,1)}, f32[512,768]{1,0:T(8,128)}, f32[3,768]{1,0:T(4,128)S(1)}) custom-call(bf16[3,768,768]{2,1,0:T(8,128)(2,1)} %pad_maximum_fusion.w_far, f32[2,256,256]{2,1,0:T(8,128)} %copy-done.2, f32[2,256,256]{2,1,0:T(8,128)} %get-tuple-element.402.strict_far, ...), custom_call_target="tpu_custom_call" | custom-call | flops 868220928 | tf_op jit(solution)/shard_map/attend_back/pallas_call | solution.py:112
  153.1 14.1 %grad_down.1 = (bf16[2,8,96,768]{3,2,1,0:T(8,128)(2,1)}, bf16[2,8,96,768]{3,2,1,0:T(8,128)(2,1)}) custom-call(s32[2]{0:T(128)S(1)} %copy-done.21, bf16[512,3072]{1,0:T(8,128)(2,1)} %get-tuple-element.217.g1_far, bf16[1024,3072]{1,0:T(8,128)(2,1)} %get-tuple-element.224.g2_far, f32[512,768]{1,0:T(8,128)} %get-tuple-element.239.dy_far, ...), custom_call_target="tpu_custom_call" | custom-call | flops 452984832 | tf_op jit(solution)/shard_map/grad_down/pallas_call | solution.py:112
  168.4 12.9 %mlp_back.1 = (bf16[512,3072]{1,0:T(8,128)(2,1)}, f32[512,768]{1,0:T(8,128)}, bf16[512,768]{1,0:T(8,128)(2,1)}, bf16[512,768]{1,0:T(8,128)(2,1)}, f32[2,768]{1,0:T(2,128)S(1)}) custom-call(f32[512,768]{1,0:T(8,128)} %get-tuple-element.239.dy_far, f32[512,768]{1,0:T(8,128)} %get-tuple-element.240.h1_far, bf16[768,768]{1,0:T(8,128)(2,1)} %pad_maximum_fusion.8.wout_far, ...), custom_call_target="tpu_custom_call" | custom-call | tf_op jit(solution)/shard_map/mlp_back/pallas_call | solution.py:112
  183.3 16.7 %grad_up.1 = (bf16[2,8,48,1920]{3,2,1,0:T(8,128)(2,1)}, bf16[2,8,48,1920]{3,2,1,0:T(8,128)(2,1)}) custom-call(s32[3]{0:T(128)} %pad_add_fusion.me_ref, bf16[512,768]{1,0:T(8,128)(2,1)} %get-tuple-element.209.n2_far.n1_far, bf16[1024,768]{1,0:T(8,128)(2,1)} %get-tuple-element.248.n2_far, bf16[512,3072]{1,0:T(8,128)(2,1)} %get-tuple-element.250.du1_far, ...), custom_call_target="tpu_custom_call" | custom-call | flops 566231040 | tf_op jit(solution)/shard_map/grad_up/pallas_call | solution.py:112
  200.0 12.8 %attend_back_even.1 = (bf16[3,512,768]{2,1,0:T(8,128)(2,1)}, bf16[512,768]{1,0:T(8,128)(2,1)S(1)}, f32[2,768]{1,0:T(2,128)S(1)}) custom-call(bf16[3,768,768]{2,1,0:T(8,128)(2,1)} %pad_maximum_fusion.w_far, f32[2,256,256]{2,1,0:T(8,128)} %copy-done.2, bf16[3,512,768]{2,1,0:T(8,128)(2,1)} %pad_maximum_fusion.2.qkve_far, ...), custom_call_target="tpu_custom_call" | custom-call | flops 364904448 | tf_op jit(solution)/shard_map/attend_back_even/pallas_call | solution.py:112
  213.7 1.6 collective-permute-start.17
  215.3 9.8 %grad_qkv.1 = (bf16[2,8,48,1152]{3,2,1,0:T(8,128)(2,1)}, bf16[2,8,48,1152]{3,2,1,0:T(8,128)(2,1)}) custom-call(s32[3]{0:T(128)S(1)} %copy-done.20, bf16[512,768]{1,0:T(8,128)(2,1)} %copy-done.4, bf16[512,768]{1,0:T(8,128)(2,1)} %get-tuple-element.215.a_far.ao_far, bf16[3,512,768]{2,1,0:T(8,128)(2,1)} %get-tuple-element.264.de_far, ...), custom_call_target="tpu_custom_call" | custom-call | flops 226492416 | tf_op jit(solution)/shard_map/grad_qkv/pallas_call | solution.py:112
  226.9 1.3 fusion.5
  230.5 1.6 collective-permute-start.20
  233.9 1.9 add_convert_fusion.2
  237.9 1.5 collective-permute-start.19
  241.2 2.0 broadcast_select_fusion.1
  244.2 1.9 pad_maximum_fusion.1
  246.1 8.3 %collective-permute-done.19.refs_1_ = bf16[2,4,48,768]{3,2,1,0:T(8,128)(2,1)} collective-permute-done((bf16[2,4,48,768]{3,2,1,0:T(8,128)(2,1)}, bf16[2,4,48,768]{3,2,1,0:T(8,128)(2,1)}, u32[]{:S(2)}, u32[]{:S(2)}) %collective-permute-start.19) | collective-permute-done | bytes 589856 | tf_op jit(solution)/shard_map/ppermute | solution.py:32
  254.4 5.1 %collective-permute-done.24.refs_7_ = bf16[2,96,768]{2,1,0:T(8,128)(2,1)S(1)} collective-permute-done((bf16[2,96,768]{2,1,0:T(8,128)(2,1)S(1)}, bf16[2,96,768]{2,1,0:T(8,128)(2,1)S(1)}, u32[]{:S(2)}, u32[]{:S(2)}) %collective-permute-start.24) | collective-permute-done | bytes 294944 | tf_op jit(solution)/shard_map/ppermute | solution.py:32
  259.5 2.2 phase.11
  261.8 1.6 collective-permute-start.26
  264.1 1.6 collective-permute-start.27
  265.7 2.6 collective-permute-start.29
  269.0 4.6 %collective-permute-done.30 = f32[5,768]{1,0:T(8,128)S(1)} collective-permute-done((f32[5,768]{1,0:T(8,128)S(1)}, f32[5,768]{1,0:T(8,128)S(1)}, u32[]{:S(2)}, u32[]{:S(2)}) %collective-permute-start.30) | collective-permute-done | bytes 15392 | tf_op jit(solution)/shard_map/ppermute | solution.py:32
  275.4 2.7 collective-permute-start.31
  279.6 1.6 collective-permute-start.34
  281.6 4.2 %collective-permute-done.35 = f32[5,768]{1,0:T(8,128)S(1)} collective-permute-done((f32[5,768]{1,0:T(8,128)S(1)}, f32[5,768]{1,0:T(8,128)S(1)}, u32[]{:S(2)}, u32[]{:S(2)}) %collective-permute-start.35) | collective-permute-done | bytes 15392 | tf_op jit(solution)/shard_map/ppermute | solution.py:32
  287.6 1.4 collective-permute-start.36
  289.0 1.6 collective-permute-start.38
  291.8 2.3 collective-permute-done.37
  294.1 6.6 %collective-permute-done.36.refs_1_ = bf16[1,48,3072]{2,1,0:T(8,128)(2,1)S(1)} collective-permute-done((bf16[1,48,3072]{2,1,0:T(8,128)(2,1)S(1)}, bf16[1,48,3072]{2,1,0:T(8,128)(2,1)S(1)}, u32[]{:S(2)}, u32[]{:S(2)}) %collective-permute-start.36) | collective-permute-done | bytes 294944 | tf_op jit(solution)/shard_map/ppermute | solution.py:32
  301.1 1.3 collective-permute-start.42
  303.3 1.9 collective-permute-start.40
  305.3 6.5 %collective-permute-done.41 = bf16[256,768]{1,0:T(8,128)(2,1)S(1)} collective-permute-done((bf16[256,768]{1,0:T(8,128)(2,1)S(1)}, bf16[256,768]{1,0:T(8,128)(2,1)S(1)}, u32[]{:S(2)}, u32[]{:S(2)}) %collective-permute-start.41) | collective-permute-done | bytes 393248 | tf_op jit(solution)/shard_map/ppermute | solution.py:1769
  311.7 5.1 %collective-permute-done.40.refs_1_ = bf16[1,48,3072]{2,1,0:T(8,128)(2,1)S(1)} collective-permute-done((bf16[1,48,3072]{2,1,0:T(8,128)(2,1)S(1)}, bf16[1,48,3072]{2,1,0:T(8,128)(2,1)S(1)}, u32[]{:S(2)}, u32[]{:S(2)}) %collective-permute-start.40) | collective-permute-done | bytes 294944 | tf_op jit(solution)/shard_map/ppermute | solution.py:32
  318.3 8.2 %collective-permute-done.43.refs_1_ = bf16[2,48,1536]{2,1,0:T(8,128)(2,1)S(1)} collective-permute-done((bf16[2,48,1536]{2,1,0:T(8,128)(2,1)S(1)}, bf16[2,48,1536]{2,1,0:T(8,128)(2,1)S(1)}, u32[]{:S(2)}, u32[]{:S(2)}) %collective-permute-start.43) | collective-permute-done | bytes 294944 | tf_op jit(solution)/shard_map/ppermute | solution.py:32
  327.1 1.7 collective-permute-start.47
  329.7 1.9 convert.1
  331.7 2.1 unpack_down.2.refs_0_
  333.8 2.1 unpack_down.3
  335.9 5.7 %collective-permute-done.46.refs_1_ = bf16[4,48,1536]{2,1,0:T(8,128)(2,1)S(1)} collective-permute-done((bf16[4,48,1536]{2,1,0:T(8,128)(2,1)S(1)}, bf16[4,48,1536]{2,1,0:T(8,128)(2,1)S(1)}, u32[]{:S(2)}, u32[]{:S(2)}) %collective-permute-start.46) | collective-permute-done | bytes 589856 | tf_op jit(solution)/shard_map/ppermute | solution.py:32
  342.0 3.0 unpack_rest.2
  344.9 1.6 collective-permute-done.48.part_ref
  346.5 2.9 unpack_rest.3
  (212 shorter events, 47.6 us)
Async XLA Ops:
  0.6 16.1 %copy-start = (bf16[4,512,768]{2,1,0:T(8,128)(2,1)S(1)}, bf16[4,512,768]{2,1,0:T(8,128)(2,1)}, u32[]{:S(2)}) copy-start(bf16[4,512,768]{2,1,0:T(8,128)(2,1)} %param.19) | copy-start | bytes 9437188
  0.7 8.4 %copy-start.37 = (f32[2,768]{1,0:T(2,128)S(1)}, f32[2,768]{1,0:T(2,128)}, u32[]{:S(2)}) copy-start(f32[2,768]{1,0:T(2,128)} %param.18) | copy-start | bytes 18436
  2.8 15.2 %collective-permute-start = (bf16[576,384]{1,0:T(8,128)(2,1)}, bf16[576,384]{1,0:T(8,128)(2,1)}, u32[]{:S(2)}, u32[]{:S(2)}) collective-permute-start(bf16[576,384]{1,0:T(8,128)(2,1)} %constant_dynamic-slice_fusion.7), channel_id=1, source_target_pairs={{0,1},{1,0},{2,3},{3,2},{4,5},{5,4},{6,7},{7,6},{8,9},{9,8},{10,11... | collective-permute-start | bytes 1327112 | tf_op jit(solution)/shard_map/ppermute | solution.py:1769
  18.0 11.9 %collective-permute-start.1 = (bf16[576,384]{1,0:T(8,128)(2,1)}, bf16[576,384]{1,0:T(8,128)(2,1)}, u32[]{:S(2)}, u32[]{:S(2)}) collective-permute-start(bf16[576,384]{1,0:T(8,128)(2,1)} %collective-permute-done), channel_id=1, source_target_pairs={{0,4},{4,0},{1,5},{5,1},{2,6},{6,2},{3,7},{7,3},{8,12},{12,8},{9,1... | collective-permute-start | bytes 1327112 | tf_op jit(solution)/shard_map/ppermute | solution.py:1736
  21.4 18.0 %collective-permute-start.3 = (bf16[768,384]{1,0:T(8,128)(2,1)}, bf16[768,384]{1,0:T(8,128)(2,1)S(1)}, u32[]{:S(2)}, u32[]{:S(2)}) collective-permute-start(bf16[768,384]{1,0:T(8,128)(2,1)} %constant_dynamic-slice_fusion.2), channel_id=1, source_target_pairs={{0,1},{1,0},{2,3},{3,2},{4,5},{5,4},{6,7},{7,6},{8,9},{9,8},{10,11... | collective-permute-start | bytes 1769480 | tf_op jit(solution)/shard_map/ppermute | solution.py:1769
  22.9 16.5 %collective-permute-start.2 = (bf16[96,768]{1,0:T(8,128)(2,1)S(1)}, bf16[96,768]{1,0:T(8,128)(2,1)}, u32[]{:S(2)}, u32[]{:S(2)}) collective-permute-start(bf16[96,768]{1,0:T(8,128)(2,1)S(1)} %constant_dynamic-slice_fusion.3), channel_id=1, source_target_pairs={{0,1},{1,0},{2,3},{3,2},{4,5},{5,4},{6,7},{7,6},{8,9},{9,8},{10,11... | collective-permute-start | bytes 442376 | tf_op jit(solution)/shard_map/ppermute | solution.py:1769
  24.5 15.0 %copy-start.22 = (bf16[1536,768]{1,0:T(8,128)(2,1)S(1)}, bf16[1536,768]{1,0:T(8,128)(2,1)}, u32[]{:S(2)}) copy-start(bf16[1536,768]{1,0:T(8,128)(2,1)} %refs_5_.3) | copy-start | bytes 7077892
  39.4 2.8 collective-permute-start.6
  40.6 28.6 %collective-permute-start.5 = (bf16[768,768]{1,0:T(8,128)(2,1)}, bf16[768,768]{1,0:T(8,128)(2,1)}, u32[]{:S(2)}, u32[]{:S(2)}) collective-permute-start(bf16[768,768]{1,0:T(8,128)(2,1)} %pad_maximum_fusion.7), channel_id=1, source_target_pairs={{0,1},{1,0},{2,3},{3,2},{4,5},{5,4},{6,7},{7,6},{8,9},{9,8},{10,11... | collective-permute-start | bytes 3538952 | tf_op jit(solution)/shard_map/ppermute | solution.py:1769
  41.2 11.2 %collective-permute-start.7 = (bf16[96,768]{1,0:T(8,128)(2,1)}, bf16[96,768]{1,0:T(8,128)(2,1)}, u32[]{:S(2)}, u32[]{:S(2)}) collective-permute-start(bf16[96,768]{1,0:T(8,128)(2,1)} %collective-permute-done.2), channel_id=1, source_target_pairs={{0,4},{4,0},{1,5},{5,1},{2,6},{6,2},{3,7},{7,3},{8,12},{12,8},{9,1... | collective-permute-start | bytes 442376 | tf_op jit(solution)/shard_map/ppermute | solution.py:1736
  53.5 1.6 collective-permute-start.8
  53.7 15.7 %collective-permute-start.4 = (bf16[768,384]{1,0:T(8,128)(2,1)S(1)}, bf16[768,384]{1,0:T(8,128)(2,1)S(1)}, u32[]{:S(2)}, u32[]{:S(2)}) collective-permute-start(bf16[768,384]{1,0:T(8,128)(2,1)S(1)} %copy-done.26), channel_id=1, source_target_pairs={{0,4},{4,0},{1,5},{5,1},{2,6},{6,2},{3,7},{7,3},{8,12},{12,8},{9,1... | collective-permute-start | bytes 1769480 | tf_op jit(solution)/shard_map/ppermute | solution.py:1736
  54.7 19.4 %copy-start.12 = (f32[5,768]{1,0:T(8,128)}, f32[5,768]{1,0:T(8,128)S(1)}, u32[]{:S(2)}) copy-start(f32[5,768]{1,0:T(8,128)S(1)} %pad_maximum_fusion.14.gb_ref) | copy-start | bytes 46084
  69.4 4.7 %collective-permute-start.11 = (bf16[768,768]{1,0:T(8,128)(2,1)}, bf16[768,768]{1,0:T(8,128)(2,1)S(1)}, u32[]{:S(2)}, u32[]{:S(2)}) collective-permute-start(bf16[768,768]{1,0:T(8,128)(2,1)} %collective-permute-done.5.refs_4_.refs_6_), channel_id=1, source_target_pairs={{0,2},{2,0},{1,3},{3,1},{4,6},{6,4},{5,7},{7,5},{8,10},{10,8},{9,1... | collective-permute-start | bytes 3538952 | tf_op jit(solution)/shard_map/ppermute | solution.py:1772
  69.4 3.3 collective-permute-start.9
  69.9 4.0 %collective-permute-start.10 = (bf16[768,384]{1,0:T(8,128)(2,1)S(1)}, bf16[768,384]{1,0:T(8,128)(2,1)S(1)}, u32[]{:S(2)}, u32[]{:S(2)}) collective-permute-start(bf16[768,384]{1,0:T(8,128)(2,1)S(1)} %collective-permute-done.4.refs_1_.refs_2_), channel_id=1, source_target_pairs={{0,2},{2,0},{1,3},{3,1},{4,6},{6,4},{5,7},{7,5},{8,10},{10,8},{9,1... | collective-permute-start | bytes 1769480 | tf_op jit(solution)/shard_map/ppermute | solution.py:1772
  97.2 35.8 %copy-start.13 = (f32[5,768]{1,0:T(8,128)S(1)}, f32[5,768]{1,0:T(8,128)}, u32[]{:S(2)}) copy-start(f32[5,768]{1,0:T(8,128)} %copy-done.12) | copy-start | bytes 46084
  131.9 20.1 %collective-permute-start.12 = (bf16[1,512,768]{2,1,0:T(8,128)(2,1)}, bf16[1,512,768]{2,1,0:T(8,128)(2,1)S(1)}, u32[]{:S(2)}, u32[]{:S(2)}) collective-permute-start(bf16[1,512,768]{2,1,0:T(8,128)(2,1)} %get-tuple-element.225), channel_id=1, source_target_pairs={{0,1},{1,0},{2,3},{3,2},{4,5},{5,4},{6,7},{7,6},{8,9},{9,8},{10,11... | collective-permute-start | bytes 2359304 | tf_op jit(solution)/shard_map/ppermute | solution.py:1769
  133.0 18.9 %copy-start.30 = (bf16[1,512,768]{2,1,0:T(8,128)(2,1)S(1)}, bf16[1,512,768]{2,1,0:T(8,128)(2,1)}, u32[]{:S(2)}) copy-start(bf16[1,512,768]{2,1,0:T(8,128)(2,1)} %get-tuple-element.234) | copy-start | bytes 2359300
  133.0 20.1 %copy-start.21 = (s32[2]{0:T(128)S(1)}, s32[2]{0:T(128)}, u32[]{:S(2)}) copy-start(s32[2]{0:T(128)} %rev.3.me_ref) | copy-start | bytes 28
  152.0 15.2 %copy-start.35 = (bf16[1,512,768]{2,1,0:T(8,128)(2,1)}, bf16[1,512,768]{2,1,0:T(8,128)(2,1)S(1)}, u32[]{:S(2)}) copy-start(bf16[1,512,768]{2,1,0:T(8,128)(2,1)S(1)} %collective-permute-done.12) | copy-start | bytes 2359300
  152.0 15.2 %collective-permute-start.13 = (bf16[1,256,768]{2,1,0:T(8,128)(2,1)S(1)}, bf16[1,256,768]{2,1,0:T(8,128)(2,1)S(1)}, u32[]{:S(2)}, u32[]{:S(2)}) collective-permute-start(bf16[1,256,768]{2,1,0:T(8,128)(2,1)S(1)} %get-tuple-element.236), channel_id=1, source_target_pairs={{0,1},{1,0},{2,3},{3,2},{4,5},{5,4},{6,7},{7,6},{8,9},{9,8},{10,11... | collective-permute-start | bytes 1179656 | tf_op jit(solution)/shard_map/ppermute | solution.py:1769
  167.2 14.1 %collective-permute-start.14 = (bf16[2,8,96,768]{3,2,1,0:T(8,128)(2,1)}, bf16[2,8,96,768]{3,2,1,0:T(8,128)(2,1)S(1)}, u32[]{:S(2)}, u32[]{:S(2)}) collective-permute-start(bf16[2,8,96,768]{3,2,1,0:T(8,128)(2,1)} %get-tuple-element.238), channel_id=1, source_target_pairs={{0,2},{2,0},{1,3},{3,1},{4,6},{6,4},{5,7},{7,5},{8,10},{10,8},{9,1... | collective-permute-start | bytes 7077896 | tf_op jit(solution)/shard_map/ppermute | solution.py:1772
  167.3 14.0 %collective-permute-start.15 = (bf16[1,256,768]{2,1,0:T(8,128)(2,1)S(1)}, bf16[1,256,768]{2,1,0:T(8,128)(2,1)S(1)}, u32[]{:S(2)}, u32[]{:S(2)}) collective-permute-start(bf16[1,256,768]{2,1,0:T(8,128)(2,1)S(1)} %get-tuple-element.245), channel_id=1, source_target_pairs={{0,1},{1,0},{2,3},{3,2},{4,5},{5,4},{6,7},{7,6},{8,9},{9,8},{10,11... | collective-permute-start | bytes 1179656 | tf_op jit(solution)/shard_map/ppermute | solution.py:1769
  168.4 12.9 %copy-start.32 = (bf16[2,8,96,768]{3,2,1,0:T(8,128)(2,1)S(1)}, bf16[2,8,96,768]{3,2,1,0:T(8,128)(2,1)}, u32[]{:S(2)}) copy-start(bf16[2,8,96,768]{3,2,1,0:T(8,128)(2,1)} %get-tuple-element.237) | copy-start | bytes 7077892
  182.2 30.6 %collective-permute-start.16 = (bf16[8,96,768]{2,1,0:T(8,128)(2,1)S(1)}, bf16[8,96,768]{2,1,0:T(8,128)(2,1)S(1)}, u32[]{:S(2)}, u32[]{:S(2)}) collective-permute-start(bf16[8,96,768]{2,1,0:T(8,128)(2,1)S(1)} %get-tuple-element.376), channel_id=1, source_target_pairs={{0,1},{1,0},{2,3},{3,2},{4,5},{5,4},{6,7},{7,6},{8,9},{9,8},{10,11... | collective-permute-start | bytes 3538952 | tf_op jit(solution)/shard_map/ppermute | solution.py:1525
  200.0 12.8 %copy-start.44 = (bf16[2,8,48,1920]{3,2,1,0:T(8,128)(2,1)S(1)}, bf16[2,8,48,1920]{3,2,1,0:T(8,128)(2,1)}, u32[]{:S(2)}) copy-start(bf16[2,8,48,1920]{3,2,1,0:T(8,128)(2,1)} %get-tuple-element.269) | copy-start | bytes 8847364
  212.8 12.3 %collective-permute-start.18 = (bf16[2,8,48,1920]{3,2,1,0:T(8,128)(2,1)S(1)}, bf16[2,8,48,1920]{3,2,1,0:T(8,128)(2,1)S(1)}, u32[]{:S(2)}, u32[]{:S(2)}) collective-permute-start(bf16[2,8,48,1920]{3,2,1,0:T(8,128)(2,1)S(1)} %copy-done.44), channel_id=1, source_target_pairs={{0,2},{2,0},{1,3},{3,1},{4,6},{6,4},{5,7},{7,5},{8,10},{10,8},{9,1... | collective-permute-start | bytes 8847368 | tf_op jit(solution)/shard_map/ppermute | solution.py:1772
  213.7 11.4 %copy-start.16 = (bf16[4,96,768]{2,1,0:T(8,128)(2,1)}, bf16[4,96,768]{2,1,0:T(8,128)(2,1)S(1)}, u32[]{:S(2)}) copy-start(bf16[4,96,768]{2,1,0:T(8,128)(2,1)S(1)} %get-tuple-element.289.refs_0_) | copy-start | bytes 1769476
  213.7 15.3 %collective-permute-start.17 = (bf16[4,96,768]{2,1,0:T(8,128)(2,1)S(1)}, bf16[4,96,768]{2,1,0:T(8,128)(2,1)S(1)}, u32[]{:S(2)}, u32[]{:S(2)}) collective-permute-start(bf16[4,96,768]{2,1,0:T(8,128)(2,1)S(1)} %get-tuple-element.263), channel_id=1, source_target_pairs={{0,8},{8,0},{16,24},{24,16},{1,9},{9,1},{17,25},{25,17},{2,10},{10... | collective-permute-start | bytes 1769480 | tf_op jit(solution)/shard_map/ppermute | solution.py:32
  215.3 9.9 %copy-start.31 = (bf16[2,8,48,1920]{3,2,1,0:T(8,128)(2,1)S(1)}, bf16[2,8,48,1920]{3,2,1,0:T(8,128)(2,1)}, u32[]{:S(2)}) copy-start(bf16[2,8,48,1920]{3,2,1,0:T(8,128)(2,1)} %get-tuple-element.268) | copy-start | bytes 8847364
  229.8 4.1 %collective-permute-start.21 = (bf16[2,8,48,1152]{3,2,1,0:T(8,128)(2,1)}, bf16[2,8,48,1152]{3,2,1,0:T(8,128)(2,1)}, u32[]{:S(2)}, u32[]{:S(2)}) collective-permute-start(bf16[2,8,48,1152]{3,2,1,0:T(8,128)(2,1)} %get-tuple-element.280), channel_id=1, source_target_pairs={{0,2},{2,0},{1,3},{3,1},{4,6},{6,4},{5,7},{7,5},{8,10},{10,8},{9,1... | collective-permute-start | bytes 5308424 | tf_op jit(solution)/shard_map/ppermute | solution.py:1772
  229.9 3.3 collective-permute-start.22
  230.5 24.0 %collective-permute-start.20 = (bf16[2,4,48,1152]{3,2,1,0:T(8,128)(2,1)}, bf16[2,4,48,1152]{3,2,1,0:T(8,128)(2,1)}, u32[]{:S(2)}, u32[]{:S(2)}) collective-permute-start(bf16[2,4,48,1152]{3,2,1,0:T(8,128)(2,1)} %get-tuple-element.271), channel_id=1, source_target_pairs={{0,8},{8,0},{16,24},{24,16},{1,9},{9,1},{17,25},{25,17},{2,10},{10... | collective-permute-start | bytes 2654216 | tf_op jit(solution)/shard_map/ppermute | solution.py:32
  236.9 22.7 %collective-permute-start.23 = (bf16[8,48,1152]{2,1,0:T(8,128)(2,1)}, bf16[8,48,1152]{2,1,0:T(8,128)(2,1)}, u32[]{:S(2)}, u32[]{:S(2)}) collective-permute-start(bf16[8,48,1152]{2,1,0:T(8,128)(2,1)} %get-tuple-element.380), channel_id=1, source_target_pairs={{0,1},{1,0},{2,3},{3,2},{4,5},{5,4},{6,7},{7,6},{8,9},{9,8},{10,11... | collective-permute-start | bytes 2654216 | tf_op jit(solution)/shard_map/ppermute | solution.py:1614
  237.9 16.5 %collective-permute-start.19 = (bf16[2,4,48,768]{3,2,1,0:T(8,128)(2,1)}, bf16[2,4,48,768]{3,2,1,0:T(8,128)(2,1)}, u32[]{:S(2)}, u32[]{:S(2)}) collective-permute-start(bf16[2,4,48,768]{3,2,1,0:T(8,128)(2,1)} %get-tuple-element.270), channel_id=1, source_target_pairs={{0,4},{4,0},{1,5},{5,1},{2,6},{6,2},{3,7},{7,3},{8,12},{12,8},{9,1... | collective-permute-start | bytes 1769480 | tf_op jit(solution)/shard_map/ppermute | solution.py:32
  239.5 20.0 %collective-permute-start.24 = (bf16[2,96,768]{2,1,0:T(8,128)(2,1)S(1)}, bf16[2,96,768]{2,1,0:T(8,128)(2,1)S(1)}, u32[]{:S(2)}, u32[]{:S(2)}) collective-permute-start(bf16[2,96,768]{2,1,0:T(8,128)(2,1)S(1)} %get-tuple-element.291), channel_id=1, source_target_pairs={{0,4},{4,0},{1,5},{5,1},{2,6},{6,2},{3,7},{7,3},{8,12},{12,8},{9,1... | collective-permute-start | bytes 884744 | tf_op jit(solution)/shard_map/ppermute | solution.py:32
  243.2 16.4 %collective-permute-start.25 = (f32[5,768]{1,0:T(8,128)S(1)}, f32[5,768]{1,0:T(8,128)S(1)}, u32[]{:S(2)}, u32[]{:S(2)}) collective-permute-start(f32[5,768]{1,0:T(8,128)S(1)} %add.144), channel_id=1, source_target_pairs={{0,1},{1,0},{2,3},{3,2},{4,5},{5,4},{6,7},{7,6},{8,9},{9,8},{10,11... | collective-permute-start | bytes 46088 | tf_op jit(solution)/shard_map/ppermute | solution.py:32
  244.2 15.3 %copy-start.8 = (bf16[2,4,48,1152]{3,2,1,0:T(8,128)(2,1)S(1)}, bf16[2,4,48,1152]{3,2,1,0:T(8,128)(2,1)}, u32[]{:S(2)}) copy-start(bf16[2,4,48,1152]{3,2,1,0:T(8,128)(2,1)} %get-tuple-element.275.refs_2_) | copy-start | bytes 2654212
  244.2 15.3 %copy-start.11 = (bf16[2,4,48,768]{3,2,1,0:T(8,128)(2,1)S(1)}, bf16[2,4,48,768]{3,2,1,0:T(8,128)(2,1)}, u32[]{:S(2)}) copy-start(bf16[2,4,48,768]{3,2,1,0:T(8,128)(2,1)} %get-tuple-element.274.refs_0_) | copy-start | bytes 1769476
  261.8 19.7 %copy-start.10 = (bf16[512,768]{1,0:T(8,128)(2,1)S(1)}, bf16[512,768]{1,0:T(8,128)(2,1)}, u32[]{:S(2)}) copy-start(bf16[512,768]{1,0:T(8,128)(2,1)} %copy-done.9) | copy-start | bytes 2359300
  261.8 13.3 %collective-permute-start.26 = (bf16[4,48,1152]{2,1,0:T(8,128)(2,1)S(1)}, bf16[4,48,1152]{2,1,0:T(8,128)(2,1)S(1)}, u32[]{:S(2)}, u32[]{:S(2)}) collective-permute-start(bf16[4,48,1152]{2,1,0:T(8,128)(2,1)S(1)} %get-tuple-element.299), channel_id=1, source_target_pairs={{0,4},{4,0},{1,5},{5,1},{2,6},{6,2},{3,7},{7,3},{8,12},{12,8},{9,1... | collective-permute-start | bytes 1327112 | tf_op jit(solution)/shard_map/ppermute | solution.py:32
  263.3 11.7 %collective-permute-start.28 = (bf16[4,48,1152]{2,1,0:T(8,128)(2,1)S(1)}, bf16[4,48,1152]{2,1,0:T(8,128)(2,1)S(1)}, u32[]{:S(2)}, u32[]{:S(2)}) collective-permute-start(bf16[4,48,1152]{2,1,0:T(8,128)(2,1)S(1)} %get-tuple-element.301), channel_id=1, source_target_pairs={{0,1},{1,0},{2,3},{3,2},{4,5},{5,4},{6,7},{7,6},{8,9},{9,8},{10,11... | collective-permute-start | bytes 1327112 | tf_op jit(solution)/shard_map/ppermute | solution.py:1614
  264.1 10.9 %collective-permute-start.27 = (bf16[2,2,48,768]{3,2,1,0:T(8,128)(2,1)S(1)}, bf16[2,2,48,768]{3,2,1,0:T(8,128)(2,1)S(1)}, u32[]{:S(2)}, u32[]{:S(2)}) collective-permute-start(bf16[2,2,48,768]{3,2,1,0:T(8,128)(2,1)S(1)} %get-tuple-element.300), channel_id=1, source_target_pairs={{0,8},{8,0},{16,24},{24,16},{1,9},{9,1},{17,25},{25,17},{2,10},{10... | collective-permute-start | bytes 884744 | tf_op jit(solution)/shard_map/ppermute | solution.py:32
  265.7 8.4 %collective-permute-start.29 = (bf16[1,96,768]{2,1,0:T(8,128)(2,1)S(1)}, bf16[1,96,768]{2,1,0:T(8,128)(2,1)S(1)}, u32[]{:S(2)}, u32[]{:S(2)}) collective-permute-start(bf16[1,96,768]{2,1,0:T(8,128)(2,1)S(1)} %get-tuple-element.302), channel_id=1, source_target_pairs={{0,16},{8,24},{16,0},{24,8},{1,17},{9,25},{17,1},{25,9},{2,18},{10... | collective-permute-start | bytes 442376 | tf_op jit(solution)/shard_map/ppermute | solution.py:32
  268.3 5.3 %collective-permute-start.30 = (f32[5,768]{1,0:T(8,128)S(1)}, f32[5,768]{1,0:T(8,128)S(1)}, u32[]{:S(2)}, u32[]{:S(2)}) collective-permute-start(f32[5,768]{1,0:T(8,128)S(1)} %add.145), channel_id=1, source_target_pairs={{0,4},{4,0},{1,5},{5,1},{2,6},{6,2},{3,7},{7,3},{8,12},{12,8},{9,1... | collective-permute-start | bytes 46088 | tf_op jit(solution)/shard_map/ppermute | solution.py:32
  275.4 12.0 %collective-permute-start.31 = (bf16[2,48,1152]{2,1,0:T(8,128)(2,1)S(1)}, bf16[2,48,1152]{2,1,0:T(8,128)(2,1)S(1)}, u32[]{:S(2)}, u32[]{:S(2)}) collective-permute-start(bf16[2,48,1152]{2,1,0:T(8,128)(2,1)S(1)} %get-tuple-element.312), channel_id=1, source_target_pairs={{0,8},{8,0},{16,24},{24,16},{1,9},{9,1},{17,25},{25,17},{2,10},{10... | collective-permute-start | bytes 663560 | tf_op jit(solution)/shard_map/ppermute | solution.py:32
  278.1 8.6 %collective-permute-start.32 = (bf16[2,48,768]{2,1,0:T(8,128)(2,1)S(1)}, bf16[2,48,768]{2,1,0:T(8,128)(2,1)S(1)}, u32[]{:S(2)}, u32[]{:S(2)}) collective-permute-start(bf16[2,48,768]{2,1,0:T(8,128)(2,1)S(1)} %get-tuple-element.313), channel_id=1, source_target_pairs={{0,1},{1,0},{2,3},{3,2},{4,5},{5,4},{6,7},{7,6},{8,9},{9,8},{10,11... | collective-permute-start | bytes 442376 | tf_op jit(solution)/shard_map/ppermute | solution.py:1614
  279.0 8.5 %collective-permute-start.33 = (bf16[2,48,1152]{2,1,0:T(8,128)(2,1)S(1)}, bf16[2,48,1152]{2,1,0:T(8,128)(2,1)S(1)}, u32[]{:S(2)}, u32[]{:S(2)}) collective-permute-start(bf16[2,48,1152]{2,1,0:T(8,128)(2,1)S(1)} %get-tuple-element.314), channel_id=1, source_target_pairs={{0,4},{4,0},{1,5},{5,1},{2,6},{6,2},{3,7},{7,3},{8,12},{12,8},{9,1... | collective-permute-start | bytes 663560 | tf_op jit(solution)/shard_map/ppermute | solution.py:32
  279.6 7.8 %collective-permute-start.34 = (bf16[1,96,768]{2,1,0:T(8,128)(2,1)S(1)}, bf16[1,96,768]{2,1,0:T(8,128)(2,1)S(1)}, u32[]{:S(2)}, u32[]{:S(2)}) collective-permute-start(bf16[1,96,768]{2,1,0:T(8,128)(2,1)S(1)} %get-tuple-element.315.refs_6_), channel_id=1, source_target_pairs={{0,16},{8,24},{16,0},{24,8},{1,17},{9,25},{17,1},{25,9},{2,18},{10... | collective-permute-start | bytes 442376 | tf_op jit(solution)/shard_map/ppermute | solution.py:32
  281.2 4.6 %collective-permute-start.35 = (f32[5,768]{1,0:T(8,128)S(1)}, f32[5,768]{1,0:T(8,128)S(1)}, u32[]{:S(2)}, u32[]{:S(2)}) collective-permute-start(f32[5,768]{1,0:T(8,128)S(1)} %add.146), channel_id=1, source_target_pairs={{0,8},{8,0},{16,24},{24,16},{1,9},{9,1},{17,25},{25,17},{2,10},{10... | collective-permute-start | bytes 46088 | tf_op jit(solution)/shard_map/ppermute | solution.py:32
  285.7 8.4 %collective-permute-start.37 = (bf16[256,768]{1,0:T(8,128)(2,1)S(1)}, bf16[256,768]{1,0:T(8,128)(2,1)S(1)}, u32[]{:S(2)}, u32[]{:S(2)}) collective-permute-start(bf16[256,768]{1,0:T(8,128)(2,1)S(1)} %get-tuple-element.326), channel_id=1, source_target_pairs={{0,1},{1,0},{2,3},{3,2},{4,5},{5,4},{6,7},{7,6},{8,9},{9,8},{10,11... | collective-permute-start | bytes 1179656 | tf_op jit(solution)/shard_map/ppermute | solution.py:1769
  287.6 13.2 %collective-permute-start.36 = (bf16[1,48,3072]{2,1,0:T(8,128)(2,1)S(1)}, bf16[1,48,3072]{2,1,0:T(8,128)(2,1)S(1)}, u32[]{:S(2)}, u32[]{:S(2)}) collective-permute-start(bf16[1,48,3072]{2,1,0:T(8,128)(2,1)S(1)} %get-tuple-element.324), channel_id=1, source_target_pairs={{0,16},{8,24},{16,0},{24,8},{1,17},{9,25},{17,1},{25,9},{2,18},{10... | collective-permute-start | bytes 884744 | tf_op jit(solution)/shard_map/ppermute | solution.py:32
  289.0 12.1 %collective-permute-start.38 = (bf16[2,96,768]{2,1,0:T(8,128)(2,1)S(1)}, bf16[2,96,768]{2,1,0:T(8,128)(2,1)S(1)}, u32[]{:S(2)}, u32[]{:S(2)}) collective-permute-start(bf16[2,96,768]{2,1,0:T(8,128)(2,1)S(1)} %get-tuple-element.328.refs_2_), channel_id=1, source_target_pairs={{0,8},{8,0},{16,24},{24,16},{1,9},{9,1},{17,25},{25,17},{2,10},{10... | collective-permute-start | bytes 884744 | tf_op jit(solution)/shard_map/ppermute | solution.py:32
  290.6 10.4 %collective-permute-start.39 = (f32[5,768]{1,0:T(8,128)S(1)}, f32[5,768]{1,0:T(8,128)S(1)}, u32[]{:S(2)}, u32[]{:S(2)}) collective-permute-start(f32[5,768]{1,0:T(8,128)S(1)} %add.147), channel_id=1, source_target_pairs={{0,16},{8,24},{16,0},{24,8},{1,17},{9,25},{17,1},{25,9},{2,18},{10... | collective-permute-start | bytes 46088 | tf_op jit(solution)/shard_map/ppermute | solution.py:32
  301.1 15.7 %collective-permute-start.42 = (bf16[4,96,768]{2,1,0:T(8,128)(2,1)S(1)}, bf16[4,96,768]{2,1,0:T(8,128)(2,1)S(1)}, u32[]{:S(2)}, u32[]{:S(2)}) collective-permute-start(bf16[4,96,768]{2,1,0:T(8,128)(2,1)S(1)} %get-tuple-element.335.refs_2_), channel_id=1, source_target_pairs={{0,4},{4,0},{1,5},{5,1},{2,6},{6,2},{3,7},{7,3},{8,12},{12,8},{9,1... | collective-permute-start | bytes 1769480 | tf_op jit(solution)/shard_map/ppermute | solution.py:32
  302.4 9.4 %collective-permute-start.41 = (bf16[256,768]{1,0:T(8,128)(2,1)S(1)}, bf16[256,768]{1,0:T(8,128)(2,1)S(1)}, u32[]{:S(2)}, u32[]{:S(2)}) collective-permute-start(bf16[256,768]{1,0:T(8,128)(2,1)S(1)} %get-tuple-element.333), channel_id=1, source_target_pairs={{0,1},{1,0},{2,3},{3,2},{4,5},{5,4},{6,7},{7,6},{8,9},{9,8},{10,11... | collective-permute-start | bytes 1179656 | tf_op jit(solution)/shard_map/ppermute | solution.py:1769
  303.3 13.5 %collective-permute-start.40 = (bf16[1,48,3072]{2,1,0:T(8,128)(2,1)S(1)}, bf16[1,48,3072]{2,1,0:T(8,128)(2,1)S(1)}, u32[]{:S(2)}, u32[]{:S(2)}) collective-permute-start(bf16[1,48,3072]{2,1,0:T(8,128)(2,1)S(1)} %get-tuple-element.332.refs_0_), channel_id=1, source_target_pairs={{0,16},{8,24},{16,0},{24,8},{1,17},{9,25},{17,1},{25,9},{2,18},{10... | collective-permute-start | bytes 884744 | tf_op jit(solution)/shard_map/ppermute | solution.py:32
  317.0 9.6 %collective-permute-start.45 = (bf16[8,96,768]{2,1,0:T(8,128)(2,1)S(1)}, bf16[8,96,768]{2,1,0:T(8,128)(2,1)S(1)}, u32[]{:S(2)}, u32[]{:S(2)}) collective-permute-start(bf16[8,96,768]{2,1,0:T(8,128)(2,1)S(1)} %get-tuple-element.346.part_ref), channel_id=1, source_target_pairs={{0,2},{2,0},{1,3},{3,1},{4,6},{6,4},{5,7},{7,5},{8,10},{10,8},{9,1... | collective-permute-start | bytes 3538952 | tf_op jit(solution)/shard_map/ppermute | solution.py:1528
  317.1 9.4 %collective-permute-start.43 = (bf16[2,48,1536]{2,1,0:T(8,128)(2,1)S(1)}, bf16[2,48,1536]{2,1,0:T(8,128)(2,1)S(1)}, u32[]{:S(2)}, u32[]{:S(2)}) collective-permute-start(bf16[2,48,1536]{2,1,0:T(8,128)(2,1)S(1)} %get-tuple-element.338.refs_0_), channel_id=1, source_target_pairs={{0,8},{8,0},{16,24},{24,16},{1,9},{9,1},{17,25},{25,17},{2,10},{10... | collective-permute-start | bytes 884744 | tf_op jit(solution)/shard_map/ppermute | solution.py:32
  317.1 9.4 %collective-permute-start.44 = (bf16[2,48,1536]{2,1,0:T(8,128)(2,1)S(1)}, bf16[2,48,1536]{2,1,0:T(8,128)(2,1)S(1)}, u32[]{:S(2)}, u32[]{:S(2)}) collective-permute-start(bf16[2,48,1536]{2,1,0:T(8,128)(2,1)S(1)} %get-tuple-element.339.refs_2_), channel_id=1, source_target_pairs={{0,4},{4,0},{1,5},{5,1},{2,6},{6,2},{3,7},{7,3},{8,12},{12,8},{9,1... | collective-permute-start | bytes 884744 | tf_op jit(solution)/shard_map/ppermute | solution.py:32
  326.6 14.9 %collective-permute-start.46 = (bf16[4,48,1536]{2,1,0:T(8,128)(2,1)S(1)}, bf16[4,48,1536]{2,1,0:T(8,128)(2,1)S(1)}, u32[]{:S(2)}, u32[]{:S(2)}) collective-permute-start(bf16[4,48,1536]{2,1,0:T(8,128)(2,1)S(1)} %get-tuple-element.343.refs_0_), channel_id=1, source_target_pairs={{0,4},{4,0},{1,5},{5,1},{2,6},{6,2},{3,7},{7,3},{8,12},{12,8},{9,1... | collective-permute-start | bytes 1769480 | tf_op jit(solution)/shard_map/ppermute | solution.py:32
  327.1 14.6 %collective-permute-start.47 = (bf16[4,48,1536]{2,1,0:T(8,128)(2,1)S(1)}, bf16[4,48,1536]{2,1,0:T(8,128)(2,1)S(1)}, u32[]{:S(2)}, u32[]{:S(2)}) collective-permute-start(bf16[4,48,1536]{2,1,0:T(8,128)(2,1)S(1)} %get-tuple-element.344.refs_2_), channel_id=1, source_target_pairs={{0,8},{8,0},{16,24},{24,16},{1,9},{9,1},{17,25},{25,17},{2,10},{10... | collective-permute-start | bytes 1769480 | tf_op jit(solution)/shard_map/ppermute | solution.py:32
  341.9 4.6 %collective-permute-start.48 = (bf16[8,48,3072]{2,1,0:T(8,128)(2,1)S(1)}, bf16[8,48,3072]{2,1,0:T(8,128)(2,1)S(1)}, u32[]{:S(2)}, u32[]{:S(2)}) collective-permute-start(bf16[8,48,3072]{2,1,0:T(8,128)(2,1)S(1)} %phase.17.part_ref), channel_id=1, source_target_pairs={{0,2},{2,0},{1,3},{3,1},{4,6},{6,4},{5,7},{7,5},{8,10},{10,8},{9,1... | collective-permute-start | bytes 7077896 | tf_op jit(solution)/shard_map/ppermute | solution.py:1528
  (30 other events, 81.7 us)
